TPU v7x, 32 devices: a whole 2x2x4 slice. The times are simulated.
32 devices in a mesh: blk: 8 (over z, x), mb: 4 (over y, core).
Axes of the slice: x: 2, y: 2, z: 4, core: 2. Of those that a mesh axis runs over, the one named last changes fastest.
Arguments:
- patches: bfloat16 [8, 1024, 1024], P('mb', 'blk'), may hold values from -6 to 6
- seg_lengths: int32 [8, 8], P('mb'), may hold values from 1 to 960, as said below
- w_query: bfloat16 [1024, 1024], replicated, may hold values from -0.1875 to 0.1875
- w_key: bfloat16 [1024, 1024], replicated, may hold values from -0.1875 to 0.1875
- w_value: bfloat16 [1024, 1024], replicated, may hold values from -0.1875 to 0.1875
- w_out: bfloat16 [1024, 1024], replicated, may hold values from -2 to 2
- w_up: bfloat16 [1024, 4096], replicated, may hold values from -0.1875 to 0.1875
- w_down: bfloat16 [4096, 1024], replicated, may hold values from -0.09375 to 0.09375
- norm1_gain: float32 [1024], replicated, may hold values from 0.25 to 1.75
- norm1_bias: float32 [1024], replicated, may hold values from -1.5 to 1.5
- norm2_gain: float32 [1024], replicated, may hold values from 0.25 to 1.75
- norm2_bias: float32 [1024], replicated, may hold values from -1.5 to 1.5
- out_grad: bfloat16 [8, 1024, 1024], P('mb', 'blk'), may hold values from -6 to 6
Outputs:
- layer_out: bfloat16 [8, 1024, 1024], P('mb', 'blk')
- patches_grad: bfloat16 [8, 1024, 1024], P('mb', 'blk')
- query_weight_grad: float32 [1024, 1024], P(('blk', 'mb'))
- key_weight_grad: float32 [1024, 1024], P(('blk', 'mb'))
- value_weight_grad: float32 [1024, 1024], P(('blk', 'mb'))
- out_weight_grad: float32 [1024, 1024], P(('blk', 'mb'))
- up_weight_grad: float32 [1024, 4096], P(('blk', 'mb'))
- down_weight_grad: float32 [4096, 1024], P(('blk', 'mb'))
- norm1_gain_grad: float32 [1024], P(('blk', 'mb'))
- norm1_bias_grad: float32 [1024], P(('blk', 'mb'))
- norm2_gain_grad: float32 [1024], P(('blk', 'mb'))
- norm2_bias_grad: float32 [1024], P(('blk', 'mb'))
Inputs may be any that keep to these rules, and one draw needn't show every extreme that they name: `seg_lengths`: row b lists the lengths of the 8 documents of micro-batch b, laid end to end from position 0; the positions after them, at most 128, are padding. Of the 2 rows on each index of mb, one holds a document of exactly 960 positions and no padding.
All inputs are finite; a program needn't handle non-finite values.
Results may differ from a plain program's by a relative error of at most 0.012.
Values may be sent and summed in bfloat16 or wider, within the bound.
No kernel may reach another device: no remote copies, remote signals or barrier semaphores. Data moves between devices by JAX's collectives and lax.ppermute only.
A program may use at most 256 MiB of HBM per device.

v0:
```python
import math

import jax
import jax.numpy as jnp
from jax import lax
from jax.sharding import PartitionSpec as P

H = 16


epsilon = 1e-05
masked_score = -1e30


def layer_norm(values, norm_gain, norm_bias):
    center = values - jnp.mean(values, axis=-1, keepdims=True)
    variance = jnp.mean(center * center, axis=-1, keepdims=True)
    return center * lax.rsqrt(variance + epsilon) * norm_gain + norm_bias


def gelu_exact(values):
    return jax.nn.gelu(values, approximate=False)


def matmul(left_side, right_side):
    return jnp.dot(left_side, right_side, preferred_element_type=jnp.float32)


def contract_rows(left_side, right_side):
    return lax.dot_general(
        left_side, right_side, (((0,), (0,)), ((), ())), preferred_element_type=jnp.float32
    )


def contract_cols(left_side, right_side):
    return lax.dot_general(
        left_side, right_side, (((1,), (1,)), ((), ())), preferred_element_type=jnp.float32
    )


def segment_ids(lengths, positions):
    doc_ends = jnp.cumsum(lengths, axis=-1)
    return jnp.sum((positions[None, :, None] >= doc_ends[:, None, :]).astype(jnp.int32), axis=-1)


def masked_scores(query_piece, keys_all, query_docs, key_docs, score_scale):
    scores = contract_cols(query_piece, keys_all) * score_scale
    return jnp.where(query_docs[:, None] == key_docs[None, :], scores, masked_score)


def soft_rows(scores):
    row_max = jnp.max(scores, axis=-1, keepdims=True)
    exponent = jnp.exp(scores - row_max)
    return exponent / jnp.sum(exponent, axis=-1, keepdims=True)


def body(
    patches,
    seg_lengths,
    w_query,
    w_key,
    w_value,
    w_out,
    w_up,
    w_down,
    norm1_gain,
    norm1_bias,
    norm2_gain,
    norm2_bias,
    out_grad,
):
    micro_count, tokens, features = patches.shape
    row_count = micro_count * tokens
    blocks = lax.axis_size("blk")
    block_index = lax.axis_index("blk")
    head_count = H
    head_dim = features // head_count
    repeat = max(1, blocks // head_count)
    per_slot = max(1, head_count // blocks)
    groups = head_count // per_slot
    rows_part = tokens // repeat
    query_rows = blocks * rows_part
    seq_length = blocks * tokens
    item_count = micro_count * per_slot
    block_rows = min(512, query_rows)
    block_count = query_rows // block_rows
    slot_width = micro_count * per_slot * head_dim
    score_scale = 1.0 / math.sqrt(head_dim)
    doc_count = seg_lengths.shape[1]

    def query_layout(values):
        shaped = values.reshape(micro_count, repeat, rows_part, groups, per_slot * head_dim)
        return shaped.transpose(3, 1, 2, 0, 4).reshape(blocks, rows_part, slot_width)

    def key_layout(values):
        shaped = values.reshape(micro_count, tokens, groups, per_slot * head_dim).transpose(
            2, 1, 0, 3
        )
        shaped = jnp.broadcast_to(
            shaped[:, None], (groups, repeat, tokens, micro_count, per_slot * head_dim)
        )
        return shaped.reshape(blocks, tokens, slot_width)

    def token_layout(values):
        shaped = values.reshape(groups, repeat, rows_part, micro_count, per_slot * head_dim)
        return shaped.transpose(3, 1, 2, 0, 4).reshape(row_count, features)

    def key_sum(values):
        shaped = values.reshape(groups, repeat, tokens, micro_count, per_slot * head_dim).sum(
            axis=1
        )
        return shaped.transpose(2, 1, 0, 3).reshape(row_count, features)

    def to_items(received):
        row_total = received.shape[1]
        shaped = received.reshape(row_total, micro_count, per_slot, head_dim).transpose(1, 2, 0, 3)
        return shaped.reshape(item_count, row_total, head_dim)

    def from_items(values):
        row_total = values.shape[1]
        shaped = values.reshape(micro_count, per_slot, row_total, head_dim).transpose(2, 0, 1, 3)
        return shaped.reshape(1, row_total, slot_width)

    row_ids = jnp.arange(query_rows)
    query_pos = (
        row_ids // rows_part * tokens + block_index % repeat * rows_part + row_ids % rows_part
    )
    query_docs = jnp.repeat(segment_ids(seg_lengths, query_pos), per_slot, axis=0)
    key_docs = jnp.repeat(segment_ids(seg_lengths, jnp.arange(seq_length)), per_slot, axis=0)
    query_valid = (query_docs < doc_count).astype(jnp.float32)
    local_pos = block_index * tokens + jnp.arange(tokens)
    row_valid = (
        (segment_ids(seg_lengths, local_pos) < doc_count).astype(jnp.float32).reshape(row_count, 1)
    )

    def forward_item(operands):
        queries_item, keys_item, values_item, docs_item, key_docs_item = operands

        def forward_one_block(block_operands):
            query_piece, docs_piece = block_operands
            weights_soft = soft_rows(
                masked_scores(query_piece, keys_item, docs_piece, key_docs_item, score_scale)
            )
            return matmul(weights_soft.astype(jnp.bfloat16), values_item)

        outputs = lax.map(
            forward_one_block,
            (
                queries_item.reshape(block_count, block_rows, head_dim),
                docs_item.reshape(block_count, block_rows),
            ),
        )
        return outputs.reshape(query_rows, head_dim)

    def backward_item(operands):
        queries_item, keys_item, values_item, grads_item, docs_item, key_docs_item = operands

        def backward_one_block(totals, block_operands):
            key_total, value_total = totals
            query_piece, grad_piece, docs_piece = block_operands
            weights_soft = soft_rows(
                masked_scores(query_piece, keys_item, docs_piece, key_docs_item, score_scale)
            )
            weights_low = weights_soft.astype(jnp.bfloat16)
            weight_grads = contract_cols(grad_piece, values_item)
            row_inner = jnp.sum(weights_soft * weight_grads, axis=-1, keepdims=True)
            score_grads = (weights_soft * (weight_grads - row_inner)).astype(jnp.bfloat16)
            query_grad = matmul(score_grads, keys_item) * score_scale
            key_total = key_total + contract_rows(score_grads, query_piece) * score_scale
            value_total = value_total + contract_rows(weights_low, grad_piece)
            return ((key_total, value_total), query_grad)

        zero_block = jnp.zeros((seq_length, head_dim), jnp.float32)
        totals, query_grads = lax.scan(
            backward_one_block,
            (zero_block, zero_block),
            (
                queries_item.reshape(block_count, block_rows, head_dim),
                grads_item.reshape(block_count, block_rows, head_dim),
                docs_item.reshape(block_count, block_rows),
            ),
        )
        return (query_grads.reshape(query_rows, head_dim), totals[0], totals[1])

    inputs = patches.astype(jnp.float32).reshape(row_count, features)
    norm_one_full, norm_one_pull = jax.vjp(layer_norm, inputs, norm1_gain, norm1_bias)
    norm_one = norm_one_full.astype(jnp.bfloat16)
    queries = matmul(norm_one, w_query).astype(jnp.bfloat16)
    keys_proj = matmul(norm_one, w_key).astype(jnp.bfloat16)
    values_proj = matmul(norm_one, w_value).astype(jnp.bfloat16)
    query_send = query_layout(queries)
    key_send = key_layout(keys_proj)
    value_send = key_layout(values_proj)
    query_heads, key_heads, value_heads = (
        lax.all_to_all(query_send, "blk", split_axis=0, concat_axis=1, tiled=True),
        lax.all_to_all(key_send, "blk", split_axis=0, concat_axis=1, tiled=True),
        lax.all_to_all(value_send, "blk", split_axis=0, concat_axis=1, tiled=True),
    )
    query_items = to_items(query_heads)
    key_items = to_items(key_heads)
    value_items = to_items(value_heads)
    attended_items = lax.map(
        forward_item, (query_items, key_items, value_items, query_docs, key_docs)
    )
    attended_items = (attended_items * query_valid[:, :, None]).astype(jnp.bfloat16)
    attended = token_layout(
        lax.all_to_all(from_items(attended_items), "blk", split_axis=1, concat_axis=0, tiled=True)
    )
    mixed_rows = inputs + matmul(attended, w_out)
    norm_two_full, norm_two_pull = jax.vjp(layer_norm, mixed_rows, norm2_gain, norm2_bias)
    norm_two = norm_two_full.astype(jnp.bfloat16)
    upper_proj = matmul(norm_two, w_up)
    active_full, gelu_pull = jax.vjp(gelu_exact, upper_proj)
    active = active_full.astype(jnp.bfloat16)
    result = mixed_rows + matmul(active, w_down)
    layer_out = result.astype(jnp.bfloat16).reshape(micro_count, tokens, features)
    dout_low = out_grad.reshape(row_count, features)
    down_grad = contract_rows(active, dout_low)
    active_grad = contract_cols(dout_low, w_down)
    upper_grad = gelu_pull(active_grad)[0].astype(jnp.bfloat16)
    up_grad = contract_rows(norm_two, upper_grad)
    norm_two_grad = contract_cols(upper_grad, w_up)
    mixed_part, gain_two_grad, bias_two_grad = norm_two_pull(norm_two_grad)
    mixed_grad = dout_low.astype(jnp.float32) + mixed_part
    mixed_low = mixed_grad.astype(jnp.bfloat16)
    out_proj_grad = contract_rows(attended, mixed_low)
    attended_grad = (contract_cols(mixed_low, w_out) * row_valid).astype(jnp.bfloat16)
    grad_send = query_layout(attended_grad)
    query_again, key_again, value_again, grad_heads = (
        lax.all_to_all(query_send, "blk", split_axis=0, concat_axis=1, tiled=True),
        lax.all_to_all(key_send, "blk", split_axis=0, concat_axis=1, tiled=True),
        lax.all_to_all(value_send, "blk", split_axis=0, concat_axis=1, tiled=True),
        lax.all_to_all(grad_send, "blk", split_axis=0, concat_axis=1, tiled=True),
    )
    back_queries = to_items(query_again)
    back_keys = to_items(key_again)
    back_values = to_items(value_again)
    grad_items = to_items(grad_heads)
    query_grad_items, key_grad_items, value_grad_items = lax.map(
        backward_item, (back_queries, back_keys, back_values, grad_items, query_docs, key_docs)
    )
    query_back, key_back, value_back = (
        lax.all_to_all(
            from_items(query_grad_items).astype(jnp.bfloat16),
            "blk",
            split_axis=1,
            concat_axis=0,
            tiled=True,
        ).astype(jnp.float32),
        lax.all_to_all(
            from_items(key_grad_items).astype(jnp.bfloat16),
            "blk",
            split_axis=1,
            concat_axis=0,
            tiled=True,
        ).astype(jnp.float32),
        lax.all_to_all(
            from_items(value_grad_items).astype(jnp.bfloat16),
            "blk",
            split_axis=1,
            concat_axis=0,
            tiled=True,
        ).astype(jnp.float32),
    )
    query_grad = token_layout(query_back).astype(jnp.bfloat16)
    key_grad = key_sum(key_back).astype(jnp.bfloat16)
    value_grad = key_sum(value_back).astype(jnp.bfloat16)
    query_proj_grad = contract_rows(norm_one, query_grad)
    key_proj_grad = contract_rows(norm_one, key_grad)
    value_proj_grad = contract_rows(norm_one, value_grad)
    norm_one_grad = (
        contract_cols(query_grad, w_query)
        + contract_cols(key_grad, w_key)
        + contract_cols(value_grad, w_value)
    )
    input_part, gain_one_grad, bias_one_grad = norm_one_pull(norm_one_grad)
    patches_grad = (
        (mixed_grad + input_part).astype(jnp.bfloat16).reshape(micro_count, tokens, features)
    )
    gradients = (
        query_proj_grad,
        key_proj_grad,
        value_proj_grad,
        out_proj_grad,
        up_grad,
        down_grad,
        gain_one_grad,
        bias_one_grad,
        gain_two_grad,
        bias_two_grad,
    )
    summed = (
        lax.psum_scatter(gradients[0], ("blk", "mb"), scatter_dimension=0, tiled=True),
        lax.psum_scatter(gradients[1], ("blk", "mb"), scatter_dimension=0, tiled=True),
        lax.psum_scatter(gradients[2], ("blk", "mb"), scatter_dimension=0, tiled=True),
        lax.psum_scatter(gradients[3], ("blk", "mb"), scatter_dimension=0, tiled=True),
        lax.psum_scatter(gradients[4], ("blk", "mb"), scatter_dimension=0, tiled=True),
        lax.psum_scatter(gradients[5], ("blk", "mb"), scatter_dimension=0, tiled=True),
        lax.psum_scatter(gradients[6], ("blk", "mb"), scatter_dimension=0, tiled=True),
        lax.psum_scatter(gradients[7], ("blk", "mb"), scatter_dimension=0, tiled=True),
        lax.psum_scatter(gradients[8], ("blk", "mb"), scatter_dimension=0, tiled=True),
        lax.psum_scatter(gradients[9], ("blk", "mb"), scatter_dimension=0, tiled=True),
    )
    return (
        layer_out,
        patches_grad,
        summed[0],
        summed[1],
        summed[2],
        summed[3],
        summed[4],
        summed[5],
        summed[6],
        summed[7],
        summed[8],
        summed[9],
    )


def solution(mesh):
    in_specs = (
        P("mb", "blk", None),
        P("mb", None),
        P(),
        P(),
        P(),
        P(),
        P(),
        P(),
        P(),
        P(),
        P(),
        P(),
        P("mb", "blk", None),
    )
    out_specs = (
        P("mb", "blk", None),
        P("mb", "blk", None),
        P(("blk", "mb"), None),
        P(("blk", "mb"), None),
        P(("blk", "mb"), None),
        P(("blk", "mb"), None),
        P(("blk", "mb"), None),
        P(("blk", "mb"), None),
        P(("blk", "mb")),
        P(("blk", "mb")),
        P(("blk", "mb")),
        P(("blk", "mb")),
    )
    return jax.shard_map(body, mesh=mesh, in_specs=in_specs, out_specs=out_specs, check_vma=False)
```

profile of v0, /device:TPU:0, one launch (start us, length us, event | category | flops | bytes accessed | tf_op | source)
XLA Modules:
  0.0 1129.3 jit_solution(15537120136822141253)
XLA Ops:
  13.8 7.3 all-to-all-start.2
  24.6 10.9 all-to-all-done.2
  44.6 9.2 all-to-all-done.1
  78.7 29.5 %while.56 = (s32[]{:T(128)}, f32[4,1024,64]{2,1,0:T(8,128)}, bf16[4,1024,64]{2,1,0:T(8,128)(2,1)}, s32[4,1024]{1,0:T(4,128)}, bf16[4,1024,64]{2,1,0:T(8,128)(2,1...) while((s32[]{:T(128)}, f32[4,1024,64]{2,1,0:T(8,128)}, ...), condition=%wide.region_10.11_spmd.clone, body=%wide.region_5.10_spmd.sunk.clone | while | flops 138935296 | bytes 9220390 | solution.py:202
  124.9 14.4 %all-to-all-done.3 = bf16[8,2,16384]{2,1,0:T(2,128)(2,1)S(1)} async-done(((bf16[8,2,16384]{2,1,0:T(2,128)(2,1)}), bf16[8,2,16384]{2,1,0:T(2,128)(2,1)S(1)}, u32[]{:S(2)}, u32[]{:S(2)}) %all-to-all-start.3) | async-done | bytes 524320 | tf_op jit(solution)/shard_map/all_to_all | solution.py:207
  150.7 6.0 fusion.74
  156.7 13.3 %add_convert_fusion = (bf16[256,4096]{1,0:T(8,128)(2,1)S(1)}, f32[256,4096]{1,0:T(8,128)}) fusion(f32[256,4096]{1,0:T(8,128)S(1)} %fusion.74, bf16[256,1024]{1,0:T(8,128)(2,1)S(1)} %bitcast.323, bf16[4096,1024]{1,0:T(8,128)(2,1)S(1)} %bitcast.351), kind=kOutput, calls=%fused_computation.54 | convolution fusion | flops 2222981120 | bytes 19398656 | tf_op jit(solution)/shard_map/dot_general | solution.py:36
  187.2 9.7 all-to-all-done.4
  198.2 63.4 %while.58 = (s32[]{:T(128)}, bf16[4,1024,64]{2,1,0:T(8,128)(2,1)}, bf16[4,1024,64]{1,2,0:T(8,128)(2,1)}, bf16[4,1024,64]{1,2,0:T(8,128)(2,1)}, bf16[4,1024,64]{2...) while((s32[]{:T(128)}, bf16[4,1024,64]{2,1,0:T(8,128)(2,1)}, ...), condition=%wide.region_22.23_spmd.clone, body=%wide.region_16.22_spmd.sunk.clone | while | flops 345340416 | bytes 25485788 | solution.py:239
  203.9 7.7 while.57
  219.7 7.7 while.57
  235.5 7.7 while.57
  251.3 7.7 while.57
  275.5 15.6 %all-to-all-done.7 = bf16[8,2,16384]{2,1,0:T(2,128)(2,1)} async-done(((bf16[8,2,16384]{2,1,0:T(2,128)(2,1)}), bf16[8,2,16384]{2,1,0:T(2,128)(2,1)}, u32[]{:S(2)}, u32[]{:S(2)}) %all-to-all-start.7) | async-done | bytes 524320 | tf_op jit(solution)/shard_map/all_to_all | solution.py:257
  317.9 17.3 %all_to_all.32 = bf16[8,2,16384]{2,1,0:T(2,128)(2,1)} all-to-all(bf16[8,2,16384]{2,1,0:T(2,128)(2,1)} %reshape.488), channel_id=1, replica_groups=mesh['blk'=8,'mb'=4] {'blk'}, dimensions={0} | all-to-all | bytes 1048576 | tf_op jit(solution)/shard_map/all_to_all | solution.py:250
  364.1 20.8 %all_to_all.33 = bf16[8,2,16384]{2,1,0:T(2,128)(2,1)} all-to-all(bf16[8,2,16384]{2,1,0:T(2,128)(2,1)} %reshape.486), channel_id=1, replica_groups=mesh['blk'=8,'mb'=4] {'blk'}, dimensions={0} | all-to-all | bytes 1048576 | tf_op jit(solution)/shard_map/all_to_all | solution.py:243
  400.5 10.1 fusion.73
  416.5 8.1 fusion.81
  424.7 7.5 fusion.31
  437.1 39.6 %all-reduce.4 = (f32[1024]{0:T(1024)S(1)}, f32[1024]{0:T(1024)S(1)}, f32[1024]{0:T(1024)S(1)}, f32[1024]{0:T(1024)S(1)}) all-reduce(f32[1024]{0:T(1024)S(1)} %get-tuple-element.328, f32[1024]{0:T(1024)S(1)} %get-tuple-element.331, f32[1024]{0:T(1024)S(1)} %copy-done.44, ...), channel_id=8, replica_groups=mesh['blk'=8,'mb'=4] {'blk','mb'}, use_global_device_ids=true, to_apply=%region_32.33.clone | all-reduce | flops 4096 | bytes 32768
  481.9 131.5 %reduce-scatter.9.cloned.1.call-done = f32[32,1024]{1,0:T(8,128)} async-done(((f32[1024,1024]{1,0:T(8,128)}), f32[32,1024]{1,0:T(8,128)}) %reduce-scatter.9.cloned.1.call-update) | async-done | bytes 131088 | tf_op jit(solution)/shard_map/reduce_scatter | solution.py:294
  613.4 139.9 %reduce-scatter.7.cloned.1.call-done = f32[32,1024]{1,0:T(8,128)} async-done(((f32[1024,1024]{1,0:T(8,128)}), f32[32,1024]{1,0:T(8,128)}) %reduce-scatter.7.cloned.1.call-update) | async-done | bytes 131088 | tf_op jit(solution)/shard_map/reduce_scatter | solution.py:293
  753.3 181.6 %reduce-scatter.15.cloned.1.call-done = f32[32,4096]{1,0:T(8,128)} async-done(((f32[1024,4096]{1,0:T(8,128)}), f32[32,4096]{1,0:T(8,128)}) %reduce-scatter.15.cloned.1.call-update) | async-done | bytes 524304 | tf_op jit(solution)/shard_map/reduce_scatter | solution.py:297
  934.9 187.3 %reduce-scatter.17.cloned.1.call-done = f32[128,1024]{1,0:T(8,128)} async-done(((f32[4096,1024]{1,0:T(8,128)}), f32[128,1024]{1,0:T(8,128)}) %reduce-scatter.17.cloned.1.call-update) | async-done | bytes 524304 | tf_op jit(solution)/shard_map/reduce_scatter | solution.py:298
  (438 shorter events, 296.6 us)
Async XLA Ops:
  13.8 21.7 %all-to-all-start.2 = ((bf16[8,128,256]{1,2,0:T(8,128)(2,1)}), bf16[8,128,256]{1,2,0:T(8,128)(2,1)S(1)}, u32[]{:S(2)}, u32[]{:S(2)}) async-start(bf16[8,128,256]{1,2,0:T(8,128)(2,1)} %bitcast.28), calls=%async_computation.2 | async-start | bytes 1048576 | tf_op jit(solution)/shard_map/all_to_all | solution.py:197
  23.4 34.8 %copy-start.46 = (s32[2,8]{1,0:T(2,128)S(1)}, s32[2,8]{1,0:T(2,128)}, u32[]{:S(2)}) copy-start(s32[2,8]{1,0:T(2,128)} %param.22) | copy-start | bytes 196
  35.5 18.3 %all-to-all-start.1 = ((bf16[8,128,256]{1,2,0:T(8,128)(2,1)}), bf16[8,128,256]{1,2,0:T(8,128)(2,1)S(1)}, u32[]{:S(2)}, u32[]{:S(2)}) async-start(bf16[8,128,256]{1,2,0:T(8,128)(2,1)} %bitcast.336), calls=%async_computation.1 | async-start | bytes 1048576 | tf_op jit(solution)/shard_map/all_to_all | solution.py:196
  53.8 18.7 %all-to-all-start = ((bf16[8,128,256]{1,2,0:T(8,128)(2,1)}), bf16[8,128,256]{1,2,0:T(8,128)(2,1)}, u32[]{:S(2)}, u32[]{:S(2)}) async-start(bf16[8,128,256]{1,2,0:T(8,128)(2,1)} %bitcast.334), calls=%async_computation | async-start | bytes 1048576 | tf_op jit(solution)/shard_map/all_to_all | solution.py:195
  114.9 32.8 %copy-start.1 = (bf16[2,128,1024]{2,1,0:T(8,128)(2,1)S(1)}, bf16[2,128,1024]{2,1,0:T(8,128)(2,1)}, u32[]{:S(2)}) copy-start(bf16[2,128,1024]{2,1,0:T(8,128)(2,1)} %param.21) | copy-start | bytes 1572868
  120.7 18.7 %all-to-all-start.3 = ((bf16[8,2,16384]{2,1,0:T(2,128)(2,1)}), bf16[8,2,16384]{2,1,0:T(2,128)(2,1)S(1)}, u32[]{:S(2)}, u32[]{:S(2)}) async-start(bf16[8,2,16384]{2,1,0:T(2,128)(2,1)} %reshape.484), calls=%async_computation.3 | async-start | bytes 1048576 | tf_op jit(solution)/shard_map/all_to_all | solution.py:207
  150.3 24.3 %copy-start.3 = (f32[256,1024]{1,0:T(8,128)}, f32[256,1024]{1,0:T(8,128)S(1)}, u32[]{:S(2)}) copy-start(f32[256,1024]{1,0:T(8,128)S(1)} %get-tuple-element.426) | copy-start | bytes 3145732
  150.3 24.3 %copy-start.29 = (f32[256]{0:T(256)}, f32[256]{0:T(256)S(1)}, u32[]{:S(2)}) copy-start(f32[256]{0:T(256)S(1)} %broadcast_multiply_fusion) | copy-start | bytes 3076
  150.6 24.0 %copy-start.33 = (f32[256]{0:T(256)}, f32[256]{0:T(256)S(1)}, u32[]{:S(2)}) copy-start(f32[256]{0:T(256)S(1)} %fusion.69) | copy-start | bytes 3076
  150.6 20.7 %slice-start = ((s8[8388608]{0:T(1024)(128)(4,1)}), s8[4194304]{0:T(1024)(128)(4,1)S(1)}, s32[]{:S(2)}) async-start(s8[8388608]{0:T(1024)(128)(4,1)} %bitcast.348), calls=%async_computation.20 | async-start | bytes 8388608
  156.7 14.7 %slice-start.1 = ((s8[8388608]{0:T(1024)(128)(4,1)}), s8[4194304]{0:T(1024)(128)(4,1)S(1)}, s32[]{:S(2)}) async-start(s8[8388608]{0:T(1024)(128)(4,1)} %bitcast.348), calls=%async_computation.21 | async-start | bytes 8388608
  178.6 18.3 %all-to-all-start.4 = ((bf16[8,128,256]{1,2,0:T(8,128)(2,1)}), bf16[8,128,256]{1,2,0:T(8,128)(2,1)S(1)}, u32[]{:S(2)}, u32[]{:S(2)}) async-start(bf16[8,128,256]{1,2,0:T(8,128)(2,1)} %bitcast.335), calls=%async_computation.4 | async-start | bytes 1048576 | tf_op jit(solution)/shard_map/all_to_all | solution.py:233
  182.2 299.7 %reduce-scatter.13.cloned.1.call-start = ((), (), s32[]{:S(2)}) async-start(), calls=%async_computation.17 | async-start | bytes 4325376 | tf_op jit(solution)/shard_map/reduce_scatter | solution.py:296
  261.6 13.6 %copy-start.2 = (bf16[2,128,1024]{2,1,0:T(8,128)(2,1)S(1)}, bf16[2,128,1024]{2,1,0:T(8,128)(2,1)}, u32[]{:S(2)}) copy-start(bf16[2,128,1024]{2,1,0:T(8,128)(2,1)} %param.21) | copy-start | bytes 1572868
  261.6 13.6 %copy-start.28 = (f32[1024]{0:T(1024)S(1)}, f32[1024]{0:T(1024)}, u32[]{:S(2)}) copy-start(f32[1024]{0:T(1024)} %param.29) | copy-start | bytes 12292
  261.6 13.6 %copy-start.35 = (f32[1024]{0:T(1024)S(1)}, f32[1024]{0:T(1024)}, u32[]{:S(2)}) copy-start(f32[1024]{0:T(1024)} %param.30) | copy-start | bytes 12292
  261.6 13.6 %copy-start.41 = (f32[2,128]{1,0:T(2,128)S(1)}, f32[2,128]{1,0:T(2,128)}, u32[]{:S(2)}) copy-start(f32[2,128]{1,0:T(2,128)} %copy-done.40) | copy-start | bytes 3076
  271.0 20.2 %all-to-all-start.7 = ((bf16[8,2,16384]{2,1,0:T(2,128)(2,1)}), bf16[8,2,16384]{2,1,0:T(2,128)(2,1)}, u32[]{:S(2)}, u32[]{:S(2)}) async-start(bf16[8,2,16384]{2,1,0:T(2,128)(2,1)} %reshape.490), calls=%async_computation.7 | async-start | bytes 1048576 | tf_op jit(solution)/shard_map/all_to_all | solution.py:257
  275.1 206.8 %reduce-scatter.11.cloned.1.call-start = ((), (), s32[]{:S(2)}) async-start(), calls=%async_computation.16 | async-start | bytes 4325376 | tf_op jit(solution)/shard_map/reduce_scatter | solution.py:295
  306.6 306.8 %reduce-scatter.9.cloned.1.call-start = ((), (), s32[]{:S(2)}) async-start(), calls=%async_computation.15 | async-start | bytes 4325376 | tf_op jit(solution)/shard_map/reduce_scatter | solution.py:294
  350.6 402.7 %reduce-scatter.7.cloned.1.call-start = ((), (), s32[]{:S(2)}) async-start(), calls=%async_computation.14 | async-start | bytes 4325376 | tf_op jit(solution)/shard_map/reduce_scatter | solution.py:293
  400.4 534.5 %reduce-scatter.15.cloned.1.call-start = ((), (), s32[]{:S(2)}) async-start(), calls=%async_computation.18 | async-start | bytes 17301504 | tf_op jit(solution)/shard_map/reduce_scatter | solution.py:297
  410.6 711.6 %reduce-scatter.17.cloned.1.call-start = ((), (), s32[]{:S(2)}) async-start(), calls=%async_computation.19 | async-start | bytes 17301504 | tf_op jit(solution)/shard_map/reduce_scatter | solution.py:298
  434.6 44.5 %copy-start.43 = (f32[256]{0:T(256)S(1)}, f32[256]{0:T(256)}, u32[]{:S(2)}) copy-start(f32[256]{0:T(256)} %copy-done.42) | copy-start | bytes 3076
  (53 other events, 166.6 us)
Sparse Core Ops, SparseCore 0:
  187.3 144.5 reduce-scatter.12
  334.7 138.1 reduce-scatter.10
  475.8 137.6 reduce-scatter.8
  616.1 137.1 reduce-scatter.6
  756.0 178.8 reduce-scatter.14
  937.6 184.5 reduce-scatter.16
where the time goes:
time: 1140 us; the launch traced here: 1130 us
  waiting for transfers between devices  706 us (62%)
  local copies, waits for them, and re-layouts  148 us (13%)
  matrix products  102 us (9%)
  blocking collectives  77.7 us (7%)
  other arithmetic  51 us (4%)
  starting transfers between devices  27.7 us (2%)
  between operations  15.1 us (1%)
    reduce_scatter x1, waiting for transfers between devices, body(): lax.psum_scatter(gradients[5], ('blk', 'mb'), scatter_dimension=0, tiled=...  187 us
    reduce_scatter x1, waiting for transfers between devices, body(): lax.psum_scatter(gradients[4], ('blk', 'mb'), scatter_dimension=0, tiled=...  182 us
    reduce_scatter x1, waiting for transfers between devices, body(): lax.psum_scatter(gradients[0], ('blk', 'mb'), scatter_dimension=0, tiled=...  140 us
    reduce_scatter x1, waiting for transfers between devices, body(): lax.psum_scatter(gradients[1], ('blk', 'mb'), scatter_dimension=0, tiled=...  131 us
    unnamed x1, blocking collectives  39.6 us
    dot_general x22, matrix products, contract_rows(): lax.dot_general(left_side, right_side, (((0,), (0,)), ((), ())), preferre...  38.1 us
    dot_general x30, matrix products, contract_cols(): lax.dot_general(left_side, right_side, (((1,), (1,)), ((), ())), preferre...  33.9 us
    unnamed x115, local copies, waits for them, and re-layouts  30.9 us
  transfers between devices with their start and end apart: 12, of which 10 were waited for; matrix products, arithmetic and copies ran while one was open for 18% of the time, Pallas kernels for 0%

commit v1 on v0

--- a/solution.py
+++ b/solution.py
@@ -3,6 +3,8 @@
 import jax
 import jax.numpy as jnp
 from jax import lax
+from jax.experimental import pallas as pl
+from jax.experimental.pallas import tpu as pltpu
 from jax.sharding import PartitionSpec as P
 
 H = 16
@@ -317,6 +319,623 @@
     )
 
 
+def _normalize(values):
+    center = values - jnp.mean(values, axis=-1, keepdims=True)
+    variance = jnp.mean(center * center, axis=-1, keepdims=True)
+    inverse = lax.rsqrt(variance + epsilon)
+    return center * inverse, inverse
+
+
+def _normalize_back(grads, gain, unit, inverse):
+    scaled = grads * gain
+    mean_scaled = jnp.mean(scaled, axis=-1, keepdims=True)
+    mean_product = jnp.mean(scaled * unit, axis=-1, keepdims=True)
+    return (scaled - mean_scaled - unit * mean_product) * inverse
+
+
+def _doc_ids(lengths_ref, micro, doc_count, positions):
+    end = jnp.int32(0)
+    ids = jnp.zeros_like(positions)
+    for doc in range(doc_count):
+        end = end + lengths_ref[micro, doc]
+        ids = ids + (positions >= end).astype(jnp.int32)
+    return ids
+
+
+def _params(mib):
+    return pltpu.CompilerParams(vmem_limit_bytes=mib << 20)
+
+
+def _cost(flops, moved, exps=0):
+    return pl.CostEstimate(flops=int(flops), bytes_accessed=int(moved), transcendentals=int(exps))
+
+
+def project_call(rows, gain, bias, w_query, w_key, w_value, blocks):
+    row_count, features = rows.shape
+    slot = features // blocks
+    per_step = max(1, min(blocks, 256 // slot))
+    wide = slot * per_step
+
+    def kernel(rows_ref, gain_ref, bias_ref, wq_ref, wk_ref, wv_ref, send_ref, norm_ref):
+        @pl.when(pl.program_id(0) == 0)
+        def _():
+            unit, _unused = _normalize(rows_ref[...].astype(jnp.float32))
+            norm_ref[...] = (unit * gain_ref[...] + bias_ref[...]).astype(jnp.bfloat16)
+
+        for part, weight_ref in enumerate((wq_ref, wk_ref, wv_ref)):
+            made = matmul(norm_ref[...], weight_ref[...]).astype(jnp.bfloat16)
+            for piece in range(per_step):
+                send_ref[piece, :, part * slot : (part + 1) * slot] = made[
+                    :, piece * slot : (piece + 1) * slot
+                ]
+
+    whole = pl.BlockSpec((row_count, features), lambda i: (0, 0))
+    vector = pl.BlockSpec((1, features), lambda i: (0, 0))
+    columns = pl.BlockSpec((features, wide), lambda i: (0, i))
+    return pl.pallas_call(
+        kernel,
+        grid=(blocks // per_step,),
+        in_specs=[whole, vector, vector, columns, columns, columns],
+        out_specs=[pl.BlockSpec((per_step, row_count, 3 * slot), lambda i: (i, 0, 0)), whole],
+        out_shape=[
+            jax.ShapeDtypeStruct((blocks, row_count, 3 * slot), jnp.bfloat16),
+            jax.ShapeDtypeStruct((row_count, features), jnp.bfloat16),
+        ],
+        compiler_params=_params(40),
+        cost_estimate=_cost(6 * row_count * features * features, 6 * features * features + 4 * row_count * features),
+        name="project",
+    )(rows, gain, bias, w_query, w_key, w_value)
+
+
+def _head_masks(slot, head_dim, dtype):
+    lanes = lax.broadcasted_iota(jnp.int32, (1, slot), 1)
+    return [(lanes // head_dim == head).astype(dtype) for head in range(slot // head_dim)]
+
+
+def attend_call(received, lengths, head_dim):
+    blocks, micro_count, tokens, width = received.shape
+    slot = width // 3
+    seq = blocks * tokens
+    doc_count = lengths.shape[1]
+    step_blocks = max(1, min(blocks, 256 // tokens))
+    rows = step_blocks * tokens
+    scale = 1.0 / math.sqrt(head_dim)
+
+    def kernel(lengths_ref, data_ref, out_ref):
+        micro = pl.program_id(0)
+        step = pl.program_id(1)
+        key_docs = _doc_ids(lengths_ref, micro, doc_count, lax.broadcasted_iota(jnp.int32, (1, seq), 1))
+        row_docs = _doc_ids(
+            lengths_ref, micro, doc_count, lax.broadcasted_iota(jnp.int32, (rows, 1), 0) + step * rows
+        )
+        same = row_docs == key_docs
+        queries = data_ref[pl.ds(step * step_blocks, step_blocks), 0, :, 0:slot].reshape(rows, slot)
+        keys = data_ref[:, 0, :, slot : 2 * slot].reshape(seq, slot)
+        values = data_ref[:, 0, :, 2 * slot : 3 * slot].reshape(seq, slot)
+        queries = queries * scale
+        total = jnp.zeros((rows, slot), jnp.float32)
+        for mask, mask_wide in zip(
+            _head_masks(slot, head_dim, jnp.bfloat16), _head_masks(slot, head_dim, jnp.float32)
+        ):
+            scores = jnp.where(same, contract_cols(queries * mask, keys), masked_score)
+            exponent = jnp.exp(scores - jnp.max(scores, axis=-1, keepdims=True))
+            share = 1.0 / jnp.sum(exponent, axis=-1, keepdims=True)
+            total = total + matmul(exponent.astype(jnp.bfloat16), values) * (share * mask_wide)
+        total = jnp.where(row_docs < doc_count, total, 0.0)
+        out_ref[...] = total.astype(jnp.bfloat16).reshape(step_blocks, 1, tokens, slot)
+
+    items = micro_count * slot // head_dim
+    return pl.pallas_call(
+        kernel,
+        grid=(micro_count, blocks // step_blocks),
+        in_specs=[
+            pl.BlockSpec(memory_space=pltpu.SMEM),
+            pl.BlockSpec((blocks, 1, tokens, width), lambda m, s: (0, m, 0, 0)),
+        ],
+        out_specs=pl.BlockSpec((step_blocks, 1, tokens, slot), lambda m, s: (s, m, 0, 0)),
+        out_shape=jax.ShapeDtypeStruct((blocks, micro_count, tokens, slot), jnp.bfloat16),
+        compiler_params=_params(40),
+        cost_estimate=_cost(16 * items * seq * seq * head_dim, 8 * seq * micro_count * slot, items * seq * seq),
+        name="attend",
+    )(lengths, received)
+
+
+def attend_back_call(received, grads, lengths, head_dim):
+    blocks, micro_count, tokens, width = received.shape
+    slot = width // 3
+    seq = blocks * tokens
+    doc_count = lengths.shape[1]
+    step_blocks = max(1, min(blocks, 256 // tokens))
+    rows = step_blocks * tokens
+    steps = blocks // step_blocks
+    scale = 1.0 / math.sqrt(head_dim)
+
+    def kernel(lengths_ref, data_ref, grads_ref, out_ref, key_total, value_total):
+        micro = pl.program_id(0)
+        step = pl.program_id(1)
+
+        @pl.when(step == 0)
+        def _():
+            key_total[...] = jnp.zeros_like(key_total)
+            value_total[...] = jnp.zeros_like(value_total)
+
+        key_docs = _doc_ids(lengths_ref, micro, doc_count, lax.broadcasted_iota(jnp.int32, (seq, 1), 0))
+        row_docs = _doc_ids(
+            lengths_ref, micro, doc_count, lax.broadcasted_iota(jnp.int32, (1, rows), 1) + step * rows
+        )
+        column_docs = _doc_ids(
+            lengths_ref, micro, doc_count, lax.broadcasted_iota(jnp.int32, (rows, 1), 0) + step * rows
+        )
+        same = row_docs == key_docs
+        queries = data_ref[pl.ds(step * step_blocks, step_blocks), 0, :, 0:slot].reshape(rows, slot)
+        keys = data_ref[:, 0, :, slot : 2 * slot].reshape(seq, slot)
+        values = data_ref[:, 0, :, 2 * slot : 3 * slot].reshape(seq, slot)
+        queries = queries * scale
+        out_grads = grads_ref[...].reshape(rows, slot)
+        out_grads = out_grads * (column_docs < doc_count).astype(jnp.float32).astype(jnp.bfloat16)
+        query_total = jnp.zeros((rows, slot), jnp.float32)
+        for mask, mask_wide in zip(
+            _head_masks(slot, head_dim, jnp.bfloat16), _head_masks(slot, head_dim, jnp.float32)
+        ):
+            queries_head = queries * mask
+            grads_head = out_grads * mask
+            scores = jnp.where(same, contract_cols(keys, queries_head), masked_score)
+            exponent = jnp.exp(scores - jnp.max(scores, axis=0, keepdims=True))
+            probs = exponent * (1.0 / jnp.sum(exponent, axis=0, keepdims=True))
+            prob_grads = contract_cols(values, grads_head)
+            inner = jnp.sum(probs * prob_grads, axis=0, keepdims=True)
+            score_grads = (probs * (prob_grads - inner)).astype(jnp.bfloat16)
+            value_total[...] += matmul(probs.astype(jnp.bfloat16), grads_head)
+            key_total[...] += matmul(score_grads, queries_head)
+            query_total = query_total + contract_rows(score_grads, keys) * mask_wide
+        out_ref[pl.ds(step * step_blocks, step_blocks), 0, :, 0:slot] = (
+            (query_total * scale).astype(jnp.bfloat16).reshape(step_blocks, tokens, slot)
+        )
+
+        @pl.when(step == steps - 1)
+        def _():
+            out_ref[:, 0, :, slot : 2 * slot] = (
+                key_total[...].astype(jnp.bfloat16).reshape(blocks, tokens, slot)
+            )
+            out_ref[:, 0, :, 2 * slot : 3 * slot] = (
+                value_total[...].astype(jnp.bfloat16).reshape(blocks, tokens, slot)
+            )
+
+    items = micro_count * slot // head_dim
+    return pl.pallas_call(
+        kernel,
+        grid=(micro_count, steps),
+        in_specs=[
+            pl.BlockSpec(memory_space=pltpu.SMEM),
+            pl.BlockSpec((blocks, 1, tokens, width), lambda m, s: (0, m, 0, 0)),
+            pl.BlockSpec((step_blocks, 1, tokens, slot), lambda m, s: (s, m, 0, 0)),
+        ],
+        out_specs=pl.BlockSpec((blocks, 1, tokens, width), lambda m, s: (0, m, 0, 0)),
+        out_shape=jax.ShapeDtypeStruct(received.shape, jnp.bfloat16),
+        scratch_shapes=[pltpu.VMEM((seq, slot), jnp.float32), pltpu.VMEM((seq, slot), jnp.float32)],
+        compiler_params=_params(48),
+        cost_estimate=_cost(40 * items * seq * seq * head_dim, 14 * seq * micro_count * slot, items * seq * seq),
+        name="attend_back",
+    )(lengths, received, grads)
+
+
+def middle_call(attended, rows, out_grad, gain, bias, w_out, w_up, w_down):
+    blocks, row_count, slot = attended.shape
+    features = rows.shape[1]
+    hidden = w_up.shape[1]
+    wide = min(512, hidden)
+    steps = hidden // wide
+    acts_width = 2 * hidden + 3 * features
+
+    def kernel(
+        att_ref, rows_ref, grad_ref, gain_ref, bias_ref, wo_ref, wu_ref, wd_ref,
+        out_ref, acts_ref, mixed_grad_ref, back_ref, sums_ref,
+        mixed, inverse, total, grad_total,
+    ):
+        step = pl.program_id(0)
+        norm_at, att_at, low_at = 2 * hidden, 2 * hidden + features, 2 * hidden + 2 * features
+
+        @pl.when(step == 0)
+        def _():
+            for block in range(blocks):
+                acts_ref[:, att_at + block * slot : att_at + (block + 1) * slot] = att_ref[block]
+            value = rows_ref[...].astype(jnp.float32) + matmul(
+                acts_ref[:, att_at : att_at + features], wo_ref[...]
+            )
+            mixed[...] = value
+            unit, scale = _normalize(value)
+            inverse[...] = scale
+            acts_ref[:, norm_at : norm_at + features] = (unit * gain_ref[...] + bias_ref[...]).astype(jnp.bfloat16)
+            total[...] = jnp.zeros_like(total)
+            grad_total[...] = jnp.zeros_like(grad_total)
+
+        upper = matmul(acts_ref[:, norm_at : norm_at + features], wu_ref[...])
+        active_grad = contract_cols(grad_ref[...], wd_ref[...])
+        half = (1.0 + lax.erf(upper * (1.0 / math.sqrt(2.0)))) * 0.5
+        active = (upper * half).astype(jnp.bfloat16)
+        slope = half + upper * jnp.exp(upper * upper * -0.5) * (1.0 / math.sqrt(2.0 * math.pi))
+        upper_grad = (active_grad * slope).astype(jnp.bfloat16)
+        acts_ref[:, pl.ds(pl.multiple_of(step * wide, wide), wide)] = active
+        acts_ref[:, pl.ds(pl.multiple_of(hidden + step * wide, wide), wide)] = upper_grad
+        total[...] += matmul(active, wd_ref[...])
+        grad_total[...] += contract_cols(upper_grad, wu_ref[...])
+
+        @pl.when(step == steps - 1)
+        def _():
+            out_ref[...] = (mixed[...] + total[...]).astype(jnp.bfloat16)
+            unit = (mixed[...] - jnp.mean(mixed[...], axis=-1, keepdims=True)) * inverse[...]
+            grads = grad_total[...]
+            sums_ref[0:1, :] = jnp.sum(grads * unit, axis=0, keepdims=True)
+            sums_ref[1:2, :] = jnp.sum(grads, axis=0, keepdims=True)
+            mixed_grad = grad_ref[...].astype(jnp.float32) + _normalize_back(grads, gain_ref[...], unit, inverse[...])
+            mixed_grad_ref[...] = mixed_grad
+            low = mixed_grad.astype(jnp.bfloat16)
+            acts_ref[:, low_at : low_at + features] = low
+            back = contract_cols(low, wo_ref[...]).astype(jnp.bfloat16)
+            for block in range(blocks):
+                back_ref[block] = back[:, block * slot : (block + 1) * slot]
+
+    def fixed(*shape):
+        return pl.BlockSpec(shape, lambda i: (0,) * len(shape))
+
+    return pl.pallas_call(
+        kernel,
+        grid=(steps,),
+        in_specs=[
+            fixed(blocks, row_count, slot),
+            fixed(row_count, features),
+            fixed(row_count, features),
+            fixed(1, features),
+            fixed(1, features),
+            fixed(features, features),
+            pl.BlockSpec((features, wide), lambda i: (0, i)),
+            pl.BlockSpec((wide, features), lambda i: (i, 0)),
+        ],
+        out_specs=[
+            fixed(row_count, features),
+            fixed(row_count, acts_width),
+            fixed(row_count, features),
+            fixed(blocks, row_count, slot),
+            fixed(2, features),
+        ],
+        out_shape=[
+            jax.ShapeDtypeStruct((row_count, features), jnp.bfloat16),
+            jax.ShapeDtypeStruct((row_count, acts_width), jnp.bfloat16),
+            jax.ShapeDtypeStruct((row_count, features), jnp.float32),
+            jax.ShapeDtypeStruct((blocks, row_count, slot), jnp.bfloat16),
+            jax.ShapeDtypeStruct((2, features), jnp.float32),
+        ],
+        scratch_shapes=[
+            pltpu.VMEM((row_count, features), jnp.float32),
+            pltpu.VMEM((row_count, 1), jnp.float32),
+            pltpu.VMEM((row_count, features), jnp.float32),
+            pltpu.VMEM((row_count, features), jnp.float32),
+        ],
+        compiler_params=_params(56),
+        cost_estimate=_cost(
+            8 * row_count * features * hidden + 4 * row_count * features * features,
+            4 * features * hidden + 2 * features * features + 2 * row_count * acts_width,
+            2 * row_count * hidden,
+        ),
+        name="middle",
+    )(attended, rows, out_grad, gain, bias, w_out, w_up, w_down)
+
+
+def finish_call(received, rows, mixed_grad, gain, sums, w_query, w_key, w_value):
+    blocks, row_count, width = received.shape
+    slot = width // 3
+    features = rows.shape[1]
+    per_step = max(1, min(blocks, 256 // slot))
+    wide = slot * per_step
+    steps = blocks // per_step
+
+    def kernel(data_ref, rows_ref, mixed_ref, gain_ref, more_ref, wq_ref, wk_ref, wv_ref, out_ref, acts_ref, total):
+        step = pl.program_id(0)
+
+        @pl.when(step == 0)
+        def _():
+            total[...] = jnp.zeros_like(total)
+
+        for part, weight_ref in enumerate((wq_ref, wk_ref, wv_ref)):
+            for piece in range(per_step):
+                at = pl.multiple_of(part * features + step * wide + piece * slot, 128)
+                acts_ref[0:row_count, pl.ds(at, slot)] = data_ref[piece, :, part * slot : (part + 1) * slot]
+            at = pl.multiple_of(part * features + step * wide, 128)
+            total[...] += contract_cols(acts_ref[0:row_count, pl.ds(at, wide)], weight_ref[...])
+
+        @pl.when(step == steps - 1)
+        def _():
+            unit, inverse = _normalize(rows_ref[...].astype(jnp.float32))
+            grads = total[...]
+            sums = jnp.concatenate(
+                [
+                    jnp.sum(grads * unit, axis=0, keepdims=True),
+                    jnp.sum(grads, axis=0, keepdims=True),
+                    more_ref[...],
+                    jnp.zeros((12, features), jnp.float32),
+                ],
+                axis=0,
+            )
+            acts_ref[row_count:, 0:features] = sums.astype(jnp.bfloat16)
+            out_ref[...] = (
+                mixed_ref[...] + _normalize_back(grads, gain_ref[...], unit, inverse)
+            ).astype(jnp.bfloat16)
+
+    def fixed(*shape):
+        return pl.BlockSpec(shape, lambda i: (0,) * len(shape))
+
+    columns = pl.BlockSpec((features, wide), lambda i: (0, i))
+    return pl.pallas_call(
+        kernel,
+        grid=(steps,),
+        in_specs=[
+            pl.BlockSpec((per_step, row_count, width), lambda i: (i, 0, 0)),
+            fixed(row_count, features),
+            fixed(row_count, features),
+            fixed(1, features),
+            fixed(2, features),
+            columns,
+            columns,
+            columns,
+        ],
+        out_specs=[fixed(row_count, features), fixed(row_count + 16, 3 * features)],
+        out_shape=[
+            jax.ShapeDtypeStruct((row_count, features), jnp.bfloat16),
+            jax.ShapeDtypeStruct((row_count + 16, 3 * features), jnp.bfloat16),
+        ],
+        scratch_shapes=[pltpu.VMEM((row_count, features), jnp.float32)],
+        compiler_params=_params(48),
+        cost_estimate=_cost(6 * row_count * features * features, 6 * features * features + 14 * row_count * features),
+        name="finish",
+    )(received, rows, mixed_grad, gain, sums, w_query, w_key, w_value)
+
+
+def _bits(count):
+    return [1 << place for place in range(count.bit_length() - 1)]
+
+
+def _ordered(bits):
+    places = [0]
+    for bit in bits:
+        places = [at + step for at in places for step in (0, bit)]
+    return places
+
+
+def _paired(values, axis, bit):
+    count = lax.axis_size(axis)
+    return lax.ppermute(values, axis, [(i, i ^ bit) for i in range(count)])
+
+
+def _bit_of(axis, bit):
+    return (lax.axis_index(axis) // bit) % 2
+
+
+def grad_rows_call(chosen, own, peer, picks, features, wide, orders, blocks, shares, out_dtype, extra=False):
+    (own_left, own_right), (peer_left, peer_right) = own, peer
+    row_count = own_left.shape[0]
+    group = features // (blocks * shares)
+    kept = len(orders) * group
+    steps = [width // wide for _, _, width in picks]
+    starts = [sum(steps[:part]) for part in range(len(picks))]
+    columns = sum(width for _, _, width in picks)
+    right_rows = own_right.shape[0]
+
+    def choose(step, per_part):
+        value = per_part[0](step)
+        for part in range(1, len(picks)):
+            value = jnp.where(step >= starts[part], per_part[part](step), value)
+        return value
+
+    def kernel(chosen_ref, ol_ref, or_ref, pl_ref, pr_ref, out_ref, turned, left, *columns_ref):
+        step = pl.program_id(0)
+        for start in starts:
+
+            @pl.when(step == start)
+            def _():
+                for side, ref in enumerate((ol_ref, pl_ref)):
+                    turned[:, :, :, side * row_count : (side + 1) * row_count] = ref[...].T.reshape(
+                        blocks, shares, group, row_count
+                    )
+                for place, (block, share) in enumerate(orders):
+                    left[place * group : (place + 1) * group, :] = turned[
+                        block + chosen_ref[0], share + chosen_ref[1]
+                    ]
+
+        made = matmul(left[:, 0:row_count], or_ref[0:row_count, :]) + matmul(
+            left[:, row_count:], pr_ref[0:row_count, :]
+        )
+        if not extra:
+            out_ref[...] = made.astype(out_dtype)
+        else:
+            out_ref[:, 0:wide] = made.astype(out_dtype)
+            sums = or_ref[row_count:, 0:features].astype(jnp.float32) + pr_ref[row_count:, 0:features].astype(jnp.float32)
+            sums = jnp.concatenate([sums, jnp.zeros((128 - sums.shape[0], features), jnp.float32)], axis=0)
+            columns_ref[0][...] = sums.T.reshape(blocks, shares, group, 128)
+            for place, (block, share) in enumerate(orders):
+                out_ref[place * group : (place + 1) * group, wide:] = columns_ref[0][
+                    block + chosen_ref[0], share + chosen_ref[1]
+                ].astype(out_dtype)
+
+    left_at = [lambda step, at=at // features: at for at, _, _ in picks]
+    right_at = [lambda step, at=at // wide, start=start: at + step - start for (_, at, _), start in zip(picks, starts)]
+    left_spec = pl.BlockSpec((row_count, features), lambda i, chosen: (0, choose(i, left_at)))
+    right_spec = pl.BlockSpec((right_rows, wide), lambda i, chosen: (0, choose(i, right_at)))
+    more = 128 if extra else 0
+    return pl.pallas_call(
+        kernel,
+        grid_spec=pltpu.PrefetchScalarGridSpec(
+            num_scalar_prefetch=1,
+            grid=(sum(steps),),
+            in_specs=[left_spec, right_spec, left_spec, right_spec],
+            out_specs=pl.BlockSpec((kept, wide + more), lambda i, chosen: (0, i)),
+            scratch_shapes=[
+                pltpu.VMEM((blocks, shares, group, 2 * row_count), jnp.bfloat16),
+                pltpu.VMEM((kept, 2 * row_count), jnp.bfloat16),
+            ]
+            + [pltpu.VMEM((blocks, shares, group, 128), jnp.float32)] * bool(extra),
+        ),
+        out_shape=jax.ShapeDtypeStruct((kept, columns + more), out_dtype),
+        compiler_params=_params(40),
+        cost_estimate=_cost(4 * row_count * kept * columns, 4 * row_count * (columns + features) + 4 * kept * columns),
+        name="grad_rows",
+    )(chosen, own_left, own_right, peer_left, peer_right)
+
+
+def grad_down_call(chosen, own_acts, peer_acts, own_right, peer_right, orders, shares, rows_each, out_dtype):
+    row_count, features = own_right.shape
+    span = len(orders)
+    strides = []
+    for place in range(span.bit_length() - 1):
+        strides.append(orders[1 << place] - orders[0])
+
+    def block_of(step, chosen):
+        value = chosen[0]
+        for place, stride in enumerate(strides):
+            value = value + (step // (1 << place)) % 2 * stride
+        return value
+
+    def kernel(chosen_ref, ol_ref, pl_ref, or_ref, pr_ref, out_ref):
+        out_ref[...] = (
+            contract_rows(ol_ref[...], or_ref[...]) + contract_rows(pl_ref[...], pr_ref[...])
+        ).astype(out_dtype)
+
+    left_spec = pl.BlockSpec((row_count, rows_each), lambda i, chosen: (0, block_of(i, chosen)))
+    whole = pl.BlockSpec((row_count, features), lambda i, chosen: (0, 0))
+    return pl.pallas_call(
+        kernel,
+        grid_spec=pltpu.PrefetchScalarGridSpec(
+            num_scalar_prefetch=1,
+            grid=(span,),
+            in_specs=[left_spec, left_spec, whole, whole],
+            out_specs=pl.BlockSpec((rows_each, features), lambda i, chosen: (i, 0)),
+        ),
+        out_shape=jax.ShapeDtypeStruct((span * rows_each, features), out_dtype),
+        compiler_params=_params(40),
+        cost_estimate=_cost(
+            4 * row_count * span * rows_each * features, 4 * row_count * (span * rows_each + features) + 4 * span * rows_each * features
+        ),
+        name="grad_down",
+    )(chosen, own_acts, peer_acts, own_right, peer_right)
+
+
+def halving(keep, received, rest):
+    for axis, bit in rest:
+        pair = (2, keep.shape[0] // 2) + keep.shape[1:]
+        keep, received = keep.reshape(pair), received.reshape(pair)
+        mine = _bit_of(axis, bit)
+
+        def half(index):
+            return lax.dynamic_index_in_dim(keep, index, 0, False) + lax.dynamic_index_in_dim(
+                received, index, 0, False
+            ).astype(jnp.float32)
+
+        theirs, keep = half(1 - mine), half(mine)
+        received = _paired(theirs.astype(jnp.bfloat16), axis, bit)
+    return keep + received.astype(jnp.float32)
+
+
+def fast_body(
+    patches, seg_lengths, w_query, w_key, w_value, w_out, w_up, w_down,
+    norm1_gain, norm1_bias, norm2_gain, norm2_bias, out_grad,
+):
+    micro_count, tokens, features = patches.shape
+    hidden = w_up.shape[1]
+    row_count = micro_count * tokens
+    blocks, shares = lax.axis_size("blk"), lax.axis_size("mb")
+    head_dim = features // H
+    slot = features // blocks
+    rows = patches.reshape(row_count, features)
+    dout = out_grad.reshape(row_count, features)
+    gain_one, bias_one, gain_two, bias_two = (
+        value.reshape(1, features) for value in (norm1_gain, norm1_bias, norm2_gain, norm2_bias)
+    )
+
+    def swap(values):
+        return lax.all_to_all(values, "blk", split_axis=0, concat_axis=0, tiled=True)
+
+    def by_micro(values):
+        return values.reshape(blocks, micro_count, tokens, values.shape[-1])
+
+    send, norm_one = project_call(rows, gain_one, bias_one, w_query, w_key, w_value, blocks)
+    received = by_micro(swap(send))
+    dout_peer = _paired(dout, "mb", 1)
+    norm_peer = _paired(norm_one, "mb", 1)
+    attended = swap(attend_call(received, seg_lengths, head_dim).reshape(blocks, row_count, slot))
+    layer_out, acts, mixed_grad, back, sums_two = middle_call(
+        attended, rows, dout, gain_two, bias_two, w_out, w_up, w_down
+    )
+    grads = by_micro(swap(back))
+    acts_peer = _paired(acts, "mb", 1)
+
+    core, other = _bit_of("mb", 1), _bit_of("mb", 2)
+    x_bit = _bit_of("blk", 1)
+    blk_bits = _bits(blocks)
+    z_order = _ordered(blk_bits[1:])
+    rest_z = [("blk", bit) for bit in blk_bits[1:]]
+
+    def picked(*values):
+        return jnp.stack([jnp.asarray(value, jnp.int32) for value in values])
+
+    down_rows = hidden // (blocks * shares)
+    down_order = [at * shares for at in _ordered(blk_bits)]
+    down_made = [
+        grad_down_call(
+            picked(2 * which + core), acts, acts_peer, dout, dout_peer, down_order, shares, down_rows, dtype
+        )
+        for which, dtype in ((1 - other, jnp.bfloat16), (other, jnp.float32))
+    ]
+    up_orders = [(at, 2 * share) for share in (0, 1) for at in z_order]
+    norm_at = 2 * hidden
+    up_picks = [(norm_at, hidden, hidden), (norm_at + features, norm_at + 2 * features, features)]
+    up_made = [
+        grad_rows_call(
+            picked(which, core), (acts, acts), (acts_peer, acts_peer), up_picks, features, 512, up_orders, blocks, shares, dtype
+        )
+        for which, dtype in ((1 - x_bit, jnp.bfloat16), (x_bit, jnp.float32))
+    ]
+
+    def pieces(values, height):
+        return values.reshape(-1, height, values.shape[-1])
+
+    down_received = _paired(pieces(down_made[0], down_rows), "mb", 2)
+    up_received = _paired(pieces(up_made[0], features // (blocks * shares)), "blk", 1)
+    down_total = halving(pieces(down_made[1], down_rows), down_received, [("blk", 1)] + rest_z)
+    up_total = halving(pieces(up_made[1], features // (blocks * shares)), up_received, [("mb", 2)] + rest_z)
+
+    (grads, _, _) = lax.optimization_barrier((grads, down_made, up_made))
+    made = attend_back_call(received, grads, seg_lengths, head_dim)
+    returned = swap(made.reshape(blocks, row_count, 3 * slot))
+    patches_grad, acts_one = finish_call(returned, rows, mixed_grad, gain_one, sums_two, w_query, w_key, w_value)
+    acts_one_peer = _paired(acts_one, "mb", 1)
+    one_made = [
+        grad_rows_call(
+            picked(which, core), (norm_one, acts_one), (norm_peer, acts_one_peer), [(0, 0, 3 * features)], features, 3 * features,
+            up_orders, blocks, shares, dtype, True,
+        )
+        for which, dtype in ((1 - x_bit, jnp.bfloat16), (x_bit, jnp.float32))
+    ]
+    one_received = _paired(pieces(one_made[0], features // (blocks * shares)), "blk", 1)
+    one_total = halving(
+        pieces(one_made[1], features // (blocks * shares)), one_received, [("mb", 2)] + rest_z
+    )
+
+    up_total, one_total, down_total = up_total[0], one_total[0], down_total[0]
+    return (
+        layer_out.reshape(patches.shape),
+        patches_grad.reshape(patches.shape),
+        one_total[:, 0:features],
+        one_total[:, features : 2 * features],
+        one_total[:, 2 * features : 3 * features],
+        up_total[:, hidden:],
+        up_total[:, 0:hidden],
+        down_total,
+        one_total[:, 3 * features],
+        one_total[:, 3 * features + 1],
+        one_total[:, 3 * features + 2],
+        one_total[:, 3 * features + 3],
+    )
+
+
 def solution(mesh):
     in_specs = (
         P("mb", "blk", None),
@@ -347,4 +966,7 @@
         P(("blk", "mb")),
         P(("blk", "mb")),
     )
-    return jax.shard_map(body, mesh=mesh, in_specs=in_specs, out_specs=out_specs, check_vma=False)
+    blocks, shares = mesh.shape["blk"], mesh.shape["mb"]
+    paired = blocks >= 2 and blocks & (blocks - 1) == 0 and shares == 4
+    chosen_body = fast_body if paired and H % blocks == 0 else body
+    return jax.shard_map(chosen_body, mesh=mesh, in_specs=in_specs, out_specs=out_specs, check_vma=False)

time: 1140 us -> 370 us (0.32)
  waiting for transfers between devices: 706 us -> 131 us
  local copies, waits for them, and re-layouts: 148 us -> 23.3 us
  matrix products: 102 us -> 0 us
  Pallas kernels: 0 us -> 102 us
  other arithmetic: 51 us -> 21 us
  blocking collectives: 77.7 us -> 61.8 us
  between operations: 15.1 us -> 0.9 us
    reduce_scatter x6 -> x0, waiting for transfers between devices: 640 us -> none  [the longest x1 187 us: body(): lax.psum_scatter(gradients[5], ('blk', 'mb'), scatter_dimension=0, tiled=...]
    dot_general x74 -> x0, matrix products: 102 us -> none  [the longest x22 38.1 us: contract_rows(): lax.dot_general(left_side, right_side, (((0,), (0,)), ((), ())), preferre...]
    pallas_call x0 -> x11, Pallas kernels: none -> 102 us  [the longest x1 25.3 us: attend_back_call(): pl.pallas_call(kernel, grid=(micro_count, steps), in_specs=[pl.BlockSpec(...]
    ppermute x0 -> x16, waiting for transfers between devices: none -> 97.3 us  [_paired(): return lax.ppermute(values, axis, [(i, i ^ bit) for i in range(count)])]
    unnamed x1 -> x0, blocking collectives: 39.6 us -> none
    all_to_all x6 -> x2, waiting for transfers between devices: 65.7 us -> 34 us  [swap(): lax.all_to_all(values, 'blk', split_axis=0, concat_axis=0, tiled=True)]
    convert_element_type x11 -> x0, local copies, waits for them, and re-layouts: 24.9 us -> none  [the longest x2 5.91 us: body(): from_items(query_grad_items).astype(jnp.bfloat16)]
    all_to_all x8 -> x0, local copies, waits for them, and re-layouts: 24.4 us -> none  [the longest x1 5.1 us: body(): lax.all_to_all(from_items(query_grad_items).astype(jnp.bfloat16), 'blk',...]
  transfers between devices with their start and end apart: 12 -> 18, of which waited for: 10 -> 11; matrix products, arithmetic and copies ran while one was open for 18% -> 6% of each run, Pallas kernels for 0% -> 11%
where the time goes in v1:
time: 370 us; the launch traced here: 368 us
  waiting for transfers between devices  131 us (35%)
  Pallas kernels  102 us (28%)
  blocking collectives  61.8 us (17%)
  starting transfers between devices  28.3 us (8%)
  local copies, waits for them, and re-layouts  23.3 us (6%)
  other arithmetic  21 us (6%)
    ppermute x16, waiting for transfers between devices, _paired(): return lax.ppermute(values, axis, [(i, i ^ bit) for i in range(count)])  97.3 us
    all_to_all x2, blocking collectives, swap(): lax.all_to_all(values, 'blk', split_axis=0, concat_axis=0, tiled=True)  61.8 us
    all_to_all x2, waiting for transfers between devices, swap(): lax.all_to_all(values, 'blk', split_axis=0, concat_axis=0, tiled=True)  34 us
    pallas_call x1, Pallas kernels, attend_back_call(): pl.pallas_call(kernel, grid=(micro_count, steps), in_specs=[pl.BlockSpec(...  25.3 us
    pallas_call x4, Pallas kernels, grad_rows_call(): pl.pallas_call(kernel, grid_spec=pltpu.PrefetchScalarGridSpec(num_scalar_...  24.5 us
    ppermute x16, starting transfers between devices, _paired(): return lax.ppermute(values, axis, [(i, i ^ bit) for i in range(count)])  20.7 us
    unnamed x46, local copies, waits for them, and re-layouts  20.3 us
    pallas_call x1, Pallas kernels, middle_call(): pl.pallas_call(kernel, grid=(steps,), in_specs=[fixed(blocks, row_count,...  20 us
  transfers between devices with their start and end apart: 18, of which 11 were waited for; matrix products, arithmetic and copies ran while one was open for 6% of the time, Pallas kernels for 11%

profile of v1, /device:TPU:0, one launch (start us, length us, event | category | flops | bytes accessed | tf_op | source)
XLA Modules:
  0.0 368.3 jit_solution(9038210695414965778)
XLA Ops:
  7.8 4.1 %project.1 = (bf16[8,256,384]{2,1,0:T(8,128)(2,1)S(1)}, bf16[256,1024]{1,0:T(8,128)(2,1)}) custom-call(bf16[256,1024]{1,0:T(8,128)(2,1)S(1)} %bitcast.92, f32[1,1024]{1,0:T(1,128)S(1)} %bitcast.99, f32[1,1024]{1,0:T(1,128)S(1)} %bitcast.101, bf16[1024,1024]{1,0:T(8,128)(2,1)S(1)} %copy-done.3, bf16[1024,1024]{1,0:T(8,128)(2,1)S(1)} %copy-done.4, ...), custom_call_target="tpu_custom_call" | custom-call | flops 1610612736 | bytes 7340032 | tf_op jit(solution)/shard_map/project/pallas_call | solution.py:375
  12.0 44.2 %all_to_all.20 = bf16[8,256,384]{2,1,0:T(8,128)(2,1)S(1)} all-to-all(bf16[8,256,384]{2,1,0:T(8,128)(2,1)S(1)} %get-tuple-element.22), channel_id=1, replica_groups=mesh['blk'=8,'mb'=4] {'blk'}, dimensions={0} | all-to-all | bytes 3145728 | tf_op jit(solution)/shard_map/all_to_all | solution.py:854
  56.2 10.3 %attend.1 = bf16[8,2,128,128]{3,2,1,0:T(8,128)(2,1)S(1)} custom-call(s32[2,8]{1,0:T(2,128)S(1)} %copy-done.17, bf16[8,2,128,384]{3,2,1,0:T(8,128)(2,1)S(1)} %bitcast.94), custom_call_target="tpu_custom_call" | custom-call | flops 4294967296 | bytes 2097152 | tf_op jit(solution)/shard_map/attend/pallas_call | solution.py:428
  66.5 17.7 %all_to_all.21.att_ref = bf16[8,256,128]{2,1,0:T(8,128)(2,1)} all-to-all(bf16[8,256,128]{2,1,0:T(8,128)(2,1)S(1)} %bitcast.98), channel_id=1, replica_groups=mesh['blk'=8,'mb'=4] {'blk'}, dimensions={0} | all-to-all | bytes 1048576 | tf_op jit(solution)/shard_map/all_to_all | solution.py:854
  84.2 20.0 %middle.1 = (bf16[256,1024]{1,0:T(8,128)(2,1)}, bf16[256,11264]{1,0:T(8,128)(2,1)}, f32[256,1024]{1,0:T(8,128)}, bf16[8,256,128]{2,1,0:T(8,128)(2,1)}, f32[2,1024]{1,0:T(2,128)}) custom-call(bf16[8,256,128]{2,1,0:T(8,128)(2,1)} %all_to_all.21.att_ref, bf16[256,1024]{1,0:T(8,128)(2,1)} %bitcast.91, bf16[256,1024]{1,0:T(8,128)(2,1)} %bitcast.86, ...), custom_call_target="tpu_custom_call" | custom-call | flops 9663676416 | bytes 24641536 | tf_op jit(solution)/shard_map/middle/pallas_call | solution.py:581
  104.6 3.7 all-to-all-start.2
  117.3 5.5 %grad_down.2 = bf16[1024,1024]{1,0:T(8,128)(2,1)S(1)} custom-call(s32[1]{0:T(128)} %bitcast.10.chosen_ref, bf16[256,11264]{1,0:T(8,128)(2,1)S(1)} %copy-done, bf16[256,11264]{1,0:T(8,128)(2,1)} %collective-permute-done.pl_ref.pr_ref, bf16[256,1024]{1,0:T(8,128)(2,1)S(1)} %bitcast.88, bf16[256,1024]{1,0:T(8,128)(2,1)S(1)} %collective-permute-done.1.pr_ref), custom_call_target="tpu_custom_call" | custom-call | flops 1073741824 | bytes 6291456 | tf_op jit(solution)/shard_map/grad_down/pallas_call | solution.py:804
  124.1 5.5 %grad_down.3 = f32[1024,1024]{1,0:T(8,128)S(1)} custom-call(s32[1]{0:T(128)} %bitcast.11.chosen_ref, bf16[256,11264]{1,0:T(8,128)(2,1)S(1)} %copy-done, bf16[256,11264]{1,0:T(8,128)(2,1)} %collective-permute-done.pl_ref.pr_ref, bf16[256,1024]{1,0:T(8,128)(2,1)S(1)} %bitcast.89, bf16[256,1024]{1,0:T(8,128)(2,1)S(1)} %collective-permute-done.1.pr_ref), custom_call_target="tpu_custom_call" | custom-call | flops 1073741824 | bytes 6291456 | tf_op jit(solution)/shard_map/grad_down/pallas_call | solution.py:804
  131.6 8.5 %grad_rows.4 = bf16[256,5120]{1,0:T(8,128)(2,1)S(1)} custom-call(s32[2]{0:T(128)S(1)} %get-tuple-element.51.chosen_ref, bf16[256,11264]{1,0:T(8,128)(2,1)S(1)} %bitcast.81, bf16[256,11264]{1,0:T(8,128)(2,1)S(1)} %bitcast.81, bf16[256,11264]{1,0:T(8,128)(2,1)} %collective-permute-done.pl_ref.pr_ref, bf16[256,11264]{1,0:T(8,128)(2,1)} %collective-permute-done.pl_ref.pr_ref), custom_call_target="tpu_custom_call" | custom-call | flops 1342177280 | bytes 11534336 | tf_op jit(solution)/shard_map/grad_rows/pallas_call | solution.py:764
  141.6 8.7 %grad_rows.5 = f32[256,5120]{1,0:T(8,128)S(1)} custom-call(s32[2]{0:T(128)S(1)} %get-tuple-element.52.chosen_ref, bf16[256,11264]{1,0:T(8,128)(2,1)S(1)} %bitcast.81, bf16[256,11264]{1,0:T(8,128)(2,1)S(1)} %bitcast.81, bf16[256,11264]{1,0:T(8,128)(2,1)} %collective-permute-done.pl_ref.pr_ref, bf16[256,11264]{1,0:T(8,128)(2,1)} %collective-permute-done.pl_ref.pr_ref), custom_call_target="tpu_custom_call" | custom-call | flops 1342177280 | bytes 11534336 | tf_op jit(solution)/shard_map/grad_rows/pallas_call | solution.py:764
  152.7 25.3 %attend_back.1 = bf16[8,2,128,384]{3,2,1,0:T(8,128)(2,1)S(1)} custom-call(s32[2,8]{1,0:T(2,128)S(1)} %copy-done.17, bf16[8,2,128,384]{3,2,1,0:T(8,128)(2,1)S(1)} %bitcast.95, bf16[8,2,128,128]{3,2,1,0:T(8,128)(2,1)S(1)} %bitcast.97), custom_call_target="tpu_custom_call" | custom-call | flops 10737418240 | bytes 3670016 | tf_op jit(solution)/shard_map/attend_back/pallas_call | solution.py:505
  179.1 3.9 %all-to-all-start.3 = ((bf16[8,256,384]{2,1,0:T(8,128)(2,1)}), bf16[8,256,384]{2,1,0:T(8,128)(2,1)S(1)}, u32[]{:S(2)}, u32[]{:S(2)}) async-start(bf16[8,256,384]{2,1,0:T(8,128)(2,1)} %bitcast.96), calls=%async_computation.3 | async-start | bytes 3145728 | tf_op jit(solution)/shard_map/all_to_all | solution.py:854
  186.4 34.0 %all-to-all-done.3.data_ref = bf16[8,256,384]{2,1,0:T(8,128)(2,1)S(1)} async-done(((bf16[8,256,384]{2,1,0:T(8,128)(2,1)}), bf16[8,256,384]{2,1,0:T(8,128)(2,1)S(1)}, u32[]{:S(2)}, u32[]{:S(2)}) %all-to-all-start.3) | async-done | bytes 1572896 | tf_op jit(solution)/shard_map/all_to_all | solution.py:854
  222.6 6.5 %finish.1 = (bf16[256,1024]{1,0:T(8,128)(2,1)}, bf16[272,3072]{1,0:T(8,128)(2,1)S(1)}) custom-call(bf16[8,256,384]{2,1,0:T(8,128)(2,1)S(1)} %all-to-all-done.3.data_ref, bf16[256,1024]{1,0:T(8,128)(2,1)S(1)} %bitcast.93, f32[256,1024]{1,0:T(8,128)S(1)} %copy-done.12, f32[1,1024]{1,0:T(1,128)S(1)} %bitcast.100, f32[2,1024]{1,0:T(2,128)S(1)} %copy-done.15, ...), custom_call_target="tpu_custom_call" | custom-call | flops 1610612736 | bytes 9961472 | tf_op jit(solution)/shard_map/finish/pallas_call | solution.py:668
  231.1 5.3 %fusion.1 = (bf16[4,128,1024]{2,1,0:T(8,128)(2,1)}, f32[1,4,128,1024]{3,2,1,0:T(8,128)}) fusion(f32[2,4,128,1024]{3,2,1,0:T(8,128)} %bitcast.83, s32[]{:T(128)S(6)} %select_n.141, bf16[2,4,128,1024]{3,2,1,0:T(8,128)(2,1)} %bitcast.39, s32[]{:T(128)S(6)} %select_n.140), kind=kLoop, calls=%fused_computation.9 | loop fusion | flops 2621440 | bytes 9437192 | tf_op jit(solution)/shard_map/convert_element_type | solution.py:833
  237.9 4.2 %grad_rows.7 = bf16[256,3200]{1,0:T(8,128)(2,1)} custom-call(s32[2]{0:T(128)S(1)} %get-tuple-element.51.chosen_ref, bf16[256,1024]{1,0:T(8,128)(2,1)} %get-tuple-element.30.ol_ref, bf16[272,3072]{1,0:T(8,128)(2,1)S(1)} %get-tuple-element.31.or_ref, bf16[256,1024]{1,0:T(8,128)(2,1)} %collective-permute-done.2.pl_ref, ...), custom_call_target="tpu_custom_call" | custom-call | flops 805306368 | bytes 7340032 | tf_op jit(solution)/shard_map/grad_rows/pallas_call | solution.py:764
  242.7 17.1 %collective-permute-done.8 = bf16[8,32,5120]{2,1,0:T(8,128)(2,1)} collective-permute-done((bf16[8,32,5120]{2,1,0:T(8,128)(2,1)}, bf16[8,32,5120]{2,1,0:T(8,128)(2,1)}, u32[]{:S(2)}, u32[]{:S(2)}) %collective-permute-start.8) | collective-permute-done | bytes 2621472 | tf_op jit(solution)/shard_map/ppermute | solution.py:706
  259.8 6.0 %fusion = (bf16[4,32,5120]{2,1,0:T(8,128)(2,1)}, f32[1,4,32,5120]{3,2,1,0:T(8,128)}) fusion(f32[2,4,32,5120]{3,2,1,0:T(8,128)} %bitcast.82, s32[]{:T(128)S(6)} %select_n.134, bf16[2,4,32,5120]{3,2,1,0:T(8,128)(2,1)} %bitcast.29, s32[]{:T(128)S(6)} %select_n.130), kind=kLoop, calls=%fused_computation.6 | loop fusion | flops 3276800 | bytes 11796488 | tf_op jit(solution)/shard_map/convert_element_type | solution.py:833
  267.3 15.0 %collective-permute-done.13 = bf16[4,128,1024]{2,1,0:T(8,128)(2,1)} collective-permute-done((bf16[4,128,1024]{2,1,0:T(8,128)(2,1)}, bf16[4,128,1024]{2,1,0:T(8,128)(2,1)}, u32[]{:S(2)}, u32[]{:S(2)}) %collective-permute-start.13) | collective-permute-done | bytes 1048608 | tf_op jit(solution)/shard_map/ppermute | solution.py:706
  286.4 10.9 %collective-permute-done.14 = bf16[2,128,1024]{2,1,0:T(8,128)(2,1)} collective-permute-done((bf16[2,128,1024]{2,1,0:T(8,128)(2,1)}, bf16[2,128,1024]{2,1,0:T(8,128)(2,1)}, u32[]{:S(2)}, u32[]{:S(2)}) %collective-permute-start.14) | collective-permute-done | bytes 524320 | tf_op jit(solution)/shard_map/ppermute | solution.py:706
  304.8 11.6 %collective-permute-done.4 = bf16[8,32,3200]{2,1,0:T(8,128)(2,1)} collective-permute-done((bf16[8,32,3200]{2,1,0:T(8,128)(2,1)}, bf16[8,32,3200]{2,1,0:T(8,128)(2,1)}, u32[]{:S(2)}, u32[]{:S(2)}) %collective-permute-start.4) | collective-permute-done | bytes 1638432 | tf_op jit(solution)/shard_map/ppermute | solution.py:706
  324.8 12.7 %collective-permute-done.5 = bf16[4,32,3200]{2,1,0:T(8,128)(2,1)S(1)} collective-permute-done((bf16[4,32,3200]{2,1,0:T(8,128)(2,1)S(1)}, bf16[4,32,3200]{2,1,0:T(8,128)(2,1)S(1)}, u32[]{:S(2)}, u32[]{:S(2)}) %collective-permute-start.5) | collective-permute-done | bytes 819232 | tf_op jit(solution)/shard_map/ppermute | solution.py:706
  341.9 12.5 %collective-permute-done.6 = bf16[2,32,3200]{2,1,0:T(8,128)(2,1)S(1)} collective-permute-done((bf16[2,32,3200]{2,1,0:T(8,128)(2,1)S(1)}, bf16[2,32,3200]{2,1,0:T(8,128)(2,1)S(1)}, u32[]{:S(2)}, u32[]{:S(2)}) %collective-permute-start.6) | collective-permute-done | bytes 409632 | tf_op jit(solution)/shard_map/ppermute | solution.py:706
  356.8 10.0 %collective-permute-done.7 = bf16[1,32,3200]{2,1,0:T(8,128)(2,1)S(1)} collective-permute-done((bf16[1,32,3200]{2,1,0:T(8,128)(2,1)S(1)}, bf16[1,32,3200]{2,1,0:T(8,128)(2,1)S(1)}, u32[]{:S(2)}, u32[]{:S(2)}) %collective-permute-start.7) | collective-permute-done | bytes 204832 | tf_op jit(solution)/shard_map/ppermute | solution.py:706
  (89 shorter events, 64.3 us)
Async XLA Ops:
  12.0 44.2 %copy-start.17 = (s32[2,8]{1,0:T(2,128)S(1)}, s32[2,8]{1,0:T(2,128)}, u32[]{:S(2)}) copy-start(s32[2,8]{1,0:T(2,128)} %lengths_ref.3) | copy-start | bytes 196
  84.2 20.0 %copy-start.7 = (bf16[2,128,1024]{2,1,0:T(8,128)(2,1)S(1)}, bf16[2,128,1024]{2,1,0:T(8,128)(2,1)}, u32[]{:S(2)}) copy-start(bf16[2,128,1024]{2,1,0:T(8,128)(2,1)} %param.25) | copy-start | bytes 1572868
  104.1 10.5 %collective-permute-start = (bf16[256,11264]{1,0:T(8,128)(2,1)}, bf16[256,11264]{1,0:T(8,128)(2,1)}, u32[]{:S(2)}, u32[]{:S(2)}) collective-permute-start(bf16[256,11264]{1,0:T(8,128)(2,1)} %get-tuple-element.25.ol_ref.or_ref), channel_id=1, source_target_pairs={{0,1},{1,0},{2,3},{3,2},{4,5},{5,4},{6,7},{7,6},{8,9},{9,8},{10,11... | collective-permute-start | bytes 17301512 | tf_op jit(solution)/shard_map/ppermute | solution.py:706
  104.1 7.4 %collective-permute-start.1 = (bf16[256,1024]{1,0:T(8,128)(2,1)S(1)}, bf16[256,1024]{1,0:T(8,128)(2,1)S(1)}, u32[]{:S(2)}, u32[]{:S(2)}) collective-permute-start(bf16[256,1024]{1,0:T(8,128)(2,1)S(1)} %bitcast.87), channel_id=1, source_target_pairs={{0,1},{1,0},{2,3},{3,2},{4,5},{5,4},{6,7},{7,6},{8,9},{9,8},{10,11... | collective-permute-start | bytes 1572872 | tf_op jit(solution)/shard_map/ppermute | solution.py:706
  104.6 48.0 %all-to-all-start.2 = ((bf16[8,256,128]{2,1,0:T(8,128)(2,1)}), bf16[8,256,128]{2,1,0:T(8,128)(2,1)S(1)}, u32[]{:S(2)}, u32[]{:S(2)}) async-start(bf16[8,256,128]{2,1,0:T(8,128)(2,1)} %get-tuple-element.24), calls=%async_computation.2 | async-start | bytes 1048576 | tf_op jit(solution)/shard_map/all_to_all | solution.py:854
  117.3 14.3 %slice-start = ((s8[5767168]{0:T(1024)(128)(4,1)}), s8[4194304]{0:T(1024)(128)(4,1)S(1)}, s32[]{:S(2)}) async-start(s8[5767168]{0:T(1024)(128)(4,1)} %bitcast.80), calls=%async_computation.4 | async-start | bytes 8388608
  179.1 41.3 %copy-start.14 = (f32[1024]{0:T(1024)S(1)}, f32[1024]{0:T(1024)}, u32[]{:S(2)}) copy-start(f32[1024]{0:T(1024)} %param.21) | copy-start | bytes 12292
  179.1 41.3 %copy-start.15 = (f32[2,1024]{1,0:T(2,128)S(1)}, f32[2,1024]{1,0:T(2,128)}, u32[]{:S(2)}) copy-start(f32[2,1024]{1,0:T(2,128)} %get-tuple-element.28.more_ref) | copy-start | bytes 24580
  179.1 41.3 %all-to-all-start.3 = ((bf16[8,256,384]{2,1,0:T(8,128)(2,1)}), bf16[8,256,384]{2,1,0:T(8,128)(2,1)S(1)}, u32[]{:S(2)}, u32[]{:S(2)}) async-start(bf16[8,256,384]{2,1,0:T(8,128)(2,1)} %bitcast.96), calls=%async_computation.3 | async-start | bytes 3145728 | tf_op jit(solution)/shard_map/all_to_all | solution.py:854
  183.0 48.1 %collective-permute-start.12 = (bf16[8,128,1024]{2,1,0:T(8,128)(2,1)}, bf16[8,128,1024]{2,1,0:T(8,128)(2,1)}, u32[]{:S(2)}, u32[]{:S(2)}) collective-permute-start(bf16[8,128,1024]{2,1,0:T(8,128)(2,1)} %bitcast.90), channel_id=1, source_target_pairs={{0,2},{1,3},{2,0},{3,1},{4,6},{5,7},{6,4},{7,5},{8,10},{9,11},{10,... | collective-permute-start | bytes 6291464 | tf_op jit(solution)/shard_map/ppermute | solution.py:706
  184.6 75.2 %collective-permute-start.8 = (bf16[8,32,5120]{2,1,0:T(8,128)(2,1)}, bf16[8,32,5120]{2,1,0:T(8,128)(2,1)}, u32[]{:S(2)}, u32[]{:S(2)}) collective-permute-start(bf16[8,32,5120]{2,1,0:T(8,128)(2,1)} %bitcast.85), channel_id=1, source_target_pairs={{0,4},{4,0},{8,12},{12,8},{16,20},{20,16},{24,28},{28,24},{1,5},{5... | collective-permute-start | bytes 7864328 | tf_op jit(solution)/shard_map/ppermute | solution.py:706
  229.1 8.8 %collective-permute-start.3 = (bf16[272,3072]{1,0:T(8,128)(2,1)S(1)}, bf16[272,3072]{1,0:T(8,128)(2,1)S(1)}, u32[]{:S(2)}, u32[]{:S(2)}) collective-permute-start(bf16[272,3072]{1,0:T(8,128)(2,1)S(1)} %get-tuple-element.31.or_ref), channel_id=1, source_target_pairs={{0,1},{1,0},{2,3},{3,2},{4,5},{5,4},{6,7},{7,6},{8,9},{9,8},{10,11... | collective-permute-start | bytes 5013512 | tf_op jit(solution)/shard_map/ppermute | solution.py:706
  229.1 8.8 %collective-permute-start.2 = (bf16[256,1024]{1,0:T(8,128)(2,1)}, bf16[256,1024]{1,0:T(8,128)(2,1)}, u32[]{:S(2)}, u32[]{:S(2)}) collective-permute-start(bf16[256,1024]{1,0:T(8,128)(2,1)} %get-tuple-element.30.ol_ref), channel_id=1, source_target_pairs={{0,1},{1,0},{2,3},{3,2},{4,5},{5,4},{6,7},{7,6},{8,9},{9,8},{10,11... | collective-permute-start | bytes 1572872 | tf_op jit(solution)/shard_map/ppermute | solution.py:706
  236.4 45.8 %collective-permute-start.13 = (bf16[4,128,1024]{2,1,0:T(8,128)(2,1)}, bf16[4,128,1024]{2,1,0:T(8,128)(2,1)}, u32[]{:S(2)}, u32[]{:S(2)}) collective-permute-start(bf16[4,128,1024]{2,1,0:T(8,128)(2,1)} %get-tuple-element.38), channel_id=1, source_target_pairs={{0,4},{4,0},{8,12},{12,8},{16,20},{20,16},{24,28},{28,24},{1,5},{5... | collective-permute-start | bytes 3145736 | tf_op jit(solution)/shard_map/ppermute | solution.py:706
  242.1 74.2 %collective-permute-start.4 = (bf16[8,32,3200]{2,1,0:T(8,128)(2,1)}, bf16[8,32,3200]{2,1,0:T(8,128)(2,1)}, u32[]{:S(2)}, u32[]{:S(2)}) collective-permute-start(bf16[8,32,3200]{2,1,0:T(8,128)(2,1)} %bitcast.18), channel_id=1, source_target_pairs={{0,4},{4,0},{8,12},{12,8},{16,20},{20,16},{24,28},{28,24},{1,5},{5... | collective-permute-start | bytes 4915208 | tf_op jit(solution)/shard_map/ppermute | solution.py:706
  259.8 22.5 %copy-start.19 = (f32[1,4,128,1024]{3,2,1,0:T(8,128)S(1)}, f32[1,4,128,1024]{3,2,1,0:T(8,128)}, u32[]{:S(2)}) copy-start(f32[1,4,128,1024]{3,2,1,0:T(8,128)} %get-tuple-element.39) | copy-start | bytes 6291460
  265.8 54.0 %collective-permute-start.9 = (bf16[4,32,5120]{2,1,0:T(8,128)(2,1)}, bf16[4,32,5120]{2,1,0:T(8,128)(2,1)}, u32[]{:S(2)}, u32[]{:S(2)}) collective-permute-start(bf16[4,32,5120]{2,1,0:T(8,128)(2,1)} %get-tuple-element.36), channel_id=1, source_target_pairs={{0,2},{1,3},{2,0},{3,1},{4,6},{5,7},{6,4},{7,5},{8,10},{9,11},{10,... | collective-permute-start | bytes 3932168 | tf_op jit(solution)/shard_map/ppermute | solution.py:706
  284.9 12.3 %collective-permute-start.14 = (bf16[2,128,1024]{2,1,0:T(8,128)(2,1)}, bf16[2,128,1024]{2,1,0:T(8,128)(2,1)}, u32[]{:S(2)}, u32[]{:S(2)}) collective-permute-start(bf16[2,128,1024]{2,1,0:T(8,128)(2,1)} %get-tuple-element.44), channel_id=1, source_target_pairs={{0,8},{4,12},{8,0},{12,4},{16,24},{20,28},{24,16},{28,20},{1,9},{5... | collective-permute-start | bytes 1572872 | tf_op jit(solution)/shard_map/ppermute | solution.py:706
  298.4 24.6 %collective-permute-start.15 = (bf16[1,128,1024]{2,1,0:T(8,128)(2,1)S(1)}, bf16[1,128,1024]{2,1,0:T(8,128)(2,1)S(1)}, u32[]{:S(2)}, u32[]{:S(2)}) collective-permute-start(bf16[1,128,1024]{2,1,0:T(8,128)(2,1)S(1)} %fusion.8), channel_id=1, source_target_pairs={{0,16},{4,20},{8,24},{12,28},{16,0},{20,4},{24,8},{28,12},{1,17},{... | collective-permute-start | bytes 786440 | tf_op jit(solution)/shard_map/ppermute | solution.py:706
  318.2 19.4 %collective-permute-start.5 = (bf16[4,32,3200]{2,1,0:T(8,128)(2,1)S(1)}, bf16[4,32,3200]{2,1,0:T(8,128)(2,1)S(1)}, u32[]{:S(2)}, u32[]{:S(2)}) collective-permute-start(bf16[4,32,3200]{2,1,0:T(8,128)(2,1)S(1)} %get-tuple-element.40), channel_id=1, source_target_pairs={{0,2},{1,3},{2,0},{3,1},{4,6},{5,7},{6,4},{7,5},{8,10},{9,11},{10,... | collective-permute-start | bytes 2457608 | tf_op jit(solution)/shard_map/ppermute | solution.py:706
  321.4 17.8 %collective-permute-start.10 = (bf16[2,32,5120]{2,1,0:T(8,128)(2,1)S(1)}, bf16[2,32,5120]{2,1,0:T(8,128)(2,1)S(1)}, u32[]{:S(2)}, u32[]{:S(2)}) collective-permute-start(bf16[2,32,5120]{2,1,0:T(8,128)(2,1)S(1)} %get-tuple-element.42), channel_id=1, source_target_pairs={{0,8},{4,12},{8,0},{12,4},{16,24},{20,28},{24,16},{28,20},{1,9},{5... | collective-permute-start | bytes 1966088 | tf_op jit(solution)/shard_map/ppermute | solution.py:706
  337.7 16.7 %collective-permute-start.6 = (bf16[2,32,3200]{2,1,0:T(8,128)(2,1)S(1)}, bf16[2,32,3200]{2,1,0:T(8,128)(2,1)S(1)}, u32[]{:S(2)}, u32[]{:S(2)}) collective-permute-start(bf16[2,32,3200]{2,1,0:T(8,128)(2,1)S(1)} %get-tuple-element.46), channel_id=1, source_target_pairs={{0,8},{4,12},{8,0},{12,4},{16,24},{20,28},{24,16},{28,20},{1,9},{5... | collective-permute-start | bytes 1228808 | tf_op jit(solution)/shard_map/ppermute | solution.py:706
  339.3 15.9 %collective-permute-start.11 = (bf16[1,32,5120]{2,1,0:T(8,128)(2,1)S(1)}, bf16[1,32,5120]{2,1,0:T(8,128)(2,1)S(1)}, u32[]{:S(2)}, u32[]{:S(2)}) collective-permute-start(bf16[1,32,5120]{2,1,0:T(8,128)(2,1)S(1)} %fusion.4), channel_id=1, source_target_pairs={{0,16},{4,20},{8,24},{12,28},{16,0},{20,4},{24,8},{28,12},{1,17},{... | collective-permute-start | bytes 983048 | tf_op jit(solution)/shard_map/ppermute | solution.py:706
  354.4 12.4 %collective-permute-start.7 = (bf16[1,32,3200]{2,1,0:T(8,128)(2,1)S(1)}, bf16[1,32,3200]{2,1,0:T(8,128)(2,1)S(1)}, u32[]{:S(2)}, u32[]{:S(2)}) collective-permute-start(bf16[1,32,3200]{2,1,0:T(8,128)(2,1)S(1)} %fusion.12), channel_id=1, source_target_pairs={{0,16},{4,20},{8,24},{12,28},{16,0},{20,4},{24,8},{28,12},{1,17},{... | collective-permute-start | bytes 614408 | tf_op jit(solution)/shard_map/ppermute | solution.py:706
  (17 other events, 34.4 us)

commit v2 on v0

--- a/solution.py
+++ b/solution.py
@@ -3,6 +3,8 @@
 import jax
 import jax.numpy as jnp
 from jax import lax
+from jax.experimental import pallas as pl
+from jax.experimental.pallas import tpu as pltpu
 from jax.sharding import PartitionSpec as P
 
 H = 16
@@ -317,6 +319,820 @@
     )
 
 
+def _normalize(values):
+    center = values - jnp.mean(values, axis=-1, keepdims=True)
+    variance = jnp.mean(center * center, axis=-1, keepdims=True)
+    inverse = lax.rsqrt(variance + epsilon)
+    return center * inverse, inverse
+
+
+def _normalize_back(grads, gain, unit, inverse):
+    scaled = grads * gain
+    mean_scaled = jnp.mean(scaled, axis=-1, keepdims=True)
+    mean_product = jnp.mean(scaled * unit, axis=-1, keepdims=True)
+    return (scaled - mean_scaled - unit * mean_product) * inverse
+
+
+def _doc_ids(lengths_ref, micro, doc_count, positions):
+    end = jnp.int32(0)
+    ids = jnp.zeros_like(positions)
+    for doc in range(doc_count):
+        end = end + lengths_ref[micro, doc]
+        ids = ids + (positions >= end).astype(jnp.int32)
+    return ids
+
+
+def _params(mib):
+    return pltpu.CompilerParams(vmem_limit_bytes=max(mib, 60) << 20)
+
+
+def _cost(microseconds):
+    return pl.CostEstimate(flops=int(microseconds * 1e9) + 1, bytes_accessed=1, transcendentals=0)
+
+
+def project_call(rows, gain, bias, w_query, w_key, w_value, blocks, tokens):
+    row_count, features = rows.shape
+    slot = features // blocks
+    per_step = max(1, min(blocks, 256 // slot))
+    wide = slot * per_step
+
+    def kernel(rows_ref, gain_ref, bias_ref, wq_ref, wk_ref, wv_ref, send_ref, *refs):
+        unit_refs, norm_ref = refs[:-1], refs[-1]
+
+
+        @pl.when(pl.program_id(0) == 0)
+        def _():
+            unit, _unused = _normalize(rows_ref[...].astype(jnp.float32))
+            for micro, unit_ref in enumerate(unit_refs):
+                unit_ref[...] = unit[micro * tokens : (micro + 1) * tokens].astype(jnp.bfloat16)
+            norm_ref[...] = (unit * gain_ref[...] + bias_ref[...]).astype(jnp.bfloat16)
+
+        for part, weight_ref in enumerate((wq_ref, wk_ref, wv_ref)):
+            made = matmul(norm_ref[...], weight_ref[...]).astype(jnp.bfloat16)
+            for piece in range(per_step):
+                send_ref[piece, :, part * slot : (part + 1) * slot] = made[
+                    :, piece * slot : (piece + 1) * slot
+                ]
+
+    whole = pl.BlockSpec((row_count, features), lambda i: (0, 0))
+    vector = pl.BlockSpec((1, features), lambda i: (0, 0))
+    columns = pl.BlockSpec((features, wide), lambda i: (0, i))
+    return pl.pallas_call(
+        kernel,
+        grid=(blocks // per_step,),
+        in_specs=[whole, vector, vector, columns, columns, columns],
+        out_specs=[pl.BlockSpec((per_step, row_count, 3 * slot), lambda i: (i, 0, 0))]
+        + [pl.BlockSpec((tokens, features), lambda i: (0, 0))] * (row_count // tokens),
+        out_shape=[jax.ShapeDtypeStruct((blocks, row_count, 3 * slot), jnp.bfloat16)]
+        + [jax.ShapeDtypeStruct((tokens, features), jnp.bfloat16)] * (row_count // tokens),
+        scratch_shapes=[pltpu.VMEM((row_count, features), jnp.bfloat16)],
+        compiler_params=_params(40),
+        cost_estimate=_cost(6),
+        name="project",
+    )(rows, gain, bias, w_query, w_key, w_value)
+
+
+def _head_masks(slot, head_dim, dtype):
+    lanes = lax.broadcasted_iota(jnp.int32, (1, slot), 1)
+    return [(lanes // head_dim == head).astype(dtype) for head in range(slot // head_dim)]
+
+
+def _key_range(lengths_ref, micro, doc_count, first_row, last_row, seq):
+    low, high, end = jnp.int32(0), jnp.int32(seq), jnp.int32(0)
+    for doc in range(doc_count):
+        end = end + lengths_ref[micro, doc]
+        low = jnp.where(end <= first_row, jnp.maximum(low, end), low)
+        high = jnp.where(end >= last_row, jnp.minimum(high, end), high)
+    return low, high
+
+
+def _by_key_range(lengths_ref, micro, doc_count, step, rows, blocks, tokens, compute):
+    low, high = _key_range(lengths_ref, micro, doc_count, step * rows, (step + 1) * rows, blocks * tokens)
+    half = blocks // 2
+    in_low, in_high = high <= half * tokens, low >= half * tokens
+
+    @pl.when(in_low | in_high)
+    def _():
+        compute(jnp.where(in_low, 0, half), half)
+
+    @pl.when(jnp.logical_not(in_low | in_high))
+    def _():
+        compute(0, blocks)
+
+
+def attend_call(received, lengths, head_dim):
+    blocks, micro_count, tokens, width = received.shape
+    slot = width // 3
+    doc_count = lengths.shape[1]
+    step_blocks = max(1, min(blocks, 256 // tokens))
+    rows = step_blocks * tokens
+    scale = 1.0 / math.sqrt(head_dim)
+
+    def kernel(lengths_ref, data_ref, out_ref):
+        micro = pl.program_id(0)
+        step = pl.program_id(1)
+        row_docs = _doc_ids(
+            lengths_ref, micro, doc_count, lax.broadcasted_iota(jnp.int32, (rows, 1), 0) + step * rows
+        )
+        queries = data_ref[pl.ds(step * step_blocks, step_blocks), 0, :, 0:slot].reshape(rows, slot) * scale
+
+        def compute(first, count):
+            seq = count * tokens
+            key_docs = _doc_ids(
+                lengths_ref, micro, doc_count, lax.broadcasted_iota(jnp.int32, (1, seq), 1) + first * tokens
+            )
+            same = row_docs == key_docs
+            keys = data_ref[pl.ds(first, count), 0, :, slot : 2 * slot].reshape(seq, slot)
+            values = data_ref[pl.ds(first, count), 0, :, 2 * slot : 3 * slot].reshape(seq, slot)
+            total = jnp.zeros((rows, slot), jnp.float32)
+            for mask, mask_wide in zip(
+                _head_masks(slot, head_dim, jnp.bfloat16), _head_masks(slot, head_dim, jnp.float32)
+            ):
+                scores = jnp.where(same, contract_cols(queries * mask, keys), masked_score)
+                exponent = jnp.exp(scores - jnp.max(scores, axis=-1, keepdims=True))
+                share = 1.0 / jnp.sum(exponent, axis=-1, keepdims=True)
+                total = total + matmul(exponent.astype(jnp.bfloat16), values) * (share * mask_wide)
+            total = jnp.where(row_docs < doc_count, total, 0.0)
+            out_ref[...] = total.astype(jnp.bfloat16).reshape(step_blocks, 1, tokens, slot)
+
+        _by_key_range(lengths_ref, micro, doc_count, step, rows, blocks, tokens, compute)
+
+    return pl.pallas_call(
+        kernel,
+        grid=(micro_count, blocks // step_blocks),
+        in_specs=[
+            pl.BlockSpec(memory_space=pltpu.SMEM),
+            pl.BlockSpec((blocks, 1, tokens, width), lambda m, s: (0, m, 0, 0)),
+        ],
+        out_specs=pl.BlockSpec((step_blocks, 1, tokens, slot), lambda m, s: (s, m, 0, 0)),
+        out_shape=jax.ShapeDtypeStruct((blocks, micro_count, tokens, slot), jnp.bfloat16),
+        compiler_params=_params(40),
+        cost_estimate=_cost(11),
+        name="attend",
+    )(lengths, received)
+
+
+def attend_back_call(received, grads, lengths, head_dim):
+    blocks, micro_count, tokens, width = received.shape
+    slot = width // 3
+    doc_count = lengths.shape[1]
+    step_blocks = max(1, min(blocks, 256 // tokens))
+    rows = step_blocks * tokens
+    steps = blocks // step_blocks
+    scale = 1.0 / math.sqrt(head_dim)
+
+    def kernel(lengths_ref, data_ref, grads_ref, *refs):
+        out_refs, (key_total, value_total) = refs[:micro_count], refs[micro_count:]
+        micro = pl.program_id(0)
+        step = pl.program_id(1)
+
+        @pl.when(step == 0)
+        def _():
+            key_total[...] = jnp.zeros_like(key_total)
+            value_total[...] = jnp.zeros_like(value_total)
+
+        row_docs = _doc_ids(
+            lengths_ref, micro, doc_count, lax.broadcasted_iota(jnp.int32, (1, rows), 1) + step * rows
+        )
+        column_docs = _doc_ids(
+            lengths_ref, micro, doc_count, lax.broadcasted_iota(jnp.int32, (rows, 1), 0) + step * rows
+        )
+        queries = data_ref[pl.ds(step * step_blocks, step_blocks), 0, :, 0:slot].reshape(rows, slot) * scale
+        out_grads = grads_ref[...].reshape(rows, slot)
+        out_grads = out_grads * (column_docs < doc_count).astype(jnp.float32).astype(jnp.bfloat16)
+
+        def compute(first, count):
+            seq = count * tokens
+            key_docs = _doc_ids(
+                lengths_ref, micro, doc_count, lax.broadcasted_iota(jnp.int32, (seq, 1), 0) + first * tokens
+            )
+            same = row_docs == key_docs
+            keys = data_ref[pl.ds(first, count), 0, :, slot : 2 * slot].reshape(seq, slot)
+            values = data_ref[pl.ds(first, count), 0, :, 2 * slot : 3 * slot].reshape(seq, slot)
+            query_total = jnp.zeros((rows, slot), jnp.float32)
+            key_parts, value_parts = [], []
+            for mask, mask_wide in zip(
+                _head_masks(slot, head_dim, jnp.bfloat16), _head_masks(slot, head_dim, jnp.float32)
+            ):
+                queries_head = queries * mask
+                grads_head = out_grads * mask
+                scores = jnp.where(same, contract_cols(keys, queries_head), masked_score)
+                exponent = jnp.exp(scores - jnp.max(scores, axis=0, keepdims=True))
+                probs = exponent * (1.0 / jnp.sum(exponent, axis=0, keepdims=True))
+                prob_grads = contract_cols(values, grads_head)
+                inner = jnp.sum(probs * prob_grads, axis=0, keepdims=True)
+                score_grads = (probs * (prob_grads - inner)).astype(jnp.bfloat16)
+                value_parts.append(matmul(probs.astype(jnp.bfloat16), grads_head))
+                key_parts.append(matmul(score_grads, queries_head))
+                query_total = query_total + contract_rows(score_grads, keys) * mask_wide
+            at = pl.ds(pl.multiple_of(first * tokens, tokens), seq)
+            key_total[at, :] += sum(key_parts)
+            value_total[at, :] += sum(value_parts)
+            query_grads = (query_total * scale).astype(jnp.bfloat16).reshape(step_blocks, tokens, slot)
+            for at, out_ref in enumerate(out_refs):
+
+                @pl.when(micro == at)
+                def _():
+                    out_ref[pl.ds(step * step_blocks, step_blocks), :, 0:slot] = query_grads
+
+        _by_key_range(lengths_ref, micro, doc_count, step, rows, blocks, tokens, compute)
+
+        for at, out_ref in enumerate(out_refs):
+
+            @pl.when((step == steps - 1) & (micro == at))
+            def _():
+                out_ref[:, :, slot : 2 * slot] = key_total[...].astype(jnp.bfloat16).reshape(blocks, tokens, slot)
+                out_ref[:, :, 2 * slot :] = value_total[...].astype(jnp.bfloat16).reshape(blocks, tokens, slot)
+
+    return pl.pallas_call(
+        kernel,
+        grid=(micro_count, steps),
+        in_specs=[
+            pl.BlockSpec(memory_space=pltpu.SMEM),
+            pl.BlockSpec((blocks, 1, tokens, width), lambda m, s: (0, m, 0, 0)),
+            pl.BlockSpec((step_blocks, 1, tokens, slot), lambda m, s: (s, m, 0, 0)),
+        ],
+        out_specs=[pl.BlockSpec((blocks, tokens, width), lambda m, s: (0, 0, 0))] * micro_count,
+        out_shape=[jax.ShapeDtypeStruct((blocks, tokens, width), jnp.bfloat16)] * micro_count,
+        scratch_shapes=[pltpu.VMEM((blocks * tokens, slot), jnp.float32)] * 2,
+        compiler_params=_params(48),
+        cost_estimate=_cost(0),
+        name="attend_back",
+    )(lengths, received, grads)
+
+
+def _fixed(*shape):
+    return pl.BlockSpec(shape, lambda *_unused: (0,) * len(shape))
+
+
+def mix_call(attended, rows, gain, bias, w_out):
+    blocks, row_count, slot = attended.shape
+    features = rows.shape[1]
+
+    def kernel(att_ref, rows_ref, gain_ref, bias_ref, wo_ref, mixed_ref, norm_ref, side_ref):
+        for block in range(blocks):
+            side_ref[:, block * slot : (block + 1) * slot] = att_ref[block]
+        value = rows_ref[...].astype(jnp.float32) + matmul(side_ref[...], wo_ref[...])
+        mixed_ref[...] = value
+        unit, _unused = _normalize(value)
+        norm_ref[...] = (unit * gain_ref[...] + bias_ref[...]).astype(jnp.bfloat16)
+
+    rows_spec, vector = _fixed(row_count, features), _fixed(1, features)
+    return pl.pallas_call(
+        kernel,
+        grid=(1,),
+        in_specs=[_fixed(blocks, row_count, slot), rows_spec, vector, vector, _fixed(features, features)],
+        out_specs=[rows_spec] * 3,
+        out_shape=[
+            jax.ShapeDtypeStruct((row_count, features), jnp.float32),
+            jax.ShapeDtypeStruct((row_count, features), jnp.bfloat16),
+            jax.ShapeDtypeStruct((row_count, features), jnp.bfloat16),
+        ],
+        compiler_params=_params(56),
+        cost_estimate=_cost(4),
+        name="mix",
+    )(attended, rows, gain, bias, w_out)
+
+
+def _hidden_parts(norm, out_grad, up_columns, down_rows):
+    upper = matmul(norm, up_columns)
+    active_grad = contract_cols(out_grad, down_rows)
+    half = (1.0 + lax.erf(upper * (1.0 / math.sqrt(2.0)))) * 0.5
+    slope = half + upper * jnp.exp(upper * upper * -0.5) * (1.0 / math.sqrt(2.0 * math.pi))
+    return (upper * half).astype(jnp.bfloat16), (active_grad * slope).astype(jnp.bfloat16)
+
+
+def middle_call(norm, mixed, out_grad, w_up, w_down):
+    row_count, features = mixed.shape
+    hidden = w_up.shape[1]
+    wide = min(1024, hidden)
+    sub = min(512, wide)
+    steps = hidden // wide
+
+    def kernel(norm_ref, mixed_ref, grad_ref, wu_ref, wd_ref, out_ref, grad_total, total, active_all, upper_all):
+        step = pl.program_id(0)
+
+        @pl.when(step == 0)
+        def _():
+            total[...] = mixed_ref[...]
+            grad_total[...] = jnp.zeros_like(grad_total)
+
+        for chunk in range(0, wide, sub):
+            active, upper_grad = _hidden_parts(
+                norm_ref[...], grad_ref[...], wu_ref[:, chunk : chunk + sub], wd_ref[chunk : chunk + sub, :]
+            )
+            active_all[:, chunk : chunk + sub] = active
+            upper_all[:, chunk : chunk + sub] = upper_grad
+        total[...] += matmul(active_all[...], wd_ref[...])
+        grad_total[...] += contract_cols(upper_all[...], wu_ref[...])
+
+        @pl.when(step == steps - 1)
+        def _():
+            out_ref[...] = total[...].astype(jnp.bfloat16)
+
+    rows_spec = _fixed(row_count, features)
+    return pl.pallas_call(
+        kernel,
+        grid=(steps,),
+        in_specs=[
+            rows_spec,
+            rows_spec,
+            rows_spec,
+            pl.BlockSpec((features, wide), lambda i: (0, i)),
+            pl.BlockSpec((wide, features), lambda i: (i, 0)),
+        ],
+        out_specs=[rows_spec] * 2,
+        scratch_shapes=[
+            pltpu.VMEM((row_count, features), jnp.float32),
+            pltpu.VMEM((row_count, wide), jnp.bfloat16),
+            pltpu.VMEM((row_count, wide), jnp.bfloat16),
+        ],
+        out_shape=[
+            jax.ShapeDtypeStruct((row_count, features), jnp.bfloat16),
+            jax.ShapeDtypeStruct((row_count, features), jnp.float32),
+        ],
+        compiler_params=_params(56),
+        cost_estimate=_cost(20),
+        name="middle",
+    )(norm, mixed, out_grad, w_up, w_down)
+
+
+def middle_back_call(place, mixed, norm_grads, out_grad, gain, w_out, blocks, shares):
+    row_count, features = mixed.shape
+    slot = features // blocks
+    part = features // shares
+
+    def kernel(place_ref, mixed_ref, norm_ref, grad_ref, gain_ref, wo_ref, mixed_grad_ref, back_ref, sums_ref, *refs):
+        low_refs, low_all = refs[:shares], refs[shares]
+        unit, inverse = _normalize(mixed_ref[...])
+        grads = norm_ref[...]
+        sums_ref[0:1, :] = jnp.sum(grads * unit, axis=0, keepdims=True)
+        sums_ref[1:2, :] = jnp.sum(grads, axis=0, keepdims=True)
+        mixed_grad = grad_ref[...].astype(jnp.float32) + _normalize_back(grads, gain_ref[...], unit, inverse)
+        mixed_grad_ref[...] = mixed_grad
+        low = mixed_grad.astype(jnp.bfloat16)
+        low_all[...] = low
+        for share, low_ref in enumerate(low_refs):
+            low_ref[...] = low_all[:, pl.ds(pl.multiple_of((place_ref[1] ^ share) * part, 128), part)]
+        back = contract_cols(low, wo_ref[...]).astype(jnp.bfloat16)
+        for block in range(blocks):
+            back_ref[block] = back[:, block * slot : (block + 1) * slot]
+
+    rows_spec = _fixed(row_count, features)
+    return pl.pallas_call(
+        kernel,
+        grid_spec=pltpu.PrefetchScalarGridSpec(
+            num_scalar_prefetch=1,
+            grid=(1,),
+            in_specs=[rows_spec, rows_spec, rows_spec, _fixed(1, features), _fixed(features, features)],
+            out_specs=[rows_spec, _fixed(blocks, row_count, slot), _fixed(2, features)]
+            + [_fixed(row_count, part)] * shares,
+            scratch_shapes=[pltpu.VMEM((row_count, features), jnp.bfloat16)],
+        ),
+        out_shape=[
+            jax.ShapeDtypeStruct((row_count, features), jnp.float32),
+            jax.ShapeDtypeStruct((blocks, row_count, slot), jnp.bfloat16),
+            jax.ShapeDtypeStruct((2, features), jnp.float32),
+        ]
+        + [jax.ShapeDtypeStruct((row_count, part), jnp.bfloat16)] * shares,
+        compiler_params=_params(56),
+        cost_estimate=_cost(0),
+        name="middle_back",
+    )(place, mixed, norm_grads, out_grad, gain, w_out)
+
+
+def finish_call(received, rows, mixed_grad, gain, w_query, w_key, w_value):
+    micro_count = len(received)
+    blocks, tokens, width = received[0].shape
+    slot = width // 3
+    row_count, features = rows.shape
+    per_step = max(1, min(blocks, 256 // slot))
+    wide = slot * per_step
+    steps = blocks // per_step
+
+    def kernel(*refs):
+        data_refs, refs = refs[:micro_count], refs[micro_count:]
+        rows_ref, mixed_ref, gain_ref, wq_ref, wk_ref, wv_ref, out_ref, total, side = refs
+        step = pl.program_id(0)
+
+        @pl.when(step == 0)
+        def _():
+            total[...] = jnp.zeros_like(total)
+
+        for part, weight_ref in enumerate((wq_ref, wk_ref, wv_ref)):
+            for micro, data_ref in enumerate(data_refs):
+                for piece in range(per_step):
+                    side[part, micro * tokens : (micro + 1) * tokens, piece * slot : (piece + 1) * slot] = data_ref[
+                        piece, :, part * slot : (part + 1) * slot
+                    ]
+            total[...] += contract_cols(side[part], weight_ref[...])
+
+        @pl.when(step == steps - 1)
+        def _():
+            unit, inverse = _normalize(rows_ref[...].astype(jnp.float32))
+            out_ref[...] = (
+                mixed_ref[...] + _normalize_back(total[...], gain_ref[...], unit, inverse)
+            ).astype(jnp.bfloat16)
+
+    def fixed(*shape):
+        return pl.BlockSpec(shape, lambda i: (0,) * len(shape))
+
+    columns = pl.BlockSpec((features, wide), lambda i: (0, i))
+    return pl.pallas_call(
+        kernel,
+        grid=(steps,),
+        in_specs=[pl.BlockSpec((per_step, tokens, width), lambda i: (i, 0, 0))] * micro_count
+        + [
+            fixed(row_count, features),
+            fixed(row_count, features),
+            fixed(1, features),
+            columns,
+            columns,
+            columns,
+        ],
+        out_specs=fixed(row_count, features),
+        out_shape=jax.ShapeDtypeStruct((row_count, features), jnp.bfloat16),
+        scratch_shapes=[
+            pltpu.VMEM((row_count, features), jnp.float32),
+            pltpu.VMEM((3, row_count, wide), jnp.bfloat16),
+        ],
+        compiler_params=_params(48),
+        cost_estimate=_cost(0),
+        name="finish",
+    )(*received, rows, mixed_grad, gain, w_query, w_key, w_value)
+
+
+def grad_heads_call(place, units, places, made, gain, bias, sums, w_query, w_key, w_value, shares):
+    micro_count = len(made)
+    blocks, tokens, width = made[0].shape
+    slot = width // 3
+    features = gain.shape[1]
+    group = features // (blocks * shares)
+    full = width + 128
+    kept = blocks * (shares // 2) * group
+
+    def kernel(place_ref, *refs):
+        unit_refs, refs = refs[: 2 * micro_count], refs[2 * micro_count :]
+        made_refs, refs = refs[:micro_count], refs[micro_count:]
+        gain_ref, bias_ref, sums_ref, wq_ref, wk_ref, wv_ref, send_ref, keep_ref, spread, ordered = refs
+        product = jnp.zeros((features, width), jnp.float32)
+        column_sum = jnp.zeros((1, width), jnp.float32)
+        for micro, made_ref in enumerate(made_refs):
+            for at, relative in enumerate(places[micro]):
+                ordered[at * tokens : (at + 1) * tokens, :] = made_ref[place_ref[0] ^ relative]
+            half = blocks * tokens // 2
+            for side in range(2):
+                rows = ordered[side * half : (side + 1) * half, :]
+                product = product + contract_rows(unit_refs[2 * micro + side][...], rows)
+                column_sum = column_sum + jnp.sum(rows.astype(jnp.float32), axis=0, keepdims=True)
+        vectors = jnp.concatenate(
+            [gain_ref[...], bias_ref[...], sums_ref[...], jnp.zeros((124, features), jnp.float32)], axis=0
+        ).T
+        total = vectors[:, 0:1] * product + vectors[:, 1:2] * column_sum
+        weights = jnp.concatenate([wq_ref[...], wk_ref[...], wv_ref[...]], axis=1).astype(jnp.float32)
+        gain_sum = jnp.sum(weights * product, axis=1, keepdims=True)
+        bias_sum = jnp.sum(weights * column_sum, axis=1, keepdims=True)
+        lanes = lax.broadcasted_iota(jnp.int32, (1, 128), 1)
+        norms = jnp.where(
+            lanes == 0, gain_sum, jnp.where(lanes == 1, bias_sum, jnp.where(lanes < 4, vectors, 0.0))
+        )
+        spread[:, :, :, 0:width] = total.reshape(blocks, shares, group, width)
+        spread[:, :, :, width:] = norms.reshape(blocks, shares, group, 128)
+        core = place_ref[1] % 2
+        for which, out_ref in enumerate((send_ref, keep_ref)):
+            for share in range(0, shares, 2):
+                for block in range(blocks):
+                    out_ref[share // 2, block] = spread[block, share + (core if which else 1 - core)].astype(out_ref.dtype)
+
+    def fixed(*shape):
+        return pl.BlockSpec(shape, lambda i, place: (0,) * len(shape))
+
+    columns = pl.BlockSpec((features, slot), lambda i, place: (0, place[0]))
+    out = (shares // 2, blocks, group, full)
+    return pl.pallas_call(
+        kernel,
+        grid_spec=pltpu.PrefetchScalarGridSpec(
+            num_scalar_prefetch=1,
+            grid=(1,),
+            in_specs=[fixed(*part.shape) for part in (*units, *made)]
+            + [fixed(1, features), fixed(1, features), fixed(2, features), columns, columns, columns],
+            out_specs=[fixed(*out), fixed(*out)],
+            scratch_shapes=[
+                pltpu.VMEM((blocks, shares, group, full), jnp.float32),
+                pltpu.VMEM((blocks * tokens, width), jnp.bfloat16),
+            ],
+        ),
+        out_shape=[jax.ShapeDtypeStruct(out, jnp.bfloat16), jax.ShapeDtypeStruct(out, jnp.float32)],
+        compiler_params=_params(48),
+        cost_estimate=_cost(0),
+        name="grad_heads",
+    )(place, *units, *made, gain, bias, sums, w_query, w_key, w_value)
+
+
+def _bits(count):
+    return [1 << place for place in range(count.bit_length() - 1)]
+
+
+def _ordered(bits):
+    places = [0]
+    for bit in bits:
+        places = [at + step for at in places for step in (0, bit)]
+    return places
+
+
+def _ordered_low(bits):
+    places = [0]
+    for bit in bits:
+        places = places + [at + bit for at in places]
+    return places
+
+
+def _paired(values, axis, bit):
+    count = lax.axis_size(axis)
+    return lax.ppermute(values, axis, [(i, i ^ bit) for i in range(count)])
+
+
+def _bit_of(axis, bit):
+    return (lax.axis_index(axis) // bit) % 2
+
+
+def _place_at(bits, step):
+    places = _ordered(bits)
+    at = jnp.int32(places[0])
+    for other in range(1, len(places)):
+        at = jnp.where(step == other, places[other], at)
+    return at
+
+
+def grad_middle_call(place, norms, out_grads, sides, lows, w_up, w_down, down_bits, up_bits):
+    shares = len(norms)
+    row_count, features = norms[0].shape
+    all_rows = shares * row_count
+    hidden = w_up.shape[1]
+    blocks = 1 << len(up_bits)
+    owned = hidden // (blocks * shares)
+    part = lows[0].shape[1]
+    half = blocks // 2
+    pair = min(2, half)
+    half_steps = half // pair
+    block_rows = features // blocks
+    sub = min(2, shares)
+
+    def kernel(place_ref, *refs):
+        groups, refs = [refs[at * shares : (at + 1) * shares] for at in range(4)], refs[4 * shares :]
+        up_refs, down_refs, refs = refs[:pair], refs[pair : 2 * pair], refs[2 * pair :]
+        down_send, down_keep, up_send, up_keep, norm_all, grad_all, active_all, upper_all, up_all = refs
+        step = pl.program_id(0)
+        low = place_ref[0] // up_bits[0] % 2
+
+        def spread():
+            for at, block in enumerate(_ordered(up_bits[1:])):
+                rows = slice(at * block_rows, (at + 1) * block_rows)
+                up_send[rows, :] = up_all[block + up_bits[0] * (1 - low)].astype(jnp.bfloat16)
+                up_keep[rows, :] = up_all[block + up_bits[0] * low]
+
+        @pl.when(step == 0)
+        def _():
+            for at in range(shares):
+                norm_all[at * row_count : (at + 1) * row_count, :] = groups[0][at][...]
+                grad_all[at * row_count : (at + 1) * row_count, :] = groups[1][at][...]
+
+        @pl.when(step < 2 * half_steps)
+        def _():
+            up_columns = jnp.concatenate([ref[...] for ref in up_refs], axis=1)
+            down_rows = jnp.concatenate([ref[...] for ref in down_refs], axis=0)
+            for at in range(0, all_rows, all_rows // sub):
+                rows = slice(at, at + all_rows // sub)
+                active_all[rows, :], upper_all[rows, :] = _hidden_parts(
+                    norm_all[rows, :], grad_all[rows, :], up_columns, down_rows
+                )
+            down_made = contract_rows(active_all[...], grad_all[...])
+
+            @pl.when(step < half_steps)
+            def _():
+                down_send[...] = down_made.astype(jnp.bfloat16)
+
+            @pl.when(step >= half_steps)
+            def _():
+                down_keep[...] = down_made
+
+            up_all[...] = contract_rows(norm_all[...], upper_all[...]).reshape(blocks, block_rows, pair * owned)
+            spread()
+
+        @pl.when(step == 2 * half_steps)
+        def _():
+            made = jnp.zeros((features, part), jnp.float32)
+            for side_ref, low_ref in zip(groups[2], groups[3]):
+                made = made + contract_rows(side_ref[...], low_ref[...])
+            up_all[...] = made.reshape(blocks, block_rows, part)
+            spread()
+
+    def first_bit(i, place):
+        return (place[0] // down_bits[0] + 1 + jnp.minimum(i, 2 * half_steps - 1) // half_steps) % 2
+
+    def unit_block(i, place, at):
+        inner = _place_at(down_bits[1:], jnp.minimum(i, 2 * half_steps - 1) % half_steps * pair + at)
+        return (inner + down_bits[0] * first_bit(i, place)) * shares + place[1]
+
+    ups = [
+        pl.BlockSpec((features, owned), lambda i, place, at=at: (0, unit_block(i, place, at))) for at in range(pair)
+    ]
+    downs = [
+        pl.BlockSpec((owned, features), lambda i, place, at=at: (unit_block(i, place, at), 0)) for at in range(pair)
+    ]
+    def up_block(i, place):
+        return (0, jnp.where(i == 2 * half_steps, i, first_bit(i, place) * half_steps + i % half_steps))
+
+    up_out = pl.BlockSpec((features // 2, pair * owned), up_block)
+    shapes = [(half * owned, features), (features // 2, blocks * owned + part)]
+    return pl.pallas_call(
+        kernel,
+        grid_spec=pltpu.PrefetchScalarGridSpec(
+            num_scalar_prefetch=1,
+            grid=(2 * half_steps + 1,),
+            in_specs=[_fixed(row_count, features)] * (3 * shares) + [_fixed(row_count, part)] * shares + ups + downs,
+            out_specs=[
+                pl.BlockSpec((pair * owned, features), lambda i, place: (jnp.minimum(i, half_steps - 1), 0)),
+                pl.BlockSpec((pair * owned, features), lambda i, place: (jnp.clip(i - half_steps, 0, half_steps - 1), 0)),
+                up_out,
+                up_out,
+            ],
+            scratch_shapes=[
+                pltpu.VMEM((all_rows, features), jnp.bfloat16),
+                pltpu.VMEM((all_rows, features), jnp.bfloat16),
+                pltpu.VMEM((all_rows, pair * owned), jnp.bfloat16),
+                pltpu.VMEM((all_rows, pair * owned), jnp.bfloat16),
+                pltpu.VMEM((blocks, block_rows, pair * owned), jnp.float32),
+            ],
+        ),
+        out_shape=[jax.ShapeDtypeStruct(shape, dtype) for shape in shapes for dtype in (jnp.bfloat16, jnp.float32)],
+        compiler_params=_params(56),
+        cost_estimate=_cost(0),
+        name="grad_middle",
+    )(place, *norms, *out_grads, *sides, *lows, *([w_up] * pair), *([w_down] * pair))
+
+
+def halved(keep, received, axis, bit):
+    pair = (2, keep.shape[0] // 2) + keep.shape[1:]
+    keep, received = keep.reshape(pair), received.reshape(pair)
+    mine = _bit_of(axis, bit)
+
+    def half(index):
+        return lax.dynamic_index_in_dim(keep, index, 0, False) + lax.dynamic_index_in_dim(
+            received, index, 0, False
+        ).astype(jnp.float32)
+
+    return half(1 - mine).astype(jnp.bfloat16), half(mine)
+
+
+def fast_body(
+    patches, seg_lengths, w_query, w_key, w_value, w_out, w_up, w_down,
+    norm1_gain, norm1_bias, norm2_gain, norm2_bias, out_grad,
+):
+    micro_count, tokens, features = patches.shape
+    hidden = w_up.shape[1]
+    row_count = micro_count * tokens
+    blocks, shares = lax.axis_size("blk"), lax.axis_size("mb")
+    head_dim = features // H
+    slot = features // blocks
+    rows = patches.reshape(row_count, features)
+    dout = out_grad.reshape(row_count, features)
+    gain_one, bias_one, gain_two, bias_two = (
+        value.reshape(1, features) for value in (norm1_gain, norm1_bias, norm2_gain, norm2_bias)
+    )
+
+    def swap(values):
+        return lax.all_to_all(values, "blk", split_axis=0, concat_axis=0, tiled=True)
+
+    def by_micro(values):
+        return values.reshape(blocks, micro_count, tokens, values.shape[-1])
+
+    place = jnp.stack([lax.axis_index("blk"), lax.axis_index("mb")]).astype(jnp.int32)
+    blk_bits = _bits(blocks)
+    down_bits = [blk_bits[1], blk_bits[0], *blk_bits[2:]]
+    each, owned, block_rows = features // (blocks * shares), hidden // (blocks * shares), features // blocks
+    tie = lax.optimization_barrier
+
+    def grown(values, bit):
+        return jnp.concatenate([values, _paired(values, "blk", bit)], axis=0)
+
+    def shared(values):
+        over = _paired(values, "mb", 2)
+        return [values, _paired(values, "mb", 1), over, _paired(over, "mb", 1)]
+
+    send, units_first, units_last = project_call(
+        rows, gain_one, bias_one, w_query, w_key, w_value, blocks, tokens
+    )
+    received = by_micro(swap(send))
+    douts = shared(dout)
+    units_last = grown(units_last, blk_bits[0])
+    units_last, received, douts = tie((units_last, received, douts))
+    units_first, received = tie((units_first, received))
+    units_first = grown(units_first, blk_bits[-1])
+    attended = attend_call(received, seg_lengths, head_dim).reshape(blocks, row_count, slot)
+    attended, units_first = tie((attended, units_first))
+    attended, units_first, units_last = tie((swap(attended), units_first, units_last))
+    for bit in blk_bits[-2:0:-1]:
+        units_first = grown(units_first, bit)
+    for bit in blk_bits[:1:-1]:
+        units_last = grown(units_last, bit)
+    places_first = _ordered_low([*blk_bits[:0:-1], blk_bits[0]])
+    places_last = _ordered_low([blk_bits[0], *blk_bits[:1:-1], blk_bits[1]])
+
+    mixed, norm, side = mix_call(attended, rows, gain_two, bias_two, w_out)
+    norm_peer, norm_over = _paired(norm, "mb", 1), _paired(norm, "mb", 2)
+    layer_out, norm_grads = middle_call(norm, mixed, dout, w_up, w_down)
+    norm_grads, units_first, units_last, norm_peer, norm_over, side = tie(
+        (norm_grads, units_first, units_last, norm_peer, norm_over, side)
+    )
+    norms = [norm, norm_peer, norm_over, _paired(norm_over, "mb", 1)]
+    sides = shared(side)
+    units_first_peer = _paired(units_first, "blk", blk_bits[0])
+    units_last_peer = _paired(units_last, "blk", blk_bits[1])
+    mixed_grad, back, sums_two, *lows = middle_back_call(
+        place, mixed, norm_grads, dout, gain_two, w_out, blocks, shares
+    )
+    grads = by_micro(swap(back))
+    lows = [lows[0]] + [_paired(lows[share], "mb", share) for share in range(1, shares)]
+    down_theirs, down_keep, up_theirs, up_keep = grad_middle_call(
+        place, norms, douts, sides, lows, w_up, w_down, down_bits, blk_bits
+    )
+    down_theirs, down_keep = (value.reshape(-1, owned, features) for value in (down_theirs, down_keep))
+    up_theirs, up_keep = (value.reshape(-1, block_rows, value.shape[-1]) for value in (up_theirs, up_keep))
+    sums = {"down": (down_theirs, down_keep, down_bits), "up": (up_theirs, up_keep, blk_bits)}
+
+    def sent(name, step):
+        return _paired(sums[name][0], "blk", sums[name][2][step])
+
+    def added(name, received, step):
+        theirs, keep = halved(sums[name][1], received, "blk", sums[name][2][step])
+        sums[name] = (theirs, keep, sums[name][2])
+
+    down_received, up_received = sent("down", 0), sent("up", 0)
+    grads, down_keep, units_first_peer, units_last_peer = tie(
+        (grads, sums["down"][1], units_first_peer, units_last_peer)
+    )
+    sums["down"] = (sums["down"][0], down_keep, down_bits)
+    made = attend_back_call(received, grads, seg_lengths, head_dim)
+    returned = [swap(made[0])]
+    added("down", down_received, 1)
+    made, theirs = tie((made, sums["down"][0]))
+    sums["down"] = (theirs, *sums["down"][1:])
+    down_received = sent("down", 1)
+    heads_send, heads_keep = grad_heads_call(
+        place, (units_first, units_first_peer, units_last, units_last_peer), (places_first, places_last),
+        made, gain_one, bias_one, sums_two, w_query, w_key, w_value, shares,
+    )
+    added("up", up_received, 1)
+    returned[0], theirs, down_received, heads_send = tie((returned[0], sums["up"][0], down_received, heads_send))
+    sums["up"] = (theirs, *sums["up"][1:])
+    returned += [swap(tie((values, returned[0]))[0]) for values in made[1:]]
+    up_received = sent("up", 1)
+    flat = (-1,) + heads_keep.shape[2:]
+    heads_received = _paired(heads_send, "mb", 1).reshape(flat)
+    for step in range(2, len(blk_bits)):
+        added("down", down_received, step)
+        down_received = sent("down", step)
+        added("up", up_received, step)
+        up_received = sent("up", step)
+    heads_theirs, heads_keep = halved(heads_keep.reshape(flat), heads_received, "mb", 2)
+    heads_total = heads_keep + _paired(heads_theirs, "mb", 2).astype(jnp.float32)
+    heads_total, returned = tie((heads_total, returned))
+    heads_total = lax.all_to_all(heads_total.astype(jnp.bfloat16), "blk", split_axis=0, concat_axis=0, tiled=True)
+    patches_grad = finish_call(returned, rows, mixed_grad, gain_one, w_query, w_key, w_value)
+    patches_grad, heads_total, up_received = tie((patches_grad, heads_total, up_received))
+    heads_total = heads_total.astype(jnp.float32)
+    down_total = (sums["down"][1] + down_received.astype(jnp.float32))[0]
+    wide_total = (sums["up"][1] + up_received.astype(jnp.float32))[0]
+    wide_total = lax.all_to_all(
+        wide_total.astype(jnp.bfloat16).reshape(shares, each, -1), "mb", split_axis=0, concat_axis=0, tiled=True
+    ).astype(jnp.float32)
+    places = len(blk_bits)
+    up_total = wide_total[:, :, 0 : blocks * owned].reshape((shares, each) + (2,) * places + (owned,))
+    order = [2 + down_bits.index(bit) for bit in reversed(blk_bits)]
+    up_total = up_total.transpose((1, *order, 0, 2 + places)).reshape(each, hidden)
+    out_total = wide_total[:, :, blocks * owned :].transpose(1, 0, 2).reshape(each, features)
+
+    def of_heads(part):
+        return heads_total[:, :, part * slot : (part + 1) * slot].transpose(1, 0, 2).reshape(each, features)
+
+    sums = jnp.sum(heads_total[:, :, 3 * slot : 3 * slot + 4], axis=0)
+    return (
+        layer_out.reshape(patches.shape),
+        patches_grad.reshape(patches.shape),
+        of_heads(0),
+        of_heads(1),
+        of_heads(2),
+        out_total,
+        up_total,
+        down_total,
+        sums[:, 0],
+        sums[:, 1],
+        sums[:, 2],
+        sums[:, 3],
+    )
+
+
 def solution(mesh):
     in_specs = (
         P("mb", "blk", None),
@@ -347,4 +1163,7 @@
         P(("blk", "mb")),
         P(("blk", "mb")),
     )
-    return jax.shard_map(body, mesh=mesh, in_specs=in_specs, out_specs=out_specs, check_vma=False)
+    blocks, shares = mesh.shape["blk"], mesh.shape["mb"]
+    paired = blocks >= 4 and blocks & (blocks - 1) == 0 and shares == 4
+    chosen_body = fast_body if paired and H % blocks == 0 else body
+    return jax.shard_map(chosen_body, mesh=mesh, in_specs=in_specs, out_specs=out_specs, check_vma=False)

time: 1140 us -> 285 us (0.25)
  waiting for transfers between devices: 706 us -> 90.7 us
  local copies, waits for them, and re-layouts: 148 us -> 9.27 us
  matrix products: 102 us -> 0 us
  Pallas kernels: 0 us -> 98.3 us
  blocking collectives: 77.7 us -> 18.5 us
  other arithmetic: 51 us -> 19.3 us
  starting transfers between devices: 27.7 us -> 47.2 us
  between operations: 15.1 us -> 0.95 us
    reduce_scatter x6 -> x0, waiting for transfers between devices: 640 us -> none  [the longest x1 187 us: body(): lax.psum_scatter(gradients[5], ('blk', 'mb'), scatter_dimension=0, tiled=...]
    dot_general x74 -> x0, matrix products: 102 us -> none  [the longest x22 38.1 us: contract_rows(): lax.dot_general(left_side, right_side, (((0,), (0,)), ((), ())), preferre...]
    pallas_call x0 -> x9, Pallas kernels: none -> 98.3 us  [the longest x1 22.7 us: attend_back_call(): pl.pallas_call(kernel, grid=(micro_count, steps), in_specs=[pl.BlockSpec(...]
    ppermute x0 -> x26, waiting for transfers between devices: none -> 68.2 us  [_paired(): return lax.ppermute(values, axis, [(i, i ^ bit) for i in range(count)])]
    all_to_all x6, waiting for transfers between devices: 65.7 us -> 22.5 us  [the longest x4 17.9 us: swap(): lax.all_to_all(values, 'blk', split_axis=0, concat_axis=0, tiled=True)]
    unnamed x1 -> x0, blocking collectives: 39.6 us -> none
    unnamed x115 -> x36, local copies, waits for them, and re-layouts: 30.9 us -> 4.65 us
    convert_element_type x11 -> x0, local copies, waits for them, and re-layouts: 24.9 us -> none  [the longest x2 5.91 us: body(): from_items(query_grad_items).astype(jnp.bfloat16)]
  transfers between devices with their start and end apart: 12 -> 32, of which waited for: 10 -> 16; matrix products, arithmetic and copies ran while one was open for 18% -> 7% of each run, Pallas kernels for 0% -> 31%
where the time goes in v2:
time: 285 us; the launch traced here: 284 us
  Pallas kernels  98.3 us (34%)
  waiting for transfers between devices  90.7 us (32%)
  starting transfers between devices  47.2 us (17%)
  other arithmetic  19.3 us (7%)
  blocking collectives  18.5 us (6%)
  local copies, waits for them, and re-layouts  9.27 us (3%)
    ppermute x26, waiting for transfers between devices, _paired(): return lax.ppermute(values, axis, [(i, i ^ bit) for i in range(count)])  68.2 us
    pallas_call x1, Pallas kernels, attend_back_call(): pl.pallas_call(kernel, grid=(micro_count, steps), in_specs=[pl.BlockSpec(...  22.7 us
    ppermute x26, starting transfers between devices, _paired(): return lax.ppermute(values, axis, [(i, i ^ bit) for i in range(count)])  21 us
    pallas_call x1, Pallas kernels, grad_middle_call(): pl.pallas_call(kernel, grid_spec=pltpu.PrefetchScalarGridSpec(num_scalar_...  19.8 us
    all_to_all x4, starting transfers between devices, swap(): lax.all_to_all(values, 'blk', split_axis=0, concat_axis=0, tiled=True)  19.3 us
    all_to_all x1, blocking collectives, swap(): lax.all_to_all(values, 'blk', split_axis=0, concat_axis=0, tiled=True)  18.5 us
    all_to_all x4, waiting for transfers between devices, swap(): lax.all_to_all(values, 'blk', split_axis=0, concat_axis=0, tiled=True)  17.9 us
    pallas_call x1, Pallas kernels, middle_call(): pl.pallas_call(kernel, grid=(steps,), in_specs=[rows_spec, rows_spec, row...  13.8 us
  transfers between devices with their start and end apart: 32, of which 16 were waited for; matrix products, arithmetic and copies ran while one was open for 7% of the time, Pallas kernels for 31%

profile of v2, /device:TPU:0, one launch (start us, length us, event | category | flops | bytes accessed | tf_op | source)
XLA Modules:
  0.0 284.2 jit_solution(13513066079007932793)
XLA Ops:
  0.6 6.4 %project.1 = (bf16[8,256,384]{2,1,0:T(8,128)(2,1)}, bf16[128,1024]{1,0:T(8,128)(2,1)}, bf16[128,1024]{1,0:T(8,128)(2,1)}) custom-call(bf16[256,1024]{1,0:T(8,128)(2,1)} %bitcast.83, f32[1,1024]{1,0:T(1,128)} %bitcast.90, f32[1,1024]{1,0:T(1,128)} %bitcast.93, bf16[1024,1024]{1,0:T(8,128)(2,1)} %refs_5_.1, bf16[1024,1024]{1,0:T(8,128)(2,1)} %refs_6_.1, ...), custom_call_target="tpu_custom_call" | custom-call | flops 6000000000 | bytes 1 | tf_op jit(solution)/shard_map/project/pallas_call | solution.py:380
  7.1 7.4 %all-to-all-start = ((bf16[8,256,384]{2,1,0:T(8,128)(2,1)}), bf16[8,256,384]{2,1,0:T(8,128)(2,1)S(1)}, u32[]{:S(2)}, u32[]{:S(2)}) async-start(bf16[8,256,384]{2,1,0:T(8,128)(2,1)} %get-tuple-element.74), calls=%async_computation | async-start | bytes 3145728 | tf_op jit(solution)/shard_map/all_to_all | solution.py:1005
  16.1 11.9 %collective-permute-done.2.refs_6_ = bf16[256,1024]{1,0:T(8,128)(2,1)S(1)} collective-permute-done((bf16[256,1024]{1,0:T(8,128)(2,1)S(1)}, bf16[256,1024]{1,0:T(8,128)(2,1)S(1)}, u32[]{:S(2)}, u32[]{:S(2)}) %collective-permute-start.2) | collective-permute-done | bytes 524320 | tf_op jit(solution)/shard_map/ppermute | solution.py:852
  29.7 13.4 %collective-permute-done = bf16[128,1024]{1,0:T(8,128)(2,1)S(1)} collective-permute-done((bf16[128,1024]{1,0:T(8,128)(2,1)S(1)}, bf16[128,1024]{1,0:T(8,128)(2,1)S(1)}, u32[]{:S(2)}, u32[]{:S(2)}) %collective-permute-start) | collective-permute-done | bytes 262176 | tf_op jit(solution)/shard_map/ppermute | solution.py:852
  44.9 6.6 %all-to-all-done = bf16[8,256,384]{2,1,0:T(8,128)(2,1)S(1)} async-done(((bf16[8,256,384]{2,1,0:T(8,128)(2,1)}), bf16[8,256,384]{2,1,0:T(8,128)(2,1)S(1)}, u32[]{:S(2)}, u32[]{:S(2)}) %all-to-all-start) | async-done | bytes 1572896 | tf_op jit(solution)/shard_map/all_to_all | solution.py:1005
  52.6 11.0 %attend.1 = bf16[8,2,128,128]{3,2,1,0:T(8,128)(2,1)} custom-call(s32[2,8]{1,0:T(2,128)} %lengths_ref.3, bf16[8,2,128,384]{3,2,1,0:T(8,128)(2,1)} %bitcast.72), custom_call_target="tpu_custom_call" | custom-call | flops 11000000512 | bytes 1 | tf_op jit(solution)/shard_map/attend/pallas_call | solution.py:460
  64.9 18.5 %all_to_all.35.att_ref = bf16[8,256,128]{2,1,0:T(8,128)(2,1)} all-to-all(bf16[8,256,128]{2,1,0:T(8,128)(2,1)} %bitcast.87), channel_id=1, replica_groups=mesh['blk'=8,'mb'=4] {'blk'}, dimensions={0} | all-to-all | bytes 1048576 | tf_op jit(solution)/shard_map/all_to_all | solution.py:1005
  83.4 4.0 %mix.1 = (f32[256,1024]{1,0:T(8,128)}, bf16[256,1024]{1,0:T(8,128)(2,1)}, bf16[256,1024]{1,0:T(8,128)(2,1)}) custom-call(bf16[8,256,128]{2,1,0:T(8,128)(2,1)} %all_to_all.35.att_ref, bf16[256,1024]{1,0:T(8,128)(2,1)} %bitcast.84, f32[1,1024]{1,0:T(1,128)} %bitcast.95, f32[1,1024]{1,0:T(1,128)} %bitcast.99, bf16[1024,1024]{1,0:T(8,128)(2,1)} %wo_ref.3), custom_call_target="tpu_custom_call" | custom-call | flops 4000000000 | bytes 1 | tf_op jit(solution)/shard_map/mix/pallas_call | solution.py:581
  90.6 13.8 %middle.1 = (bf16[256,1024]{1,0:T(8,128)(2,1)}, f32[256,1024]{1,0:T(8,128)}) custom-call(bf16[256,1024]{1,0:T(8,128)(2,1)} %get-tuple-element.82.norm_ref.refs_0_, f32[256,1024]{1,0:T(8,128)} %get-tuple-element.83.mixed_ref, bf16[256,1024]{1,0:T(8,128)(2,1)} %bitcast.75, bf16[1024,4096]{1,0:T(8,128)(2,1)} %refs_17_.1, bf16[4096,1024]{1,0:T(8,128)(2,1)} %refs_19_.1), custom_call_target="tpu_custom_call" | custom-call | flops 20000000000 | bytes 1 | tf_op jit(solution)/shard_map/middle/pallas_call | solution.py:634
  104.4 8.6 %collective-permute-done.5 = bf16[256,1024]{1,0:T(8,128)(2,1)S(1)} collective-permute-done((bf16[256,1024]{1,0:T(8,128)(2,1)S(1)}, bf16[256,1024]{1,0:T(8,128)(2,1)S(1)}, u32[]{:S(2)}, u32[]{:S(2)}) %collective-permute-start.5) | collective-permute-done | bytes 524320 | tf_op jit(solution)/shard_map/ppermute | solution.py:852
  118.4 5.4 %middle_back.1 = (f32[256,1024]{1,0:T(8,128)}, bf16[8,256,128]{2,1,0:T(8,128)(2,1)}, f32[2,1024]{1,0:T(2,128)}, bf16[256,256]{1,0:T(8,128)(2,1)}, bf16[256,256]{...) custom-call(s32[2]{0:T(128)} %pad_add_fusion.place_ref, f32[256,1024]{1,0:T(8,128)} %get-tuple-element.83.mixed_ref, ...), custom_call_target="tpu_custom_call" | custom-call | flops 1 | bytes 1 | tf_op jit(solution)/shard_map/middle_back/pallas_call | solution.py:682
  126.6 3.7 %all-to-all-start.2 = ((bf16[8,256,128]{2,1,0:T(8,128)(2,1)}), bf16[8,256,128]{2,1,0:T(8,128)(2,1)S(1)}, u32[]{:S(2)}, u32[]{:S(2)}) async-start(bf16[8,256,128]{2,1,0:T(8,128)(2,1)} %get-tuple-element.91), calls=%async_computation.2 | async-start | bytes 1048576 | tf_op jit(solution)/shard_map/all_to_all | solution.py:1005
  130.3 4.2 %collective-permute-done.14.refs_14_ = bf16[256,256]{1,0:T(8,128)(2,1)S(1)} collective-permute-done((bf16[256,256]{1,0:T(8,128)(2,1)}, bf16[256,256]{1,0:T(8,128)(2,1)S(1)}, u32[]{:S(2)}, u32[]{:S(2)}) %collective-permute-start.14) | collective-permute-done | bytes 131104 | tf_op jit(solution)/shard_map/ppermute | solution.py:852
  139.7 19.8 %grad_middle.1 = (bf16[512,1024]{1,0:T(8,128)(2,1)}, f32[512,1024]{1,0:T(8,128)}, bf16[512,1280]{1,0:T(8,128)(2,1)}, f32[512,1280]{1,0:T(8,128)}) custom-call(s32[2]{0:T(128)} %pad_add_fusion.place_ref, bf16[256,1024]{1,0:T(8,128)(2,1)} %get-tuple-element.82.norm_ref.refs_0_, bf16[256,1024]{1,0:T(8,128)(2,1)} %collective-permute-done.7.refs_1_, ...), custom_call_target="tpu_custom_call" | custom-call | flops 1 | bytes 1 | tf_op jit(solution)/shard_map/grad_middle/pallas_call | solution.py:948
  161.4 22.7 %attend_back.1 = (bf16[8,128,384]{2,1,0:T(8,128)(2,1)}, bf16[8,128,384]{2,1,0:T(8,128)(2,1)}) custom-call(s32[2,8]{1,0:T(2,128)} %lengths_ref.3, bf16[8,2,128,384]{3,2,1,0:T(8,128)(2,1)} %bitcast.73, bf16[8,2,128,128]{3,2,1,0:T(8,128)(2,1)} %bitcast.82), custom_call_target="tpu_custom_call" | custom-call | flops 1 | bytes 1 | tf_op jit(solution)/shard_map/attend_back/pallas_call | solution.py:547
  184.0 3.8 %all-to-all-start.3 = ((bf16[8,128,384]{2,1,0:T(8,128)(2,1)}), bf16[8,128,384]{2,1,0:T(8,128)(2,1)S(1)}, u32[]{:S(2)}, u32[]{:S(2)}) async-start(bf16[8,128,384]{2,1,0:T(8,128)(2,1)} %get-tuple-element.112.refs_4_), calls=%async_computation.3 | async-start | bytes 1572864 | tf_op jit(solution)/shard_map/all_to_all | solution.py:1005
  192.8 8.0 %grad_heads.1 = (bf16[2,8,32,512]{3,2,1,0:T(8,128)(2,1)}, f32[2,8,32,512]{3,2,1,0:T(8,128)}) custom-call(s32[2]{0:T(128)} %pad_add_fusion.place_ref, bf16[512,1024]{1,0:T(8,128)(2,1)} %copy-done.1, bf16[512,1024]{1,0:T(8,128)(2,1)} %collective-permute-done.16.refs_1_, bf16[512,1024]{1,0:T(8,128)(2,1)} %copy-done.2, ...), custom_call_target="tpu_custom_call" | custom-call | flops 1 | bytes 1 | tf_op jit(solution)/shard_map/grad_heads/pallas_call | solution.py:812
  204.0 4.2 %all-to-all-done.3.refs_0_ = bf16[8,128,384]{2,1,0:T(8,128)(2,1)S(1)} async-done(((bf16[8,128,384]{2,1,0:T(8,128)(2,1)}), bf16[8,128,384]{2,1,0:T(8,128)(2,1)S(1)}, u32[]{:S(2)}, u32[]{:S(2)}) %all-to-all-start.3) | async-done | bytes 786464 | tf_op jit(solution)/shard_map/all_to_all | solution.py:1005
  210.7 4.5 %all-to-all-start.4 = ((bf16[8,128,384]{2,1,0:T(8,128)(2,1)}), bf16[8,128,384]{2,1,0:T(8,128)(2,1)}, u32[]{:S(2)}, u32[]{:S(2)}) async-start(bf16[8,128,384]{2,1,0:T(8,128)(2,1)} %get-tuple-element.122.refs_5_), calls=%async_computation.4 | async-start | bytes 1572864 | tf_op jit(solution)/shard_map/all_to_all | solution.py:1005
  229.8 7.2 %all-to-all-done.4.refs_1_ = bf16[8,128,384]{2,1,0:T(8,128)(2,1)} async-done(((bf16[8,128,384]{2,1,0:T(8,128)(2,1)}), bf16[8,128,384]{2,1,0:T(8,128)(2,1)}, u32[]{:S(2)}, u32[]{:S(2)}) %all-to-all-start.4) | async-done | bytes 786464 | tf_op jit(solution)/shard_map/all_to_all | solution.py:1005
  240.4 11.7 %collective-permute-done.23 = bf16[2,128,1280]{2,1,0:T(8,128)(2,1)} collective-permute-done((bf16[2,128,1280]{2,1,0:T(8,128)(2,1)}, bf16[2,128,1280]{2,1,0:T(8,128)(2,1)}, u32[]{:S(2)}, u32[]{:S(2)}) %collective-permute-start.23) | collective-permute-done | bytes 655392 | tf_op jit(solution)/shard_map/ppermute | solution.py:852
  255.9 7.3 %finish.1 = bf16[256,1024]{1,0:T(8,128)(2,1)} custom-call(bf16[8,128,384]{2,1,0:T(8,128)(2,1)} %copy-done.3, bf16[8,128,384]{2,1,0:T(8,128)(2,1)} %all-to-all-done.4.refs_1_, bf16[256,1024]{1,0:T(8,128)(2,1)} %bitcast.85, f32[256,1024]{1,0:T(8,128)} %get-tuple-element.125.refs_3_, f32[1,1024]{1,0:T(1,128)} %bitcast.92, bf16[1024,1024]{1,0:T(8,128)(2,1)} %refs_5_.1, ...), custom_call_target="tpu_custom_call" | custom-call | flops 1 | bytes 1 | tf_op jit(solution)/shard_map/finish/pallas_call | solution.py:741
  263.2 6.3 %collective-permute-done.24 = bf16[1,128,1280]{2,1,0:T(8,128)(2,1)S(1)} collective-permute-done((bf16[1,128,1280]{2,1,0:T(8,128)(2,1)S(1)}, bf16[1,128,1280]{2,1,0:T(8,128)(2,1)S(1)}, u32[]{:S(2)}, u32[]{:S(2)}) %collective-permute-start.24) | collective-permute-done | bytes 327712 | tf_op jit(solution)/shard_map/ppermute | solution.py:852
  277.0 4.6 %all-to-all-done.6 = bf16[4,32,1280]{2,1,0:T(8,128)(2,1)S(1)} async-done(((bf16[4,32,1280]{2,1,0:T(8,128)(2,1)}), bf16[4,32,1280]{2,1,0:T(8,128)(2,1)S(1)}, u32[]{:S(2)}, u32[]{:S(2)}) %all-to-all-start.6) | async-done | bytes 327712 | tf_op jit(solution)/shard_map/all_to_all | solution.py:1107
  (110 shorter events, 68.4 us)
Async XLA Ops:
  7.1 44.4 %all-to-all-start = ((bf16[8,256,384]{2,1,0:T(8,128)(2,1)}), bf16[8,256,384]{2,1,0:T(8,128)(2,1)S(1)}, u32[]{:S(2)}, u32[]{:S(2)}) async-start(bf16[8,256,384]{2,1,0:T(8,128)(2,1)} %get-tuple-element.74), calls=%async_computation | async-start | bytes 3145728 | tf_op jit(solution)/shard_map/all_to_all | solution.py:1005
  14.5 13.4 %collective-permute-start.2 = (bf16[256,1024]{1,0:T(8,128)(2,1)S(1)}, bf16[256,1024]{1,0:T(8,128)(2,1)S(1)}, u32[]{:S(2)}, u32[]{:S(2)}) collective-permute-start(bf16[256,1024]{1,0:T(8,128)(2,1)S(1)} %bitcast.78), channel_id=1, source_target_pairs={{0,2},{1,3},{2,0},{3,1},{4,6},{5,7},{6,4},{7,5},{8,10},{9,11},{10,... | collective-permute-start | bytes 1572872 | tf_op jit(solution)/shard_map/ppermute | solution.py:852
  16.1 28.0 %collective-permute-start.1 = (bf16[256,1024]{1,0:T(8,128)(2,1)S(1)}, bf16[256,1024]{1,0:T(8,128)(2,1)S(1)}, u32[]{:S(2)}, u32[]{:S(2)}) collective-permute-start(bf16[256,1024]{1,0:T(8,128)(2,1)S(1)} %bitcast.79), channel_id=1, source_target_pairs={{0,1},{1,0},{2,3},{3,2},{4,5},{5,4},{6,7},{7,6},{8,9},{9,8},{10,11... | collective-permute-start | bytes 1572872 | tf_op jit(solution)/shard_map/ppermute | solution.py:852
  27.9 17.0 %collective-permute-start.3 = (bf16[256,1024]{1,0:T(8,128)(2,1)S(1)}, bf16[256,1024]{1,0:T(8,128)(2,1)}, u32[]{:S(2)}, u32[]{:S(2)}) collective-permute-start(bf16[256,1024]{1,0:T(8,128)(2,1)S(1)} %collective-permute-done.2.refs_6_), channel_id=1, source_target_pairs={{0,1},{1,0},{2,3},{3,2},{4,5},{5,4},{6,7},{7,6},{8,9},{9,8},{10,11... | collective-permute-start | bytes 1572872 | tf_op jit(solution)/shard_map/ppermute | solution.py:852
  27.9 15.1 %collective-permute-start = (bf16[128,1024]{1,0:T(8,128)(2,1)S(1)}, bf16[128,1024]{1,0:T(8,128)(2,1)S(1)}, u32[]{:S(2)}, u32[]{:S(2)}) collective-permute-start(bf16[128,1024]{1,0:T(8,128)(2,1)S(1)} %copy-done.13), channel_id=1, source_target_pairs={{0,4},{4,0},{8,12},{12,8},{16,20},{20,16},{24,28},{28,24},{1,5},{5... | collective-permute-start | bytes 786440 | tf_op jit(solution)/shard_map/ppermute | solution.py:852
  51.5 13.4 %collective-permute-start.4 = (bf16[128,1024]{1,0:T(8,128)(2,1)S(1)}, bf16[128,1024]{1,0:T(8,128)(2,1)S(1)}, u32[]{:S(2)}, u32[]{:S(2)}) collective-permute-start(bf16[128,1024]{1,0:T(8,128)(2,1)S(1)} %copy-done.12), channel_id=1, source_target_pairs={{0,16},{4,20},{8,24},{12,28},{16,0},{20,4},{24,8},{28,12},{1,17},{... | collective-permute-start | bytes 786440 | tf_op jit(solution)/shard_map/ppermute | solution.py:852
  87.4 29.8 %collective-permute-start.7 = (bf16[256,1024]{1,0:T(8,128)(2,1)}, bf16[256,1024]{1,0:T(8,128)(2,1)}, u32[]{:S(2)}, u32[]{:S(2)}) collective-permute-start(bf16[256,1024]{1,0:T(8,128)(2,1)} %get-tuple-element.82.norm_ref.refs_0_), channel_id=1, source_target_pairs={{0,1},{1,0},{2,3},{3,2},{4,5},{5,4},{6,7},{7,6},{8,9},{9,8},{10,11... | collective-permute-start | bytes 1572872 | tf_op jit(solution)/shard_map/ppermute | solution.py:852
  87.4 29.8 %collective-permute-start.8 = (bf16[256,1024]{1,0:T(8,128)(2,1)}, bf16[256,1024]{1,0:T(8,128)(2,1)}, u32[]{:S(2)}, u32[]{:S(2)}) collective-permute-start(bf16[256,1024]{1,0:T(8,128)(2,1)} %get-tuple-element.82.norm_ref.refs_0_), channel_id=1, source_target_pairs={{0,2},{1,3},{2,0},{3,1},{4,6},{5,7},{6,4},{7,5},{8,10},{9,11},{10,... | collective-permute-start | bytes 1572872 | tf_op jit(solution)/shard_map/ppermute | solution.py:852
  88.9 24.1 %collective-permute-start.5 = (bf16[256,1024]{1,0:T(8,128)(2,1)S(1)}, bf16[256,1024]{1,0:T(8,128)(2,1)S(1)}, u32[]{:S(2)}, u32[]{:S(2)}) collective-permute-start(bf16[256,1024]{1,0:T(8,128)(2,1)S(1)} %pad_maximum_fusion.3), channel_id=1, source_target_pairs={{0,8},{4,12},{8,0},{12,4},{16,24},{20,28},{24,16},{28,20},{1,9},{5... | collective-permute-start | bytes 1572872 | tf_op jit(solution)/shard_map/ppermute | solution.py:852
  90.1 26.1 %collective-permute-start.6 = (bf16[256,1024]{1,0:T(8,128)(2,1)S(1)}, bf16[256,1024]{1,0:T(8,128)(2,1)}, u32[]{:S(2)}, u32[]{:S(2)}) collective-permute-start(bf16[256,1024]{1,0:T(8,128)(2,1)S(1)} %pad_maximum_fusion.2), channel_id=1, source_target_pairs={{0,16},{4,20},{8,24},{12,28},{16,0},{20,4},{24,8},{28,12},{1,17},{... | collective-permute-start | bytes 1572872 | tf_op jit(solution)/shard_map/ppermute | solution.py:852
  117.3 18.9 %collective-permute-start.11 = (bf16[256,1024]{1,0:T(8,128)(2,1)S(1)}, bf16[256,1024]{1,0:T(8,128)(2,1)}, u32[]{:S(2)}, u32[]{:S(2)}) collective-permute-start(bf16[256,1024]{1,0:T(8,128)(2,1)S(1)} %copy-done.8), channel_id=1, source_target_pairs={{0,2},{1,3},{2,0},{3,1},{4,6},{5,7},{6,4},{7,5},{8,10},{9,11},{10,... | collective-permute-start | bytes 1572872 | tf_op jit(solution)/shard_map/ppermute | solution.py:852
  123.8 36.8 %collective-permute-start.16 = (bf16[512,1024]{1,0:T(8,128)(2,1)S(1)}, bf16[512,1024]{1,0:T(8,128)(2,1)}, u32[]{:S(2)}, u32[]{:S(2)}) collective-permute-start(bf16[512,1024]{1,0:T(8,128)(2,1)S(1)} %pad_maximum_fusion.refs_0_), channel_id=1, source_target_pairs={{0,4},{4,0},{8,12},{12,8},{16,20},{20,16},{24,28},{28,24},{1,5},{5... | collective-permute-start | bytes 3145736 | tf_op jit(solution)/shard_map/ppermute | solution.py:852
  124.5 36.1 %collective-permute-start.17 = (bf16[512,1024]{1,0:T(8,128)(2,1)S(1)}, bf16[512,1024]{1,0:T(8,128)(2,1)}, u32[]{:S(2)}, u32[]{:S(2)}) collective-permute-start(bf16[512,1024]{1,0:T(8,128)(2,1)S(1)} %pad_maximum_fusion.1.refs_2_), channel_id=1, source_target_pairs={{0,8},{4,12},{8,0},{12,4},{16,24},{20,28},{24,16},{28,20},{1,9},{5... | collective-permute-start | bytes 3145736 | tf_op jit(solution)/shard_map/ppermute | solution.py:852
  126.6 34.0 %all-to-all-start.2 = ((bf16[8,256,128]{2,1,0:T(8,128)(2,1)}), bf16[8,256,128]{2,1,0:T(8,128)(2,1)S(1)}, u32[]{:S(2)}, u32[]{:S(2)}) async-start(bf16[8,256,128]{2,1,0:T(8,128)(2,1)} %get-tuple-element.91), calls=%async_computation.2 | async-start | bytes 1048576 | tf_op jit(solution)/shard_map/all_to_all | solution.py:1005
  159.5 28.3 %collective-permute-start.18 = (bf16[4,128,1024]{2,1,0:T(8,128)(2,1)}, bf16[4,128,1024]{2,1,0:T(8,128)(2,1)}, u32[]{:S(2)}, u32[]{:S(2)}) collective-permute-start(bf16[4,128,1024]{2,1,0:T(8,128)(2,1)} %bitcast.98), channel_id=1, source_target_pairs={{0,8},{4,12},{8,0},{12,4},{16,24},{20,28},{24,16},{28,20},{1,9},{5... | collective-permute-start | bytes 3145736 | tf_op jit(solution)/shard_map/ppermute | solution.py:852
  159.6 41.2 %collective-permute-start.19 = (bf16[4,128,1280]{2,1,0:T(8,128)(2,1)}, bf16[4,128,1280]{2,1,0:T(8,128)(2,1)}, u32[]{:S(2)}, u32[]{:S(2)}) collective-permute-start(bf16[4,128,1280]{2,1,0:T(8,128)(2,1)} %bitcast.97), channel_id=1, source_target_pairs={{0,4},{4,0},{8,12},{12,8},{16,20},{20,16},{24,28},{28,24},{1,5},{5... | collective-permute-start | bytes 3932168 | tf_op jit(solution)/shard_map/ppermute | solution.py:852
  184.0 24.1 %all-to-all-start.3 = ((bf16[8,128,384]{2,1,0:T(8,128)(2,1)}), bf16[8,128,384]{2,1,0:T(8,128)(2,1)S(1)}, u32[]{:S(2)}, u32[]{:S(2)}) async-start(bf16[8,128,384]{2,1,0:T(8,128)(2,1)} %get-tuple-element.112.refs_4_), calls=%async_computation.3 | async-start | bytes 1572864 | tf_op jit(solution)/shard_map/all_to_all | solution.py:1005
  190.8 19.9 %collective-permute-start.20 = (bf16[2,128,1024]{2,1,0:T(8,128)(2,1)}, bf16[2,128,1024]{2,1,0:T(8,128)(2,1)}, u32[]{:S(2)}, u32[]{:S(2)}) collective-permute-start(bf16[2,128,1024]{2,1,0:T(8,128)(2,1)} %get-tuple-element.118), channel_id=1, source_target_pairs={{0,4},{4,0},{8,12},{12,8},{16,20},{20,16},{24,28},{28,24},{1,5},{5... | collective-permute-start | bytes 1572872 | tf_op jit(solution)/shard_map/ppermute | solution.py:852
  210.7 26.2 %all-to-all-start.4 = ((bf16[8,128,384]{2,1,0:T(8,128)(2,1)}), bf16[8,128,384]{2,1,0:T(8,128)(2,1)}, u32[]{:S(2)}, u32[]{:S(2)}) async-start(bf16[8,128,384]{2,1,0:T(8,128)(2,1)} %get-tuple-element.122.refs_5_), calls=%async_computation.4 | async-start | bytes 1572864 | tf_op jit(solution)/shard_map/all_to_all | solution.py:1005
  215.2 37.0 %collective-permute-start.23 = (bf16[2,128,1280]{2,1,0:T(8,128)(2,1)}, bf16[2,128,1280]{2,1,0:T(8,128)(2,1)}, u32[]{:S(2)}, u32[]{:S(2)}) collective-permute-start(bf16[2,128,1280]{2,1,0:T(8,128)(2,1)} %get-tuple-element.127), channel_id=1, source_target_pairs={{0,8},{4,12},{8,0},{12,4},{16,24},{20,28},{24,16},{28,20},{1,9},{5... | collective-permute-start | bytes 1966088 | tf_op jit(solution)/shard_map/ppermute | solution.py:852
  221.6 32.4 %collective-permute-start.25 = (bf16[1,128,1024]{2,1,0:T(8,128)(2,1)}, bf16[1,128,1024]{2,1,0:T(8,128)(2,1)}, u32[]{:S(2)}, u32[]{:S(2)}) collective-permute-start(bf16[1,128,1024]{2,1,0:T(8,128)(2,1)} %fusion.5), channel_id=1, source_target_pairs={{0,16},{4,20},{8,24},{12,28},{16,0},{20,4},{24,8},{28,12},{1,17},{... | collective-permute-start | bytes 786440 | tf_op jit(solution)/shard_map/ppermute | solution.py:852
  236.9 32.6 %all-to-all-start.5 = ((bf16[8,32,512]{2,1,0:T(8,128)(2,1)}), bf16[8,32,512]{2,1,0:T(8,128)(2,1)S(1)}, u32[]{:S(2)}, u32[]{:S(2)}) async-start(bf16[8,32,512]{2,1,0:T(8,128)(2,1)} %bitcast_add_fusion.4), calls=%async_computation.5 | async-start | bytes 524288 | tf_op jit(solution)/shard_map/all_to_all | solution.py:1101
  253.1 16.4 %collective-permute-start.24 = (bf16[1,128,1280]{2,1,0:T(8,128)(2,1)S(1)}, bf16[1,128,1280]{2,1,0:T(8,128)(2,1)S(1)}, u32[]{:S(2)}, u32[]{:S(2)}) collective-permute-start(bf16[1,128,1280]{2,1,0:T(8,128)(2,1)S(1)} %fusion.3), channel_id=1, source_target_pairs={{0,16},{4,20},{8,24},{12,28},{16,0},{20,4},{24,8},{28,12},{1,17},{... | collective-permute-start | bytes 983048 | tf_op jit(solution)/shard_map/ppermute | solution.py:852
  271.4 10.2 %all-to-all-start.6 = ((bf16[4,32,1280]{2,1,0:T(8,128)(2,1)}), bf16[4,32,1280]{2,1,0:T(8,128)(2,1)S(1)}, u32[]{:S(2)}, u32[]{:S(2)}) async-start(bf16[4,32,1280]{2,1,0:T(8,128)(2,1)} %bitcast.29), calls=%async_computation.6 | async-start | bytes 655360 | tf_op jit(solution)/shard_map/all_to_all | solution.py:1107
  (25 other events, 230.7 us)

commit v3 on v2

--- a/solution.py
+++ b/solution.py
@@ -8,6 +8,7 @@
 from jax.sharding import PartitionSpec as P
 
 H = 16
+CHUNK = 8
 
 
 epsilon = 1e-05
@@ -343,7 +344,7 @@
 
 
 def _params(mib):
-    return pltpu.CompilerParams(vmem_limit_bytes=max(mib, 60) << 20)
+    return pltpu.CompilerParams(vmem_limit_bytes=mib << 20)
 
 
 def _cost(microseconds):
@@ -386,7 +387,7 @@
         out_shape=[jax.ShapeDtypeStruct((blocks, row_count, 3 * slot), jnp.bfloat16)]
         + [jax.ShapeDtypeStruct((tokens, features), jnp.bfloat16)] * (row_count // tokens),
         scratch_shapes=[pltpu.VMEM((row_count, features), jnp.bfloat16)],
-        compiler_params=_params(40),
+        compiler_params=_params(60),
         cost_estimate=_cost(6),
         name="project",
     )(rows, gain, bias, w_query, w_key, w_value)
@@ -428,7 +429,7 @@
     rows = step_blocks * tokens
     scale = 1.0 / math.sqrt(head_dim)
 
-    def kernel(lengths_ref, data_ref, out_ref):
+    def kernel(lengths_ref, data_ref, out_ref, exact_ref, log_ref):
         micro = pl.program_id(0)
         step = pl.program_id(1)
         row_docs = _doc_ids(
@@ -445,15 +446,22 @@
             keys = data_ref[pl.ds(first, count), 0, :, slot : 2 * slot].reshape(seq, slot)
             values = data_ref[pl.ds(first, count), 0, :, 2 * slot : 3 * slot].reshape(seq, slot)
             total = jnp.zeros((rows, slot), jnp.float32)
-            for mask, mask_wide in zip(
-                _head_masks(slot, head_dim, jnp.bfloat16), _head_masks(slot, head_dim, jnp.float32)
+            logs = jnp.zeros((rows, 128), jnp.float32)
+            lanes = lax.broadcasted_iota(jnp.int32, (1, 128), 1)
+            for head, (mask, mask_wide) in enumerate(
+                zip(_head_masks(slot, head_dim, jnp.bfloat16), _head_masks(slot, head_dim, jnp.float32))
             ):
                 scores = jnp.where(same, contract_cols(queries * mask, keys), masked_score)
-                exponent = jnp.exp(scores - jnp.max(scores, axis=-1, keepdims=True))
-                share = 1.0 / jnp.sum(exponent, axis=-1, keepdims=True)
+                most = jnp.max(scores, axis=-1, keepdims=True)
+                exponent = jnp.exp(scores - most)
+                exponent_sum = jnp.sum(exponent, axis=-1, keepdims=True)
+                share = 1.0 / exponent_sum
+                logs = jnp.where(lanes == head, most + jnp.log(exponent_sum), logs)
                 total = total + matmul(exponent.astype(jnp.bfloat16), values) * (share * mask_wide)
             total = jnp.where(row_docs < doc_count, total, 0.0)
             out_ref[...] = total.astype(jnp.bfloat16).reshape(step_blocks, 1, tokens, slot)
+            exact_ref[...] = total.reshape(step_blocks, 1, tokens, slot)
+            log_ref[0] = logs.T[0:8, :]
 
         _by_key_range(lengths_ref, micro, doc_count, step, rows, blocks, tokens, compute)
 
@@ -464,15 +472,23 @@
             pl.BlockSpec(memory_space=pltpu.SMEM),
             pl.BlockSpec((blocks, 1, tokens, width), lambda m, s: (0, m, 0, 0)),
         ],
-        out_specs=pl.BlockSpec((step_blocks, 1, tokens, slot), lambda m, s: (s, m, 0, 0)),
-        out_shape=jax.ShapeDtypeStruct((blocks, micro_count, tokens, slot), jnp.bfloat16),
-        compiler_params=_params(40),
+        out_specs=[
+            pl.BlockSpec((step_blocks, 1, tokens, slot), lambda m, s: (s, m, 0, 0)),
+            pl.BlockSpec((step_blocks, 1, tokens, slot), lambda m, s: (s, m, 0, 0)),
+            pl.BlockSpec((1, 8, rows), lambda m, s: (m, 0, s)),
+        ],
+        out_shape=[
+            jax.ShapeDtypeStruct((blocks, micro_count, tokens, slot), jnp.bfloat16),
+            jax.ShapeDtypeStruct((blocks, micro_count, tokens, slot), jnp.float32),
+            jax.ShapeDtypeStruct((micro_count, 8, blocks * tokens), jnp.float32),
+        ],
+        compiler_params=_params(32),
         cost_estimate=_cost(11),
         name="attend",
     )(lengths, received)
 
 
-def attend_back_call(received, grads, lengths, head_dim):
+def attend_back_call(received, grads, attended, logs, lengths, head_dim):
     blocks, micro_count, tokens, width = received.shape
     slot = width // 3
     doc_count = lengths.shape[1]
@@ -481,8 +497,8 @@
     steps = blocks // step_blocks
     scale = 1.0 / math.sqrt(head_dim)
 
-    def kernel(lengths_ref, data_ref, grads_ref, *refs):
-        out_refs, (key_total, value_total) = refs[:micro_count], refs[micro_count:]
+    def kernel(lengths_ref, data_ref, grads_ref, att_ref, log_ref, *refs):
+        out_refs, (key_total, value_total, turned) = refs[:micro_count], refs[micro_count:]
         micro = pl.program_id(0)
         step = pl.program_id(1)
 
@@ -490,6 +506,8 @@
         def _():
             key_total[...] = jnp.zeros_like(key_total)
             value_total[...] = jnp.zeros_like(value_total)
+            for block in range(blocks):
+                turned[block] = data_ref[block, 0, :, slot : 2 * slot].T
 
         row_docs = _doc_ids(
             lengths_ref, micro, doc_count, lax.broadcasted_iota(jnp.int32, (1, rows), 1) + step * rows
@@ -501,34 +519,41 @@
         out_grads = grads_ref[...].reshape(rows, slot)
         out_grads = out_grads * (column_docs < doc_count).astype(jnp.float32).astype(jnp.bfloat16)
 
+        inner = (out_grads.astype(jnp.float32) * att_ref[...].reshape(rows, slot)).T
+
         def compute(first, count):
-            seq = count * tokens
-            key_docs = _doc_ids(
-                lengths_ref, micro, doc_count, lax.broadcasted_iota(jnp.int32, (seq, 1), 0) + first * tokens
-            )
-            same = row_docs == key_docs
-            keys = data_ref[pl.ds(first, count), 0, :, slot : 2 * slot].reshape(seq, slot)
-            values = data_ref[pl.ds(first, count), 0, :, 2 * slot : 3 * slot].reshape(seq, slot)
-            query_total = jnp.zeros((rows, slot), jnp.float32)
-            key_parts, value_parts = [], []
-            for mask, mask_wide in zip(
-                _head_masks(slot, head_dim, jnp.bfloat16), _head_masks(slot, head_dim, jnp.float32)
-            ):
-                queries_head = queries * mask
-                grads_head = out_grads * mask
-                scores = jnp.where(same, contract_cols(keys, queries_head), masked_score)
-                exponent = jnp.exp(scores - jnp.max(scores, axis=0, keepdims=True))
-                probs = exponent * (1.0 / jnp.sum(exponent, axis=0, keepdims=True))
-                prob_grads = contract_cols(values, grads_head)
-                inner = jnp.sum(probs * prob_grads, axis=0, keepdims=True)
-                score_grads = (probs * (prob_grads - inner)).astype(jnp.bfloat16)
-                value_parts.append(matmul(probs.astype(jnp.bfloat16), grads_head))
-                key_parts.append(matmul(score_grads, queries_head))
-                query_total = query_total + contract_rows(score_grads, keys) * mask_wide
-            at = pl.ds(pl.multiple_of(first * tokens, tokens), seq)
-            key_total[at, :] += sum(key_parts)
-            value_total[at, :] += sum(value_parts)
-            query_grads = (query_total * scale).astype(jnp.bfloat16).reshape(step_blocks, tokens, slot)
+            chunk = min(CHUNK, count)
+            query_parts = [jnp.zeros((head_dim, rows), jnp.float32) for _ in range(slot // head_dim)]
+            masks = _head_masks(slot, head_dim, jnp.bfloat16)
+            for at in range(0, count, chunk):
+                seq = chunk * tokens
+                key_docs = _doc_ids(
+                    lengths_ref,
+                    micro,
+                    doc_count,
+                    lax.broadcasted_iota(jnp.int32, (seq, 1), 0) + (first + at) * tokens,
+                )
+                same = row_docs == key_docs
+                keys = data_ref[pl.ds(first + at, chunk), 0, :, slot : 2 * slot].reshape(seq, slot)
+                values = data_ref[pl.ds(first + at, chunk), 0, :, 2 * slot : 3 * slot].reshape(seq, slot)
+                keys_turned = jnp.concatenate([turned[first + at + other] for other in range(chunk)], axis=1)
+                key_made = jnp.zeros((seq, slot), jnp.float32)
+                value_made = jnp.zeros((seq, slot), jnp.float32)
+                for head, mask in enumerate(masks):
+                    lanes = slice(head * head_dim, (head + 1) * head_dim)
+                    queries_head, grads_head = queries * mask, out_grads * mask
+                    scores = jnp.where(same, contract_cols(keys, queries_head), masked_score)
+                    probs = jnp.exp(scores - log_ref[0, head : head + 1, :])
+                    prob_grads = contract_cols(values, grads_head)
+                    head_inner = jnp.sum(inner[lanes], axis=0, keepdims=True)
+                    score_grads = (probs * (prob_grads - head_inner)).astype(jnp.bfloat16)
+                    value_made = value_made + matmul(probs.astype(jnp.bfloat16), grads_head)
+                    key_made = key_made + matmul(score_grads, queries_head)
+                    query_parts[head] = query_parts[head] + matmul(keys_turned[lanes], score_grads)
+                to = pl.ds(pl.multiple_of((first + at) * tokens, tokens), seq)
+                key_total[to, :] += key_made
+                value_total[to, :] += value_made
+            query_grads = (jnp.concatenate(query_parts, axis=0).T * scale).astype(jnp.bfloat16).reshape(step_blocks, tokens, slot)
             for at, out_ref in enumerate(out_refs):
 
                 @pl.when(micro == at)
@@ -551,14 +576,17 @@
             pl.BlockSpec(memory_space=pltpu.SMEM),
             pl.BlockSpec((blocks, 1, tokens, width), lambda m, s: (0, m, 0, 0)),
             pl.BlockSpec((step_blocks, 1, tokens, slot), lambda m, s: (s, m, 0, 0)),
+            pl.BlockSpec((step_blocks, 1, tokens, slot), lambda m, s: (s, m, 0, 0)),
+            pl.BlockSpec((1, 8, rows), lambda m, s: (m, 0, s)),
         ],
         out_specs=[pl.BlockSpec((blocks, tokens, width), lambda m, s: (0, 0, 0))] * micro_count,
         out_shape=[jax.ShapeDtypeStruct((blocks, tokens, width), jnp.bfloat16)] * micro_count,
-        scratch_shapes=[pltpu.VMEM((blocks * tokens, slot), jnp.float32)] * 2,
-        compiler_params=_params(48),
-        cost_estimate=_cost(0),
+        scratch_shapes=[pltpu.VMEM((blocks * tokens, slot), jnp.float32)] * 2
+        + [pltpu.VMEM((blocks, slot, tokens), jnp.bfloat16)],
+        compiler_params=_params(60),
+        cost_estimate=_cost(3),
         name="attend_back",
-    )(lengths, received, grads)
+    )(lengths, received, grads, attended, logs)
 
 
 def _fixed(*shape):
@@ -569,26 +597,25 @@
     blocks, row_count, slot = attended.shape
     features = rows.shape[1]
 
-    def kernel(att_ref, rows_ref, gain_ref, bias_ref, wo_ref, mixed_ref, norm_ref, side_ref):
+    def kernel(att_ref, rows_ref, gain_ref, bias_ref, wo_ref, mixed_ref, both_ref):
         for block in range(blocks):
-            side_ref[:, block * slot : (block + 1) * slot] = att_ref[block]
-        value = rows_ref[...].astype(jnp.float32) + matmul(side_ref[...], wo_ref[...])
+            both_ref[1, :, block * slot : (block + 1) * slot] = att_ref[block]
+        value = rows_ref[...].astype(jnp.float32) + matmul(both_ref[1], wo_ref[...])
         mixed_ref[...] = value
         unit, _unused = _normalize(value)
-        norm_ref[...] = (unit * gain_ref[...] + bias_ref[...]).astype(jnp.bfloat16)
+        both_ref[0] = (unit * gain_ref[...] + bias_ref[...]).astype(jnp.bfloat16)
 
     rows_spec, vector = _fixed(row_count, features), _fixed(1, features)
     return pl.pallas_call(
         kernel,
         grid=(1,),
         in_specs=[_fixed(blocks, row_count, slot), rows_spec, vector, vector, _fixed(features, features)],
-        out_specs=[rows_spec] * 3,
+        out_specs=[rows_spec, _fixed(2, row_count, features)],
         out_shape=[
             jax.ShapeDtypeStruct((row_count, features), jnp.float32),
-            jax.ShapeDtypeStruct((row_count, features), jnp.bfloat16),
-            jax.ShapeDtypeStruct((row_count, features), jnp.bfloat16),
+            jax.ShapeDtypeStruct((2, row_count, features), jnp.bfloat16),
         ],
-        compiler_params=_params(56),
+        compiler_params=_params(24),
         cost_estimate=_cost(4),
         name="mix",
     )(attended, rows, gain, bias, w_out)
@@ -602,14 +629,17 @@
     return (upper * half).astype(jnp.bfloat16), (active_grad * slope).astype(jnp.bfloat16)
 
 
-def middle_call(norm, mixed, out_grad, w_up, w_down):
+def middle_call(place, both, mixed, out_grad, gain, w_out, w_up, w_down, blocks, shares):
     row_count, features = mixed.shape
     hidden = w_up.shape[1]
     wide = min(1024, hidden)
     sub = min(512, wide)
     steps = hidden // wide
-
-    def kernel(norm_ref, mixed_ref, grad_ref, wu_ref, wd_ref, out_ref, grad_total, total, active_all, upper_all):
+    slot, part = features // blocks, features // shares
+
+    def kernel(place_ref, norm_ref, mixed_ref, grad_ref, gain_ref, wo_ref, wu_ref, wd_ref, *refs):
+        out_ref, mixed_grad_ref, back_ref, sums_ref = refs[:4]
+        low_refs, (total, grad_total, active_all, upper_all, low_all) = refs[4 : 4 + shares], refs[4 + shares :]
         step = pl.program_id(0)
 
         @pl.when(step == 0)
@@ -619,7 +649,7 @@
 
         for chunk in range(0, wide, sub):
             active, upper_grad = _hidden_parts(
-                norm_ref[...], grad_ref[...], wu_ref[:, chunk : chunk + sub], wd_ref[chunk : chunk + sub, :]
+                norm_ref[0], grad_ref[...], wu_ref[:, chunk : chunk + sub], wd_ref[chunk : chunk + sub, :]
             )
             active_all[:, chunk : chunk + sub] = active
             upper_all[:, chunk : chunk + sub] = upper_grad
@@ -629,76 +659,56 @@
         @pl.when(step == steps - 1)
         def _():
             out_ref[...] = total[...].astype(jnp.bfloat16)
-
-    rows_spec = _fixed(row_count, features)
-    return pl.pallas_call(
-        kernel,
-        grid=(steps,),
-        in_specs=[
-            rows_spec,
-            rows_spec,
-            rows_spec,
-            pl.BlockSpec((features, wide), lambda i: (0, i)),
-            pl.BlockSpec((wide, features), lambda i: (i, 0)),
-        ],
-        out_specs=[rows_spec] * 2,
-        scratch_shapes=[
-            pltpu.VMEM((row_count, features), jnp.float32),
-            pltpu.VMEM((row_count, wide), jnp.bfloat16),
-            pltpu.VMEM((row_count, wide), jnp.bfloat16),
-        ],
-        out_shape=[
-            jax.ShapeDtypeStruct((row_count, features), jnp.bfloat16),
-            jax.ShapeDtypeStruct((row_count, features), jnp.float32),
-        ],
-        compiler_params=_params(56),
-        cost_estimate=_cost(20),
-        name="middle",
-    )(norm, mixed, out_grad, w_up, w_down)
-
-
-def middle_back_call(place, mixed, norm_grads, out_grad, gain, w_out, blocks, shares):
-    row_count, features = mixed.shape
-    slot = features // blocks
-    part = features // shares
-
-    def kernel(place_ref, mixed_ref, norm_ref, grad_ref, gain_ref, wo_ref, mixed_grad_ref, back_ref, sums_ref, *refs):
-        low_refs, low_all = refs[:shares], refs[shares]
-        unit, inverse = _normalize(mixed_ref[...])
-        grads = norm_ref[...]
-        sums_ref[0:1, :] = jnp.sum(grads * unit, axis=0, keepdims=True)
-        sums_ref[1:2, :] = jnp.sum(grads, axis=0, keepdims=True)
-        mixed_grad = grad_ref[...].astype(jnp.float32) + _normalize_back(grads, gain_ref[...], unit, inverse)
-        mixed_grad_ref[...] = mixed_grad
-        low = mixed_grad.astype(jnp.bfloat16)
-        low_all[...] = low
-        for share, low_ref in enumerate(low_refs):
-            low_ref[...] = low_all[:, pl.ds(pl.multiple_of((place_ref[1] ^ share) * part, 128), part)]
-        back = contract_cols(low, wo_ref[...]).astype(jnp.bfloat16)
-        for block in range(blocks):
-            back_ref[block] = back[:, block * slot : (block + 1) * slot]
+            unit, inverse = _normalize(mixed_ref[...])
+            grads = grad_total[...]
+            sums_ref[0:1, :] = jnp.sum(grads * unit, axis=0, keepdims=True)
+            sums_ref[1:2, :] = jnp.sum(grads, axis=0, keepdims=True)
+            mixed_grad = grad_ref[...].astype(jnp.float32) + _normalize_back(grads, gain_ref[...], unit, inverse)
+            mixed_grad_ref[...] = mixed_grad
+            low = mixed_grad.astype(jnp.bfloat16)
+            low_all[...] = low
+            for share, low_ref in enumerate(low_refs):
+                low_ref[...] = low_all[:, pl.ds(pl.multiple_of((place_ref[2] ^ share) * part, 128), part)]
+            back = contract_cols(low, wo_ref[...]).astype(jnp.bfloat16)
+            for block in range(blocks):
+                back_ref[block] = back[:, block * slot : (block + 1) * slot]
 
     rows_spec = _fixed(row_count, features)
     return pl.pallas_call(
         kernel,
         grid_spec=pltpu.PrefetchScalarGridSpec(
             num_scalar_prefetch=1,
-            grid=(1,),
-            in_specs=[rows_spec, rows_spec, rows_spec, _fixed(1, features), _fixed(features, features)],
-            out_specs=[rows_spec, _fixed(blocks, row_count, slot), _fixed(2, features)]
+            grid=(steps,),
+            in_specs=[
+                _fixed(1, row_count, features),
+                rows_spec,
+                rows_spec,
+                _fixed(1, features),
+                _fixed(features, features),
+                pl.BlockSpec((features, wide), lambda i, place: (0, i)),
+                pl.BlockSpec((wide, features), lambda i, place: (i, 0)),
+            ],
+            out_specs=[rows_spec, rows_spec, _fixed(blocks, row_count, slot), _fixed(2, features)]
             + [_fixed(row_count, part)] * shares,
-            scratch_shapes=[pltpu.VMEM((row_count, features), jnp.bfloat16)],
+            scratch_shapes=[
+                pltpu.VMEM((row_count, features), jnp.float32),
+                pltpu.VMEM((row_count, features), jnp.float32),
+                pltpu.VMEM((row_count, wide), jnp.bfloat16),
+                pltpu.VMEM((row_count, wide), jnp.bfloat16),
+                pltpu.VMEM((row_count, features), jnp.bfloat16),
+            ],
         ),
         out_shape=[
+            jax.ShapeDtypeStruct((row_count, features), jnp.bfloat16),
             jax.ShapeDtypeStruct((row_count, features), jnp.float32),
             jax.ShapeDtypeStruct((blocks, row_count, slot), jnp.bfloat16),
             jax.ShapeDtypeStruct((2, features), jnp.float32),
         ]
         + [jax.ShapeDtypeStruct((row_count, part), jnp.bfloat16)] * shares,
-        compiler_params=_params(56),
-        cost_estimate=_cost(0),
-        name="middle_back",
-    )(place, mixed, norm_grads, out_grad, gain, w_out)
+        compiler_params=_params(44),
+        cost_estimate=_cost(20),
+        name="middle",
+    )(place, both, mixed, out_grad, gain, w_out, w_up, w_down)
 
 
 def finish_call(received, rows, mixed_grad, gain, w_query, w_key, w_value):
@@ -756,8 +766,8 @@
             pltpu.VMEM((row_count, features), jnp.float32),
             pltpu.VMEM((3, row_count, wide), jnp.bfloat16),
         ],
-        compiler_params=_params(48),
-        cost_estimate=_cost(0),
+        compiler_params=_params(60),
+        cost_estimate=_cost(20),
         name="finish",
     )(*received, rows, mixed_grad, gain, w_query, w_key, w_value)
 
@@ -823,10 +833,42 @@
             ],
         ),
         out_shape=[jax.ShapeDtypeStruct(out, jnp.bfloat16), jax.ShapeDtypeStruct(out, jnp.float32)],
-        compiler_params=_params(48),
-        cost_estimate=_cost(0),
+        compiler_params=_params(60),
+        cost_estimate=_cost(20),
         name="grad_heads",
     )(place, *units, *made, gain, bias, sums, w_query, w_key, w_value)
+
+
+def assemble_call(place, parts, down_steps, blocks, owned):
+    shares = len(parts)
+    rows, width = parts[0].shape
+    part = width - blocks * owned
+
+    def kernel(place_ref, *refs):
+        part_refs, (up_ref, out_ref) = refs[:shares], refs[shares:]
+        for other, part_ref in enumerate(part_refs):
+            share = place_ref[2] ^ other
+            for at, block in enumerate(_ordered([_owner_stride(*step, shares) for step in down_steps])):
+                to = pl.multiple_of((block + share % 2 + share // 2 * shares) * owned, 128)
+                up_ref[:, pl.ds(to, owned)] = part_ref[:, at * owned : (at + 1) * owned].astype(jnp.float32)
+            out_ref[:, pl.ds(pl.multiple_of(share * part, 128), part)] = part_ref[:, blocks * owned :].astype(jnp.float32)
+
+    return pl.pallas_call(
+        kernel,
+        grid_spec=pltpu.PrefetchScalarGridSpec(
+            num_scalar_prefetch=1,
+            grid=(1,),
+            in_specs=[_fixed(rows, width)] * shares,
+            out_specs=[_fixed(rows, blocks * shares * owned), _fixed(rows, shares * part)],
+        ),
+        out_shape=[
+            jax.ShapeDtypeStruct((rows, blocks * shares * owned), jnp.float32),
+            jax.ShapeDtypeStruct((rows, shares * part), jnp.float32),
+        ],
+        compiler_params=_params(8),
+        cost_estimate=_cost(0),
+        name="assemble",
+    )(place, *parts)
 
 
 def _bits(count):
@@ -854,6 +896,19 @@
 
 def _bit_of(axis, bit):
     return (lax.axis_index(axis) // bit) % 2
+
+
+def _mesh_bit(place, step):
+    axis, bit = step
+    return place[("blk", "mb").index(axis)] // bit % 2
+
+
+def _owner_stride(axis, bit, shares):
+    return bit * shares if axis == "blk" else bit
+
+
+def _share_places(shares):
+    return [0, 1, shares, shares + 1]
 
 
 def _place_at(bits, step):
@@ -864,38 +919,43 @@
     return at
 
 
-def grad_middle_call(place, norms, out_grads, sides, lows, w_up, w_down, down_bits, up_bits):
-    shares = len(norms)
-    row_count, features = norms[0].shape
+def grad_middle_call(place, boths, out_grads, lows, w_up, w_down, down_steps, up_steps):
+    shares = len(boths)
+    _, row_count, features = boths[0].shape
     all_rows = shares * row_count
     hidden = w_up.shape[1]
-    blocks = 1 << len(up_bits)
-    owned = hidden // (blocks * shares)
+    blocks = 1 << len(up_steps)
+    owned, each = hidden // (blocks * shares), features // (blocks * shares)
+    down_places = [_owner_stride(*step, shares) for step in down_steps]
+    up_places = [_owner_stride(*step, shares) for step in up_steps]
+    share_places = _share_places(shares)
     part = lows[0].shape[1]
     half = blocks // 2
     pair = min(2, half)
     half_steps = half // pair
-    block_rows = features // blocks
     sub = min(2, shares)
 
     def kernel(place_ref, *refs):
-        groups, refs = [refs[at * shares : (at + 1) * shares] for at in range(4)], refs[4 * shares :]
+        groups, refs = [refs[at * shares : (at + 1) * shares] for at in range(3)], refs[3 * shares :]
         up_refs, down_refs, refs = refs[:pair], refs[pair : 2 * pair], refs[2 * pair :]
-        down_send, down_keep, up_send, up_keep, norm_all, grad_all, active_all, upper_all, up_all = refs
+        down_send, down_keep, up_send, up_keep, norm_all, norm_turned, grad_all, active_all, upper_all, up_all = refs
         step = pl.program_id(0)
-        low = place_ref[0] // up_bits[0] % 2
+        mine = _mesh_bit(place_ref, up_steps[0])
 
         def spread():
-            for at, block in enumerate(_ordered(up_bits[1:])):
-                rows = slice(at * block_rows, (at + 1) * block_rows)
-                up_send[rows, :] = up_all[block + up_bits[0] * (1 - low)].astype(jnp.bfloat16)
-                up_keep[rows, :] = up_all[block + up_bits[0] * low]
+            for at, block in enumerate(_ordered(up_places[1:])):
+                for share, other in enumerate(share_places):
+                    rows = slice((at * shares + share) * each, (at * shares + share + 1) * each)
+                    up_send[rows, :] = up_all[block + other + up_places[0] * (1 - mine)].astype(jnp.bfloat16)
+                    up_keep[rows, :] = up_all[block + other + up_places[0] * mine]
 
         @pl.when(step == 0)
         def _():
             for at in range(shares):
-                norm_all[at * row_count : (at + 1) * row_count, :] = groups[0][at][...]
-                grad_all[at * row_count : (at + 1) * row_count, :] = groups[1][at][...]
+                rows = slice(at * row_count, (at + 1) * row_count)
+                norm_all[rows, :] = groups[0][at][0]
+                norm_turned[:, rows] = groups[0][at][0].T
+                grad_all[rows, :] = groups[1][at][...]
 
         @pl.when(step < 2 * half_steps)
         def _():
@@ -916,23 +976,23 @@
             def _():
                 down_keep[...] = down_made
 
-            up_all[...] = contract_rows(norm_all[...], upper_all[...]).reshape(blocks, block_rows, pair * owned)
+            up_all[...] = matmul(norm_turned[...], upper_all[...]).reshape(blocks * shares, each, pair * owned)
             spread()
 
         @pl.when(step == 2 * half_steps)
         def _():
             made = jnp.zeros((features, part), jnp.float32)
-            for side_ref, low_ref in zip(groups[2], groups[3]):
-                made = made + contract_rows(side_ref[...], low_ref[...])
-            up_all[...] = made.reshape(blocks, block_rows, part)
+            for both_ref, low_ref in zip(groups[0], groups[2]):
+                made = made + contract_rows(both_ref[1], low_ref[...])
+            up_all[...] = made.reshape(blocks * shares, each, part)
             spread()
 
     def first_bit(i, place):
-        return (place[0] // down_bits[0] + 1 + jnp.minimum(i, 2 * half_steps - 1) // half_steps) % 2
+        return (_mesh_bit(place, down_steps[0]) + 1 + jnp.minimum(i, 2 * half_steps - 1) // half_steps) % 2
 
     def unit_block(i, place, at):
-        inner = _place_at(down_bits[1:], jnp.minimum(i, 2 * half_steps - 1) % half_steps * pair + at)
-        return (inner + down_bits[0] * first_bit(i, place)) * shares + place[1]
+        inner = _place_at(down_places[1:], jnp.minimum(i, 2 * half_steps - 1) % half_steps * pair + at)
+        return inner + down_places[0] * first_bit(i, place) + place[0] % 2 * shares + place[1] % 2
 
     ups = [
         pl.BlockSpec((features, owned), lambda i, place, at=at: (0, unit_block(i, place, at))) for at in range(pair)
@@ -950,7 +1010,11 @@
         grid_spec=pltpu.PrefetchScalarGridSpec(
             num_scalar_prefetch=1,
             grid=(2 * half_steps + 1,),
-            in_specs=[_fixed(row_count, features)] * (3 * shares) + [_fixed(row_count, part)] * shares + ups + downs,
+            in_specs=[_fixed(2, row_count, features)] * shares
+            + [_fixed(row_count, features)] * shares
+            + [_fixed(row_count, part)] * shares
+            + ups
+            + downs,
             out_specs=[
                 pl.BlockSpec((pair * owned, features), lambda i, place: (jnp.minimum(i, half_steps - 1), 0)),
                 pl.BlockSpec((pair * owned, features), lambda i, place: (jnp.clip(i - half_steps, 0, half_steps - 1), 0)),
@@ -959,30 +1023,103 @@
             ],
             scratch_shapes=[
                 pltpu.VMEM((all_rows, features), jnp.bfloat16),
+                pltpu.VMEM((features, all_rows), jnp.bfloat16),
                 pltpu.VMEM((all_rows, features), jnp.bfloat16),
                 pltpu.VMEM((all_rows, pair * owned), jnp.bfloat16),
                 pltpu.VMEM((all_rows, pair * owned), jnp.bfloat16),
-                pltpu.VMEM((blocks, block_rows, pair * owned), jnp.float32),
+                pltpu.VMEM((blocks * shares, each, pair * owned), jnp.float32),
             ],
         ),
         out_shape=[jax.ShapeDtypeStruct(shape, dtype) for shape in shapes for dtype in (jnp.bfloat16, jnp.float32)],
-        compiler_params=_params(56),
+        compiler_params=_params(60),
+        cost_estimate=_cost(20),
+        name="grad_middle",
+    )(place, *boths, *out_grads, *lows, *([w_up] * pair), *([w_down] * pair))
+
+
+def halve_call(place, keep, received, step, cost):
+    count, rows, columns = keep.shape
+    half = count // 2
+
+    def kernel(place_ref, keep_theirs, keep_mine, got_theirs, got_mine, theirs_ref, mine_ref):
+        theirs_ref[...] = (keep_theirs[...] + got_theirs[...].astype(jnp.float32)).astype(jnp.bfloat16)
+        mine_ref[...] = keep_mine[...] + got_mine[...].astype(jnp.float32)
+
+    def block(which):
+        return pl.BlockSpec(
+            (1, rows, columns), lambda i, place: (i + half * ((_mesh_bit(place, step) + which) % 2), 0, 0)
+        )
+
+    out = pl.BlockSpec((1, rows, columns), lambda i, place: (i, 0, 0))
+    return pl.pallas_call(
+        kernel,
+        grid_spec=pltpu.PrefetchScalarGridSpec(
+            num_scalar_prefetch=1,
+            grid=(half,),
+            in_specs=[block(1), block(0), block(1), block(0)],
+            out_specs=[out, out],
+        ),
+        out_shape=[
+            jax.ShapeDtypeStruct((half, rows, columns), jnp.bfloat16),
+            jax.ShapeDtypeStruct((half, rows, columns), jnp.float32),
+        ],
+        compiler_params=_params(16),
+        cost_estimate=_cost(cost),
+        name="halve",
+    )(place, keep, keep, received, received)
+
+
+def close_call(place, keep, received, shares):
+    rows, width = keep.shape
+    each = rows // shares
+
+    def kernel(place_ref, keep_ref, got_ref, *refs):
+        out_refs, total = refs[:-1], refs[-1]
+        total[...] = (keep_ref[...] + got_ref[...].astype(jnp.float32)).reshape(shares, each, width)
+        for share, out_ref in enumerate(out_refs):
+            out_ref[...] = total[place_ref[2] ^ share].astype(jnp.bfloat16)
+
+    return pl.pallas_call(
+        kernel,
+        grid_spec=pltpu.PrefetchScalarGridSpec(
+            num_scalar_prefetch=1,
+            grid=(1,),
+            in_specs=[_fixed(rows, width)] * 2,
+            out_specs=[_fixed(each, width)] * shares,
+            scratch_shapes=[pltpu.VMEM((shares, each, width), jnp.float32)],
+        ),
+        out_shape=[jax.ShapeDtypeStruct((each, width), jnp.bfloat16)] * shares,
+        compiler_params=_params(8),
         cost_estimate=_cost(0),
-        name="grad_middle",
-    )(place, *norms, *out_grads, *sides, *lows, *([w_up] * pair), *([w_down] * pair))
-
-
-def halved(keep, received, axis, bit):
-    pair = (2, keep.shape[0] // 2) + keep.shape[1:]
-    keep, received = keep.reshape(pair), received.reshape(pair)
-    mine = _bit_of(axis, bit)
-
-    def half(index):
-        return lax.dynamic_index_in_dim(keep, index, 0, False) + lax.dynamic_index_in_dim(
-            received, index, 0, False
-        ).astype(jnp.float32)
-
-    return half(1 - mine).astype(jnp.bfloat16), half(mine)
+        name="close",
+    )(place, keep, received)
+
+
+def assemble_heads_call(parts, slot):
+    blocks, rows, _ = parts.shape
+
+    def kernel(parts_ref, *refs):
+        weight_refs, norm_refs = refs[:3], refs[3:]
+        for part, ref in enumerate(weight_refs):
+            for block in range(blocks):
+                ref[:, block * slot : (block + 1) * slot] = parts_ref[
+                    block, :, part * slot : (part + 1) * slot
+                ].astype(jnp.float32)
+        sums = jnp.zeros((rows, 128), jnp.float32)
+        for block in range(blocks):
+            sums = sums + parts_ref[block, :, 3 * slot :].astype(jnp.float32)
+        turned = jnp.concatenate([sums, jnp.zeros((128 - rows, 128), jnp.float32)], axis=0).T
+        for at, ref in enumerate(norm_refs):
+            ref[...] = turned[at : at + 1, 0:rows]
+
+    return pl.pallas_call(
+        kernel,
+        out_shape=[jax.ShapeDtypeStruct((rows, blocks * slot), jnp.float32)] * 3
+        + [jax.ShapeDtypeStruct((1, rows), jnp.float32)] * 4,
+        compiler_params=_params(8),
+        cost_estimate=_cost(0),
+        name="assemble_heads",
+    )(parts)
 
 
 def fast_body(
@@ -1007,31 +1144,44 @@
     def by_micro(values):
         return values.reshape(blocks, micro_count, tokens, values.shape[-1])
 
-    place = jnp.stack([lax.axis_index("blk"), lax.axis_index("mb")]).astype(jnp.int32)
+    at_blk, at_mb = lax.axis_index("blk"), lax.axis_index("mb")
+    place = jnp.stack([at_blk, at_mb, at_mb % 2 + at_blk % 2 * 2]).astype(jnp.int32)
     blk_bits = _bits(blocks)
-    down_bits = [blk_bits[1], blk_bits[0], *blk_bits[2:]]
+    up_steps = [("mb", 2), *(("blk", bit) for bit in blk_bits[1:])]
+    down_steps = [up_steps[1], up_steps[0], *up_steps[2:]]
     each, owned, block_rows = features // (blocks * shares), hidden // (blocks * shares), features // blocks
     tie = lax.optimization_barrier
 
     def grown(values, bit):
         return jnp.concatenate([values, _paired(values, "blk", bit)], axis=0)
 
+    def to_share(values, other):
+        if other == 1:
+            return _paired(values, "mb", 1)
+        if other == 2:
+            return _paired(values, "blk", 1)
+        return lax.ppermute(values, ("blk", "mb"), [(i, i ^ (shares + 1)) for i in range(blocks * shares)])
+
     def shared(values):
-        over = _paired(values, "mb", 2)
-        return [values, _paired(values, "mb", 1), over, _paired(over, "mb", 1)]
+        over = to_share(values, 2)
+        return [values, to_share(values, 1), over, to_share(over, 1)]
 
     send, units_first, units_last = project_call(
         rows, gain_one, bias_one, w_query, w_key, w_value, blocks, tokens
     )
     received = by_micro(swap(send))
-    douts = shared(dout)
+    dout_parts = [out_grad[micro] for micro in range(micro_count)]
+    dout_over = [to_share(part, 2) for part in dout_parts]
     units_last = grown(units_last, blk_bits[0])
-    units_last, received, douts = tie((units_last, received, douts))
+    units_last, received, dout_over[0] = tie((units_last, received, dout_over[0]))
     units_first, received = tie((units_first, received))
     units_first = grown(units_first, blk_bits[-1])
-    attended = attend_call(received, seg_lengths, head_dim).reshape(blocks, row_count, slot)
-    attended, units_first = tie((attended, units_first))
+    own_attended, exact, logs = attend_call(received, seg_lengths, head_dim)
+    attended, units_first, dout_over = tie((own_attended.reshape(blocks, row_count, slot), units_first, dout_over))
     attended, units_first, units_last = tie((swap(attended), units_first, units_last))
+    dout_peer = to_share(dout, 1)
+    dout_over = jnp.concatenate(dout_over, axis=0)
+    douts = [dout, dout_peer, dout_over, to_share(dout_over, 1)]
     for bit in blk_bits[-2:0:-1]:
         units_first = grown(units_first, bit)
     for bit in blk_bits[:1:-1]:
@@ -1039,97 +1189,79 @@
     places_first = _ordered_low([*blk_bits[:0:-1], blk_bits[0]])
     places_last = _ordered_low([blk_bits[0], *blk_bits[:1:-1], blk_bits[1]])
 
-    mixed, norm, side = mix_call(attended, rows, gain_two, bias_two, w_out)
-    norm_peer, norm_over = _paired(norm, "mb", 1), _paired(norm, "mb", 2)
-    layer_out, norm_grads = middle_call(norm, mixed, dout, w_up, w_down)
-    norm_grads, units_first, units_last, norm_peer, norm_over, side = tie(
-        (norm_grads, units_first, units_last, norm_peer, norm_over, side)
-    )
-    norms = [norm, norm_peer, norm_over, _paired(norm_over, "mb", 1)]
-    sides = shared(side)
+    mixed, both = mix_call(attended, rows, gain_two, bias_two, w_out)
+    both_peer, both_over = to_share(both, 1), to_share(both, 2)
+    layer_out, mixed_grad, back, sums_two, *lows = middle_call(
+        place, both, mixed, dout, gain_two, w_out, w_up, w_down, blocks, shares
+    )
+    back, lows, units_first, units_last, both_peer, both_over = tie(
+        (back, lows, units_first, units_last, both_peer, both_over)
+    )
+    boths = [both, both_peer, both_over, to_share(both_over, 1)]
     units_first_peer = _paired(units_first, "blk", blk_bits[0])
     units_last_peer = _paired(units_last, "blk", blk_bits[1])
-    mixed_grad, back, sums_two, *lows = middle_back_call(
-        place, mixed, norm_grads, dout, gain_two, w_out, blocks, shares
-    )
     grads = by_micro(swap(back))
-    lows = [lows[0]] + [_paired(lows[share], "mb", share) for share in range(1, shares)]
+    lows = [lows[0]] + [to_share(lows[share], share) for share in range(1, shares)]
     down_theirs, down_keep, up_theirs, up_keep = grad_middle_call(
-        place, norms, douts, sides, lows, w_up, w_down, down_bits, blk_bits
+        place, boths, douts, lows, w_up, w_down, down_steps, up_steps
     )
     down_theirs, down_keep = (value.reshape(-1, owned, features) for value in (down_theirs, down_keep))
     up_theirs, up_keep = (value.reshape(-1, block_rows, value.shape[-1]) for value in (up_theirs, up_keep))
-    sums = {"down": (down_theirs, down_keep, down_bits), "up": (up_theirs, up_keep, blk_bits)}
-
-    def sent(name, step):
-        return _paired(sums[name][0], "blk", sums[name][2][step])
-
-    def added(name, received, step):
-        theirs, keep = halved(sums[name][1], received, "blk", sums[name][2][step])
-        sums[name] = (theirs, keep, sums[name][2])
-
-    down_received, up_received = sent("down", 0), sent("up", 0)
-    grads, down_keep, units_first_peer, units_last_peer = tie(
-        (grads, sums["down"][1], units_first_peer, units_last_peer)
-    )
-    sums["down"] = (sums["down"][0], down_keep, down_bits)
-    made = attend_back_call(received, grads, seg_lengths, head_dim)
+    down_received, up_received = _paired(down_theirs, *down_steps[0]), _paired(up_theirs, *up_steps[0])
+    grads, down_keep, units_first_peer, units_last_peer = tie((grads, down_keep, units_first_peer, units_last_peer))
+    made = attend_back_call(received, grads, exact, logs, seg_lengths, head_dim)
     returned = [swap(made[0])]
-    added("down", down_received, 1)
-    made, theirs = tie((made, sums["down"][0]))
-    sums["down"] = (theirs, *sums["down"][1:])
-    down_received = sent("down", 1)
+
+    def then(done, *values):
+        return tie((done, values))[1]
+
+    returned += [swap(tie((values, returned[0]))[0]) for values in made[1:]]
+    made = tie(made)
+    down_theirs, down_keep = halve_call(place, *then(made[0], down_keep, down_received), down_steps[1], 0)
+    down_received = _paired(down_theirs, *down_steps[1])
+    up_theirs, up_keep = halve_call(place, *then(down_keep, up_keep, up_received), up_steps[1], 5)
+    up_received = _paired(up_theirs, *up_steps[1])
+    made = then(up_keep, *made)
     heads_send, heads_keep = grad_heads_call(
         place, (units_first, units_first_peer, units_last, units_last_peer), (places_first, places_last),
         made, gain_one, bias_one, sums_two, w_query, w_key, w_value, shares,
     )
-    added("up", up_received, 1)
-    returned[0], theirs, down_received, heads_send = tie((returned[0], sums["up"][0], down_received, heads_send))
-    sums["up"] = (theirs, *sums["up"][1:])
-    returned += [swap(tie((values, returned[0]))[0]) for values in made[1:]]
-    up_received = sent("up", 1)
-    flat = (-1,) + heads_keep.shape[2:]
-    heads_received = _paired(heads_send, "mb", 1).reshape(flat)
-    for step in range(2, len(blk_bits)):
-        added("down", down_received, step)
-        down_received = sent("down", step)
-        added("up", up_received, step)
-        up_received = sent("up", step)
-    heads_theirs, heads_keep = halved(heads_keep.reshape(flat), heads_received, "mb", 2)
-    heads_total = heads_keep + _paired(heads_theirs, "mb", 2).astype(jnp.float32)
-    heads_total, returned = tie((heads_total, returned))
-    heads_total = lax.all_to_all(heads_total.astype(jnp.bfloat16), "blk", split_axis=0, concat_axis=0, tiled=True)
+    pair = (shares // 2, -1, heads_keep.shape[-1])
+    heads_received = _paired(heads_send, "mb", 1).reshape(pair)
+    down_keep, down_received = then(heads_keep, down_keep, down_received)
+    for step in down_steps[2:]:
+        down_theirs, down_keep = halve_call(place, down_keep, down_received, step, 0)
+        down_received = _paired(down_theirs, *step)
+    up_keep, up_received = then(down_keep, up_keep, up_received)
+    for step in up_steps[2:]:
+        up_theirs, up_keep = halve_call(place, up_keep, up_received, step, 3)
+        up_received = _paired(up_theirs, *step)
+    heads_theirs, heads_keep = halve_call(
+        place, *then(up_keep, heads_keep.reshape(pair), heads_received), ("mb", 2), 0
+    )
+    heads_received = _paired(heads_theirs, "mb", 2)
+    returned = list(then(heads_keep, *returned))
     patches_grad = finish_call(returned, rows, mixed_grad, gain_one, w_query, w_key, w_value)
-    patches_grad, heads_total, up_received = tie((patches_grad, heads_total, up_received))
-    heads_total = heads_total.astype(jnp.float32)
-    down_total = (sums["down"][1] + down_received.astype(jnp.float32))[0]
-    wide_total = (sums["up"][1] + up_received.astype(jnp.float32))[0]
-    wide_total = lax.all_to_all(
-        wide_total.astype(jnp.bfloat16).reshape(shares, each, -1), "mb", split_axis=0, concat_axis=0, tiled=True
-    ).astype(jnp.float32)
-    places = len(blk_bits)
-    up_total = wide_total[:, :, 0 : blocks * owned].reshape((shares, each) + (2,) * places + (owned,))
-    order = [2 + down_bits.index(bit) for bit in reversed(blk_bits)]
-    up_total = up_total.transpose((1, *order, 0, 2 + places)).reshape(each, hidden)
-    out_total = wide_total[:, :, blocks * owned :].transpose(1, 0, 2).reshape(each, features)
-
-    def of_heads(part):
-        return heads_total[:, :, part * slot : (part + 1) * slot].transpose(1, 0, 2).reshape(each, features)
-
-    sums = jnp.sum(heads_total[:, :, 3 * slot : 3 * slot + 4], axis=0)
+    up_keep, up_received = then(patches_grad, up_keep, up_received)
+    parts = close_call(place, up_keep[0], up_received[0], shares)
+    heads_keep, heads_received = then(parts, heads_keep, heads_received)
+    heads_total = (heads_keep + heads_received.astype(jnp.float32)).astype(jnp.bfloat16)
+    heads_total = swap(heads_total.reshape(blocks, each, heads_keep.shape[-1]))
+    parts = [parts[0]] + [to_share(parts[share], share) for share in range(1, shares)]
+    up_total, out_total = assemble_call(place, parts, down_steps, blocks, owned)
+    down_keep, down_received = then(up_total, down_keep, down_received)
+    down_total = (down_keep + down_received.astype(jnp.float32))[0]
+    query_total, key_total, value_total, *sums = assemble_heads_call(then(down_total, heads_total)[0], slot)
     return (
         layer_out.reshape(patches.shape),
         patches_grad.reshape(patches.shape),
-        of_heads(0),
-        of_heads(1),
-        of_heads(2),
+        query_total,
+        key_total,
+        value_total,
         out_total,
         up_total,
         down_total,
-        sums[:, 0],
-        sums[:, 1],
-        sums[:, 2],
-        sums[:, 3],
+        *(value.reshape(each) for value in sums),
     )
 
 

time: 285 us -> 266 us (0.933)
  blocking collectives: 18.5 us -> 0 us
  other arithmetic: 19.3 us -> 3.5 us
  starting transfers between devices: 47.2 us -> 57.6 us
  waiting for transfers between devices: 90.7 us -> 99.3 us
  Pallas kernels: 98.3 us -> 95.3 us
    all_to_all x4 -> x6, waiting for transfers between devices: 17.9 us -> 44.3 us  [swap(): lax.all_to_all(values, 'blk', split_axis=0, concat_axis=0, tiled=True)]
    all_to_all x1 -> x0, blocking collectives: 18.5 us -> none  [swap(): lax.all_to_all(values, 'blk', split_axis=0, concat_axis=0, tiled=True)]
    ppermute x26 -> x25, waiting for transfers between devices: 68.2 us -> 53.8 us  [_paired(): return lax.ppermute(values, axis, [(i, i ^ bit) for i in range(count)])]
    all_to_all x4 -> x6, starting transfers between devices: 19.3 us -> 28.3 us  [swap(): lax.all_to_all(values, 'blk', split_axis=0, concat_axis=0, tiled=True)]
    add x3 -> x0, other arithmetic: 8.05 us -> none  [the longest x2 6.13 us: half(): lax.dynamic_index_in_dim(keep, index, 0, False)]
    ppermute x26 -> x25, starting transfers between devices: 21 us -> 28.8 us  [_paired(): return lax.ppermute(values, axis, [(i, i ^ bit) for i in range(count)])]
    all_to_all x2 -> x0, starting transfers between devices: 6.87 us -> none  [the longest x1 3.45 us: fast_body(): lax.all_to_all(wide_total.astype(jnp.bfloat16).reshape(shares, each, -1),...]
    convert_element_type x6 -> x1, other arithmetic: 6.51 us -> 0.77 us  [fast_body(): (heads_keep + heads_received.astype(jnp.float32)).astype(jnp.bfloat16)]
  transfers between devices with their start and end apart: 32 -> 33, of which waited for: 16 -> 14; matrix products, arithmetic and copies ran while one was open for 7% -> 2% of each run, Pallas kernels for 31% -> 33%
where the time goes in v3:
time: 266 us; the launch traced here: 265 us
  waiting for transfers between devices  99.3 us (37%)
  Pallas kernels  95.3 us (36%)
  starting transfers between devices  57.6 us (22%)
  local copies, waits for them, and re-layouts  8.61 us (3%)
  other arithmetic  3.5 us (1%)
    ppermute x25, waiting for transfers between devices, _paired(): return lax.ppermute(values, axis, [(i, i ^ bit) for i in range(count)])  53.8 us
    all_to_all x6, waiting for transfers between devices, swap(): lax.all_to_all(values, 'blk', split_axis=0, concat_axis=0, tiled=True)  44.3 us
    ppermute x25, starting transfers between devices, _paired(): return lax.ppermute(values, axis, [(i, i ^ bit) for i in range(count)])  28.8 us
    all_to_all x6, starting transfers between devices, swap(): lax.all_to_all(values, 'blk', split_axis=0, concat_axis=0, tiled=True)  28.3 us
    pallas_call x1, Pallas kernels, grad_middle_call(): pl.pallas_call(kernel, grid_spec=pltpu.PrefetchScalarGridSpec(num_scalar_...  20.7 us
    pallas_call x1, Pallas kernels, attend_back_call(): pl.pallas_call(kernel, grid=(micro_count, steps), in_specs=[pl.BlockSpec(...  17.1 us
    pallas_call x1, Pallas kernels, middle_call(): pl.pallas_call(kernel, grid_spec=pltpu.PrefetchScalarGridSpec(num_scalar_...  15.2 us
    pallas_call x1, Pallas kernels, attend_call(): pl.pallas_call(kernel, grid=(micro_count, blocks // step_blocks), in_spec...  10.5 us
  transfers between devices with their start and end apart: 33, of which 14 were waited for; matrix products, arithmetic and copies ran while one was open for 2% of the time, Pallas kernels for 33%

profile of v3, /device:TPU:0, one launch (start us, length us, event | category | flops | bytes accessed | tf_op | source)
XLA Modules:
  0.0 265.3 jit_solution(9493487794470879499)
XLA Ops:
  0.6 6.4 %project.1 = (bf16[8,256,384]{2,1,0:T(8,128)(2,1)}, bf16[128,1024]{1,0:T(8,128)(2,1)}, bf16[128,1024]{1,0:T(8,128)(2,1)}) custom-call(bf16[256,1024]{1,0:T(8,128)(2,1)} %bitcast.46, f32[1,1024]{1,0:T(1,128)} %bitcast.59, f32[1,1024]{1,0:T(1,128)} %bitcast.57, bf16[1024,1024]{1,0:T(8,128)(2,1)} %refs_5_.1, bf16[1024,1024]{1,0:T(8,128)(2,1)} %refs_6_.1, ...), custom_call_target="tpu_custom_call" | custom-call | flops 6000000000 | bytes 1 | tf_op jit(solution)/shard_map/project/pallas_call | solution.py:381
  7.0 7.4 %all-to-all-start = ((bf16[8,256,384]{2,1,0:T(8,128)(2,1)}), bf16[8,256,384]{2,1,0:T(8,128)(2,1)S(1)}, u32[]{:S(2)}, u32[]{:S(2)}) async-start(bf16[8,256,384]{2,1,0:T(8,128)(2,1)} %get-tuple-element.110), calls=%async_computation | async-start | bytes 3145728 | tf_op jit(solution)/shard_map/all_to_all | solution.py:1142
  19.2 18.7 %collective-permute-done = bf16[128,1024]{1,0:T(8,128)(2,1)S(1)} collective-permute-done((bf16[128,1024]{1,0:T(8,128)(2,1)S(1)}, bf16[128,1024]{1,0:T(8,128)(2,1)S(1)}, u32[]{:S(2)}, u32[]{:S(2)}) %collective-permute-start) | collective-permute-done | bytes 262176 | tf_op jit(solution)/shard_map/ppermute | solution.py:894
  38.8 7.6 %collective-permute-done.1 = bf16[128,1024]{1,0:T(8,128)(2,1)S(1)} collective-permute-done((bf16[128,1024]{1,0:T(8,128)(2,1)S(1)}, bf16[128,1024]{1,0:T(8,128)(2,1)S(1)}, u32[]{:S(2)}, u32[]{:S(2)}) %collective-permute-start.1) | collective-permute-done | bytes 262176 | tf_op jit(solution)/shard_map/ppermute | solution.py:894
  46.3 5.1 %all-to-all-done = bf16[8,256,384]{2,1,0:T(8,128)(2,1)S(1)} async-done(((bf16[8,256,384]{2,1,0:T(8,128)(2,1)}), bf16[8,256,384]{2,1,0:T(8,128)(2,1)S(1)}, u32[]{:S(2)}, u32[]{:S(2)}) %all-to-all-start) | async-done | bytes 1572896 | tf_op jit(solution)/shard_map/all_to_all | solution.py:1142
  51.5 10.5 %attend.1 = (bf16[8,2,128,128]{3,2,1,0:T(8,128)(2,1)}, f32[8,2,128,128]{3,2,1,0:T(8,128)S(1)}, f32[2,8,1024]{2,1,0:T(8,128)S(1)}) custom-call(s32[2,8]{1,0:T(2,128)S(1)} %copy-done.15, bf16[8,2,128,384]{3,2,1,0:T(8,128)(2,1)S(1)} %bitcast.39), custom_call_target="tpu_custom_call" | custom-call | flops 11000000512 | bytes 1 | tf_op jit(solution)/shard_map/attend/pallas_call | solution.py:468
  65.7 3.8 %all-to-all-start.1 = ((bf16[8,256,128]{2,1,0:T(8,128)(2,1)}), bf16[8,256,128]{2,1,0:T(8,128)(2,1)S(1)}, u32[]{:S(2)}, u32[]{:S(2)}) async-start(bf16[8,256,128]{2,1,0:T(8,128)(2,1)} %bitcast.8), calls=%async_computation.1 | async-start | bytes 1048576 | tf_op jit(solution)/shard_map/all_to_all | solution.py:1142
  69.5 14.5 %all-to-all-done.1.att_ref = bf16[8,256,128]{2,1,0:T(8,128)(2,1)S(1)} async-done(((bf16[8,256,128]{2,1,0:T(8,128)(2,1)}), bf16[8,256,128]{2,1,0:T(8,128)(2,1)S(1)}, u32[]{:S(2)}, u32[]{:S(2)}) %all-to-all-start.1) | async-done | bytes 524320 | tf_op jit(solution)/shard_map/all_to_all | solution.py:1142
  90.4 15.2 %middle.1 = (bf16[256,1024]{1,0:T(8,128)(2,1)}, f32[256,1024]{1,0:T(8,128)S(1)}, bf16[8,256,128]{2,1,0:T(8,128)(2,1)}, f32[2,1024]{1,0:T(2,128)S(1)}, bf16[256,2...) custom-call(s32[3]{0:T(128)S(1)} %pad_add_fusion.place_ref, ...), custom_call_target="tpu_custom_call" | custom-call | flops 20000000000 | bytes 1 | tf_op jit(solution)/shard_map/middle/pallas_call | solution.py:677
  105.7 8.0 %collective-permute-done.5 = bf16[256,1024]{1,0:T(8,128)(2,1)S(1)} collective-permute-done((bf16[256,1024]{1,0:T(8,128)(2,1)S(1)}, bf16[256,1024]{1,0:T(8,128)(2,1)S(1)}, u32[]{:S(2)}, u32[]{:S(2)}) %collective-permute-start.5) | collective-permute-done | bytes 524320 | tf_op jit(solution)/shard_map/ppermute | solution.py:894
  119.3 3.7 %all-to-all-start.2 = ((bf16[8,256,128]{2,1,0:T(8,128)(2,1)}), bf16[8,256,128]{2,1,0:T(8,128)(2,1)S(1)}, u32[]{:S(2)}, u32[]{:S(2)}) async-start(bf16[8,256,128]{2,1,0:T(8,128)(2,1)} %get-tuple-element.131), calls=%async_computation.2 | async-start | bytes 1048576 | tf_op jit(solution)/shard_map/all_to_all | solution.py:1142
  126.6 20.7 %grad_middle.1 = (bf16[512,1024]{1,0:T(8,128)(2,1)}, f32[512,1024]{1,0:T(8,128)}, bf16[512,1280]{1,0:T(8,128)(2,1)}, f32[512,1280]{1,0:T(8,128)}) custom-call(s32[3]{0:T(128)} %copy-done.6, bf16[2,256,1024]{2,1,0:T(8,128)(2,1)} %copy-done.11, bf16[2,256,1024]{2,1,0:T(8,128)(2,1)} %copy-done.31, bf16[2,256,1024]{2,1,0:T(8,128)(2,1)} %collective-permute-done.7.refs_2_, ...), custom_call_target="tpu_custom_call" | custom-call | flops 20000000000 | bytes 1 | tf_op jit(solution)/shard_map/grad_middle/pallas_call | solution.py:1008
  148.9 5.2 %collective-permute-done.14.refs_1_ = bf16[512,1024]{1,0:T(8,128)(2,1)} collective-permute-done((bf16[512,1024]{1,0:T(8,128)(2,1)S(1)}, bf16[512,1024]{1,0:T(8,128)(2,1)}, u32[]{:S(2)}, u32[]{:S(2)}) %collective-permute-start.14) | collective-permute-done | bytes 1048608 | tf_op jit(solution)/shard_map/ppermute | solution.py:894
  157.6 17.1 %attend_back.1 = (bf16[8,128,384]{2,1,0:T(8,128)(2,1)}, bf16[8,128,384]{2,1,0:T(8,128)(2,1)}) custom-call(s32[2,8]{1,0:T(2,128)} %lengths_ref.3, bf16[8,2,128,384]{3,2,1,0:T(8,128)(2,1)} %bitcast.40, bf16[8,2,128,128]{3,2,1,0:T(8,128)(2,1)} %bitcast.54, f32[8,2,128,128]{3,2,1,0:T(8,128)} %copy-done.19, f32[2,8,1024]{2,1,0:T(8,128)} %copy-done.20), custom_call_target="tpu_custom_call" | custom-call | flops 3000000000 | bytes 1 | tf_op jit(solution)/shard_map/attend_back/pallas_call | solution.py:572
  174.7 5.4 %all-to-all-start.3 = ((bf16[8,128,384]{2,1,0:T(8,128)(2,1)}), bf16[8,128,384]{2,1,0:T(8,128)(2,1)}, u32[]{:S(2)}, u32[]{:S(2)}) async-start(bf16[8,128,384]{2,1,0:T(8,128)(2,1)} %get-tuple-element.175), calls=%async_computation.3 | async-start | bytes 1572864 | tf_op jit(solution)/shard_map/all_to_all | solution.py:1142
  191.1 8.5 %all-to-all-done.3.refs_0_ = bf16[8,128,384]{2,1,0:T(8,128)(2,1)} async-done(((bf16[8,128,384]{2,1,0:T(8,128)(2,1)}), bf16[8,128,384]{2,1,0:T(8,128)(2,1)}, u32[]{:S(2)}, u32[]{:S(2)}) %all-to-all-start.3) | async-done | bytes 786464 | tf_op jit(solution)/shard_map/all_to_all | solution.py:1142
  199.5 4.4 %all-to-all-start.4 = ((bf16[8,128,384]{2,1,0:T(8,128)(2,1)}), bf16[8,128,384]{2,1,0:T(8,128)(2,1)}, u32[]{:S(2)}, u32[]{:S(2)}) async-start(bf16[8,128,384]{2,1,0:T(8,128)(2,1)} %get-tuple-element.177), calls=%async_computation.4 | async-start | bytes 1572864 | tf_op jit(solution)/shard_map/all_to_all | solution.py:1142
  204.0 8.0 %grad_heads.1 = (bf16[2,8,32,512]{3,2,1,0:T(8,128)(2,1)}, f32[2,8,32,512]{3,2,1,0:T(8,128)}) custom-call(s32[3]{0:T(128)} %copy-done.6, bf16[512,1024]{1,0:T(8,128)(2,1)} %copy-done.27, bf16[512,1024]{1,0:T(8,128)(2,1)} %collective-permute-done.14.refs_1_, bf16[512,1024]{1,0:T(8,128)(2,1)} %copy-done.26, bf16[512,1024]{1,0:T(8,128)(2,1)} %collective-permute-done.15.refs_3_, ...), custom_call_target="tpu_custom_call" | custom-call | flops 20000000000 | bytes 1 | tf_op jit(solution)/shard_map/grad_heads/pallas_call | solution.py:822
  216.1 3.6 %collective-permute-start.21 = (bf16[1,128,1280]{2,1,0:T(8,128)(2,1)S(1)}, bf16[1,128,1280]{2,1,0:T(8,128)(2,1)S(1)}, u32[]{:S(2)}, u32[]{:S(2)}) collective-permute-start(bf16[1,128,1280]{2,1,0:T(8,128)(2,1)S(1)} %get-tuple-element.181), channel_id=1, source_target_pairs={{0,16},{4,20},{8,24},{12,28},{16,0},{20,4},{24,8},{28,12},{1,17},{... | collective-permute-start | bytes 983048 | tf_op jit(solution)/shard_map/ppermute | solution.py:894
  221.6 16.1 %all-to-all-done.4.refs_1_ = bf16[8,128,384]{2,1,0:T(8,128)(2,1)} async-done(((bf16[8,128,384]{2,1,0:T(8,128)(2,1)}), bf16[8,128,384]{2,1,0:T(8,128)(2,1)}, u32[]{:S(2)}, u32[]{:S(2)}) %all-to-all-start.4) | async-done | bytes 786464 | tf_op jit(solution)/shard_map/all_to_all | solution.py:1142
  237.7 7.3 %finish.1 = bf16[256,1024]{1,0:T(8,128)(2,1)} custom-call(bf16[8,128,384]{2,1,0:T(8,128)(2,1)} %all-to-all-done.3.refs_0_, bf16[8,128,384]{2,1,0:T(8,128)(2,1)} %all-to-all-done.4.refs_1_, bf16[256,1024]{1,0:T(8,128)(2,1)} %bitcast.47, f32[256,1024]{1,0:T(8,128)} %copy-done.21, f32[1,1024]{1,0:T(1,128)} %bitcast.61, bf16[1024,1024]{1,0:T(8,128)(2,1)} %refs_5_.1, ...), custom_call_target="tpu_custom_call" | custom-call | flops 20000000000 | bytes 1 | tf_op jit(solution)/shard_map/finish/pallas_call | solution.py:751
  245.0 3.7 %collective-permute-done.21 = bf16[1,128,1280]{2,1,0:T(8,128)(2,1)S(1)} collective-permute-done((bf16[1,128,1280]{2,1,0:T(8,128)(2,1)S(1)}, bf16[1,128,1280]{2,1,0:T(8,128)(2,1)S(1)}, u32[]{:S(2)}, u32[]{:S(2)}) %collective-permute-start.21) | collective-permute-done | bytes 327712 | tf_op jit(solution)/shard_map/ppermute | solution.py:894
  250.2 3.6 %all-to-all-start.5 = ((bf16[8,32,512]{2,1,0:T(8,128)(2,1)}), bf16[8,32,512]{2,1,0:T(8,128)(2,1)S(1)}, u32[]{:S(2)}, u32[]{:S(2)}) async-start(bf16[8,32,512]{2,1,0:T(8,128)(2,1)} %bitcast.25), calls=%async_computation.5 | async-start | bytes 524288 | tf_op jit(solution)/shard_map/all_to_all | solution.py:1142
  256.0 5.1 %collective-permute-done.23.refs_2_ = bf16[32,1280]{1,0:T(8,128)(2,1)S(1)} collective-permute-done((bf16[32,1280]{1,0:T(8,128)(2,1)S(1)}, bf16[32,1280]{1,0:T(8,128)(2,1)S(1)}, u32[]{:S(2)}, u32[]{:S(2)}) %collective-permute-start.23) | collective-permute-done | bytes 81952 | tf_op jit(solution)/shard_map/ppermute | solution.py:894
  (136 shorter events, 54.6 us)
Async XLA Ops:
  7.0 44.4 %all-to-all-start = ((bf16[8,256,384]{2,1,0:T(8,128)(2,1)}), bf16[8,256,384]{2,1,0:T(8,128)(2,1)S(1)}, u32[]{:S(2)}, u32[]{:S(2)}) async-start(bf16[8,256,384]{2,1,0:T(8,128)(2,1)} %get-tuple-element.110), calls=%async_computation | async-start | bytes 3145728 | tf_op jit(solution)/shard_map/all_to_all | solution.py:1142
  14.4 23.5 %collective-permute-start = (bf16[128,1024]{1,0:T(8,128)(2,1)S(1)}, bf16[128,1024]{1,0:T(8,128)(2,1)S(1)}, u32[]{:S(2)}, u32[]{:S(2)}) collective-permute-start(bf16[128,1024]{1,0:T(8,128)(2,1)S(1)} %copy-done.30), channel_id=1, source_target_pairs={{0,4},{4,0},{8,12},{12,8},{16,20},{20,16},{24,28},{28,24},{1,5},{5... | collective-permute-start | bytes 786440 | tf_op jit(solution)/shard_map/ppermute | solution.py:894
  17.2 29.1 %collective-permute-start.1 = (bf16[128,1024]{1,0:T(8,128)(2,1)S(1)}, bf16[128,1024]{1,0:T(8,128)(2,1)S(1)}, u32[]{:S(2)}, u32[]{:S(2)}) collective-permute-start(bf16[128,1024]{1,0:T(8,128)(2,1)S(1)} %get-tuple-element.205), channel_id=1, source_target_pairs={{0,4},{4,0},{8,12},{12,8},{16,20},{20,16},{24,28},{28,24},{1,5},{5... | collective-permute-start | bytes 786440 | tf_op jit(solution)/shard_map/ppermute | solution.py:894
  17.3 48.4 %collective-permute-start.3 = (bf16[128,1024]{1,0:T(8,128)(2,1)}, bf16[128,1024]{1,0:T(8,128)(2,1)S(1)}, u32[]{:S(2)}, u32[]{:S(2)}) collective-permute-start(bf16[128,1024]{1,0:T(8,128)(2,1)} %get-tuple-element.204), channel_id=1, source_target_pairs={{0,4},{4,0},{8,12},{12,8},{16,20},{20,16},{24,28},{28,24},{1,5},{5... | collective-permute-start | bytes 786440 | tf_op jit(solution)/shard_map/ppermute | solution.py:894
  51.5 13.4 %collective-permute-start.2 = (bf16[128,1024]{1,0:T(8,128)(2,1)S(1)}, bf16[128,1024]{1,0:T(8,128)(2,1)S(1)}, u32[]{:S(2)}, u32[]{:S(2)}) collective-permute-start(bf16[128,1024]{1,0:T(8,128)(2,1)S(1)} %copy-done.29), channel_id=1, source_target_pairs={{0,16},{4,20},{8,24},{12,28},{16,0},{20,4},{24,8},{28,12},{1,17},{... | collective-permute-start | bytes 786440 | tf_op jit(solution)/shard_map/ppermute | solution.py:894
  65.7 18.4 %all-to-all-start.1 = ((bf16[8,256,128]{2,1,0:T(8,128)(2,1)}), bf16[8,256,128]{2,1,0:T(8,128)(2,1)S(1)}, u32[]{:S(2)}, u32[]{:S(2)}) async-start(bf16[8,256,128]{2,1,0:T(8,128)(2,1)} %bitcast.8), calls=%async_computation.1 | async-start | bytes 1048576 | tf_op jit(solution)/shard_map/all_to_all | solution.py:1142
  86.8 27.1 %collective-permute-start.6 = (bf16[2,256,1024]{2,1,0:T(8,128)(2,1)S(1)}, bf16[2,256,1024]{2,1,0:T(8,128)(2,1)S(1)}, u32[]{:S(2)}, u32[]{:S(2)}) collective-permute-start(bf16[2,256,1024]{2,1,0:T(8,128)(2,1)S(1)} %get-tuple-element.120.norm_ref.refs_0_), channel_id=1, source_target_pairs={{0,1},{1,0},{2,3},{3,2},{4,5},{5,4},{6,7},{7,6},{8,9},{9,8},{10,11... | collective-permute-start | bytes 3145736 | tf_op jit(solution)/shard_map/ppermute | solution.py:894
  86.8 27.0 %collective-permute-start.7 = (bf16[2,256,1024]{2,1,0:T(8,128)(2,1)S(1)}, bf16[2,256,1024]{2,1,0:T(8,128)(2,1)}, u32[]{:S(2)}, u32[]{:S(2)}) collective-permute-start(bf16[2,256,1024]{2,1,0:T(8,128)(2,1)S(1)} %get-tuple-element.120.norm_ref.refs_0_), channel_id=1, source_target_pairs={{0,4},{4,0},{8,12},{12,8},{16,20},{20,16},{24,28},{28,24},{1,5},{5... | collective-permute-start | bytes 3145736 | tf_op jit(solution)/shard_map/ppermute | solution.py:894
  88.4 25.2 %collective-permute-start.5 = (bf16[256,1024]{1,0:T(8,128)(2,1)S(1)}, bf16[256,1024]{1,0:T(8,128)(2,1)S(1)}, u32[]{:S(2)}, u32[]{:S(2)}) collective-permute-start(bf16[256,1024]{1,0:T(8,128)(2,1)S(1)} %copy-done.24), channel_id=1, source_target_pairs={{0,16},{4,20},{8,24},{12,28},{16,0},{20,4},{24,8},{28,12},{1,17},{... | collective-permute-start | bytes 1572872 | tf_op jit(solution)/shard_map/ppermute | solution.py:894
  88.4 25.3 %collective-permute-start.4 = (bf16[256,1024]{1,0:T(8,128)(2,1)S(1)}, bf16[256,1024]{1,0:T(8,128)(2,1)S(1)}, u32[]{:S(2)}, u32[]{:S(2)}) collective-permute-start(bf16[256,1024]{1,0:T(8,128)(2,1)S(1)} %copy-done.25), channel_id=1, source_target_pairs={{0,8},{4,12},{8,0},{12,4},{16,24},{20,28},{24,16},{28,20},{1,9},{5... | collective-permute-start | bytes 1572872 | tf_op jit(solution)/shard_map/ppermute | solution.py:894
  113.8 12.7 %collective-permute-start.8 = (bf16[2,256,1024]{2,1,0:T(8,128)(2,1)}, bf16[2,256,1024]{2,1,0:T(8,128)(2,1)}, u32[]{:S(2)}, u32[]{:S(2)}) collective-permute-start(bf16[2,256,1024]{2,1,0:T(8,128)(2,1)} %collective-permute-done.7.refs_2_), channel_id=1, source_target_pairs={{0,1},{1,0},{2,3},{3,2},{4,5},{5,4},{6,7},{7,6},{8,9},{9,8},{10,11... | collective-permute-start | bytes 3145736 | tf_op jit(solution)/shard_map/ppermute | solution.py:894
  119.3 29.5 %all-to-all-start.2 = ((bf16[8,256,128]{2,1,0:T(8,128)(2,1)}), bf16[8,256,128]{2,1,0:T(8,128)(2,1)S(1)}, u32[]{:S(2)}, u32[]{:S(2)}) async-start(bf16[8,256,128]{2,1,0:T(8,128)(2,1)} %get-tuple-element.131), calls=%async_computation.2 | async-start | bytes 1048576 | tf_op jit(solution)/shard_map/all_to_all | solution.py:1142
  123.0 31.1 %collective-permute-start.14 = (bf16[512,1024]{1,0:T(8,128)(2,1)S(1)}, bf16[512,1024]{1,0:T(8,128)(2,1)}, u32[]{:S(2)}, u32[]{:S(2)}) collective-permute-start(bf16[512,1024]{1,0:T(8,128)(2,1)S(1)} %pad_maximum_fusion.refs_0_), channel_id=1, source_target_pairs={{0,4},{4,0},{8,12},{12,8},{16,20},{20,16},{24,28},{28,24},{1,5},{5... | collective-permute-start | bytes 3145736 | tf_op jit(solution)/shard_map/ppermute | solution.py:894
  125.1 31.8 %collective-permute-start.15 = (bf16[512,1024]{1,0:T(8,128)(2,1)S(1)}, bf16[512,1024]{1,0:T(8,128)(2,1)}, u32[]{:S(2)}, u32[]{:S(2)}) collective-permute-start(bf16[512,1024]{1,0:T(8,128)(2,1)S(1)} %pad_maximum_fusion.1.refs_2_), channel_id=1, source_target_pairs={{0,8},{4,12},{8,0},{12,4},{16,24},{20,28},{24,16},{28,20},{1,9},{5... | collective-permute-start | bytes 3145736 | tf_op jit(solution)/shard_map/ppermute | solution.py:894
  147.3 38.2 %collective-permute-start.17 = (bf16[4,128,1280]{2,1,0:T(8,128)(2,1)}, bf16[4,128,1280]{2,1,0:T(8,128)(2,1)}, u32[]{:S(2)}, u32[]{:S(2)}) collective-permute-start(bf16[4,128,1280]{2,1,0:T(8,128)(2,1)} %bitcast.55), channel_id=1, source_target_pairs={{0,2},{1,3},{2,0},{3,1},{4,6},{5,7},{6,4},{7,5},{8,10},{9,11},{10,... | collective-permute-start | bytes 3932168 | tf_op jit(solution)/shard_map/ppermute | solution.py:894
  156.9 24.6 %collective-permute-start.16 = (bf16[4,128,1024]{2,1,0:T(8,128)(2,1)}, bf16[4,128,1024]{2,1,0:T(8,128)(2,1)S(1)}, u32[]{:S(2)}, u32[]{:S(2)}) collective-permute-start(bf16[4,128,1024]{2,1,0:T(8,128)(2,1)} %bitcast.56), channel_id=1, source_target_pairs={{0,8},{4,12},{8,0},{12,4},{16,24},{20,28},{24,16},{28,20},{1,9},{5... | collective-permute-start | bytes 3145736 | tf_op jit(solution)/shard_map/ppermute | solution.py:894
  174.7 24.9 %all-to-all-start.3 = ((bf16[8,128,384]{2,1,0:T(8,128)(2,1)}), bf16[8,128,384]{2,1,0:T(8,128)(2,1)}, u32[]{:S(2)}, u32[]{:S(2)}) async-start(bf16[8,128,384]{2,1,0:T(8,128)(2,1)} %get-tuple-element.175), calls=%async_computation.3 | async-start | bytes 1572864 | tf_op jit(solution)/shard_map/all_to_all | solution.py:1142
  183.9 28.1 %collective-permute-start.18 = (bf16[2,128,1024]{2,1,0:T(8,128)(2,1)}, bf16[2,128,1024]{2,1,0:T(8,128)(2,1)S(1)}, u32[]{:S(2)}, u32[]{:S(2)}) collective-permute-start(bf16[2,128,1024]{2,1,0:T(8,128)(2,1)} %get-tuple-element.163), channel_id=1, source_target_pairs={{0,2},{1,3},{2,0},{3,1},{4,6},{5,7},{6,4},{7,5},{8,10},{9,11},{10,... | collective-permute-start | bytes 1572872 | tf_op jit(solution)/shard_map/ppermute | solution.py:894
  189.2 26.1 %collective-permute-start.19 = (bf16[2,128,1280]{2,1,0:T(8,128)(2,1)}, bf16[2,128,1280]{2,1,0:T(8,128)(2,1)S(1)}, u32[]{:S(2)}, u32[]{:S(2)}) collective-permute-start(bf16[2,128,1280]{2,1,0:T(8,128)(2,1)} %get-tuple-element.167), channel_id=1, source_target_pairs={{0,8},{4,12},{8,0},{12,4},{16,24},{20,28},{24,16},{28,20},{1,9},{5... | collective-permute-start | bytes 1966088 | tf_op jit(solution)/shard_map/ppermute | solution.py:894
  199.5 38.2 %all-to-all-start.4 = ((bf16[8,128,384]{2,1,0:T(8,128)(2,1)}), bf16[8,128,384]{2,1,0:T(8,128)(2,1)}, u32[]{:S(2)}, u32[]{:S(2)}) async-start(bf16[8,128,384]{2,1,0:T(8,128)(2,1)} %get-tuple-element.177), calls=%async_computation.4 | async-start | bytes 1572864 | tf_op jit(solution)/shard_map/all_to_all | solution.py:1142
  212.7 51.0 %collective-permute-start.25 = (bf16[1,128,1024]{2,1,0:T(8,128)(2,1)S(1)}, bf16[1,128,1024]{2,1,0:T(8,128)(2,1)S(1)}, u32[]{:S(2)}, u32[]{:S(2)}) collective-permute-start(bf16[1,128,1024]{2,1,0:T(8,128)(2,1)S(1)} %get-tuple-element.189), channel_id=1, source_target_pairs={{0,16},{4,20},{8,24},{12,28},{16,0},{20,4},{24,8},{28,12},{1,17},{... | collective-permute-start | bytes 786440 | tf_op jit(solution)/shard_map/ppermute | solution.py:894
  216.1 32.7 %collective-permute-start.21 = (bf16[1,128,1280]{2,1,0:T(8,128)(2,1)S(1)}, bf16[1,128,1280]{2,1,0:T(8,128)(2,1)S(1)}, u32[]{:S(2)}, u32[]{:S(2)}) collective-permute-start(bf16[1,128,1280]{2,1,0:T(8,128)(2,1)S(1)} %get-tuple-element.181), channel_id=1, source_target_pairs={{0,16},{4,20},{8,24},{12,28},{16,0},{20,4},{24,8},{28,12},{1,17},{... | collective-permute-start | bytes 983048 | tf_op jit(solution)/shard_map/ppermute | solution.py:894
  220.4 29.1 %collective-permute-start.26 = (bf16[1,256,512]{2,1,0:T(8,128)(2,1)S(1)}, bf16[1,256,512]{2,1,0:T(8,128)(2,1)S(1)}, u32[]{:S(2)}, u32[]{:S(2)}) collective-permute-start(bf16[1,256,512]{2,1,0:T(8,128)(2,1)S(1)} %get-tuple-element.192), channel_id=1, source_target_pairs={{0,2},{1,3},{2,0},{3,1},{4,6},{5,7},{6,4},{7,5},{8,10},{9,11},{10,... | collective-permute-start | bytes 786440 | tf_op jit(solution)/shard_map/ppermute | solution.py:894
  250.2 14.4 %all-to-all-start.5 = ((bf16[8,32,512]{2,1,0:T(8,128)(2,1)}), bf16[8,32,512]{2,1,0:T(8,128)(2,1)S(1)}, u32[]{:S(2)}, u32[]{:S(2)}) async-start(bf16[8,32,512]{2,1,0:T(8,128)(2,1)} %bitcast.25), calls=%async_computation.5 | async-start | bytes 524288 | tf_op jit(solution)/shard_map/all_to_all | solution.py:1142
  (43 other events, 451.9 us)

commit v4 on v3

--- a/solution.py
+++ b/solution.py
@@ -354,7 +354,7 @@
 def project_call(rows, gain, bias, w_query, w_key, w_value, blocks, tokens):
     row_count, features = rows.shape
     slot = features // blocks
-    per_step = max(1, min(blocks, 256 // slot))
+    per_step = max(1, min(blocks, 512 // slot))
     wide = slot * per_step
 
     def kernel(rows_ref, gain_ref, bias_ref, wq_ref, wk_ref, wv_ref, send_ref, *refs):
@@ -425,7 +425,7 @@
     blocks, micro_count, tokens, width = received.shape
     slot = width // 3
     doc_count = lengths.shape[1]
-    step_blocks = max(1, min(blocks, 256 // tokens))
+    step_blocks = max(1, min(blocks // 2, 512 // tokens))
     rows = step_blocks * tokens
     scale = 1.0 / math.sqrt(head_dim)
 
@@ -492,7 +492,7 @@
     blocks, micro_count, tokens, width = received.shape
     slot = width // 3
     doc_count = lengths.shape[1]
-    step_blocks = max(1, min(blocks, 256 // tokens))
+    step_blocks = max(1, min(blocks // 2, 512 // tokens))
     rows = step_blocks * tokens
     steps = blocks // step_blocks
     scale = 1.0 / math.sqrt(head_dim)
@@ -716,7 +716,7 @@
     blocks, tokens, width = received[0].shape
     slot = width // 3
     row_count, features = rows.shape
-    per_step = max(1, min(blocks, 256 // slot))
+    per_step = max(1, min(blocks, 512 // slot))
     wide = slot * per_step
     steps = blocks // per_step
 
@@ -1172,22 +1172,19 @@
     received = by_micro(swap(send))
     dout_parts = [out_grad[micro] for micro in range(micro_count)]
     dout_over = [to_share(part, 2) for part in dout_parts]
-    units_last = grown(units_last, blk_bits[0])
-    units_last, received, dout_over[0] = tie((units_last, received, dout_over[0]))
+    received, dout_over[0] = tie((received, dout_over[0]))
     units_first, received = tie((units_first, received))
     units_first = grown(units_first, blk_bits[-1])
     own_attended, exact, logs = attend_call(received, seg_lengths, head_dim)
     attended, units_first, dout_over = tie((own_attended.reshape(blocks, row_count, slot), units_first, dout_over))
-    attended, units_first, units_last = tie((swap(attended), units_first, units_last))
-    dout_peer = to_share(dout, 1)
     dout_over = jnp.concatenate(dout_over, axis=0)
-    douts = [dout, dout_peer, dout_over, to_share(dout_over, 1)]
+    attended, units_first, units_last, *douts = tie(
+        (swap(attended), units_first, units_last, dout, to_share(dout, 1), dout_over, to_share(dout_over, 1))
+    )
     for bit in blk_bits[-2:0:-1]:
         units_first = grown(units_first, bit)
-    for bit in blk_bits[:1:-1]:
-        units_last = grown(units_last, bit)
-    places_first = _ordered_low([*blk_bits[:0:-1], blk_bits[0]])
-    places_last = _ordered_low([blk_bits[0], *blk_bits[:1:-1], blk_bits[1]])
+    units_last = grown(units_last, blk_bits[-1])
+    places = _ordered_low([*blk_bits[:0:-1], blk_bits[0]])
 
     mixed, both = mix_call(attended, rows, gain_two, bias_two, w_out)
     both_peer, both_over = to_share(both, 1), to_share(both, 2)
@@ -1199,7 +1196,8 @@
     )
     boths = [both, both_peer, both_over, to_share(both_over, 1)]
     units_first_peer = _paired(units_first, "blk", blk_bits[0])
-    units_last_peer = _paired(units_last, "blk", blk_bits[1])
+    for bit in blk_bits[-2:0:-1]:
+        units_last = grown(units_last, bit)
     grads = by_micro(swap(back))
     lows = [lows[0]] + [to_share(lows[share], share) for share in range(1, shares)]
     down_theirs, down_keep, up_theirs, up_keep = grad_middle_call(
@@ -1208,7 +1206,8 @@
     down_theirs, down_keep = (value.reshape(-1, owned, features) for value in (down_theirs, down_keep))
     up_theirs, up_keep = (value.reshape(-1, block_rows, value.shape[-1]) for value in (up_theirs, up_keep))
     down_received, up_received = _paired(down_theirs, *down_steps[0]), _paired(up_theirs, *up_steps[0])
-    grads, down_keep, units_first_peer, units_last_peer = tie((grads, down_keep, units_first_peer, units_last_peer))
+    grads, down_keep, units_last = tie((grads, down_keep, units_last))
+    units_last_peer = _paired(units_last, "blk", blk_bits[0])
     made = attend_back_call(received, grads, exact, logs, seg_lengths, head_dim)
     returned = [swap(made[0])]
 
@@ -1217,13 +1216,15 @@
 
     returned += [swap(tie((values, returned[0]))[0]) for values in made[1:]]
     made = tie(made)
-    down_theirs, down_keep = halve_call(place, *then(made[0], down_keep, down_received), down_steps[1], 0)
+    up_keep, up_received, units_first_peer = then(made[0], up_keep, up_received, units_first_peer)
+    up_theirs, up_keep = halve_call(place, up_keep, up_received, up_steps[1], 0)
+    up_received = _paired(up_theirs, *up_steps[1])
+    down_keep, down_received, units_last_peer = then(up_keep, down_keep, down_received, units_last_peer)
+    down_theirs, down_keep = halve_call(place, down_keep, down_received, down_steps[1], 5)
     down_received = _paired(down_theirs, *down_steps[1])
-    up_theirs, up_keep = halve_call(place, *then(down_keep, up_keep, up_received), up_steps[1], 5)
-    up_received = _paired(up_theirs, *up_steps[1])
-    made = then(up_keep, *made)
+    made = then(down_keep, *made)
     heads_send, heads_keep = grad_heads_call(
-        place, (units_first, units_first_peer, units_last, units_last_peer), (places_first, places_last),
+        place, (units_first, units_first_peer, units_last, units_last_peer), (places, places),
         made, gain_one, bias_one, sums_two, w_query, w_key, w_value, shares,
     )
     pair = (shares // 2, -1, heads_keep.shape[-1])

time: 266 us -> 256 us (0.962)
  starting transfers between devices: 57.6 us -> 50.6 us
  Pallas kernels: 95.3 us -> 92 us
    ppermute x25, starting transfers between devices: 28.8 us -> 22.3 us  [_paired(): return lax.ppermute(values, axis, [(i, i ^ bit) for i in range(count)])]
    ppermute x25, waiting for transfers between devices: 53.8 us -> 50.1 us  [_paired(): return lax.ppermute(values, axis, [(i, i ^ bit) for i in range(count)])]
    all_to_all x6, waiting for transfers between devices: 44.3 us -> 47.1 us  [swap(): lax.all_to_all(values, 'blk', split_axis=0, concat_axis=0, tiled=True)]
    unnamed x69 -> x67, local copies, waits for them, and re-layouts: 7.15 us -> 6.42 us
  transfers between devices with their start and end apart: 33 -> 33, of which waited for: 14 -> 17; matrix products, arithmetic and copies ran while one was open for 2% -> 3% of each run, Pallas kernels for 33% -> 33%
where the time goes in v4:
time: 256 us; the launch traced here: 255 us
  waiting for transfers between devices  99 us (39%)
  Pallas kernels  92 us (36%)
  starting transfers between devices  50.6 us (20%)
  local copies, waits for them, and re-layouts  8.13 us (3%)
  other arithmetic  4.77 us (2%)
    ppermute x25, waiting for transfers between devices, _paired(): return lax.ppermute(values, axis, [(i, i ^ bit) for i in range(count)])  50.1 us
    all_to_all x6, waiting for transfers between devices, swap(): lax.all_to_all(values, 'blk', split_axis=0, concat_axis=0, tiled=True)  47.1 us
    all_to_all x6, starting transfers between devices, swap(): lax.all_to_all(values, 'blk', split_axis=0, concat_axis=0, tiled=True)  28.2 us
    ppermute x25, starting transfers between devices, _paired(): return lax.ppermute(values, axis, [(i, i ^ bit) for i in range(count)])  22.3 us
    pallas_call x1, Pallas kernels, grad_middle_call(): pl.pallas_call(kernel, grid_spec=pltpu.PrefetchScalarGridSpec(num_scalar_...  20.7 us
    pallas_call x1, Pallas kernels, attend_back_call(): pl.pallas_call(kernel, grid=(micro_count, steps), in_specs=[pl.BlockSpec(...  15.4 us
    pallas_call x1, Pallas kernels, middle_call(): pl.pallas_call(kernel, grid_spec=pltpu.PrefetchScalarGridSpec(num_scalar_...  15.2 us
    pallas_call x1, Pallas kernels, attend_call(): pl.pallas_call(kernel, grid=(micro_count, blocks // step_blocks), in_spec...  9.52 us
  transfers between devices with their start and end apart: 33, of which 17 were waited for; matrix products, arithmetic and copies ran while one was open for 3% of the time, Pallas kernels for 33%

profile of v4, /device:TPU:0, one launch (start us, length us, event | category | flops | bytes accessed | tf_op | source)
XLA Modules:
  0.0 255.4 jit_solution(18251560306249516936)
XLA Ops:
  0.6 5.6 %project.1 = (bf16[8,256,384]{2,1,0:T(8,128)(2,1)}, bf16[128,1024]{1,0:T(8,128)(2,1)}, bf16[128,1024]{1,0:T(8,128)(2,1)}) custom-call(bf16[256,1024]{1,0:T(8,128)(2,1)} %bitcast.46, f32[1,1024]{1,0:T(1,128)} %bitcast.58, f32[1,1024]{1,0:T(1,128)} %bitcast.56, bf16[1024,1024]{1,0:T(8,128)(2,1)} %refs_5_.1, bf16[1024,1024]{1,0:T(8,128)(2,1)} %refs_6_.1, ...), custom_call_target="tpu_custom_call" | custom-call | flops 6000000000 | bytes 1 | tf_op jit(solution)/shard_map/project/pallas_call | solution.py:381
  6.3 7.4 %all-to-all-start = ((bf16[8,256,384]{2,1,0:T(8,128)(2,1)}), bf16[8,256,384]{2,1,0:T(8,128)(2,1)S(1)}, u32[]{:S(2)}, u32[]{:S(2)}) async-start(bf16[8,256,384]{2,1,0:T(8,128)(2,1)} %get-tuple-element.113), calls=%async_computation | async-start | bytes 3145728 | tf_op jit(solution)/shard_map/all_to_all | solution.py:1142
  16.5 20.7 %collective-permute-done = bf16[128,1024]{1,0:T(8,128)(2,1)S(1)} collective-permute-done((bf16[128,1024]{1,0:T(8,128)(2,1)S(1)}, bf16[128,1024]{1,0:T(8,128)(2,1)S(1)}, u32[]{:S(2)}, u32[]{:S(2)}) %collective-permute-start) | collective-permute-done | bytes 262176 | tf_op jit(solution)/shard_map/ppermute | solution.py:894
  37.2 13.5 %all-to-all-done = bf16[8,256,384]{2,1,0:T(8,128)(2,1)S(1)} async-done(((bf16[8,256,384]{2,1,0:T(8,128)(2,1)}), bf16[8,256,384]{2,1,0:T(8,128)(2,1)S(1)}, u32[]{:S(2)}, u32[]{:S(2)}) %all-to-all-start) | async-done | bytes 1572896 | tf_op jit(solution)/shard_map/all_to_all | solution.py:1142
  50.7 9.5 %attend.1 = (bf16[8,2,128,128]{3,2,1,0:T(8,128)(2,1)}, f32[8,2,128,128]{3,2,1,0:T(8,128)S(1)}, f32[2,8,1024]{2,1,0:T(8,128)S(1)}) custom-call(s32[2,8]{1,0:T(2,128)S(1)} %copy-done.15, bf16[8,2,128,384]{3,2,1,0:T(8,128)(2,1)S(1)} %bitcast.39), custom_call_target="tpu_custom_call" | custom-call | flops 11000000512 | bytes 1 | tf_op jit(solution)/shard_map/attend/pallas_call | solution.py:468
  64.2 3.7 %all-to-all-start.1 = ((bf16[8,256,128]{2,1,0:T(8,128)(2,1)}), bf16[8,256,128]{2,1,0:T(8,128)(2,1)S(1)}, u32[]{:S(2)}, u32[]{:S(2)}) async-start(bf16[8,256,128]{2,1,0:T(8,128)(2,1)} %bitcast.8), calls=%async_computation.1 | async-start | bytes 1048576 | tf_op jit(solution)/shard_map/all_to_all | solution.py:1142
  71.1 11.4 %all-to-all-done.1.att_ref = bf16[8,256,128]{2,1,0:T(8,128)(2,1)S(1)} async-done(((bf16[8,256,128]{2,1,0:T(8,128)(2,1)}), bf16[8,256,128]{2,1,0:T(8,128)(2,1)S(1)}, u32[]{:S(2)}, u32[]{:S(2)}) %all-to-all-start.1) | async-done | bytes 524320 | tf_op jit(solution)/shard_map/all_to_all | solution.py:1142
  88.9 15.2 %middle.1 = (bf16[256,1024]{1,0:T(8,128)(2,1)}, f32[256,1024]{1,0:T(8,128)S(1)}, bf16[8,256,128]{2,1,0:T(8,128)(2,1)}, f32[2,1024]{1,0:T(2,128)S(1)}, bf16[256,2...) custom-call(s32[3]{0:T(128)S(1)} %pad_add_fusion.place_ref, ...), custom_call_target="tpu_custom_call" | custom-call | flops 20000000000 | bytes 1 | tf_op jit(solution)/shard_map/middle/pallas_call | solution.py:677
  107.5 3.5 %collective-permute-done.8.refs_2_ = bf16[2,256,1024]{2,1,0:T(8,128)(2,1)} collective-permute-done((bf16[2,256,1024]{2,1,0:T(8,128)(2,1)S(1)}, bf16[2,256,1024]{2,1,0:T(8,128)(2,1)}, u32[]{:S(2)}, u32[]{:S(2)}) %collective-permute-start.8) | collective-permute-done | bytes 1048608 | tf_op jit(solution)/shard_map/ppermute | solution.py:894
  113.0 3.7 %all-to-all-start.2 = ((bf16[8,256,128]{2,1,0:T(8,128)(2,1)}), bf16[8,256,128]{2,1,0:T(8,128)(2,1)S(1)}, u32[]{:S(2)}, u32[]{:S(2)}) async-start(bf16[8,256,128]{2,1,0:T(8,128)(2,1)} %get-tuple-element.136), calls=%async_computation.2 | async-start | bytes 1048576 | tf_op jit(solution)/shard_map/all_to_all | solution.py:1142
  122.2 20.7 %grad_middle.1 = (bf16[512,1024]{1,0:T(8,128)(2,1)}, f32[512,1024]{1,0:T(8,128)}, bf16[512,1280]{1,0:T(8,128)(2,1)}, f32[512,1280]{1,0:T(8,128)}) custom-call(s32[3]{0:T(128)} %copy-done.4, bf16[2,256,1024]{2,1,0:T(8,128)(2,1)} %copy-done.11, bf16[2,256,1024]{2,1,0:T(8,128)(2,1)} %copy-done.27, bf16[2,256,1024]{2,1,0:T(8,128)(2,1)} %collective-permute-done.8.refs_2_, ...), custom_call_target="tpu_custom_call" | custom-call | flops 20000000000 | bytes 1 | tf_op jit(solution)/shard_map/grad_middle/pallas_call | solution.py:1008
  146.2 15.4 %attend_back.1 = (bf16[8,128,384]{2,1,0:T(8,128)(2,1)}, bf16[8,128,384]{2,1,0:T(8,128)(2,1)}) custom-call(s32[2,8]{1,0:T(2,128)} %lengths_ref.3, bf16[8,2,128,384]{3,2,1,0:T(8,128)(2,1)} %bitcast.40, bf16[8,2,128,128]{3,2,1,0:T(8,128)(2,1)} %bitcast.54, f32[8,2,128,128]{3,2,1,0:T(8,128)} %copy-done.17, f32[2,8,1024]{2,1,0:T(8,128)} %copy-done.18), custom_call_target="tpu_custom_call" | custom-call | flops 3000000000 | bytes 1 | tf_op jit(solution)/shard_map/attend_back/pallas_call | solution.py:572
  161.6 5.3 %all-to-all-start.3 = ((bf16[8,128,384]{2,1,0:T(8,128)(2,1)}), bf16[8,128,384]{2,1,0:T(8,128)(2,1)}, u32[]{:S(2)}, u32[]{:S(2)}) async-start(bf16[8,128,384]{2,1,0:T(8,128)(2,1)} %get-tuple-element.183), calls=%async_computation.3 | async-start | bytes 1572864 | tf_op jit(solution)/shard_map/all_to_all | solution.py:1142
  167.0 6.2 %collective-permute-done.14.got_theirs.got_mine = bf16[4,128,1280]{2,1,0:T(8,128)(2,1)} collective-permute-done((bf16[4,128,1280]{2,1,0:T(8,128)(2,1)}, bf16[4,128,1280]{2,1,0:T(8,128)(2,1)}, u32[]{:S(2)}, u32[]{:S(2)}) %collective-permute-start.14) | collective-permute-done | bytes 1310752 | tf_op jit(solution)/shard_map/ppermute | solution.py:894
  180.4 7.8 %all-to-all-done.3.refs_0_ = bf16[8,128,384]{2,1,0:T(8,128)(2,1)} async-done(((bf16[8,128,384]{2,1,0:T(8,128)(2,1)}), bf16[8,128,384]{2,1,0:T(8,128)(2,1)}, u32[]{:S(2)}, u32[]{:S(2)}) %all-to-all-start.3) | async-done | bytes 786464 | tf_op jit(solution)/shard_map/all_to_all | solution.py:1142
  188.2 4.4 %all-to-all-start.4 = ((bf16[8,128,384]{2,1,0:T(8,128)(2,1)}), bf16[8,128,384]{2,1,0:T(8,128)(2,1)}, u32[]{:S(2)}, u32[]{:S(2)}) async-start(bf16[8,128,384]{2,1,0:T(8,128)(2,1)} %get-tuple-element.168.refs_5_), calls=%async_computation.4 | async-start | bytes 1572864 | tf_op jit(solution)/shard_map/all_to_all | solution.py:1142
  192.6 8.0 %grad_heads.1 = (bf16[2,8,32,512]{3,2,1,0:T(8,128)(2,1)}, f32[2,8,32,512]{3,2,1,0:T(8,128)}) custom-call(s32[3]{0:T(128)} %copy-done.4, bf16[512,1024]{1,0:T(8,128)(2,1)} %pad_maximum_fusion.refs_0_, bf16[512,1024]{1,0:T(8,128)(2,1)} %collective-permute-done.15.refs_1_, bf16[512,1024]{1,0:T(8,128)(2,1)} %pad_maximum_fusion.1.refs_2_, ...), custom_call_target="tpu_custom_call" | custom-call | flops 20000000000 | bytes 1 | tf_op jit(solution)/shard_map/grad_heads/pallas_call | solution.py:822
  201.3 2.7 %collective-permute-start.25 = (bf16[1,128,1024]{2,1,0:T(8,128)(2,1)S(1)}, bf16[1,128,1024]{2,1,0:T(8,128)(2,1)}, u32[]{:S(2)}, u32[]{:S(2)}) collective-permute-start(bf16[1,128,1024]{2,1,0:T(8,128)(2,1)S(1)} %get-tuple-element.197), channel_id=1, source_target_pairs={{0,16},{4,20},{8,24},{12,28},{16,0},{20,4},{24,8},{28,12},{1,17},{... | collective-permute-start | bytes 786440 | tf_op jit(solution)/shard_map/ppermute | solution.py:894
  204.0 3.5 %collective-permute-done.19.got_theirs.got_mine = bf16[2,128,1280]{2,1,0:T(8,128)(2,1)} collective-permute-done((bf16[2,128,1280]{2,1,0:T(8,128)(2,1)S(1)}, bf16[2,128,1280]{2,1,0:T(8,128)(2,1)}, u32[]{:S(2)}, u32[]{:S(2)}) %collective-permute-start.19) | collective-permute-done | bytes 655392 | tf_op jit(solution)/shard_map/ppermute | solution.py:894
  211.9 14.3 %all-to-all-done.4.refs_1_ = bf16[8,128,384]{2,1,0:T(8,128)(2,1)} async-done(((bf16[8,128,384]{2,1,0:T(8,128)(2,1)}), bf16[8,128,384]{2,1,0:T(8,128)(2,1)}, u32[]{:S(2)}, u32[]{:S(2)}) %all-to-all-start.4) | async-done | bytes 786464 | tf_op jit(solution)/shard_map/all_to_all | solution.py:1142
  226.3 6.6 %finish.1 = bf16[256,1024]{1,0:T(8,128)(2,1)} custom-call(bf16[8,128,384]{2,1,0:T(8,128)(2,1)} %all-to-all-done.3.refs_0_, bf16[8,128,384]{2,1,0:T(8,128)(2,1)} %all-to-all-done.4.refs_1_, bf16[256,1024]{1,0:T(8,128)(2,1)} %bitcast.47, f32[256,1024]{1,0:T(8,128)} %copy-done.19, f32[1,1024]{1,0:T(1,128)} %bitcast.60, bf16[1024,1024]{1,0:T(8,128)(2,1)} %refs_5_.1, ...), custom_call_target="tpu_custom_call" | custom-call | flops 20000000000 | bytes 1 | tf_op jit(solution)/shard_map/finish/pallas_call | solution.py:751
  232.8 4.9 %collective-permute-done.21 = bf16[1,128,1280]{2,1,0:T(8,128)(2,1)S(1)} collective-permute-done((bf16[1,128,1280]{2,1,0:T(8,128)(2,1)S(1)}, bf16[1,128,1280]{2,1,0:T(8,128)(2,1)S(1)}, u32[]{:S(2)}, u32[]{:S(2)}) %collective-permute-start.21) | collective-permute-done | bytes 327712 | tf_op jit(solution)/shard_map/ppermute | solution.py:894
  239.2 3.7 %all-to-all-start.5 = ((bf16[8,32,512]{2,1,0:T(8,128)(2,1)}), bf16[8,32,512]{2,1,0:T(8,128)(2,1)S(1)}, u32[]{:S(2)}, u32[]{:S(2)}) async-start(bf16[8,32,512]{2,1,0:T(8,128)(2,1)} %bitcast.25), calls=%async_computation.5 | async-start | bytes 524288 | tf_op jit(solution)/shard_map/all_to_all | solution.py:1142
  245.0 5.1 %collective-permute-done.23.refs_2_ = bf16[32,1280]{1,0:T(8,128)(2,1)S(1)} collective-permute-done((bf16[32,1280]{1,0:T(8,128)(2,1)S(1)}, bf16[32,1280]{1,0:T(8,128)(2,1)S(1)}, u32[]{:S(2)}, u32[]{:S(2)}) %collective-permute-start.23) | collective-permute-done | bytes 81952 | tf_op jit(solution)/shard_map/ppermute | solution.py:894
  (134 shorter events, 51.5 us)
Async XLA Ops:
  6.3 44.4 %all-to-all-start = ((bf16[8,256,384]{2,1,0:T(8,128)(2,1)}), bf16[8,256,384]{2,1,0:T(8,128)(2,1)S(1)}, u32[]{:S(2)}, u32[]{:S(2)}) async-start(bf16[8,256,384]{2,1,0:T(8,128)(2,1)} %get-tuple-element.113), calls=%async_computation | async-start | bytes 3145728 | tf_op jit(solution)/shard_map/all_to_all | solution.py:1142
  14.4 22.8 %collective-permute-start = (bf16[128,1024]{1,0:T(8,128)(2,1)S(1)}, bf16[128,1024]{1,0:T(8,128)(2,1)S(1)}, u32[]{:S(2)}, u32[]{:S(2)}) collective-permute-start(bf16[128,1024]{1,0:T(8,128)(2,1)S(1)} %get-tuple-element.213), channel_id=1, source_target_pairs={{0,4},{4,0},{8,12},{12,8},{16,20},{20,16},{24,28},{28,24},{1,5},{5... | collective-permute-start | bytes 786440 | tf_op jit(solution)/shard_map/ppermute | solution.py:894
  16.5 47.7 %collective-permute-start.2 = (bf16[128,1024]{1,0:T(8,128)(2,1)}, bf16[128,1024]{1,0:T(8,128)(2,1)}, u32[]{:S(2)}, u32[]{:S(2)}) collective-permute-start(bf16[128,1024]{1,0:T(8,128)(2,1)} %get-tuple-element.212), channel_id=1, source_target_pairs={{0,4},{4,0},{8,12},{12,8},{16,20},{20,16},{24,28},{28,24},{1,5},{5... | collective-permute-start | bytes 786440 | tf_op jit(solution)/shard_map/ppermute | solution.py:894
  50.7 13.4 %collective-permute-start.1 = (bf16[128,1024]{1,0:T(8,128)(2,1)S(1)}, bf16[128,1024]{1,0:T(8,128)(2,1)S(1)}, u32[]{:S(2)}, u32[]{:S(2)}) collective-permute-start(bf16[128,1024]{1,0:T(8,128)(2,1)S(1)} %copy-done.24), channel_id=1, source_target_pairs={{0,16},{4,20},{8,24},{12,28},{16,0},{20,4},{24,8},{28,12},{1,17},{... | collective-permute-start | bytes 786440 | tf_op jit(solution)/shard_map/ppermute | solution.py:894
  64.2 18.4 %all-to-all-start.1 = ((bf16[8,256,128]{2,1,0:T(8,128)(2,1)}), bf16[8,256,128]{2,1,0:T(8,128)(2,1)S(1)}, u32[]{:S(2)}, u32[]{:S(2)}) async-start(bf16[8,256,128]{2,1,0:T(8,128)(2,1)} %bitcast.8), calls=%async_computation.1 | async-start | bytes 1048576 | tf_op jit(solution)/shard_map/all_to_all | solution.py:1142
  85.2 22.2 %collective-permute-start.7 = (bf16[2,256,1024]{2,1,0:T(8,128)(2,1)S(1)}, bf16[2,256,1024]{2,1,0:T(8,128)(2,1)S(1)}, u32[]{:S(2)}, u32[]{:S(2)}) collective-permute-start(bf16[2,256,1024]{2,1,0:T(8,128)(2,1)S(1)} %get-tuple-element.125.norm_ref.refs_0_), channel_id=1, source_target_pairs={{0,1},{1,0},{2,3},{3,2},{4,5},{5,4},{6,7},{7,6},{8,9},{9,8},{10,11... | collective-permute-start | bytes 3145736 | tf_op jit(solution)/shard_map/ppermute | solution.py:894
  85.3 25.7 %collective-permute-start.8 = (bf16[2,256,1024]{2,1,0:T(8,128)(2,1)S(1)}, bf16[2,256,1024]{2,1,0:T(8,128)(2,1)}, u32[]{:S(2)}, u32[]{:S(2)}) collective-permute-start(bf16[2,256,1024]{2,1,0:T(8,128)(2,1)S(1)} %get-tuple-element.125.norm_ref.refs_0_), channel_id=1, source_target_pairs={{0,4},{4,0},{8,12},{12,8},{16,20},{20,16},{24,28},{28,24},{1,5},{5... | collective-permute-start | bytes 3145736 | tf_op jit(solution)/shard_map/ppermute | solution.py:894
  86.8 19.6 %collective-permute-start.5 = (bf16[256,1024]{1,0:T(8,128)(2,1)S(1)}, bf16[256,1024]{1,0:T(8,128)(2,1)S(1)}, u32[]{:S(2)}, u32[]{:S(2)}) collective-permute-start(bf16[256,1024]{1,0:T(8,128)(2,1)S(1)} %pad_maximum_fusion.2), channel_id=1, source_target_pairs={{0,8},{4,12},{8,0},{12,4},{16,24},{20,28},{24,16},{28,20},{1,9},{5... | collective-permute-start | bytes 1572872 | tf_op jit(solution)/shard_map/ppermute | solution.py:894
  86.8 17.4 %collective-permute-start.6 = (bf16[128,1024]{1,0:T(8,128)(2,1)S(1)}, bf16[128,1024]{1,0:T(8,128)(2,1)S(1)}, u32[]{:S(2)}, u32[]{:S(2)}) collective-permute-start(bf16[128,1024]{1,0:T(8,128)(2,1)S(1)} %copy-done.23), channel_id=1, source_target_pairs={{0,16},{4,20},{8,24},{12,28},{16,0},{20,4},{24,8},{28,12},{1,17},{... | collective-permute-start | bytes 786440 | tf_op jit(solution)/shard_map/ppermute | solution.py:894
  111.0 9.5 %collective-permute-start.9 = (bf16[2,256,1024]{2,1,0:T(8,128)(2,1)}, bf16[2,256,1024]{2,1,0:T(8,128)(2,1)S(1)}, u32[]{:S(2)}, u32[]{:S(2)}) collective-permute-start(bf16[2,256,1024]{2,1,0:T(8,128)(2,1)} %collective-permute-done.8.refs_2_), channel_id=1, source_target_pairs={{0,1},{1,0},{2,3},{3,2},{4,5},{5,4},{6,7},{7,6},{8,9},{9,8},{10,11... | collective-permute-start | bytes 3145736 | tf_op jit(solution)/shard_map/ppermute | solution.py:894
  113.0 32.4 %all-to-all-start.2 = ((bf16[8,256,128]{2,1,0:T(8,128)(2,1)}), bf16[8,256,128]{2,1,0:T(8,128)(2,1)S(1)}, u32[]{:S(2)}, u32[]{:S(2)}) async-start(bf16[8,256,128]{2,1,0:T(8,128)(2,1)} %get-tuple-element.136), calls=%async_computation.2 | async-start | bytes 1048576 | tf_op jit(solution)/shard_map/all_to_all | solution.py:1142
  116.7 27.7 %collective-permute-start.13 = (bf16[256,1024]{1,0:T(8,128)(2,1)S(1)}, bf16[256,1024]{1,0:T(8,128)(2,1)S(1)}, u32[]{:S(2)}, u32[]{:S(2)}) collective-permute-start(bf16[256,1024]{1,0:T(8,128)(2,1)S(1)} %pad_maximum_fusion.3), channel_id=1, source_target_pairs={{0,8},{4,12},{8,0},{12,4},{16,24},{20,28},{24,16},{28,20},{1,9},{5... | collective-permute-start | bytes 1572872 | tf_op jit(solution)/shard_map/ppermute | solution.py:894
  118.5 48.4 %collective-permute-start.15 = (bf16[512,1024]{1,0:T(8,128)(2,1)}, bf16[512,1024]{1,0:T(8,128)(2,1)}, u32[]{:S(2)}, u32[]{:S(2)}) collective-permute-start(bf16[512,1024]{1,0:T(8,128)(2,1)} %pad_maximum_fusion.refs_0_), channel_id=1, source_target_pairs={{0,4},{4,0},{8,12},{12,8},{16,20},{20,16},{24,28},{28,24},{1,5},{5... | collective-permute-start | bytes 3145736 | tf_op jit(solution)/shard_map/ppermute | solution.py:894
  142.8 30.3 %collective-permute-start.14 = (bf16[4,128,1280]{2,1,0:T(8,128)(2,1)}, bf16[4,128,1280]{2,1,0:T(8,128)(2,1)}, u32[]{:S(2)}, u32[]{:S(2)}) collective-permute-start(bf16[4,128,1280]{2,1,0:T(8,128)(2,1)} %bitcast.55), channel_id=1, source_target_pairs={{0,2},{1,3},{2,0},{3,1},{4,6},{5,7},{6,4},{7,5},{8,10},{9,11},{10,... | collective-permute-start | bytes 3932168 | tf_op jit(solution)/shard_map/ppermute | solution.py:894
  145.4 30.9 %collective-permute-start.16 = (bf16[4,128,1024]{2,1,0:T(8,128)(2,1)}, bf16[4,128,1024]{2,1,0:T(8,128)(2,1)}, u32[]{:S(2)}, u32[]{:S(2)}) collective-permute-start(bf16[4,128,1024]{2,1,0:T(8,128)(2,1)} %bitcast.18), channel_id=1, source_target_pairs={{0,8},{4,12},{8,0},{12,4},{16,24},{20,28},{24,16},{28,20},{1,9},{5... | collective-permute-start | bytes 3145736 | tf_op jit(solution)/shard_map/ppermute | solution.py:894
  145.6 30.8 %collective-permute-start.17 = (bf16[512,1024]{1,0:T(8,128)(2,1)}, bf16[512,1024]{1,0:T(8,128)(2,1)}, u32[]{:S(2)}, u32[]{:S(2)}) collective-permute-start(bf16[512,1024]{1,0:T(8,128)(2,1)} %pad_maximum_fusion.1.refs_2_), channel_id=1, source_target_pairs={{0,4},{4,0},{8,12},{12,8},{16,20},{20,16},{24,28},{28,24},{1,5},{5... | collective-permute-start | bytes 3145736 | tf_op jit(solution)/shard_map/ppermute | solution.py:894
  161.6 26.6 %all-to-all-start.3 = ((bf16[8,128,384]{2,1,0:T(8,128)(2,1)}), bf16[8,128,384]{2,1,0:T(8,128)(2,1)}, u32[]{:S(2)}, u32[]{:S(2)}) async-start(bf16[8,128,384]{2,1,0:T(8,128)(2,1)} %get-tuple-element.183), calls=%async_computation.3 | async-start | bytes 1572864 | tf_op jit(solution)/shard_map/all_to_all | solution.py:1142
  178.2 22.4 %collective-permute-start.18 = (bf16[2,128,1024]{2,1,0:T(8,128)(2,1)S(1)}, bf16[2,128,1024]{2,1,0:T(8,128)(2,1)S(1)}, u32[]{:S(2)}, u32[]{:S(2)}) collective-permute-start(bf16[2,128,1024]{2,1,0:T(8,128)(2,1)S(1)} %get-tuple-element.171), channel_id=1, source_target_pairs={{0,2},{1,3},{2,0},{3,1},{4,6},{5,7},{6,4},{7,5},{8,10},{9,11},{10,... | collective-permute-start | bytes 1572872 | tf_op jit(solution)/shard_map/ppermute | solution.py:894
  179.8 27.7 %collective-permute-start.19 = (bf16[2,128,1280]{2,1,0:T(8,128)(2,1)S(1)}, bf16[2,128,1280]{2,1,0:T(8,128)(2,1)}, u32[]{:S(2)}, u32[]{:S(2)}) collective-permute-start(bf16[2,128,1280]{2,1,0:T(8,128)(2,1)S(1)} %get-tuple-element.175), channel_id=1, source_target_pairs={{0,8},{4,12},{8,0},{12,4},{16,24},{20,28},{24,16},{28,20},{1,9},{5... | collective-permute-start | bytes 1966088 | tf_op jit(solution)/shard_map/ppermute | solution.py:894
  188.2 38.1 %all-to-all-start.4 = ((bf16[8,128,384]{2,1,0:T(8,128)(2,1)}), bf16[8,128,384]{2,1,0:T(8,128)(2,1)}, u32[]{:S(2)}, u32[]{:S(2)}) async-start(bf16[8,128,384]{2,1,0:T(8,128)(2,1)} %get-tuple-element.168.refs_5_), calls=%async_computation.4 | async-start | bytes 1572864 | tf_op jit(solution)/shard_map/all_to_all | solution.py:1142
  201.3 51.5 %collective-permute-start.25 = (bf16[1,128,1024]{2,1,0:T(8,128)(2,1)S(1)}, bf16[1,128,1024]{2,1,0:T(8,128)(2,1)}, u32[]{:S(2)}, u32[]{:S(2)}) collective-permute-start(bf16[1,128,1024]{2,1,0:T(8,128)(2,1)S(1)} %get-tuple-element.197), channel_id=1, source_target_pairs={{0,16},{4,20},{8,24},{12,28},{16,0},{20,4},{24,8},{28,12},{1,17},{... | collective-permute-start | bytes 786440 | tf_op jit(solution)/shard_map/ppermute | solution.py:894
  209.3 28.4 %collective-permute-start.21 = (bf16[1,128,1280]{2,1,0:T(8,128)(2,1)S(1)}, bf16[1,128,1280]{2,1,0:T(8,128)(2,1)S(1)}, u32[]{:S(2)}, u32[]{:S(2)}) collective-permute-start(bf16[1,128,1280]{2,1,0:T(8,128)(2,1)S(1)} %get-tuple-element.189), channel_id=1, source_target_pairs={{0,16},{4,20},{8,24},{12,28},{16,0},{20,4},{24,8},{28,12},{1,17},{... | collective-permute-start | bytes 983048 | tf_op jit(solution)/shard_map/ppermute | solution.py:894
  211.3 27.1 %collective-permute-start.26 = (bf16[1,256,512]{2,1,0:T(8,128)(2,1)S(1)}, bf16[1,256,512]{2,1,0:T(8,128)(2,1)S(1)}, u32[]{:S(2)}, u32[]{:S(2)}) collective-permute-start(bf16[1,256,512]{2,1,0:T(8,128)(2,1)S(1)} %get-tuple-element.200), channel_id=1, source_target_pairs={{0,2},{1,3},{2,0},{3,1},{4,6},{5,7},{6,4},{7,5},{8,10},{9,11},{10,... | collective-permute-start | bytes 786440 | tf_op jit(solution)/shard_map/ppermute | solution.py:894
  239.2 15.5 %all-to-all-start.5 = ((bf16[8,32,512]{2,1,0:T(8,128)(2,1)}), bf16[8,32,512]{2,1,0:T(8,128)(2,1)S(1)}, u32[]{:S(2)}, u32[]{:S(2)}) async-start(bf16[8,32,512]{2,1,0:T(8,128)(2,1)} %bitcast.25), calls=%async_computation.5 | async-start | bytes 524288 | tf_op jit(solution)/shard_map/all_to_all | solution.py:1142
  (42 other events, 422.2 us)

commit v5 on v4

--- a/solution.py
+++ b/solution.py
@@ -711,18 +711,16 @@
     )(place, both, mixed, out_grad, gain, w_out, w_up, w_down)
 
 
-def finish_call(received, rows, mixed_grad, gain, w_query, w_key, w_value):
-    micro_count = len(received)
-    blocks, tokens, width = received[0].shape
+def finish_call(received, patches, mixed_grad, gain, w_query, w_key, w_value, micro, before, cost):
+    blocks, row_count, width = received.shape
     slot = width // 3
-    row_count, features = rows.shape
+    features = patches.shape[2]
     per_step = max(1, min(blocks, 512 // slot))
     wide = slot * per_step
     steps = blocks // per_step
 
-    def kernel(*refs):
-        data_refs, refs = refs[:micro_count], refs[micro_count:]
-        rows_ref, mixed_ref, gain_ref, wq_ref, wk_ref, wv_ref, out_ref, total, side = refs
+    def kernel(data_ref, rows_ref, mixed_ref, gain_ref, wq_ref, wk_ref, wv_ref, *refs):
+        out_ref, total, side = refs[-3:]
         step = pl.program_id(0)
 
         @pl.when(step == 0)
@@ -730,17 +728,16 @@
             total[...] = jnp.zeros_like(total)
 
         for part, weight_ref in enumerate((wq_ref, wk_ref, wv_ref)):
-            for micro, data_ref in enumerate(data_refs):
-                for piece in range(per_step):
-                    side[part, micro * tokens : (micro + 1) * tokens, piece * slot : (piece + 1) * slot] = data_ref[
-                        piece, :, part * slot : (part + 1) * slot
-                    ]
+            for piece in range(per_step):
+                side[part, :, piece * slot : (piece + 1) * slot] = data_ref[
+                    piece, :, part * slot : (part + 1) * slot
+                ]
             total[...] += contract_cols(side[part], weight_ref[...])
 
         @pl.when(step == steps - 1)
         def _():
-            unit, inverse = _normalize(rows_ref[...].astype(jnp.float32))
-            out_ref[...] = (
+            unit, inverse = _normalize(rows_ref[0].astype(jnp.float32))
+            out_ref[0] = (
                 mixed_ref[...] + _normalize_back(total[...], gain_ref[...], unit, inverse)
             ).astype(jnp.bfloat16)
 
@@ -751,25 +748,27 @@
     return pl.pallas_call(
         kernel,
         grid=(steps,),
-        in_specs=[pl.BlockSpec((per_step, tokens, width), lambda i: (i, 0, 0))] * micro_count
-        + [
-            fixed(row_count, features),
-            fixed(row_count, features),
+        in_specs=[
+            pl.BlockSpec((per_step, row_count, width), lambda i: (i, 0, 0)),
+            pl.BlockSpec((1, row_count, features), lambda i: (micro, 0, 0)),
+            pl.BlockSpec((row_count, features), lambda i: (micro, 0)),
             fixed(1, features),
             columns,
             columns,
             columns,
-        ],
-        out_specs=fixed(row_count, features),
-        out_shape=jax.ShapeDtypeStruct((row_count, features), jnp.bfloat16),
+        ]
+        + [pl.BlockSpec(memory_space=pl.ANY)] * (before is not None),
+        out_specs=pl.BlockSpec((1, row_count, features), lambda i: (micro, 0, 0)),
+        out_shape=jax.ShapeDtypeStruct(patches.shape, jnp.bfloat16),
+        input_output_aliases={7: 0} if before is not None else {},
         scratch_shapes=[
             pltpu.VMEM((row_count, features), jnp.float32),
             pltpu.VMEM((3, row_count, wide), jnp.bfloat16),
         ],
         compiler_params=_params(60),
-        cost_estimate=_cost(20),
+        cost_estimate=_cost(cost),
         name="finish",
-    )(*received, rows, mixed_grad, gain, w_query, w_key, w_value)
+    )(received, patches, mixed_grad, gain, w_query, w_key, w_value, *([before] if before is not None else []))
 
 
 def grad_heads_call(place, units, places, made, gain, bias, sums, w_query, w_key, w_value, shares):
@@ -1069,6 +1068,19 @@
     )(place, keep, keep, received, received)
 
 
+def heads_total_call(keep, received):
+    def kernel(keep_ref, got_ref, out_ref):
+        out_ref[...] = (keep_ref[...] + got_ref[...].astype(jnp.float32)).astype(jnp.bfloat16)
+
+    return pl.pallas_call(
+        kernel,
+        out_shape=jax.ShapeDtypeStruct(keep.shape, jnp.bfloat16),
+        compiler_params=_params(8),
+        cost_estimate=_cost(20),
+        name="heads_total",
+    )(keep, received)
+
+
 def close_call(place, keep, received, shares):
     rows, width = keep.shape
     each = rows // shares
@@ -1090,7 +1102,7 @@
         ),
         out_shape=[jax.ShapeDtypeStruct((each, width), jnp.bfloat16)] * shares,
         compiler_params=_params(8),
-        cost_estimate=_cost(0),
+        cost_estimate=_cost(6),
         name="close",
     )(place, keep, received)
 
@@ -1147,8 +1159,8 @@
     at_blk, at_mb = lax.axis_index("blk"), lax.axis_index("mb")
     place = jnp.stack([at_blk, at_mb, at_mb % 2 + at_blk % 2 * 2]).astype(jnp.int32)
     blk_bits = _bits(blocks)
-    up_steps = [("mb", 2), *(("blk", bit) for bit in blk_bits[1:])]
-    down_steps = [up_steps[1], up_steps[0], *up_steps[2:]]
+    down_steps = [("mb", 2), *(("blk", bit) for bit in blk_bits[1:])]
+    up_steps = [down_steps[1], down_steps[0], *down_steps[2:]]
     each, owned, block_rows = features // (blocks * shares), hidden // (blocks * shares), features // blocks
     tie = lax.optimization_barrier
 
@@ -1230,9 +1242,10 @@
     pair = (shares // 2, -1, heads_keep.shape[-1])
     heads_received = _paired(heads_send, "mb", 1).reshape(pair)
     down_keep, down_received = then(heads_keep, down_keep, down_received)
-    for step in down_steps[2:]:
+    for step in down_steps[2:-1]:
         down_theirs, down_keep = halve_call(place, down_keep, down_received, step, 0)
         down_received = _paired(down_theirs, *step)
+    down_theirs, down_keep = halve_call(place, down_keep, down_received, down_steps[-1], 0)
     up_keep, up_received = then(down_keep, up_keep, up_received)
     for step in up_steps[2:]:
         up_theirs, up_keep = halve_call(place, up_keep, up_received, step, 3)
@@ -1240,19 +1253,27 @@
     heads_theirs, heads_keep = halve_call(
         place, *then(up_keep, heads_keep.reshape(pair), heads_received), ("mb", 2), 0
     )
+    heads_theirs, down_theirs = tie((heads_theirs, down_theirs))
     heads_received = _paired(heads_theirs, "mb", 2)
-    returned = list(then(heads_keep, *returned))
-    patches_grad = finish_call(returned, rows, mixed_grad, gain_one, w_query, w_key, w_value)
-    up_keep, up_received = then(patches_grad, up_keep, up_received)
+    down_received = _paired(down_theirs, *down_steps[-1])
+    finish = (patches, mixed_grad, gain_one, w_query, w_key, w_value)
+    patches_grad = None
+    for micro in range(micro_count - 1):
+        first, heads_keep, heads_received = then(down_keep, returned[micro], heads_keep, heads_received)
+        patches_grad = finish_call(first, *finish, micro, patches_grad, 0)
+        heads_keep, heads_received = then(patches_grad, heads_keep, heads_received)
+    returned[-1], heads_keep, heads_received = tie((returned[-1], heads_keep, heads_received))
+    heads_total = heads_total_call(heads_keep[0], heads_received[0]).reshape(blocks, each, heads_keep.shape[-1])
+    heads_parts = swap(heads_total)
+    up_keep, up_received = then(heads_total, up_keep, up_received)
     parts = close_call(place, up_keep[0], up_received[0], shares)
-    heads_keep, heads_received = then(parts, heads_keep, heads_received)
-    heads_total = (heads_keep + heads_received.astype(jnp.float32)).astype(jnp.bfloat16)
-    heads_total = swap(heads_total.reshape(blocks, each, heads_keep.shape[-1]))
+    last = then(parts[0], returned[-1])[0]
     parts = [parts[0]] + [to_share(parts[share], share) for share in range(1, shares)]
-    up_total, out_total = assemble_call(place, parts, down_steps, blocks, owned)
+    patches_grad = finish_call(last, *finish, micro_count - 1, patches_grad, 20)
+    up_total, out_total = assemble_call(place, then(patches_grad, *parts), down_steps, blocks, owned)
     down_keep, down_received = then(up_total, down_keep, down_received)
     down_total = (down_keep + down_received.astype(jnp.float32))[0]
-    query_total, key_total, value_total, *sums = assemble_heads_call(then(down_total, heads_total)[0], slot)
+    query_total, key_total, value_total, *sums = assemble_heads_call(then(down_total, heads_parts)[0], slot)
     return (
         layer_out.reshape(patches.shape),
         patches_grad.reshape(patches.shape),

time: 256 us -> 246 us (0.961)
  waiting for transfers between devices: 99 us -> 76.9 us
  starting transfers between devices: 50.6 us -> 56.9 us
  Pallas kernels: 92 us -> 97.7 us
    all_to_all x6, waiting for transfers between devices: 47.1 us -> 30.2 us  [swap(): lax.all_to_all(values, 'blk', split_axis=0, concat_axis=0, tiled=True)]
    pallas_call x1 -> x3, Pallas kernels: 6.57 us -> 12.7 us  [the longest x2 11.9 us: finish_call(): pl.pallas_call(kernel, grid=(steps,), in_specs=[pl.BlockSpec((per_step, r...]
    ppermute x25, starting transfers between devices: 22.3 us -> 28.1 us  [_paired(): return lax.ppermute(values, axis, [(i, i ^ bit) for i in range(count)])]
    ppermute x25, waiting for transfers between devices: 50.1 us -> 46.2 us  [_paired(): return lax.ppermute(values, axis, [(i, i ^ bit) for i in range(count)])]
  transfers between devices with their start and end apart: 33 -> 33, of which waited for: 17 -> 14; matrix products, arithmetic and copies ran while one was open for 3% -> 3% of each run, Pallas kernels for 33% -> 37%
where the time goes in v5:
time: 246 us
  Pallas kernels  97.7 us (40%)
  waiting for transfers between devices  76.9 us (31%)
  starting transfers between devices  56.9 us (23%)
  local copies, waits for them, and re-layouts  8.39 us (3%)
  other arithmetic  4.9 us (2%)
    ppermute x25, waiting for transfers between devices, _paired(): return lax.ppermute(values, axis, [(i, i ^ bit) for i in range(count)])  46.2 us
    all_to_all x6, waiting for transfers between devices, swap(): lax.all_to_all(values, 'blk', split_axis=0, concat_axis=0, tiled=True)  30.2 us
    all_to_all x6, starting transfers between devices, swap(): lax.all_to_all(values, 'blk', split_axis=0, concat_axis=0, tiled=True)  28.7 us
    ppermute x25, starting transfers between devices, _paired(): return lax.ppermute(values, axis, [(i, i ^ bit) for i in range(count)])  28.1 us
    pallas_call x1, Pallas kernels, grad_middle_call(): pl.pallas_call(kernel, grid_spec=pltpu.PrefetchScalarGridSpec(num_scalar_...  20.3 us
    pallas_call x1, Pallas kernels, attend_back_call(): pl.pallas_call(kernel, grid=(micro_count, steps), in_specs=[pl.BlockSpec(...  15.4 us
    pallas_call x1, Pallas kernels, middle_call(): pl.pallas_call(kernel, grid_spec=pltpu.PrefetchScalarGridSpec(num_scalar_...  15.2 us
    pallas_call x2, Pallas kernels, finish_call(): pl.pallas_call(kernel, grid=(steps,), in_specs=[pl.BlockSpec((per_step, r...  11.9 us
  transfers between devices with their start and end apart: 33, of which 14 were waited for; matrix products, arithmetic and copies ran while one was open for 3% of the time, Pallas kernels for 37%

profile of v5, /device:TPU:0, one launch (start us, length us, event | category | flops | bytes accessed | tf_op | source)
XLA Modules:
  0.0 245.7 jit_solution(9277295881576448865)
XLA Ops:
  0.6 5.6 %project.1 = (bf16[8,256,384]{2,1,0:T(8,128)(2,1)}, bf16[128,1024]{1,0:T(8,128)(2,1)}, bf16[128,1024]{1,0:T(8,128)(2,1)}) custom-call(bf16[256,1024]{1,0:T(8,128)(2,1)} %bitcast.42, f32[1,1024]{1,0:T(1,128)} %bitcast.57, f32[1,1024]{1,0:T(1,128)} %bitcast.62, bf16[1024,1024]{1,0:T(8,128)(2,1)} %wq_ref.5, bf16[1024,1024]{1,0:T(8,128)(2,1)} %wk_ref.5, ...), custom_call_target="tpu_custom_call" | custom-call | flops 6000000000 | bytes 1 | tf_op jit(solution)/shard_map/project/pallas_call | solution.py:381
  6.3 7.4 %all-to-all-start = ((bf16[8,256,384]{2,1,0:T(8,128)(2,1)}), bf16[8,256,384]{2,1,0:T(8,128)(2,1)S(1)}, u32[]{:S(2)}, u32[]{:S(2)}) async-start(bf16[8,256,384]{2,1,0:T(8,128)(2,1)} %get-tuple-element.124), calls=%async_computation | async-start | bytes 3145728 | tf_op jit(solution)/shard_map/all_to_all | solution.py:1154
  16.5 20.7 %collective-permute-done = bf16[128,1024]{1,0:T(8,128)(2,1)S(1)} collective-permute-done((bf16[128,1024]{1,0:T(8,128)(2,1)S(1)}, bf16[128,1024]{1,0:T(8,128)(2,1)S(1)}, u32[]{:S(2)}, u32[]{:S(2)}) %collective-permute-start) | collective-permute-done | bytes 262176 | tf_op jit(solution)/shard_map/ppermute | solution.py:893
  37.2 13.5 %all-to-all-done = bf16[8,256,384]{2,1,0:T(8,128)(2,1)S(1)} async-done(((bf16[8,256,384]{2,1,0:T(8,128)(2,1)}), bf16[8,256,384]{2,1,0:T(8,128)(2,1)S(1)}, u32[]{:S(2)}, u32[]{:S(2)}) %all-to-all-start) | async-done | bytes 1572896 | tf_op jit(solution)/shard_map/all_to_all | solution.py:1154
  50.7 9.5 %attend.1 = (bf16[8,2,128,128]{3,2,1,0:T(8,128)(2,1)}, f32[8,2,128,128]{3,2,1,0:T(8,128)S(1)}, f32[2,8,1024]{2,1,0:T(8,128)S(1)}) custom-call(s32[2,8]{1,0:T(2,128)S(1)} %copy-done.16, bf16[8,2,128,384]{3,2,1,0:T(8,128)(2,1)S(1)} %bitcast.40), custom_call_target="tpu_custom_call" | custom-call | flops 11000000512 | bytes 1 | tf_op jit(solution)/shard_map/attend/pallas_call | solution.py:468
  61.2 2.9 %collective-permute-done.1 = bf16[128,1024]{1,0:T(8,128)(2,1)S(1)} collective-permute-done((bf16[128,1024]{1,0:T(8,128)(2,1)S(1)}, bf16[128,1024]{1,0:T(8,128)(2,1)S(1)}, u32[]{:S(2)}, u32[]{:S(2)}) %collective-permute-start.1) | collective-permute-done | bytes 262176 | tf_op jit(solution)/shard_map/ppermute | solution.py:893
  65.0 3.7 %all-to-all-start.1 = ((bf16[8,256,128]{2,1,0:T(8,128)(2,1)}), bf16[8,256,128]{2,1,0:T(8,128)(2,1)S(1)}, u32[]{:S(2)}, u32[]{:S(2)}) async-start(bf16[8,256,128]{2,1,0:T(8,128)(2,1)} %bitcast.8), calls=%async_computation.1 | async-start | bytes 1048576 | tf_op jit(solution)/shard_map/all_to_all | solution.py:1154
  71.8 11.6 %all-to-all-done.1.att_ref = bf16[8,256,128]{2,1,0:T(8,128)(2,1)S(1)} async-done(((bf16[8,256,128]{2,1,0:T(8,128)(2,1)}), bf16[8,256,128]{2,1,0:T(8,128)(2,1)S(1)}, u32[]{:S(2)}, u32[]{:S(2)}) %all-to-all-start.1) | async-done | bytes 524320 | tf_op jit(solution)/shard_map/all_to_all | solution.py:1154
  89.7 15.2 %middle.1 = (bf16[256,1024]{1,0:T(8,128)(2,1)}, f32[256,1024]{1,0:T(8,128)S(1)}, bf16[8,256,128]{2,1,0:T(8,128)(2,1)}, f32[2,1024]{1,0:T(2,128)S(1)}, bf16[256,2...) custom-call(s32[3]{0:T(128)S(1)} %pad_add_fusion.place_ref, ...), custom_call_target="tpu_custom_call" | custom-call | flops 20000000000 | bytes 1 | tf_op jit(solution)/shard_map/middle/pallas_call | solution.py:677
  113.8 3.7 %all-to-all-start.2 = ((bf16[8,256,128]{2,1,0:T(8,128)(2,1)}), bf16[8,256,128]{2,1,0:T(8,128)(2,1)S(1)}, u32[]{:S(2)}, u32[]{:S(2)}) async-start(bf16[8,256,128]{2,1,0:T(8,128)(2,1)} %get-tuple-element.146), calls=%async_computation.2 | async-start | bytes 1048576 | tf_op jit(solution)/shard_map/all_to_all | solution.py:1154
  122.9 20.3 %grad_middle.1 = (bf16[512,1024]{1,0:T(8,128)(2,1)}, f32[512,1024]{1,0:T(8,128)}, bf16[512,1280]{1,0:T(8,128)(2,1)}, f32[512,1280]{1,0:T(8,128)}) custom-call(s32[3]{0:T(128)} %copy-done.6, bf16[2,256,1024]{2,1,0:T(8,128)(2,1)} %copy-done.13, bf16[2,256,1024]{2,1,0:T(8,128)(2,1)} %copy-done.26, bf16[2,256,1024]{2,1,0:T(8,128)(2,1)} %collective-permute-done.8.refs_2_, ...), custom_call_target="tpu_custom_call" | custom-call | flops 20000000000 | bytes 1 | tf_op jit(solution)/shard_map/grad_middle/pallas_call | solution.py:1007
  146.2 15.4 %attend_back.1 = (bf16[8,128,384]{2,1,0:T(8,128)(2,1)}, bf16[8,128,384]{2,1,0:T(8,128)(2,1)}) custom-call(s32[2,8]{1,0:T(2,128)} %lengths_ref.3, bf16[8,2,128,384]{3,2,1,0:T(8,128)(2,1)} %bitcast.41, bf16[8,2,128,128]{3,2,1,0:T(8,128)(2,1)} %bitcast.56, f32[8,2,128,128]{3,2,1,0:T(8,128)} %copy-done.18, f32[2,8,1024]{2,1,0:T(8,128)} %copy-done.19), custom_call_target="tpu_custom_call" | custom-call | flops 3000000000 | bytes 1 | tf_op jit(solution)/shard_map/attend_back/pallas_call | solution.py:572
  161.6 5.7 %all-to-all-start.3 = ((bf16[8,128,384]{2,1,0:T(8,128)(2,1)}), bf16[8,128,384]{2,1,0:T(8,128)(2,1)}, u32[]{:S(2)}, u32[]{:S(2)}) async-start(bf16[8,128,384]{2,1,0:T(8,128)(2,1)} %get-tuple-element.163), calls=%async_computation.3 | async-start | bytes 1572864 | tf_op jit(solution)/shard_map/all_to_all | solution.py:1154
  167.3 8.0 %collective-permute-done.14.got_theirs.got_mine = bf16[4,128,1280]{2,1,0:T(8,128)(2,1)} collective-permute-done((bf16[4,128,1280]{2,1,0:T(8,128)(2,1)}, bf16[4,128,1280]{2,1,0:T(8,128)(2,1)}, u32[]{:S(2)}, u32[]{:S(2)}) %collective-permute-start.14) | collective-permute-done | bytes 1310752 | tf_op jit(solution)/shard_map/ppermute | solution.py:893
  180.5 8.9 %collective-permute-start.19 = (bf16[2,128,1280]{2,1,0:T(8,128)(2,1)S(1)}, bf16[2,128,1280]{2,1,0:T(8,128)(2,1)}, u32[]{:S(2)}, u32[]{:S(2)}) collective-permute-start(bf16[2,128,1280]{2,1,0:T(8,128)(2,1)S(1)} %get-tuple-element.189), channel_id=1, source_target_pairs={{0,2},{1,3},{2,0},{3,1},{4,6},{5,7},{6,4},{7,5},{8,10},{9,11},{10,... | collective-permute-start | bytes 1966088 | tf_op jit(solution)/shard_map/ppermute | solution.py:893
  189.4 4.4 %all-to-all-start.4 = ((bf16[8,128,384]{2,1,0:T(8,128)(2,1)}), bf16[8,128,384]{2,1,0:T(8,128)(2,1)}, u32[]{:S(2)}, u32[]{:S(2)}) async-start(bf16[8,128,384]{2,1,0:T(8,128)(2,1)} %get-tuple-element.164), calls=%async_computation.4 | async-start | bytes 1572864 | tf_op jit(solution)/shard_map/all_to_all | solution.py:1154
  193.9 8.0 %grad_heads.1 = (bf16[2,8,32,512]{3,2,1,0:T(8,128)(2,1)}, f32[2,8,32,512]{3,2,1,0:T(8,128)}) custom-call(s32[3]{0:T(128)} %copy-done.6, bf16[512,1024]{1,0:T(8,128)(2,1)} %pad_maximum_fusion.refs_0_, bf16[512,1024]{1,0:T(8,128)(2,1)} %collective-permute-done.15.refs_1_, bf16[512,1024]{1,0:T(8,128)(2,1)} %pad_maximum_fusion.1.refs_2_, ...), custom_call_target="tpu_custom_call" | custom-call | flops 20000000000 | bytes 1 | tf_op jit(solution)/shard_map/grad_heads/pallas_call | solution.py:821
  205.8 2.7 %collective-permute-start.22 = (bf16[1,128,1280]{2,1,0:T(8,128)(2,1)S(1)}, bf16[1,128,1280]{2,1,0:T(8,128)(2,1)S(1)}, u32[]{:S(2)}, u32[]{:S(2)}) collective-permute-start(bf16[1,128,1280]{2,1,0:T(8,128)(2,1)S(1)} %get-tuple-element.208), channel_id=1, source_target_pairs={{0,16},{4,20},{8,24},{12,28},{16,0},{20,4},{24,8},{28,12},{1,17},{... | collective-permute-start | bytes 983048 | tf_op jit(solution)/shard_map/ppermute | solution.py:893
  208.7 5.1 %collective-permute-done.21 = bf16[1,256,512]{2,1,0:T(8,128)(2,1)S(1)} collective-permute-done((bf16[1,256,512]{2,1,0:T(8,128)(2,1)S(1)}, bf16[1,256,512]{2,1,0:T(8,128)(2,1)S(1)}, u32[]{:S(2)}, u32[]{:S(2)}) %collective-permute-start.21) | collective-permute-done | bytes 262176 | tf_op jit(solution)/shard_map/ppermute | solution.py:893
  213.8 6.0 %finish.2.refs_0_ = bf16[2,128,1024]{2,1,0:T(8,128)(2,1)} custom-call(bf16[8,128,384]{2,1,0:T(8,128)(2,1)} %all-to-all-done.3.data_ref, bf16[2,128,1024]{2,1,0:T(8,128)(2,1)} %rows_ref.3, f32[256,1024]{1,0:T(8,128)} %copy-done.3, f32[1,1024]{1,0:T(1,128)} %bitcast.59, bf16[1024,1024]{1,0:T(8,128)(2,1)} %wq_ref.5, bf16[1024,1024]{1,0:T(8,128)(2,1)} %wk_ref.5, ...), custom_call_target="tpu_custom_call" | custom-call | flops 1 | bytes 1 | tf_op jit(solution)/shard_map/finish/pallas_call | solution.py:748
  219.8 5.2 %all-to-all-done.4.data_ref = bf16[8,128,384]{2,1,0:T(8,128)(2,1)} async-done(((bf16[8,128,384]{2,1,0:T(8,128)(2,1)}), bf16[8,128,384]{2,1,0:T(8,128)(2,1)}, u32[]{:S(2)}, u32[]{:S(2)}) %all-to-all-start.4) | async-done | bytes 786464 | tf_op jit(solution)/shard_map/all_to_all | solution.py:1154
  225.7 3.8 %all-to-all-start.5 = ((bf16[8,32,512]{2,1,0:T(8,128)(2,1)}), bf16[8,32,512]{2,1,0:T(8,128)(2,1)S(1)}, u32[]{:S(2)}, u32[]{:S(2)}) async-start(bf16[8,32,512]{2,1,0:T(8,128)(2,1)} %bitcast.23), calls=%async_computation.5 | async-start | bytes 524288 | tf_op jit(solution)/shard_map/all_to_all | solution.py:1154
  229.4 3.8 %collective-permute-done.22 = bf16[1,128,1280]{2,1,0:T(8,128)(2,1)S(1)} collective-permute-done((bf16[1,128,1280]{2,1,0:T(8,128)(2,1)S(1)}, bf16[1,128,1280]{2,1,0:T(8,128)(2,1)S(1)}, u32[]{:S(2)}, u32[]{:S(2)}) %collective-permute-start.22) | collective-permute-done | bytes 327712 | tf_op jit(solution)/shard_map/ppermute | solution.py:893
  236.6 6.0 %finish.3 = bf16[2,128,1024]{2,1,0:T(8,128)(2,1)} custom-call(bf16[8,128,384]{2,1,0:T(8,128)(2,1)} %all-to-all-done.4.data_ref, bf16[2,128,1024]{2,1,0:T(8,128)(2,1)} %rows_ref.3, f32[256,1024]{1,0:T(8,128)} %copy-done.3, f32[1,1024]{1,0:T(1,128)} %bitcast.60, bf16[1024,1024]{1,0:T(8,128)(2,1)} %wq_ref.5, ...), custom_call_target="tpu_custom_call", output_to_operand_aliasing={{}: (7, {})} | custom-call | flops 20000000000 | bytes 1 | tf_op jit(solution)/shard_map/finish/pallas_call | solution.py:748
  (135 shorter events, 47.6 us)
Async XLA Ops:
  6.3 44.4 %all-to-all-start = ((bf16[8,256,384]{2,1,0:T(8,128)(2,1)}), bf16[8,256,384]{2,1,0:T(8,128)(2,1)S(1)}, u32[]{:S(2)}, u32[]{:S(2)}) async-start(bf16[8,256,384]{2,1,0:T(8,128)(2,1)} %get-tuple-element.124), calls=%async_computation | async-start | bytes 3145728 | tf_op jit(solution)/shard_map/all_to_all | solution.py:1154
  14.4 22.8 %collective-permute-start = (bf16[128,1024]{1,0:T(8,128)(2,1)S(1)}, bf16[128,1024]{1,0:T(8,128)(2,1)S(1)}, u32[]{:S(2)}, u32[]{:S(2)}) collective-permute-start(bf16[128,1024]{1,0:T(8,128)(2,1)S(1)} %get-tuple-element.235), channel_id=1, source_target_pairs={{0,4},{4,0},{8,12},{12,8},{16,20},{20,16},{24,28},{28,24},{1,5},{5... | collective-permute-start | bytes 786440 | tf_op jit(solution)/shard_map/ppermute | solution.py:893
  16.5 48.5 %collective-permute-start.2 = (bf16[128,1024]{1,0:T(8,128)(2,1)}, bf16[128,1024]{1,0:T(8,128)(2,1)}, u32[]{:S(2)}, u32[]{:S(2)}) collective-permute-start(bf16[128,1024]{1,0:T(8,128)(2,1)} %get-tuple-element.234), channel_id=1, source_target_pairs={{0,4},{4,0},{8,12},{12,8},{16,20},{20,16},{24,28},{28,24},{1,5},{5... | collective-permute-start | bytes 786440 | tf_op jit(solution)/shard_map/ppermute | solution.py:893
  50.7 13.4 %collective-permute-start.1 = (bf16[128,1024]{1,0:T(8,128)(2,1)S(1)}, bf16[128,1024]{1,0:T(8,128)(2,1)S(1)}, u32[]{:S(2)}, u32[]{:S(2)}) collective-permute-start(bf16[128,1024]{1,0:T(8,128)(2,1)S(1)} %copy-done.24), channel_id=1, source_target_pairs={{0,16},{4,20},{8,24},{12,28},{16,0},{20,4},{24,8},{28,12},{1,17},{... | collective-permute-start | bytes 786440 | tf_op jit(solution)/shard_map/ppermute | solution.py:893
  65.0 18.4 %all-to-all-start.1 = ((bf16[8,256,128]{2,1,0:T(8,128)(2,1)}), bf16[8,256,128]{2,1,0:T(8,128)(2,1)S(1)}, u32[]{:S(2)}, u32[]{:S(2)}) async-start(bf16[8,256,128]{2,1,0:T(8,128)(2,1)} %bitcast.8), calls=%async_computation.1 | async-start | bytes 1048576 | tf_op jit(solution)/shard_map/all_to_all | solution.py:1154
  86.0 23.5 %collective-permute-start.7 = (bf16[2,256,1024]{2,1,0:T(8,128)(2,1)S(1)}, bf16[2,256,1024]{2,1,0:T(8,128)(2,1)S(1)}, u32[]{:S(2)}, u32[]{:S(2)}) collective-permute-start(bf16[2,256,1024]{2,1,0:T(8,128)(2,1)S(1)} %get-tuple-element.136.norm_ref.refs_0_), channel_id=1, source_target_pairs={{0,1},{1,0},{2,3},{3,2},{4,5},{5,4},{6,7},{7,6},{8,9},{9,8},{10,11... | collective-permute-start | bytes 3145736 | tf_op jit(solution)/shard_map/ppermute | solution.py:893
  86.1 25.7 %collective-permute-start.8 = (bf16[2,256,1024]{2,1,0:T(8,128)(2,1)S(1)}, bf16[2,256,1024]{2,1,0:T(8,128)(2,1)}, u32[]{:S(2)}, u32[]{:S(2)}) collective-permute-start(bf16[2,256,1024]{2,1,0:T(8,128)(2,1)S(1)} %get-tuple-element.136.norm_ref.refs_0_), channel_id=1, source_target_pairs={{0,4},{4,0},{8,12},{12,8},{16,20},{20,16},{24,28},{28,24},{1,5},{5... | collective-permute-start | bytes 3145736 | tf_op jit(solution)/shard_map/ppermute | solution.py:893
  87.6 19.8 %collective-permute-start.5 = (bf16[256,1024]{1,0:T(8,128)(2,1)}, bf16[256,1024]{1,0:T(8,128)(2,1)S(1)}, u32[]{:S(2)}, u32[]{:S(2)}) collective-permute-start(bf16[256,1024]{1,0:T(8,128)(2,1)} %pad_maximum_fusion.2), channel_id=1, source_target_pairs={{0,8},{4,12},{8,0},{12,4},{16,24},{20,28},{24,16},{28,20},{1,9},{5... | collective-permute-start | bytes 1572872 | tf_op jit(solution)/shard_map/ppermute | solution.py:893
  87.6 18.2 %collective-permute-start.6 = (bf16[128,1024]{1,0:T(8,128)(2,1)S(1)}, bf16[128,1024]{1,0:T(8,128)(2,1)S(1)}, u32[]{:S(2)}, u32[]{:S(2)}) collective-permute-start(bf16[128,1024]{1,0:T(8,128)(2,1)S(1)} %copy-done.23), channel_id=1, source_target_pairs={{0,16},{4,20},{8,24},{12,28},{16,0},{20,4},{24,8},{28,12},{1,17},{... | collective-permute-start | bytes 786440 | tf_op jit(solution)/shard_map/ppermute | solution.py:893
  111.8 9.5 %collective-permute-start.9 = (bf16[2,256,1024]{2,1,0:T(8,128)(2,1)}, bf16[2,256,1024]{2,1,0:T(8,128)(2,1)S(1)}, u32[]{:S(2)}, u32[]{:S(2)}) collective-permute-start(bf16[2,256,1024]{2,1,0:T(8,128)(2,1)} %collective-permute-done.8.refs_2_), channel_id=1, source_target_pairs={{0,1},{1,0},{2,3},{3,2},{4,5},{5,4},{6,7},{7,6},{8,9},{9,8},{10,11... | collective-permute-start | bytes 3145736 | tf_op jit(solution)/shard_map/ppermute | solution.py:893
  113.8 30.6 %all-to-all-start.2 = ((bf16[8,256,128]{2,1,0:T(8,128)(2,1)}), bf16[8,256,128]{2,1,0:T(8,128)(2,1)S(1)}, u32[]{:S(2)}, u32[]{:S(2)}) async-start(bf16[8,256,128]{2,1,0:T(8,128)(2,1)} %get-tuple-element.146), calls=%async_computation.2 | async-start | bytes 1048576 | tf_op jit(solution)/shard_map/all_to_all | solution.py:1154
  117.5 25.9 %collective-permute-start.13 = (bf16[256,1024]{1,0:T(8,128)(2,1)S(1)}, bf16[256,1024]{1,0:T(8,128)(2,1)S(1)}, u32[]{:S(2)}, u32[]{:S(2)}) collective-permute-start(bf16[256,1024]{1,0:T(8,128)(2,1)S(1)} %pad_maximum_fusion.3), channel_id=1, source_target_pairs={{0,8},{4,12},{8,0},{12,4},{16,24},{20,28},{24,16},{28,20},{1,9},{5... | collective-permute-start | bytes 1572872 | tf_op jit(solution)/shard_map/ppermute | solution.py:893
  119.3 48.0 %collective-permute-start.15 = (bf16[512,1024]{1,0:T(8,128)(2,1)}, bf16[512,1024]{1,0:T(8,128)(2,1)}, u32[]{:S(2)}, u32[]{:S(2)}) collective-permute-start(bf16[512,1024]{1,0:T(8,128)(2,1)} %pad_maximum_fusion.refs_0_), channel_id=1, source_target_pairs={{0,4},{4,0},{8,12},{12,8},{16,20},{20,16},{24,28},{28,24},{1,5},{5... | collective-permute-start | bytes 3145736 | tf_op jit(solution)/shard_map/ppermute | solution.py:893
  143.2 32.2 %collective-permute-start.14 = (bf16[4,128,1280]{2,1,0:T(8,128)(2,1)}, bf16[4,128,1280]{2,1,0:T(8,128)(2,1)}, u32[]{:S(2)}, u32[]{:S(2)}) collective-permute-start(bf16[4,128,1280]{2,1,0:T(8,128)(2,1)} %bitcast.61), channel_id=1, source_target_pairs={{0,8},{4,12},{8,0},{12,4},{16,24},{20,28},{24,16},{28,20},{1,9},{5... | collective-permute-start | bytes 3932168 | tf_op jit(solution)/shard_map/ppermute | solution.py:893
  144.4 34.1 %collective-permute-start.16 = (bf16[4,128,1024]{2,1,0:T(8,128)(2,1)}, bf16[4,128,1024]{2,1,0:T(8,128)(2,1)}, u32[]{:S(2)}, u32[]{:S(2)}) collective-permute-start(bf16[4,128,1024]{2,1,0:T(8,128)(2,1)} %bitcast.18), channel_id=1, source_target_pairs={{0,2},{1,3},{2,0},{3,1},{4,6},{5,7},{6,4},{7,5},{8,10},{9,11},{10,... | collective-permute-start | bytes 3145736 | tf_op jit(solution)/shard_map/ppermute | solution.py:893
  145.9 32.6 %collective-permute-start.17 = (bf16[512,1024]{1,0:T(8,128)(2,1)}, bf16[512,1024]{1,0:T(8,128)(2,1)}, u32[]{:S(2)}, u32[]{:S(2)}) collective-permute-start(bf16[512,1024]{1,0:T(8,128)(2,1)} %pad_maximum_fusion.1.refs_2_), channel_id=1, source_target_pairs={{0,4},{4,0},{8,12},{12,8},{16,20},{20,16},{24,28},{28,24},{1,5},{5... | collective-permute-start | bytes 3145736 | tf_op jit(solution)/shard_map/ppermute | solution.py:893
  161.6 27.8 %all-to-all-start.3 = ((bf16[8,128,384]{2,1,0:T(8,128)(2,1)}), bf16[8,128,384]{2,1,0:T(8,128)(2,1)}, u32[]{:S(2)}, u32[]{:S(2)}) async-start(bf16[8,128,384]{2,1,0:T(8,128)(2,1)} %get-tuple-element.163), calls=%async_computation.3 | async-start | bytes 1572864 | tf_op jit(solution)/shard_map/all_to_all | solution.py:1154
  180.5 21.8 %collective-permute-start.18 = (bf16[2,128,1024]{2,1,0:T(8,128)(2,1)S(1)}, bf16[2,128,1024]{2,1,0:T(8,128)(2,1)S(1)}, u32[]{:S(2)}, u32[]{:S(2)}) collective-permute-start(bf16[2,128,1024]{2,1,0:T(8,128)(2,1)S(1)} %get-tuple-element.185), channel_id=1, source_target_pairs={{0,8},{4,12},{8,0},{12,4},{16,24},{20,28},{24,16},{28,20},{1,9},{5... | collective-permute-start | bytes 1572872 | tf_op jit(solution)/shard_map/ppermute | solution.py:893
  180.5 22.4 %collective-permute-start.19 = (bf16[2,128,1280]{2,1,0:T(8,128)(2,1)S(1)}, bf16[2,128,1280]{2,1,0:T(8,128)(2,1)}, u32[]{:S(2)}, u32[]{:S(2)}) collective-permute-start(bf16[2,128,1280]{2,1,0:T(8,128)(2,1)S(1)} %get-tuple-element.189), channel_id=1, source_target_pairs={{0,2},{1,3},{2,0},{3,1},{4,6},{5,7},{6,4},{7,5},{8,10},{9,11},{10,... | collective-permute-start | bytes 1966088 | tf_op jit(solution)/shard_map/ppermute | solution.py:893
  189.4 35.5 %all-to-all-start.4 = ((bf16[8,128,384]{2,1,0:T(8,128)(2,1)}), bf16[8,128,384]{2,1,0:T(8,128)(2,1)}, u32[]{:S(2)}, u32[]{:S(2)}) async-start(bf16[8,128,384]{2,1,0:T(8,128)(2,1)} %get-tuple-element.164), calls=%async_computation.4 | async-start | bytes 1572864 | tf_op jit(solution)/shard_map/all_to_all | solution.py:1154
  205.8 27.5 %collective-permute-start.22 = (bf16[1,128,1280]{2,1,0:T(8,128)(2,1)S(1)}, bf16[1,128,1280]{2,1,0:T(8,128)(2,1)S(1)}, u32[]{:S(2)}, u32[]{:S(2)}) collective-permute-start(bf16[1,128,1280]{2,1,0:T(8,128)(2,1)S(1)} %get-tuple-element.208), channel_id=1, source_target_pairs={{0,16},{4,20},{8,24},{12,28},{16,0},{20,4},{24,8},{28,12},{1,17},{... | collective-permute-start | bytes 983048 | tf_op jit(solution)/shard_map/ppermute | solution.py:893
  208.5 35.5 %collective-permute-start.26 = (bf16[1,128,1024]{2,1,0:T(8,128)(2,1)S(1)}, bf16[1,128,1024]{2,1,0:T(8,128)(2,1)S(1)}, u32[]{:S(2)}, u32[]{:S(2)}) collective-permute-start(bf16[1,128,1024]{2,1,0:T(8,128)(2,1)S(1)} %get-tuple-element.222), channel_id=1, source_target_pairs={{0,16},{4,20},{8,24},{12,28},{16,0},{20,4},{24,8},{28,12},{1,17},{... | collective-permute-start | bytes 786440 | tf_op jit(solution)/shard_map/ppermute | solution.py:893
  225.7 19.2 %all-to-all-start.5 = ((bf16[8,32,512]{2,1,0:T(8,128)(2,1)}), bf16[8,32,512]{2,1,0:T(8,128)(2,1)S(1)}, u32[]{:S(2)}, u32[]{:S(2)}) async-start(bf16[8,32,512]{2,1,0:T(8,128)(2,1)} %bitcast.23), calls=%async_computation.5 | async-start | bytes 524288 | tf_op jit(solution)/shard_map/all_to_all | solution.py:1154
  233.9 8.6 %collective-permute-start.23 = (bf16[32,1280]{1,0:T(8,128)(2,1)S(1)}, bf16[32,1280]{1,0:T(8,128)(2,1)S(1)}, u32[]{:S(2)}, u32[]{:S(2)}) collective-permute-start(bf16[32,1280]{1,0:T(8,128)(2,1)S(1)} %get-tuple-element.214), channel_id=1, source_target_pairs={{0,1},{1,0},{2,3},{3,2},{4,5},{5,4},{6,7},{7,6},{8,9},{9,8},{10,11... | collective-permute-start | bytes 245768 | tf_op jit(solution)/shard_map/ppermute | solution.py:893
  (42 other events, 419.2 us)

commit v6 on v5

--- a/solution.py
+++ b/solution.py
@@ -351,7 +351,7 @@
     return pl.CostEstimate(flops=int(microseconds * 1e9) + 1, bytes_accessed=1, transcendentals=0)
 
 
-def project_call(rows, gain, bias, w_query, w_key, w_value, blocks, tokens):
+def project_call(rows, gain, bias, w_query, w_key, w_value, blocks, cuts):
     row_count, features = rows.shape
     slot = features // blocks
     per_step = max(1, min(blocks, 512 // slot))
@@ -364,8 +364,8 @@
         @pl.when(pl.program_id(0) == 0)
         def _():
             unit, _unused = _normalize(rows_ref[...].astype(jnp.float32))
-            for micro, unit_ref in enumerate(unit_refs):
-                unit_ref[...] = unit[micro * tokens : (micro + 1) * tokens].astype(jnp.bfloat16)
+            for (first, last), unit_ref in zip(cuts, unit_refs):
+                unit_ref[...] = unit[first:last].astype(jnp.bfloat16)
             norm_ref[...] = (unit * gain_ref[...] + bias_ref[...]).astype(jnp.bfloat16)
 
         for part, weight_ref in enumerate((wq_ref, wk_ref, wv_ref)):
@@ -383,9 +383,9 @@
         grid=(blocks // per_step,),
         in_specs=[whole, vector, vector, columns, columns, columns],
         out_specs=[pl.BlockSpec((per_step, row_count, 3 * slot), lambda i: (i, 0, 0))]
-        + [pl.BlockSpec((tokens, features), lambda i: (0, 0))] * (row_count // tokens),
+        + [pl.BlockSpec((last - first, features), lambda i: (0, 0)) for first, last in cuts],
         out_shape=[jax.ShapeDtypeStruct((blocks, row_count, 3 * slot), jnp.bfloat16)]
-        + [jax.ShapeDtypeStruct((tokens, features), jnp.bfloat16)] * (row_count // tokens),
+        + [jax.ShapeDtypeStruct((last - first, features), jnp.bfloat16) for first, last in cuts],
         scratch_shapes=[pltpu.VMEM((row_count, features), jnp.bfloat16)],
         compiler_params=_params(60),
         cost_estimate=_cost(6),
@@ -488,8 +488,8 @@
     )(lengths, received)
 
 
-def attend_back_call(received, grads, attended, logs, lengths, head_dim):
-    blocks, micro_count, tokens, width = received.shape
+def attend_back_call(received, grads, attended, logs, lengths, micro, cost, head_dim):
+    blocks, _, tokens, width = received.shape
     slot = width // 3
     doc_count = lengths.shape[1]
     step_blocks = max(1, min(blocks // 2, 512 // tokens))
@@ -497,10 +497,8 @@
     steps = blocks // step_blocks
     scale = 1.0 / math.sqrt(head_dim)
 
-    def kernel(lengths_ref, data_ref, grads_ref, att_ref, log_ref, *refs):
-        out_refs, (key_total, value_total, turned) = refs[:micro_count], refs[micro_count:]
-        micro = pl.program_id(0)
-        step = pl.program_id(1)
+    def kernel(lengths_ref, data_ref, grads_ref, att_ref, log_ref, out_ref, key_total, value_total, turned):
+        step = pl.program_id(0)
 
         @pl.when(step == 0)
         def _():
@@ -554,37 +552,31 @@
                 key_total[to, :] += key_made
                 value_total[to, :] += value_made
             query_grads = (jnp.concatenate(query_parts, axis=0).T * scale).astype(jnp.bfloat16).reshape(step_blocks, tokens, slot)
-            for at, out_ref in enumerate(out_refs):
-
-                @pl.when(micro == at)
-                def _():
-                    out_ref[pl.ds(step * step_blocks, step_blocks), :, 0:slot] = query_grads
+            out_ref[pl.ds(step * step_blocks, step_blocks), :, 0:slot] = query_grads
 
         _by_key_range(lengths_ref, micro, doc_count, step, rows, blocks, tokens, compute)
 
-        for at, out_ref in enumerate(out_refs):
-
-            @pl.when((step == steps - 1) & (micro == at))
-            def _():
-                out_ref[:, :, slot : 2 * slot] = key_total[...].astype(jnp.bfloat16).reshape(blocks, tokens, slot)
-                out_ref[:, :, 2 * slot :] = value_total[...].astype(jnp.bfloat16).reshape(blocks, tokens, slot)
+        @pl.when(step == steps - 1)
+        def _():
+            out_ref[:, :, slot : 2 * slot] = key_total[...].astype(jnp.bfloat16).reshape(blocks, tokens, slot)
+            out_ref[:, :, 2 * slot :] = value_total[...].astype(jnp.bfloat16).reshape(blocks, tokens, slot)
 
     return pl.pallas_call(
         kernel,
-        grid=(micro_count, steps),
+        grid=(steps,),
         in_specs=[
             pl.BlockSpec(memory_space=pltpu.SMEM),
-            pl.BlockSpec((blocks, 1, tokens, width), lambda m, s: (0, m, 0, 0)),
-            pl.BlockSpec((step_blocks, 1, tokens, slot), lambda m, s: (s, m, 0, 0)),
-            pl.BlockSpec((step_blocks, 1, tokens, slot), lambda m, s: (s, m, 0, 0)),
-            pl.BlockSpec((1, 8, rows), lambda m, s: (m, 0, s)),
+            pl.BlockSpec((blocks, 1, tokens, width), lambda s: (0, micro, 0, 0)),
+            pl.BlockSpec((step_blocks, 1, tokens, slot), lambda s: (s, micro, 0, 0)),
+            pl.BlockSpec((step_blocks, 1, tokens, slot), lambda s: (s, micro, 0, 0)),
+            pl.BlockSpec((1, 8, rows), lambda s: (micro, 0, s)),
         ],
-        out_specs=[pl.BlockSpec((blocks, tokens, width), lambda m, s: (0, 0, 0))] * micro_count,
-        out_shape=[jax.ShapeDtypeStruct((blocks, tokens, width), jnp.bfloat16)] * micro_count,
+        out_specs=_fixed(blocks, tokens, width),
+        out_shape=jax.ShapeDtypeStruct((blocks, tokens, width), jnp.bfloat16),
         scratch_shapes=[pltpu.VMEM((blocks * tokens, slot), jnp.float32)] * 2
         + [pltpu.VMEM((blocks, slot, tokens), jnp.bfloat16)],
         compiler_params=_params(60),
-        cost_estimate=_cost(3),
+        cost_estimate=_cost(cost),
         name="attend_back",
     )(lengths, received, grads, attended, logs)
 
@@ -771,7 +763,7 @@
     )(received, patches, mixed_grad, gain, w_query, w_key, w_value, *([before] if before is not None else []))
 
 
-def grad_heads_call(place, units, places, made, gain, bias, sums, w_query, w_key, w_value, shares):
+def grad_heads_call(place, units, cuts, places, made, gain, bias, sums, w_query, w_key, w_value, shares):
     micro_count = len(made)
     blocks, tokens, width = made[0].shape
     slot = width // 3
@@ -781,18 +773,23 @@
     kept = blocks * (shares // 2) * group
 
     def kernel(place_ref, *refs):
-        unit_refs, refs = refs[: 2 * micro_count], refs[2 * micro_count :]
+        unit_refs, refs = refs[: len(units)], refs[len(units) :]
         made_refs, refs = refs[:micro_count], refs[micro_count:]
         gain_ref, bias_ref, sums_ref, wq_ref, wk_ref, wv_ref, send_ref, keep_ref, spread, ordered = refs
         product = jnp.zeros((features, width), jnp.float32)
         column_sum = jnp.zeros((1, width), jnp.float32)
-        for micro, made_ref in enumerate(made_refs):
-            for at, relative in enumerate(places[micro]):
-                ordered[at * tokens : (at + 1) * tokens, :] = made_ref[place_ref[0] ^ relative]
-            half = blocks * tokens // 2
+        for cut, (first, last) in enumerate(cuts):
+            at = 0
+            for relative in places:
+                for micro, made_ref in enumerate(made_refs):
+                    low, high = max(first - micro * tokens, 0), min(last - micro * tokens, tokens)
+                    if low < high:
+                        ordered[at : at + high - low, :] = made_ref[place_ref[0] ^ relative, low:high]
+                        at += high - low
+            half = at // 2
             for side in range(2):
                 rows = ordered[side * half : (side + 1) * half, :]
-                product = product + contract_rows(unit_refs[2 * micro + side][...], rows)
+                product = product + contract_rows(unit_refs[2 * cut + side][...], rows)
                 column_sum = column_sum + jnp.sum(rows.astype(jnp.float32), axis=0, keepdims=True)
         vectors = jnp.concatenate(
             [gain_ref[...], bias_ref[...], sums_ref[...], jnp.zeros((124, features), jnp.float32)], axis=0
@@ -828,7 +825,7 @@
             out_specs=[fixed(*out), fixed(*out)],
             scratch_shapes=[
                 pltpu.VMEM((blocks, shares, group, full), jnp.float32),
-                pltpu.VMEM((blocks * tokens, width), jnp.bfloat16),
+                pltpu.VMEM((blocks * max(last - first for first, last in cuts), width), jnp.bfloat16),
             ],
         ),
         out_shape=[jax.ShapeDtypeStruct(out, jnp.bfloat16), jax.ShapeDtypeStruct(out, jnp.float32)],
@@ -932,12 +929,11 @@
     half = blocks // 2
     pair = min(2, half)
     half_steps = half // pair
-    sub = min(2, shares)
 
     def kernel(place_ref, *refs):
         groups, refs = [refs[at * shares : (at + 1) * shares] for at in range(3)], refs[3 * shares :]
         up_refs, down_refs, refs = refs[:pair], refs[pair : 2 * pair], refs[2 * pair :]
-        down_send, down_keep, up_send, up_keep, norm_all, norm_turned, grad_all, active_all, upper_all, up_all = refs
+        down_send, down_keep, up_send, up_keep, norm_turned, grad_all, active_all, upper_all, up_all = refs
         step = pl.program_id(0)
         mine = _mesh_bit(place_ref, up_steps[0])
 
@@ -952,7 +948,6 @@
         def _():
             for at in range(shares):
                 rows = slice(at * row_count, (at + 1) * row_count)
-                norm_all[rows, :] = groups[0][at][0]
                 norm_turned[:, rows] = groups[0][at][0].T
                 grad_all[rows, :] = groups[1][at][...]
 
@@ -960,10 +955,10 @@
         def _():
             up_columns = jnp.concatenate([ref[...] for ref in up_refs], axis=1)
             down_rows = jnp.concatenate([ref[...] for ref in down_refs], axis=0)
-            for at in range(0, all_rows, all_rows // sub):
-                rows = slice(at, at + all_rows // sub)
+            for at in range(shares):
+                rows = slice(at * row_count, (at + 1) * row_count)
                 active_all[rows, :], upper_all[rows, :] = _hidden_parts(
-                    norm_all[rows, :], grad_all[rows, :], up_columns, down_rows
+                    groups[0][at][0], groups[1][at][...], up_columns, down_rows
                 )
             down_made = contract_rows(active_all[...], grad_all[...])
 
@@ -1021,7 +1016,6 @@
                 up_out,
             ],
             scratch_shapes=[
-                pltpu.VMEM((all_rows, features), jnp.bfloat16),
                 pltpu.VMEM((features, all_rows), jnp.bfloat16),
                 pltpu.VMEM((all_rows, features), jnp.bfloat16),
                 pltpu.VMEM((all_rows, pair * owned), jnp.bfloat16),
@@ -1030,7 +1024,7 @@
             ],
         ),
         out_shape=[jax.ShapeDtypeStruct(shape, dtype) for shape in shapes for dtype in (jnp.bfloat16, jnp.float32)],
-        compiler_params=_params(60),
+        compiler_params=_params(52),
         cost_estimate=_cost(20),
         name="grad_middle",
     )(place, *boths, *out_grads, *lows, *([w_up] * pair), *([w_down] * pair))
@@ -1178,17 +1172,20 @@
         over = to_share(values, 2)
         return [values, to_share(values, 1), over, to_share(over, 1)]
 
+    first_rows = max(16, tokens * 3 // 4 // 16 * 16)
+    cuts = [(0, first_rows), (first_rows, row_count)]
     send, units_first, units_last = project_call(
-        rows, gain_one, bias_one, w_query, w_key, w_value, blocks, tokens
+        rows, gain_one, bias_one, w_query, w_key, w_value, blocks, cuts
     )
     received = by_micro(swap(send))
     dout_parts = [out_grad[micro] for micro in range(micro_count)]
     dout_over = [to_share(part, 2) for part in dout_parts]
     received, dout_over[0] = tie((received, dout_over[0]))
     units_first, received = tie((units_first, received))
-    units_first = grown(units_first, blk_bits[-1])
+    first_over = _paired(units_first, "blk", blk_bits[-1])
     own_attended, exact, logs = attend_call(received, seg_lengths, head_dim)
-    attended, units_first, dout_over = tie((own_attended.reshape(blocks, row_count, slot), units_first, dout_over))
+    attended, first_over, dout_over = tie((own_attended.reshape(blocks, row_count, slot), first_over, dout_over))
+    units_first = jnp.concatenate([units_first, first_over], axis=0)
     dout_over = jnp.concatenate(dout_over, axis=0)
     attended, units_first, units_last, *douts = tie(
         (swap(attended), units_first, units_last, dout, to_share(dout, 1), dout_over, to_share(dout_over, 1))
@@ -1218,9 +1215,13 @@
     down_theirs, down_keep = (value.reshape(-1, owned, features) for value in (down_theirs, down_keep))
     up_theirs, up_keep = (value.reshape(-1, block_rows, value.shape[-1]) for value in (up_theirs, up_keep))
     down_received, up_received = _paired(down_theirs, *down_steps[0]), _paired(up_theirs, *up_steps[0])
-    grads, down_keep, units_last = tie((grads, down_keep, units_last))
+    grads, down_keep, units_first_peer, units_last = tie((grads, down_keep, units_first_peer, units_last))
     units_last_peer = _paired(units_last, "blk", blk_bits[0])
-    made = attend_back_call(received, grads, exact, logs, seg_lengths, head_dim)
+    made = []
+    for micro in range(micro_count):
+        cost = 3 if micro == micro_count - 1 else 0
+        made.append(attend_back_call(received, grads, exact, logs, seg_lengths, micro, cost, head_dim))
+        grads, made[micro] = tie((grads, made[micro]))
     returned = [swap(made[0])]
 
     def then(done, *values):
@@ -1228,15 +1229,14 @@
 
     returned += [swap(tie((values, returned[0]))[0]) for values in made[1:]]
     made = tie(made)
-    up_keep, up_received, units_first_peer = then(made[0], up_keep, up_received, units_first_peer)
-    up_theirs, up_keep = halve_call(place, up_keep, up_received, up_steps[1], 0)
+    up_theirs, up_keep = halve_call(place, *then(made[-1], up_keep, up_received), up_steps[1], 0)
     up_received = _paired(up_theirs, *up_steps[1])
     down_keep, down_received, units_last_peer = then(up_keep, down_keep, down_received, units_last_peer)
     down_theirs, down_keep = halve_call(place, down_keep, down_received, down_steps[1], 5)
     down_received = _paired(down_theirs, *down_steps[1])
     made = then(down_keep, *made)
     heads_send, heads_keep = grad_heads_call(
-        place, (units_first, units_first_peer, units_last, units_last_peer), (places, places),
+        place, (units_first, units_first_peer, units_last, units_last_peer), cuts, places,
         made, gain_one, bias_one, sums_two, w_query, w_key, w_value, shares,
     )
     pair = (shares // 2, -1, heads_keep.shape[-1])

time: 246 us -> 242 us (0.984)
  waiting for transfers between devices: 76.9 us -> 67.1 us
  starting transfers between devices: 56.9 us -> 61.6 us
    all_to_all x6, waiting for transfers between devices: 30.2 us -> 22.6 us  [swap(): lax.all_to_all(values, 'blk', split_axis=0, concat_axis=0, tiled=True)]
    all_to_all x6, starting transfers between devices: 28.7 us -> 34.2 us  [swap(): lax.all_to_all(values, 'blk', split_axis=0, concat_axis=0, tiled=True)]
    pallas_call x1 -> x2, Pallas kernels: 15.4 us -> 17.2 us  [attend_back_call(): pl.pallas_call(kernel, grid=(steps,), in_specs=[pl.BlockSpec(memory_space...]
    unnamed x67 -> x61, local copies, waits for them, and re-layouts: 6.68 us -> 7.51 us
  transfers between devices with their start and end apart: 33 -> 33, of which waited for: 14 -> 10; matrix products, arithmetic and copies ran while one was open for 3% -> 3% of each run, Pallas kernels for 37% -> 37%
where the time goes in v6:
time: 242 us; the launch traced here: 241 us
  Pallas kernels  97.5 us (40%)
  waiting for transfers between devices  67.1 us (28%)
  starting transfers between devices  61.6 us (25%)
  local copies, waits for them, and re-layouts  8.52 us (4%)
  other arithmetic  5.73 us (2%)
    ppermute x25, waiting for transfers between devices, _paired(): return lax.ppermute(values, axis, [(i, i ^ bit) for i in range(count)])  44.5 us
    all_to_all x6, starting transfers between devices, swap(): lax.all_to_all(values, 'blk', split_axis=0, concat_axis=0, tiled=True)  34.2 us
    ppermute x25, starting transfers between devices, _paired(): return lax.ppermute(values, axis, [(i, i ^ bit) for i in range(count)])  26.2 us
    all_to_all x6, waiting for transfers between devices, swap(): lax.all_to_all(values, 'blk', split_axis=0, concat_axis=0, tiled=True)  22.6 us
    pallas_call x1, Pallas kernels, grad_middle_call(): pl.pallas_call(kernel, grid_spec=pltpu.PrefetchScalarGridSpec(num_scalar_...  19.4 us
    pallas_call x2, Pallas kernels, attend_back_call(): pl.pallas_call(kernel, grid=(steps,), in_specs=[pl.BlockSpec(memory_space...  17.2 us
    pallas_call x1, Pallas kernels, middle_call(): pl.pallas_call(kernel, grid_spec=pltpu.PrefetchScalarGridSpec(num_scalar_...  15.2 us
    pallas_call x2, Pallas kernels, finish_call(): pl.pallas_call(kernel, grid=(steps,), in_specs=[pl.BlockSpec((per_step, r...  11.9 us
  transfers between devices with their start and end apart: 33, of which 10 were waited for; matrix products, arithmetic and copies ran while one was open for 3% of the time, Pallas kernels for 37%

profile of v6, /device:TPU:0, one launch (start us, length us, event | category | flops | bytes accessed | tf_op | source)
XLA Modules:
  0.0 241.4 jit_solution(18094507507774516336)
XLA Ops:
  0.6 5.7 %project.1 = (bf16[8,256,384]{2,1,0:T(8,128)(2,1)}, bf16[96,1024]{1,0:T(8,128)(2,1)}, bf16[160,1024]{1,0:T(8,128)(2,1)}) custom-call(bf16[256,1024]{1,0:T(8,128)(2,1)} %bitcast.43, f32[1,1024]{1,0:T(1,128)} %bitcast.57, f32[1,1024]{1,0:T(1,128)} %bitcast.63, bf16[1024,1024]{1,0:T(8,128)(2,1)} %wq_ref.5, bf16[1024,1024]{1,0:T(8,128)(2,1)} %wk_ref.5, ...), custom_call_target="tpu_custom_call" | custom-call | flops 6000000000 | bytes 1 | tf_op jit(solution)/shard_map/project/pallas_call | solution.py:381
  6.3 7.4 %all-to-all-start = ((bf16[8,256,384]{2,1,0:T(8,128)(2,1)}), bf16[8,256,384]{2,1,0:T(8,128)(2,1)S(1)}, u32[]{:S(2)}, u32[]{:S(2)}) async-start(bf16[8,256,384]{2,1,0:T(8,128)(2,1)} %get-tuple-element.125), calls=%async_computation | async-start | bytes 3145728 | tf_op jit(solution)/shard_map/all_to_all | solution.py:1148
  15.9 21.3 %collective-permute-done = bf16[128,1024]{1,0:T(8,128)(2,1)S(1)} collective-permute-done((bf16[128,1024]{1,0:T(8,128)(2,1)S(1)}, bf16[128,1024]{1,0:T(8,128)(2,1)S(1)}, u32[]{:S(2)}, u32[]{:S(2)}) %collective-permute-start) | collective-permute-done | bytes 262176 | tf_op jit(solution)/shard_map/ppermute | solution.py:890
  37.2 13.5 %all-to-all-done = bf16[8,256,384]{2,1,0:T(8,128)(2,1)S(1)} async-done(((bf16[8,256,384]{2,1,0:T(8,128)(2,1)}), bf16[8,256,384]{2,1,0:T(8,128)(2,1)S(1)}, u32[]{:S(2)}, u32[]{:S(2)}) %all-to-all-start) | async-done | bytes 1572896 | tf_op jit(solution)/shard_map/all_to_all | solution.py:1148
  50.7 9.5 %attend.1 = (bf16[8,2,128,128]{3,2,1,0:T(8,128)(2,1)}, f32[8,2,128,128]{3,2,1,0:T(8,128)S(1)}, f32[2,8,1024]{2,1,0:T(8,128)S(1)}) custom-call(s32[2,8]{1,0:T(2,128)S(1)} %copy-done.10, bf16[8,2,128,384]{3,2,1,0:T(8,128)(2,1)S(1)} %bitcast.36), custom_call_target="tpu_custom_call" | custom-call | flops 11000000512 | bytes 1 | tf_op jit(solution)/shard_map/attend/pallas_call | solution.py:468
  62.0 5.2 %all-to-all-start.1 = ((bf16[8,256,128]{2,1,0:T(8,128)(2,1)}), bf16[8,256,128]{2,1,0:T(8,128)(2,1)S(1)}, u32[]{:S(2)}, u32[]{:S(2)}) async-start(bf16[8,256,128]{2,1,0:T(8,128)(2,1)} %bitcast.8), calls=%async_computation.1 | async-start | bytes 1048576 | tf_op jit(solution)/shard_map/all_to_all | solution.py:1148
  71.6 9.1 %all-to-all-done.1.att_ref = bf16[8,256,128]{2,1,0:T(8,128)(2,1)S(1)} async-done(((bf16[8,256,128]{2,1,0:T(8,128)(2,1)}), bf16[8,256,128]{2,1,0:T(8,128)(2,1)S(1)}, u32[]{:S(2)}, u32[]{:S(2)}) %all-to-all-start.1) | async-done | bytes 524320 | tf_op jit(solution)/shard_map/all_to_all | solution.py:1148
  87.1 15.2 %middle.1 = (bf16[256,1024]{1,0:T(8,128)(2,1)}, f32[256,1024]{1,0:T(8,128)S(1)}, bf16[8,256,128]{2,1,0:T(8,128)(2,1)}, f32[2,1024]{1,0:T(2,128)S(1)}, bf16[256,2...) custom-call(s32[3]{0:T(128)S(1)} %pad_add_fusion.place_ref, ...), custom_call_target="tpu_custom_call" | custom-call | flops 20000000000 | bytes 1 | tf_op jit(solution)/shard_map/middle/pallas_call | solution.py:669
  105.2 4.0 %collective-permute-done.8.refs_2_ = bf16[2,256,1024]{2,1,0:T(8,128)(2,1)} collective-permute-done((bf16[2,256,1024]{2,1,0:T(8,128)(2,1)S(1)}, bf16[2,256,1024]{2,1,0:T(8,128)(2,1)}, u32[]{:S(2)}, u32[]{:S(2)}) %collective-permute-start.8) | collective-permute-done | bytes 1048608 | tf_op jit(solution)/shard_map/ppermute | solution.py:890
  111.1 4.3 %all-to-all-start.2 = ((bf16[8,256,128]{2,1,0:T(8,128)(2,1)}), bf16[8,256,128]{2,1,0:T(8,128)(2,1)}, u32[]{:S(2)}, u32[]{:S(2)}) async-start(bf16[8,256,128]{2,1,0:T(8,128)(2,1)} %get-tuple-element.147), calls=%async_computation.2 | async-start | bytes 1048576 | tf_op jit(solution)/shard_map/all_to_all | solution.py:1148
  118.7 19.4 %grad_middle.1 = (bf16[512,1024]{1,0:T(8,128)(2,1)}, f32[512,1024]{1,0:T(8,128)}, bf16[512,1280]{1,0:T(8,128)(2,1)}, f32[512,1280]{1,0:T(8,128)}) custom-call(s32[3]{0:T(128)S(1)} %pad_add_fusion.place_ref, bf16[2,256,1024]{2,1,0:T(8,128)(2,1)} %copy-done.15, bf16[2,256,1024]{2,1,0:T(8,128)(2,1)} %copy-done.28, ...), custom_call_target="tpu_custom_call" | custom-call | flops 20000000000 | bytes 1 | tf_op jit(solution)/shard_map/grad_middle/pallas_call | solution.py:1002
  138.7 2.8 %collective-permute-done.14 = bf16[320,1024]{1,0:T(8,128)(2,1)S(1)} collective-permute-done((bf16[320,1024]{1,0:T(8,128)(2,1)}, bf16[320,1024]{1,0:T(8,128)(2,1)S(1)}, u32[]{:S(2)}, u32[]{:S(2)}) %collective-permute-start.14) | collective-permute-done | bytes 655392 | tf_op jit(solution)/shard_map/ppermute | solution.py:890
  145.6 10.1 %attend_back.2.refs_4_ = bf16[8,128,384]{2,1,0:T(8,128)(2,1)} custom-call(s32[2,8]{1,0:T(2,128)} %lengths_ref.5, bf16[8,2,128,384]{3,2,1,0:T(8,128)(2,1)} %bitcast.37, bf16[8,2,128,128]{3,2,1,0:T(8,128)(2,1)} %bitcast.14.grads_ref, f32[8,2,128,128]{3,2,1,0:T(8,128)} %copy-done.3, f32[2,8,1024]{2,1,0:T(8,128)} %copy-done.7), custom_call_target="tpu_custom_call" | custom-call | flops 1 | bytes 1 | tf_op jit(solution)/shard_map/attend_back/pallas_call | solution.py:564
  155.7 4.4 %all-to-all-start.3 = ((bf16[8,128,384]{2,1,0:T(8,128)(2,1)}), bf16[8,128,384]{2,1,0:T(8,128)(2,1)}, u32[]{:S(2)}, u32[]{:S(2)}) async-start(bf16[8,128,384]{2,1,0:T(8,128)(2,1)} %attend_back.2.refs_4_), calls=%async_computation.3 | async-start | bytes 1572864 | tf_op jit(solution)/shard_map/all_to_all | solution.py:1148
  160.2 7.0 %attend_back.3.refs_5_ = bf16[8,128,384]{2,1,0:T(8,128)(2,1)} custom-call(s32[2,8]{1,0:T(2,128)} %lengths_ref.5, bf16[8,2,128,384]{3,2,1,0:T(8,128)(2,1)} %bitcast.38, bf16[8,2,128,128]{3,2,1,0:T(8,128)(2,1)} %bitcast.14.grads_ref, f32[8,2,128,128]{3,2,1,0:T(8,128)} %copy-done.3, f32[2,8,1024]{2,1,0:T(8,128)} %copy-done.7), custom_call_target="tpu_custom_call" | custom-call | flops 3000000000 | bytes 1 | tf_op jit(solution)/shard_map/attend_back/pallas_call | solution.py:564
  167.2 9.2 %collective-permute-done.15.got_theirs.got_mine = bf16[4,128,1280]{2,1,0:T(8,128)(2,1)S(1)} collective-permute-done((bf16[4,128,1280]{2,1,0:T(8,128)(2,1)}, bf16[4,128,1280]{2,1,0:T(8,128)(2,1)S(1)}, u32[]{:S(2)}, u32[]{:S(2)}) %collective-permute-start.15) | collective-permute-done | bytes 1310752 | tf_op jit(solution)/shard_map/ppermute | solution.py:890
  185.0 5.0 %all-to-all-start.4 = ((bf16[8,128,384]{2,1,0:T(8,128)(2,1)}), bf16[8,128,384]{2,1,0:T(8,128)(2,1)}, u32[]{:S(2)}, u32[]{:S(2)}) async-start(bf16[8,128,384]{2,1,0:T(8,128)(2,1)} %attend_back.3.refs_5_), calls=%async_computation.4 | async-start | bytes 1572864 | tf_op jit(solution)/shard_map/all_to_all | solution.py:1148
  190.1 8.5 %grad_heads.1 = (bf16[2,8,32,512]{3,2,1,0:T(8,128)(2,1)}, f32[2,8,32,512]{3,2,1,0:T(8,128)}) custom-call(s32[3]{0:T(128)} %copy-done.8, bf16[384,1024]{1,0:T(8,128)(2,1)} %pad_maximum_fusion.1.refs_0_, bf16[384,1024]{1,0:T(8,128)(2,1)} %collective-permute-done.13.refs_1_, bf16[640,1024]{1,0:T(8,128)(2,1)} %pad_maximum_fusion.refs_2_, ...), custom_call_target="tpu_custom_call" | custom-call | flops 20000000000 | bytes 1 | tf_op jit(solution)/shard_map/grad_heads/pallas_call | solution.py:818
  198.6 3.1 %collective-permute-done.18.got_theirs.got_mine = bf16[2,128,1024]{2,1,0:T(8,128)(2,1)S(1)} collective-permute-done((bf16[2,128,1024]{2,1,0:T(8,128)(2,1)S(1)}, bf16[2,128,1024]{2,1,0:T(8,128)(2,1)S(1)}, u32[]{:S(2)}, u32[]{:S(2)}) %collective-permute-start.18) | collective-permute-done | bytes 524320 | tf_op jit(solution)/shard_map/ppermute | solution.py:890
  206.4 4.7 %collective-permute-start.22 = (bf16[1,128,1280]{2,1,0:T(8,128)(2,1)S(1)}, bf16[1,128,1280]{2,1,0:T(8,128)(2,1)S(1)}, u32[]{:S(2)}, u32[]{:S(2)}) collective-permute-start(bf16[1,128,1280]{2,1,0:T(8,128)(2,1)S(1)} %get-tuple-element.210), channel_id=1, source_target_pairs={{0,16},{4,20},{8,24},{12,28},{16,0},{20,4},{24,8},{28,12},{1,17},{... | collective-permute-start | bytes 983048 | tf_op jit(solution)/shard_map/ppermute | solution.py:890
  211.3 6.0 %finish.2.refs_0_ = bf16[2,128,1024]{2,1,0:T(8,128)(2,1)} custom-call(bf16[8,128,384]{2,1,0:T(8,128)(2,1)} %all-to-all-done.3.data_ref, bf16[2,128,1024]{2,1,0:T(8,128)(2,1)} %rows_ref.3, f32[256,1024]{1,0:T(8,128)} %copy-done.4, f32[1,1024]{1,0:T(1,128)} %bitcast.59, bf16[1024,1024]{1,0:T(8,128)(2,1)} %wq_ref.5, bf16[1024,1024]{1,0:T(8,128)(2,1)} %wk_ref.5, ...), custom_call_target="tpu_custom_call" | custom-call | flops 1 | bytes 1 | tf_op jit(solution)/shard_map/finish/pallas_call | solution.py:740
  218.0 7.9 %all-to-all-start.5 = ((bf16[8,32,512]{2,1,0:T(8,128)(2,1)}), bf16[8,32,512]{2,1,0:T(8,128)(2,1)S(1)}, u32[]{:S(2)}, u32[]{:S(2)}) async-start(bf16[8,32,512]{2,1,0:T(8,128)(2,1)} %bitcast.23), calls=%async_computation.5 | async-start | bytes 524288 | tf_op jit(solution)/shard_map/all_to_all | solution.py:1148
  225.9 3.8 %collective-permute-done.22 = bf16[1,128,1280]{2,1,0:T(8,128)(2,1)S(1)} collective-permute-done((bf16[1,128,1280]{2,1,0:T(8,128)(2,1)S(1)}, bf16[1,128,1280]{2,1,0:T(8,128)(2,1)S(1)}, u32[]{:S(2)}, u32[]{:S(2)}) %collective-permute-start.22) | collective-permute-done | bytes 327712 | tf_op jit(solution)/shard_map/ppermute | solution.py:890
  232.3 6.0 %finish.3 = bf16[2,128,1024]{2,1,0:T(8,128)(2,1)} custom-call(bf16[8,128,384]{2,1,0:T(8,128)(2,1)} %all-to-all-done.4.data_ref, bf16[2,128,1024]{2,1,0:T(8,128)(2,1)} %rows_ref.3, f32[256,1024]{1,0:T(8,128)} %copy-done.4, f32[1,1024]{1,0:T(1,128)} %bitcast.60, bf16[1024,1024]{1,0:T(8,128)(2,1)} %wq_ref.5, ...), custom_call_target="tpu_custom_call", output_to_operand_aliasing={{}: (7, {})} | custom-call | flops 20000000000 | bytes 1 | tf_op jit(solution)/shard_map/finish/pallas_call | solution.py:740
  (130 shorter events, 47.4 us)
Async XLA Ops:
  6.3 44.4 %all-to-all-start = ((bf16[8,256,384]{2,1,0:T(8,128)(2,1)}), bf16[8,256,384]{2,1,0:T(8,128)(2,1)S(1)}, u32[]{:S(2)}, u32[]{:S(2)}) async-start(bf16[8,256,384]{2,1,0:T(8,128)(2,1)} %get-tuple-element.125), calls=%async_computation | async-start | bytes 3145728 | tf_op jit(solution)/shard_map/all_to_all | solution.py:1148
  13.8 23.5 %collective-permute-start = (bf16[128,1024]{1,0:T(8,128)(2,1)S(1)}, bf16[128,1024]{1,0:T(8,128)(2,1)S(1)}, u32[]{:S(2)}, u32[]{:S(2)}) collective-permute-start(bf16[128,1024]{1,0:T(8,128)(2,1)S(1)} %get-tuple-element.237), channel_id=1, source_target_pairs={{0,4},{4,0},{8,12},{12,8},{16,20},{20,16},{24,28},{28,24},{1,5},{5... | collective-permute-start | bytes 786440 | tf_op jit(solution)/shard_map/ppermute | solution.py:890
  15.8 46.1 %collective-permute-start.2 = (bf16[128,1024]{1,0:T(8,128)(2,1)S(1)}, bf16[128,1024]{1,0:T(8,128)(2,1)S(1)}, u32[]{:S(2)}, u32[]{:S(2)}) collective-permute-start(bf16[128,1024]{1,0:T(8,128)(2,1)S(1)} %get-tuple-element.236), channel_id=1, source_target_pairs={{0,4},{4,0},{8,12},{12,8},{16,20},{20,16},{24,28},{28,24},{1,5},{5... | collective-permute-start | bytes 786440 | tf_op jit(solution)/shard_map/ppermute | solution.py:890
  50.7 11.2 %collective-permute-start.1 = (bf16[96,1024]{1,0:T(8,128)(2,1)}, bf16[96,1024]{1,0:T(8,128)(2,1)}, u32[]{:S(2)}, u32[]{:S(2)}) collective-permute-start(bf16[96,1024]{1,0:T(8,128)(2,1)} %get-tuple-element.129), channel_id=1, source_target_pairs={{0,16},{4,20},{8,24},{12,28},{16,0},{20,4},{24,8},{28,12},{1,17},{... | collective-permute-start | bytes 589832 | tf_op jit(solution)/shard_map/ppermute | solution.py:890
  62.0 18.7 %all-to-all-start.1 = ((bf16[8,256,128]{2,1,0:T(8,128)(2,1)}), bf16[8,256,128]{2,1,0:T(8,128)(2,1)S(1)}, u32[]{:S(2)}, u32[]{:S(2)}) async-start(bf16[8,256,128]{2,1,0:T(8,128)(2,1)} %bitcast.8), calls=%async_computation.1 | async-start | bytes 1048576 | tf_op jit(solution)/shard_map/all_to_all | solution.py:1148
  83.4 21.8 %collective-permute-start.7 = (bf16[2,256,1024]{2,1,0:T(8,128)(2,1)S(1)}, bf16[2,256,1024]{2,1,0:T(8,128)(2,1)S(1)}, u32[]{:S(2)}, u32[]{:S(2)}) collective-permute-start(bf16[2,256,1024]{2,1,0:T(8,128)(2,1)S(1)} %get-tuple-element.137.norm_ref.refs_0_), channel_id=1, source_target_pairs={{0,1},{1,0},{2,3},{3,2},{4,5},{5,4},{6,7},{7,6},{8,9},{9,8},{10,11... | collective-permute-start | bytes 3145736 | tf_op jit(solution)/shard_map/ppermute | solution.py:890
  83.5 25.7 %collective-permute-start.8 = (bf16[2,256,1024]{2,1,0:T(8,128)(2,1)S(1)}, bf16[2,256,1024]{2,1,0:T(8,128)(2,1)}, u32[]{:S(2)}, u32[]{:S(2)}) collective-permute-start(bf16[2,256,1024]{2,1,0:T(8,128)(2,1)S(1)} %get-tuple-element.137.norm_ref.refs_0_), channel_id=1, source_target_pairs={{0,4},{4,0},{8,12},{12,8},{16,20},{20,16},{24,28},{28,24},{1,5},{5... | collective-permute-start | bytes 3145736 | tf_op jit(solution)/shard_map/ppermute | solution.py:890
  85.0 19.2 %collective-permute-start.5 = (bf16[192,1024]{1,0:T(8,128)(2,1)S(1)}, bf16[192,1024]{1,0:T(8,128)(2,1)S(1)}, u32[]{:S(2)}, u32[]{:S(2)}) collective-permute-start(bf16[192,1024]{1,0:T(8,128)(2,1)S(1)} %copy-done.23), channel_id=1, source_target_pairs={{0,8},{4,12},{8,0},{12,4},{16,24},{20,28},{24,16},{28,20},{1,9},{5... | collective-permute-start | bytes 1179656 | tf_op jit(solution)/shard_map/ppermute | solution.py:890
  85.0 18.3 %collective-permute-start.6 = (bf16[160,1024]{1,0:T(8,128)(2,1)S(1)}, bf16[160,1024]{1,0:T(8,128)(2,1)S(1)}, u32[]{:S(2)}, u32[]{:S(2)}) collective-permute-start(bf16[160,1024]{1,0:T(8,128)(2,1)S(1)} %copy-done.24), channel_id=1, source_target_pairs={{0,16},{4,20},{8,24},{12,28},{16,0},{20,4},{24,8},{28,12},{1,17},{... | collective-permute-start | bytes 983048 | tf_op jit(solution)/shard_map/ppermute | solution.py:890
  109.1 9.5 %collective-permute-start.9 = (bf16[2,256,1024]{2,1,0:T(8,128)(2,1)}, bf16[2,256,1024]{2,1,0:T(8,128)(2,1)}, u32[]{:S(2)}, u32[]{:S(2)}) collective-permute-start(bf16[2,256,1024]{2,1,0:T(8,128)(2,1)} %collective-permute-done.8.refs_2_), channel_id=1, source_target_pairs={{0,1},{1,0},{2,3},{3,2},{4,5},{5,4},{6,7},{7,6},{8,9},{9,8},{10,11... | collective-permute-start | bytes 3145736 | tf_op jit(solution)/shard_map/ppermute | solution.py:890
  109.7 9.0 %collective-permute-start.11 = (bf16[256,256]{1,0:T(8,128)(2,1)S(1)}, bf16[256,256]{1,0:T(8,128)(2,1)S(1)}, u32[]{:S(2)}, u32[]{:S(2)}) collective-permute-start(bf16[256,256]{1,0:T(8,128)(2,1)S(1)} %get-tuple-element.156), channel_id=1, source_target_pairs={{0,4},{4,0},{8,12},{12,8},{16,20},{20,16},{24,28},{28,24},{1,5},{5... | collective-permute-start | bytes 393224 | tf_op jit(solution)/shard_map/ppermute | solution.py:890
  111.1 31.5 %all-to-all-start.2 = ((bf16[8,256,128]{2,1,0:T(8,128)(2,1)}), bf16[8,256,128]{2,1,0:T(8,128)(2,1)}, u32[]{:S(2)}, u32[]{:S(2)}) async-start(bf16[8,256,128]{2,1,0:T(8,128)(2,1)} %get-tuple-element.147), calls=%async_computation.2 | async-start | bytes 1048576 | tf_op jit(solution)/shard_map/all_to_all | solution.py:1148
  115.5 27.1 %collective-permute-start.13 = (bf16[384,1024]{1,0:T(8,128)(2,1)}, bf16[384,1024]{1,0:T(8,128)(2,1)}, u32[]{:S(2)}, u32[]{:S(2)}) collective-permute-start(bf16[384,1024]{1,0:T(8,128)(2,1)} %pad_maximum_fusion.1.refs_0_), channel_id=1, source_target_pairs={{0,4},{4,0},{8,12},{12,8},{16,20},{20,16},{24,28},{28,24},{1,5},{5... | collective-permute-start | bytes 2359304 | tf_op jit(solution)/shard_map/ppermute | solution.py:890
  117.2 24.3 %collective-permute-start.14 = (bf16[320,1024]{1,0:T(8,128)(2,1)}, bf16[320,1024]{1,0:T(8,128)(2,1)S(1)}, u32[]{:S(2)}, u32[]{:S(2)}) collective-permute-start(bf16[320,1024]{1,0:T(8,128)(2,1)} %pad_maximum_fusion.2), channel_id=1, source_target_pairs={{0,8},{4,12},{8,0},{12,4},{16,24},{20,28},{24,16},{28,20},{1,9},{5... | collective-permute-start | bytes 1966088 | tf_op jit(solution)/shard_map/ppermute | solution.py:890
  138.1 38.3 %collective-permute-start.15 = (bf16[4,128,1280]{2,1,0:T(8,128)(2,1)}, bf16[4,128,1280]{2,1,0:T(8,128)(2,1)S(1)}, u32[]{:S(2)}, u32[]{:S(2)}) collective-permute-start(bf16[4,128,1280]{2,1,0:T(8,128)(2,1)} %bitcast.61), channel_id=1, source_target_pairs={{0,8},{4,12},{8,0},{12,4},{16,24},{20,28},{24,16},{28,20},{1,9},{5... | collective-permute-start | bytes 3932168 | tf_op jit(solution)/shard_map/ppermute | solution.py:890
  142.6 36.6 %collective-permute-start.17 = (bf16[640,1024]{1,0:T(8,128)(2,1)}, bf16[640,1024]{1,0:T(8,128)(2,1)}, u32[]{:S(2)}, u32[]{:S(2)}) collective-permute-start(bf16[640,1024]{1,0:T(8,128)(2,1)} %pad_maximum_fusion.refs_2_), channel_id=1, source_target_pairs={{0,4},{4,0},{8,12},{12,8},{16,20},{20,16},{24,28},{28,24},{1,5},{5... | collective-permute-start | bytes 3932168 | tf_op jit(solution)/shard_map/ppermute | solution.py:890
  144.0 35.0 %collective-permute-start.16 = (bf16[4,128,1024]{2,1,0:T(8,128)(2,1)}, bf16[4,128,1024]{2,1,0:T(8,128)(2,1)}, u32[]{:S(2)}, u32[]{:S(2)}) collective-permute-start(bf16[4,128,1024]{2,1,0:T(8,128)(2,1)} %bitcast.62), channel_id=1, source_target_pairs={{0,2},{1,3},{2,0},{3,1},{4,6},{5,7},{6,4},{7,5},{8,10},{9,11},{10,... | collective-permute-start | bytes 3145736 | tf_op jit(solution)/shard_map/ppermute | solution.py:890
  155.7 29.3 %all-to-all-start.3 = ((bf16[8,128,384]{2,1,0:T(8,128)(2,1)}), bf16[8,128,384]{2,1,0:T(8,128)(2,1)}, u32[]{:S(2)}, u32[]{:S(2)}) async-start(bf16[8,128,384]{2,1,0:T(8,128)(2,1)} %attend_back.2.refs_4_), calls=%async_computation.3 | async-start | bytes 1572864 | tf_op jit(solution)/shard_map/all_to_all | solution.py:1148
  181.1 20.5 %collective-permute-start.18 = (bf16[2,128,1024]{2,1,0:T(8,128)(2,1)S(1)}, bf16[2,128,1024]{2,1,0:T(8,128)(2,1)S(1)}, u32[]{:S(2)}, u32[]{:S(2)}) collective-permute-start(bf16[2,128,1024]{2,1,0:T(8,128)(2,1)S(1)} %get-tuple-element.187), channel_id=1, source_target_pairs={{0,8},{4,12},{8,0},{12,4},{16,24},{20,28},{24,16},{28,20},{1,9},{5... | collective-permute-start | bytes 1572872 | tf_op jit(solution)/shard_map/ppermute | solution.py:890
  183.5 18.8 %collective-permute-start.19 = (bf16[2,128,1280]{2,1,0:T(8,128)(2,1)}, bf16[2,128,1280]{2,1,0:T(8,128)(2,1)S(1)}, u32[]{:S(2)}, u32[]{:S(2)}) collective-permute-start(bf16[2,128,1280]{2,1,0:T(8,128)(2,1)} %get-tuple-element.191), channel_id=1, source_target_pairs={{0,2},{1,3},{2,0},{3,1},{4,6},{5,7},{6,4},{7,5},{8,10},{9,11},{10,... | collective-permute-start | bytes 1966088 | tf_op jit(solution)/shard_map/ppermute | solution.py:890
  185.0 32.2 %all-to-all-start.4 = ((bf16[8,128,384]{2,1,0:T(8,128)(2,1)}), bf16[8,128,384]{2,1,0:T(8,128)(2,1)}, u32[]{:S(2)}, u32[]{:S(2)}) async-start(bf16[8,128,384]{2,1,0:T(8,128)(2,1)} %attend_back.3.refs_5_), calls=%async_computation.4 | async-start | bytes 1572864 | tf_op jit(solution)/shard_map/all_to_all | solution.py:1148
  206.4 23.3 %collective-permute-start.22 = (bf16[1,128,1280]{2,1,0:T(8,128)(2,1)S(1)}, bf16[1,128,1280]{2,1,0:T(8,128)(2,1)S(1)}, u32[]{:S(2)}, u32[]{:S(2)}) collective-permute-start(bf16[1,128,1280]{2,1,0:T(8,128)(2,1)S(1)} %get-tuple-element.210), channel_id=1, source_target_pairs={{0,16},{4,20},{8,24},{12,28},{16,0},{20,4},{24,8},{28,12},{1,17},{... | collective-permute-start | bytes 983048 | tf_op jit(solution)/shard_map/ppermute | solution.py:890
  211.1 28.7 %collective-permute-start.26 = (bf16[1,128,1024]{2,1,0:T(8,128)(2,1)S(1)}, bf16[1,128,1024]{2,1,0:T(8,128)(2,1)S(1)}, u32[]{:S(2)}, u32[]{:S(2)}) collective-permute-start(bf16[1,128,1024]{2,1,0:T(8,128)(2,1)S(1)} %get-tuple-element.224), channel_id=1, source_target_pairs={{0,16},{4,20},{8,24},{12,28},{16,0},{20,4},{24,8},{28,12},{1,17},{... | collective-permute-start | bytes 786440 | tf_op jit(solution)/shard_map/ppermute | solution.py:890
  218.0 22.6 %all-to-all-start.5 = ((bf16[8,32,512]{2,1,0:T(8,128)(2,1)}), bf16[8,32,512]{2,1,0:T(8,128)(2,1)S(1)}, u32[]{:S(2)}, u32[]{:S(2)}) async-start(bf16[8,32,512]{2,1,0:T(8,128)(2,1)} %bitcast.23), calls=%async_computation.5 | async-start | bytes 524288 | tf_op jit(solution)/shard_map/all_to_all | solution.py:1148
  (39 other events, 444.3 us)

commit v7 on v6

--- a/solution.py
+++ b/solution.py
@@ -835,36 +835,49 @@
     )(place, *units, *made, gain, bias, sums, w_query, w_key, w_value)
 
 
-def assemble_call(place, parts, down_steps, blocks, owned):
+def assemble_call(place, parts, down_keep, down_received, heads, down_steps, blocks, owned):
     shares = len(parts)
     rows, width = parts[0].shape
     part = width - blocks * owned
+    slot = (heads.shape[2] - 128) // 3
 
     def kernel(place_ref, *refs):
-        part_refs, (up_ref, out_ref) = refs[:shares], refs[shares:]
+        part_refs, (keep_ref, got_ref, heads_ref, up_ref, out_ref, down_ref, *refs) = refs[:shares], refs[shares:]
+        weight_refs, norm_refs = refs[:3], refs[3:]
         for other, part_ref in enumerate(part_refs):
             share = place_ref[2] ^ other
             for at, block in enumerate(_ordered([_owner_stride(*step, shares) for step in down_steps])):
                 to = pl.multiple_of((block + share % 2 + share // 2 * shares) * owned, 128)
                 up_ref[:, pl.ds(to, owned)] = part_ref[:, at * owned : (at + 1) * owned].astype(jnp.float32)
             out_ref[:, pl.ds(pl.multiple_of(share * part, 128), part)] = part_ref[:, blocks * owned :].astype(jnp.float32)
-
+        down_ref[...] = keep_ref[...] + got_ref[...].astype(jnp.float32)
+        for at, ref in enumerate(weight_refs):
+            for block in range(blocks):
+                ref[:, block * slot : (block + 1) * slot] = heads_ref[
+                    block, :, at * slot : (at + 1) * slot
+                ].astype(jnp.float32)
+        sums = jnp.zeros((rows, 128), jnp.float32)
+        for block in range(blocks):
+            sums = sums + heads_ref[block, :, 3 * slot :].astype(jnp.float32)
+        turned = jnp.concatenate([sums, jnp.zeros((128 - rows, 128), jnp.float32)], axis=0).T
+        for at, ref in enumerate(norm_refs):
+            ref[...] = turned[at : at + 1, 0:rows]
+
+    shapes = [(rows, blocks * shares * owned), (rows, shares * part), down_keep.shape]
+    shapes += [(rows, blocks * slot)] * 3 + [(1, rows)] * 4
     return pl.pallas_call(
         kernel,
         grid_spec=pltpu.PrefetchScalarGridSpec(
             num_scalar_prefetch=1,
             grid=(1,),
-            in_specs=[_fixed(rows, width)] * shares,
-            out_specs=[_fixed(rows, blocks * shares * owned), _fixed(rows, shares * part)],
+            in_specs=[_fixed(*array.shape) for array in (*parts, down_keep, down_received, heads)],
+            out_specs=[_fixed(*shape) for shape in shapes],
         ),
-        out_shape=[
-            jax.ShapeDtypeStruct((rows, blocks * shares * owned), jnp.float32),
-            jax.ShapeDtypeStruct((rows, shares * part), jnp.float32),
-        ],
-        compiler_params=_params(8),
+        out_shape=[jax.ShapeDtypeStruct(shape, jnp.float32) for shape in shapes],
+        compiler_params=_params(16),
         cost_estimate=_cost(0),
         name="assemble",
-    )(place, *parts)
+    )(place, *parts, down_keep, down_received, heads)
 
 
 def _bits(count):
@@ -1101,33 +1114,6 @@
     )(place, keep, received)
 
 
-def assemble_heads_call(parts, slot):
-    blocks, rows, _ = parts.shape
-
-    def kernel(parts_ref, *refs):
-        weight_refs, norm_refs = refs[:3], refs[3:]
-        for part, ref in enumerate(weight_refs):
-            for block in range(blocks):
-                ref[:, block * slot : (block + 1) * slot] = parts_ref[
-                    block, :, part * slot : (part + 1) * slot
-                ].astype(jnp.float32)
-        sums = jnp.zeros((rows, 128), jnp.float32)
-        for block in range(blocks):
-            sums = sums + parts_ref[block, :, 3 * slot :].astype(jnp.float32)
-        turned = jnp.concatenate([sums, jnp.zeros((128 - rows, 128), jnp.float32)], axis=0).T
-        for at, ref in enumerate(norm_refs):
-            ref[...] = turned[at : at + 1, 0:rows]
-
-    return pl.pallas_call(
-        kernel,
-        out_shape=[jax.ShapeDtypeStruct((rows, blocks * slot), jnp.float32)] * 3
-        + [jax.ShapeDtypeStruct((1, rows), jnp.float32)] * 4,
-        compiler_params=_params(8),
-        cost_estimate=_cost(0),
-        name="assemble_heads",
-    )(parts)
-
-
 def fast_body(
     patches, seg_lengths, w_query, w_key, w_value, w_out, w_up, w_down,
     norm1_gain, norm1_bias, norm2_gain, norm2_bias, out_grad,
@@ -1270,10 +1256,12 @@
     last = then(parts[0], returned[-1])[0]
     parts = [parts[0]] + [to_share(parts[share], share) for share in range(1, shares)]
     patches_grad = finish_call(last, *finish, micro_count - 1, patches_grad, 20)
-    up_total, out_total = assemble_call(place, then(patches_grad, *parts), down_steps, blocks, owned)
-    down_keep, down_received = then(up_total, down_keep, down_received)
-    down_total = (down_keep + down_received.astype(jnp.float32))[0]
-    query_total, key_total, value_total, *sums = assemble_heads_call(then(down_total, heads_parts)[0], slot)
+    *parts, down_keep, down_received, heads_parts = then(
+        patches_grad, *parts, down_keep[0], down_received[0], heads_parts
+    )
+    up_total, out_total, down_total, query_total, key_total, value_total, *sums = assemble_call(
+        place, parts, down_keep, down_received, heads_parts, down_steps, blocks, owned
+    )
     return (
         layer_out.reshape(patches.shape),
         patches_grad.reshape(patches.shape),

time: 242 us -> 242 us (level)
  transfers between devices with their start and end apart: 33 -> 33, of which waited for: 10 -> 11; matrix products, arithmetic and copies ran while one was open for 3% -> 3% of each run, Pallas kernels for 37% -> 37%
where the time goes in v7:
time: 242 us; the launch traced here: 241 us
  Pallas kernels  97.1 us (40%)
  waiting for transfers between devices  67.2 us (28%)
  starting transfers between devices  61.5 us (25%)
  local copies, waits for them, and re-layouts  9.62 us (4%)
  other arithmetic  4.84 us (2%)
    ppermute x25, waiting for transfers between devices, _paired(): return lax.ppermute(values, axis, [(i, i ^ bit) for i in range(count)])  44.5 us
    all_to_all x6, starting transfers between devices, swap(): lax.all_to_all(values, 'blk', split_axis=0, concat_axis=0, tiled=True)  34.2 us
    ppermute x25, starting transfers between devices, _paired(): return lax.ppermute(values, axis, [(i, i ^ bit) for i in range(count)])  26.2 us
    all_to_all x6, waiting for transfers between devices, swap(): lax.all_to_all(values, 'blk', split_axis=0, concat_axis=0, tiled=True)  22.8 us
    pallas_call x1, Pallas kernels, grad_middle_call(): pl.pallas_call(kernel, grid_spec=pltpu.PrefetchScalarGridSpec(num_scalar_...  19.5 us
    pallas_call x2, Pallas kernels, attend_back_call(): pl.pallas_call(kernel, grid=(steps,), in_specs=[pl.BlockSpec(memory_space...  17.2 us
    pallas_call x1, Pallas kernels, middle_call(): pl.pallas_call(kernel, grid_spec=pltpu.PrefetchScalarGridSpec(num_scalar_...  15.2 us
    pallas_call x2, Pallas kernels, finish_call(): pl.pallas_call(kernel, grid=(steps,), in_specs=[pl.BlockSpec((per_step, r...  11.9 us
  transfers between devices with their start and end apart: 33, of which 11 were waited for; matrix products, arithmetic and copies ran while one was open for 3% of the time, Pallas kernels for 37%

profile of v7, /device:TPU:0, one launch (start us, length us, event | category | flops | bytes accessed | tf_op | source)
XLA Modules:
  0.0 241.2 jit_solution(4336787209875174025)
XLA Ops:
  0.6 5.7 %project.1 = (bf16[8,256,384]{2,1,0:T(8,128)(2,1)}, bf16[96,1024]{1,0:T(8,128)(2,1)}, bf16[160,1024]{1,0:T(8,128)(2,1)}) custom-call(bf16[256,1024]{1,0:T(8,128)(2,1)} %bitcast.43, f32[1,1024]{1,0:T(1,128)} %bitcast.59, f32[1,1024]{1,0:T(1,128)} %bitcast.65, bf16[1024,1024]{1,0:T(8,128)(2,1)} %wq_ref.5, bf16[1024,1024]{1,0:T(8,128)(2,1)} %wk_ref.5, ...), custom_call_target="tpu_custom_call" | custom-call | flops 6000000000 | bytes 1 | tf_op jit(solution)/shard_map/project/pallas_call | solution.py:381
  6.3 7.4 %all-to-all-start = ((bf16[8,256,384]{2,1,0:T(8,128)(2,1)}), bf16[8,256,384]{2,1,0:T(8,128)(2,1)S(1)}, u32[]{:S(2)}, u32[]{:S(2)}) async-start(bf16[8,256,384]{2,1,0:T(8,128)(2,1)} %get-tuple-element.126), calls=%async_computation | async-start | bytes 3145728 | tf_op jit(solution)/shard_map/all_to_all | solution.py:1134
  15.9 21.3 %collective-permute-done = bf16[128,1024]{1,0:T(8,128)(2,1)S(1)} collective-permute-done((bf16[128,1024]{1,0:T(8,128)(2,1)S(1)}, bf16[128,1024]{1,0:T(8,128)(2,1)S(1)}, u32[]{:S(2)}, u32[]{:S(2)}) %collective-permute-start) | collective-permute-done | bytes 262176 | tf_op jit(solution)/shard_map/ppermute | solution.py:903
  37.2 13.5 %all-to-all-done = bf16[8,256,384]{2,1,0:T(8,128)(2,1)S(1)} async-done(((bf16[8,256,384]{2,1,0:T(8,128)(2,1)}), bf16[8,256,384]{2,1,0:T(8,128)(2,1)S(1)}, u32[]{:S(2)}, u32[]{:S(2)}) %all-to-all-start) | async-done | bytes 1572896 | tf_op jit(solution)/shard_map/all_to_all | solution.py:1134
  50.7 9.5 %attend.1 = (bf16[8,2,128,128]{3,2,1,0:T(8,128)(2,1)}, f32[8,2,128,128]{3,2,1,0:T(8,128)S(1)}, f32[2,8,1024]{2,1,0:T(8,128)S(1)}) custom-call(s32[2,8]{1,0:T(2,128)S(1)} %copy-done.10, bf16[8,2,128,384]{3,2,1,0:T(8,128)(2,1)S(1)} %bitcast.36), custom_call_target="tpu_custom_call" | custom-call | flops 11000000512 | bytes 1 | tf_op jit(solution)/shard_map/attend/pallas_call | solution.py:468
  62.0 5.2 %all-to-all-start.1 = ((bf16[8,256,128]{2,1,0:T(8,128)(2,1)}), bf16[8,256,128]{2,1,0:T(8,128)(2,1)S(1)}, u32[]{:S(2)}, u32[]{:S(2)}) async-start(bf16[8,256,128]{2,1,0:T(8,128)(2,1)} %bitcast.8), calls=%async_computation.1 | async-start | bytes 1048576 | tf_op jit(solution)/shard_map/all_to_all | solution.py:1134
  71.6 9.1 %all-to-all-done.1.att_ref = bf16[8,256,128]{2,1,0:T(8,128)(2,1)S(1)} async-done(((bf16[8,256,128]{2,1,0:T(8,128)(2,1)}), bf16[8,256,128]{2,1,0:T(8,128)(2,1)S(1)}, u32[]{:S(2)}, u32[]{:S(2)}) %all-to-all-start.1) | async-done | bytes 524320 | tf_op jit(solution)/shard_map/all_to_all | solution.py:1134
  87.1 15.2 %middle.1 = (bf16[256,1024]{1,0:T(8,128)(2,1)}, f32[256,1024]{1,0:T(8,128)S(1)}, bf16[8,256,128]{2,1,0:T(8,128)(2,1)}, f32[2,1024]{1,0:T(2,128)S(1)}, bf16[256,2...) custom-call(s32[3]{0:T(128)S(1)} %pad_add_fusion.place_ref, ...), custom_call_target="tpu_custom_call" | custom-call | flops 20000000000 | bytes 1 | tf_op jit(solution)/shard_map/middle/pallas_call | solution.py:669
  105.2 4.0 %collective-permute-done.8.refs_2_ = bf16[2,256,1024]{2,1,0:T(8,128)(2,1)} collective-permute-done((bf16[2,256,1024]{2,1,0:T(8,128)(2,1)S(1)}, bf16[2,256,1024]{2,1,0:T(8,128)(2,1)}, u32[]{:S(2)}, u32[]{:S(2)}) %collective-permute-start.8) | collective-permute-done | bytes 1048608 | tf_op jit(solution)/shard_map/ppermute | solution.py:903
  111.1 4.3 %all-to-all-start.2 = ((bf16[8,256,128]{2,1,0:T(8,128)(2,1)}), bf16[8,256,128]{2,1,0:T(8,128)(2,1)}, u32[]{:S(2)}, u32[]{:S(2)}) async-start(bf16[8,256,128]{2,1,0:T(8,128)(2,1)} %get-tuple-element.148), calls=%async_computation.2 | async-start | bytes 1048576 | tf_op jit(solution)/shard_map/all_to_all | solution.py:1134
  118.7 19.5 %grad_middle.1 = (bf16[512,1024]{1,0:T(8,128)(2,1)}, f32[512,1024]{1,0:T(8,128)}, bf16[512,1280]{1,0:T(8,128)(2,1)}, f32[512,1280]{1,0:T(8,128)}) custom-call(s32[3]{0:T(128)S(1)} %pad_add_fusion.place_ref, bf16[2,256,1024]{2,1,0:T(8,128)(2,1)} %copy-done.15, bf16[2,256,1024]{2,1,0:T(8,128)(2,1)} %copy-done.28, ...), custom_call_target="tpu_custom_call" | custom-call | flops 20000000000 | bytes 1 | tf_op jit(solution)/shard_map/grad_middle/pallas_call | solution.py:1015
  138.8 2.6 %collective-permute-done.14 = bf16[320,1024]{1,0:T(8,128)(2,1)S(1)} collective-permute-done((bf16[320,1024]{1,0:T(8,128)(2,1)}, bf16[320,1024]{1,0:T(8,128)(2,1)S(1)}, u32[]{:S(2)}, u32[]{:S(2)}) %collective-permute-start.14) | collective-permute-done | bytes 655392 | tf_op jit(solution)/shard_map/ppermute | solution.py:903
  145.6 6.9 %attend_back.2.refs_4_ = bf16[8,128,384]{2,1,0:T(8,128)(2,1)} custom-call(s32[2,8]{1,0:T(2,128)} %lengths_ref.5, bf16[8,2,128,384]{3,2,1,0:T(8,128)(2,1)} %bitcast.37, bf16[8,2,128,128]{3,2,1,0:T(8,128)(2,1)} %bitcast.14.grads_ref, f32[8,2,128,128]{3,2,1,0:T(8,128)} %copy-done.3, f32[2,8,1024]{2,1,0:T(8,128)} %copy-done.7), custom_call_target="tpu_custom_call" | custom-call | flops 1 | bytes 1 | tf_op jit(solution)/shard_map/attend_back/pallas_call | solution.py:564
  152.4 4.4 %all-to-all-start.3 = ((bf16[8,128,384]{2,1,0:T(8,128)(2,1)}), bf16[8,128,384]{2,1,0:T(8,128)(2,1)}, u32[]{:S(2)}, u32[]{:S(2)}) async-start(bf16[8,128,384]{2,1,0:T(8,128)(2,1)} %attend_back.2.refs_4_), calls=%async_computation.3 | async-start | bytes 1572864 | tf_op jit(solution)/shard_map/all_to_all | solution.py:1134
  156.9 10.3 %attend_back.3.refs_5_ = bf16[8,128,384]{2,1,0:T(8,128)(2,1)} custom-call(s32[2,8]{1,0:T(2,128)} %lengths_ref.5, bf16[8,2,128,384]{3,2,1,0:T(8,128)(2,1)} %bitcast.38, bf16[8,2,128,128]{3,2,1,0:T(8,128)(2,1)} %bitcast.14.grads_ref, f32[8,2,128,128]{3,2,1,0:T(8,128)} %copy-done.3, f32[2,8,1024]{2,1,0:T(8,128)} %copy-done.7), custom_call_target="tpu_custom_call" | custom-call | flops 3000000000 | bytes 1 | tf_op jit(solution)/shard_map/attend_back/pallas_call | solution.py:564
  167.2 9.3 %collective-permute-done.15.got_theirs.got_mine = bf16[4,128,1280]{2,1,0:T(8,128)(2,1)S(1)} collective-permute-done((bf16[4,128,1280]{2,1,0:T(8,128)(2,1)}, bf16[4,128,1280]{2,1,0:T(8,128)(2,1)S(1)}, u32[]{:S(2)}, u32[]{:S(2)}) %collective-permute-start.15) | collective-permute-done | bytes 1310752 | tf_op jit(solution)/shard_map/ppermute | solution.py:903
  185.0 5.0 %all-to-all-start.4 = ((bf16[8,128,384]{2,1,0:T(8,128)(2,1)}), bf16[8,128,384]{2,1,0:T(8,128)(2,1)}, u32[]{:S(2)}, u32[]{:S(2)}) async-start(bf16[8,128,384]{2,1,0:T(8,128)(2,1)} %attend_back.3.refs_5_), calls=%async_computation.4 | async-start | bytes 1572864 | tf_op jit(solution)/shard_map/all_to_all | solution.py:1134
  190.1 8.5 %grad_heads.1 = (bf16[2,8,32,512]{3,2,1,0:T(8,128)(2,1)}, f32[2,8,32,512]{3,2,1,0:T(8,128)}) custom-call(s32[3]{0:T(128)} %copy-done.8, bf16[384,1024]{1,0:T(8,128)(2,1)} %pad_maximum_fusion.1.refs_0_, bf16[384,1024]{1,0:T(8,128)(2,1)} %collective-permute-done.13.refs_1_, bf16[640,1024]{1,0:T(8,128)(2,1)} %pad_maximum_fusion.refs_2_, ...), custom_call_target="tpu_custom_call" | custom-call | flops 20000000000 | bytes 1 | tf_op jit(solution)/shard_map/grad_heads/pallas_call | solution.py:818
  198.6 3.1 %collective-permute-done.18.got_theirs.got_mine = bf16[2,128,1024]{2,1,0:T(8,128)(2,1)S(1)} collective-permute-done((bf16[2,128,1024]{2,1,0:T(8,128)(2,1)S(1)}, bf16[2,128,1024]{2,1,0:T(8,128)(2,1)S(1)}, u32[]{:S(2)}, u32[]{:S(2)}) %collective-permute-start.18) | collective-permute-done | bytes 524320 | tf_op jit(solution)/shard_map/ppermute | solution.py:903
  206.4 4.6 %collective-permute-start.22 = (bf16[1,128,1280]{2,1,0:T(8,128)(2,1)S(1)}, bf16[1,128,1280]{2,1,0:T(8,128)(2,1)S(1)}, u32[]{:S(2)}, u32[]{:S(2)}) collective-permute-start(bf16[1,128,1280]{2,1,0:T(8,128)(2,1)S(1)} %get-tuple-element.211), channel_id=1, source_target_pairs={{0,16},{4,20},{8,24},{12,28},{16,0},{20,4},{24,8},{28,12},{1,17},{... | collective-permute-start | bytes 983048 | tf_op jit(solution)/shard_map/ppermute | solution.py:903
  211.3 6.0 %finish.2.refs_0_ = bf16[2,128,1024]{2,1,0:T(8,128)(2,1)} custom-call(bf16[8,128,384]{2,1,0:T(8,128)(2,1)} %all-to-all-done.3.data_ref, bf16[2,128,1024]{2,1,0:T(8,128)(2,1)} %rows_ref.3, f32[256,1024]{1,0:T(8,128)} %copy-done.4, f32[1,1024]{1,0:T(1,128)} %bitcast.61, bf16[1024,1024]{1,0:T(8,128)(2,1)} %wq_ref.5, bf16[1024,1024]{1,0:T(8,128)(2,1)} %wk_ref.5, ...), custom_call_target="tpu_custom_call" | custom-call | flops 1 | bytes 1 | tf_op jit(solution)/shard_map/finish/pallas_call | solution.py:740
  218.0 7.8 %all-to-all-start.5 = ((bf16[8,32,512]{2,1,0:T(8,128)(2,1)}), bf16[8,32,512]{2,1,0:T(8,128)(2,1)S(1)}, u32[]{:S(2)}, u32[]{:S(2)}) async-start(bf16[8,32,512]{2,1,0:T(8,128)(2,1)} %bitcast.23), calls=%async_computation.5 | async-start | bytes 524288 | tf_op jit(solution)/shard_map/all_to_all | solution.py:1134
  225.8 3.8 %collective-permute-done.22 = bf16[1,128,1280]{2,1,0:T(8,128)(2,1)S(1)} collective-permute-done((bf16[1,128,1280]{2,1,0:T(8,128)(2,1)S(1)}, bf16[1,128,1280]{2,1,0:T(8,128)(2,1)S(1)}, u32[]{:S(2)}, u32[]{:S(2)}) %collective-permute-start.22) | collective-permute-done | bytes 327712 | tf_op jit(solution)/shard_map/ppermute | solution.py:903
  233.4 6.0 %finish.3 = bf16[2,128,1024]{2,1,0:T(8,128)(2,1)} custom-call(bf16[8,128,384]{2,1,0:T(8,128)(2,1)} %all-to-all-done.4.data_ref, bf16[2,128,1024]{2,1,0:T(8,128)(2,1)} %rows_ref.3, f32[256,1024]{1,0:T(8,128)} %copy-done.4, f32[1,1024]{1,0:T(1,128)} %bitcast.62, bf16[1024,1024]{1,0:T(8,128)(2,1)} %wq_ref.5, ...), custom_call_target="tpu_custom_call", output_to_operand_aliasing={{}: (7, {})} | custom-call | flops 20000000000 | bytes 1 | tf_op jit(solution)/shard_map/finish/pallas_call | solution.py:740
  (128 shorter events, 47.3 us)
Async XLA Ops:
  6.3 44.4 %all-to-all-start = ((bf16[8,256,384]{2,1,0:T(8,128)(2,1)}), bf16[8,256,384]{2,1,0:T(8,128)(2,1)S(1)}, u32[]{:S(2)}, u32[]{:S(2)}) async-start(bf16[8,256,384]{2,1,0:T(8,128)(2,1)} %get-tuple-element.126), calls=%async_computation | async-start | bytes 3145728 | tf_op jit(solution)/shard_map/all_to_all | solution.py:1134
  13.8 23.5 %collective-permute-start = (bf16[128,1024]{1,0:T(8,128)(2,1)S(1)}, bf16[128,1024]{1,0:T(8,128)(2,1)S(1)}, u32[]{:S(2)}, u32[]{:S(2)}) collective-permute-start(bf16[128,1024]{1,0:T(8,128)(2,1)S(1)} %get-tuple-element.239), channel_id=1, source_target_pairs={{0,4},{4,0},{8,12},{12,8},{16,20},{20,16},{24,28},{28,24},{1,5},{5... | collective-permute-start | bytes 786440 | tf_op jit(solution)/shard_map/ppermute | solution.py:903
  15.8 46.1 %collective-permute-start.2 = (bf16[128,1024]{1,0:T(8,128)(2,1)S(1)}, bf16[128,1024]{1,0:T(8,128)(2,1)S(1)}, u32[]{:S(2)}, u32[]{:S(2)}) collective-permute-start(bf16[128,1024]{1,0:T(8,128)(2,1)S(1)} %get-tuple-element.238), channel_id=1, source_target_pairs={{0,4},{4,0},{8,12},{12,8},{16,20},{20,16},{24,28},{28,24},{1,5},{5... | collective-permute-start | bytes 786440 | tf_op jit(solution)/shard_map/ppermute | solution.py:903
  50.7 11.2 %collective-permute-start.1 = (bf16[96,1024]{1,0:T(8,128)(2,1)}, bf16[96,1024]{1,0:T(8,128)(2,1)}, u32[]{:S(2)}, u32[]{:S(2)}) collective-permute-start(bf16[96,1024]{1,0:T(8,128)(2,1)} %get-tuple-element.130), channel_id=1, source_target_pairs={{0,16},{4,20},{8,24},{12,28},{16,0},{20,4},{24,8},{28,12},{1,17},{... | collective-permute-start | bytes 589832 | tf_op jit(solution)/shard_map/ppermute | solution.py:903
  62.0 18.7 %all-to-all-start.1 = ((bf16[8,256,128]{2,1,0:T(8,128)(2,1)}), bf16[8,256,128]{2,1,0:T(8,128)(2,1)S(1)}, u32[]{:S(2)}, u32[]{:S(2)}) async-start(bf16[8,256,128]{2,1,0:T(8,128)(2,1)} %bitcast.8), calls=%async_computation.1 | async-start | bytes 1048576 | tf_op jit(solution)/shard_map/all_to_all | solution.py:1134
  83.4 21.8 %collective-permute-start.7 = (bf16[2,256,1024]{2,1,0:T(8,128)(2,1)S(1)}, bf16[2,256,1024]{2,1,0:T(8,128)(2,1)S(1)}, u32[]{:S(2)}, u32[]{:S(2)}) collective-permute-start(bf16[2,256,1024]{2,1,0:T(8,128)(2,1)S(1)} %get-tuple-element.138.norm_ref.refs_0_), channel_id=1, source_target_pairs={{0,1},{1,0},{2,3},{3,2},{4,5},{5,4},{6,7},{7,6},{8,9},{9,8},{10,11... | collective-permute-start | bytes 3145736 | tf_op jit(solution)/shard_map/ppermute | solution.py:903
  83.5 25.7 %collective-permute-start.8 = (bf16[2,256,1024]{2,1,0:T(8,128)(2,1)S(1)}, bf16[2,256,1024]{2,1,0:T(8,128)(2,1)}, u32[]{:S(2)}, u32[]{:S(2)}) collective-permute-start(bf16[2,256,1024]{2,1,0:T(8,128)(2,1)S(1)} %get-tuple-element.138.norm_ref.refs_0_), channel_id=1, source_target_pairs={{0,4},{4,0},{8,12},{12,8},{16,20},{20,16},{24,28},{28,24},{1,5},{5... | collective-permute-start | bytes 3145736 | tf_op jit(solution)/shard_map/ppermute | solution.py:903
  85.0 19.2 %collective-permute-start.5 = (bf16[192,1024]{1,0:T(8,128)(2,1)S(1)}, bf16[192,1024]{1,0:T(8,128)(2,1)S(1)}, u32[]{:S(2)}, u32[]{:S(2)}) collective-permute-start(bf16[192,1024]{1,0:T(8,128)(2,1)S(1)} %copy-done.23), channel_id=1, source_target_pairs={{0,8},{4,12},{8,0},{12,4},{16,24},{20,28},{24,16},{28,20},{1,9},{5... | collective-permute-start | bytes 1179656 | tf_op jit(solution)/shard_map/ppermute | solution.py:903
  85.0 18.3 %collective-permute-start.6 = (bf16[160,1024]{1,0:T(8,128)(2,1)S(1)}, bf16[160,1024]{1,0:T(8,128)(2,1)S(1)}, u32[]{:S(2)}, u32[]{:S(2)}) collective-permute-start(bf16[160,1024]{1,0:T(8,128)(2,1)S(1)} %copy-done.24), channel_id=1, source_target_pairs={{0,16},{4,20},{8,24},{12,28},{16,0},{20,4},{24,8},{28,12},{1,17},{... | collective-permute-start | bytes 983048 | tf_op jit(solution)/shard_map/ppermute | solution.py:903
  109.2 9.5 %collective-permute-start.9 = (bf16[2,256,1024]{2,1,0:T(8,128)(2,1)}, bf16[2,256,1024]{2,1,0:T(8,128)(2,1)}, u32[]{:S(2)}, u32[]{:S(2)}) collective-permute-start(bf16[2,256,1024]{2,1,0:T(8,128)(2,1)} %collective-permute-done.8.refs_2_), channel_id=1, source_target_pairs={{0,1},{1,0},{2,3},{3,2},{4,5},{5,4},{6,7},{7,6},{8,9},{9,8},{10,11... | collective-permute-start | bytes 3145736 | tf_op jit(solution)/shard_map/ppermute | solution.py:903
  109.7 9.0 %collective-permute-start.11 = (bf16[256,256]{1,0:T(8,128)(2,1)S(1)}, bf16[256,256]{1,0:T(8,128)(2,1)S(1)}, u32[]{:S(2)}, u32[]{:S(2)}) collective-permute-start(bf16[256,256]{1,0:T(8,128)(2,1)S(1)} %get-tuple-element.157), channel_id=1, source_target_pairs={{0,4},{4,0},{8,12},{12,8},{16,20},{20,16},{24,28},{28,24},{1,5},{5... | collective-permute-start | bytes 393224 | tf_op jit(solution)/shard_map/ppermute | solution.py:903
  111.1 31.4 %all-to-all-start.2 = ((bf16[8,256,128]{2,1,0:T(8,128)(2,1)}), bf16[8,256,128]{2,1,0:T(8,128)(2,1)}, u32[]{:S(2)}, u32[]{:S(2)}) async-start(bf16[8,256,128]{2,1,0:T(8,128)(2,1)} %get-tuple-element.148), calls=%async_computation.2 | async-start | bytes 1048576 | tf_op jit(solution)/shard_map/all_to_all | solution.py:1134
  115.5 27.0 %collective-permute-start.13 = (bf16[384,1024]{1,0:T(8,128)(2,1)}, bf16[384,1024]{1,0:T(8,128)(2,1)}, u32[]{:S(2)}, u32[]{:S(2)}) collective-permute-start(bf16[384,1024]{1,0:T(8,128)(2,1)} %pad_maximum_fusion.1.refs_0_), channel_id=1, source_target_pairs={{0,4},{4,0},{8,12},{12,8},{16,20},{20,16},{24,28},{28,24},{1,5},{5... | collective-permute-start | bytes 2359304 | tf_op jit(solution)/shard_map/ppermute | solution.py:903
  117.2 24.2 %collective-permute-start.14 = (bf16[320,1024]{1,0:T(8,128)(2,1)}, bf16[320,1024]{1,0:T(8,128)(2,1)S(1)}, u32[]{:S(2)}, u32[]{:S(2)}) collective-permute-start(bf16[320,1024]{1,0:T(8,128)(2,1)} %pad_maximum_fusion.2), channel_id=1, source_target_pairs={{0,8},{4,12},{8,0},{12,4},{16,24},{20,28},{24,16},{28,20},{1,9},{5... | collective-permute-start | bytes 1966088 | tf_op jit(solution)/shard_map/ppermute | solution.py:903
  138.2 38.3 %collective-permute-start.15 = (bf16[4,128,1280]{2,1,0:T(8,128)(2,1)}, bf16[4,128,1280]{2,1,0:T(8,128)(2,1)S(1)}, u32[]{:S(2)}, u32[]{:S(2)}) collective-permute-start(bf16[4,128,1280]{2,1,0:T(8,128)(2,1)} %bitcast.63), channel_id=1, source_target_pairs={{0,8},{4,12},{8,0},{12,4},{16,24},{20,28},{24,16},{28,20},{1,9},{5... | collective-permute-start | bytes 3932168 | tf_op jit(solution)/shard_map/ppermute | solution.py:903
  142.5 36.7 %collective-permute-start.17 = (bf16[640,1024]{1,0:T(8,128)(2,1)}, bf16[640,1024]{1,0:T(8,128)(2,1)}, u32[]{:S(2)}, u32[]{:S(2)}) collective-permute-start(bf16[640,1024]{1,0:T(8,128)(2,1)} %pad_maximum_fusion.refs_2_), channel_id=1, source_target_pairs={{0,4},{4,0},{8,12},{12,8},{16,20},{20,16},{24,28},{28,24},{1,5},{5... | collective-permute-start | bytes 3932168 | tf_op jit(solution)/shard_map/ppermute | solution.py:903
  144.0 35.0 %collective-permute-start.16 = (bf16[4,128,1024]{2,1,0:T(8,128)(2,1)}, bf16[4,128,1024]{2,1,0:T(8,128)(2,1)}, u32[]{:S(2)}, u32[]{:S(2)}) collective-permute-start(bf16[4,128,1024]{2,1,0:T(8,128)(2,1)} %bitcast.64), channel_id=1, source_target_pairs={{0,2},{1,3},{2,0},{3,1},{4,6},{5,7},{6,4},{7,5},{8,10},{9,11},{10,... | collective-permute-start | bytes 3145736 | tf_op jit(solution)/shard_map/ppermute | solution.py:903
  152.4 32.6 %all-to-all-start.3 = ((bf16[8,128,384]{2,1,0:T(8,128)(2,1)}), bf16[8,128,384]{2,1,0:T(8,128)(2,1)}, u32[]{:S(2)}, u32[]{:S(2)}) async-start(bf16[8,128,384]{2,1,0:T(8,128)(2,1)} %attend_back.2.refs_4_), calls=%async_computation.3 | async-start | bytes 1572864 | tf_op jit(solution)/shard_map/all_to_all | solution.py:1134
  181.1 20.5 %collective-permute-start.18 = (bf16[2,128,1024]{2,1,0:T(8,128)(2,1)S(1)}, bf16[2,128,1024]{2,1,0:T(8,128)(2,1)S(1)}, u32[]{:S(2)}, u32[]{:S(2)}) collective-permute-start(bf16[2,128,1024]{2,1,0:T(8,128)(2,1)S(1)} %get-tuple-element.188), channel_id=1, source_target_pairs={{0,8},{4,12},{8,0},{12,4},{16,24},{20,28},{24,16},{28,20},{1,9},{5... | collective-permute-start | bytes 1572872 | tf_op jit(solution)/shard_map/ppermute | solution.py:903
  183.5 18.8 %collective-permute-start.19 = (bf16[2,128,1280]{2,1,0:T(8,128)(2,1)}, bf16[2,128,1280]{2,1,0:T(8,128)(2,1)S(1)}, u32[]{:S(2)}, u32[]{:S(2)}) collective-permute-start(bf16[2,128,1280]{2,1,0:T(8,128)(2,1)} %get-tuple-element.192), channel_id=1, source_target_pairs={{0,2},{1,3},{2,0},{3,1},{4,6},{5,7},{6,4},{7,5},{8,10},{9,11},{10,... | collective-permute-start | bytes 1966088 | tf_op jit(solution)/shard_map/ppermute | solution.py:903
  185.0 32.2 %all-to-all-start.4 = ((bf16[8,128,384]{2,1,0:T(8,128)(2,1)}), bf16[8,128,384]{2,1,0:T(8,128)(2,1)}, u32[]{:S(2)}, u32[]{:S(2)}) async-start(bf16[8,128,384]{2,1,0:T(8,128)(2,1)} %attend_back.3.refs_5_), calls=%async_computation.4 | async-start | bytes 1572864 | tf_op jit(solution)/shard_map/all_to_all | solution.py:1134
  206.4 23.2 %collective-permute-start.22 = (bf16[1,128,1280]{2,1,0:T(8,128)(2,1)S(1)}, bf16[1,128,1280]{2,1,0:T(8,128)(2,1)S(1)}, u32[]{:S(2)}, u32[]{:S(2)}) collective-permute-start(bf16[1,128,1280]{2,1,0:T(8,128)(2,1)S(1)} %get-tuple-element.211), channel_id=1, source_target_pairs={{0,16},{4,20},{8,24},{12,28},{16,0},{20,4},{24,8},{28,12},{1,17},{... | collective-permute-start | bytes 983048 | tf_op jit(solution)/shard_map/ppermute | solution.py:903
  211.1 28.3 %collective-permute-start.26 = (bf16[1,128,1024]{2,1,0:T(8,128)(2,1)S(1)}, bf16[1,128,1024]{2,1,0:T(8,128)(2,1)S(1)}, u32[]{:S(2)}, u32[]{:S(2)}) collective-permute-start(bf16[1,128,1024]{2,1,0:T(8,128)(2,1)S(1)} %get-tuple-element.220), channel_id=1, source_target_pairs={{0,16},{4,20},{8,24},{12,28},{16,0},{20,4},{24,8},{28,12},{1,17},{... | collective-permute-start | bytes 786440 | tf_op jit(solution)/shard_map/ppermute | solution.py:903
  218.0 21.5 %all-to-all-start.5 = ((bf16[8,32,512]{2,1,0:T(8,128)(2,1)}), bf16[8,32,512]{2,1,0:T(8,128)(2,1)S(1)}, u32[]{:S(2)}, u32[]{:S(2)}) async-start(bf16[8,32,512]{2,1,0:T(8,128)(2,1)} %bitcast.23), calls=%async_computation.5 | async-start | bytes 524288 | tf_op jit(solution)/shard_map/all_to_all | solution.py:1134
  (39 other events, 436.2 us)

commit v8 on v7

--- a/solution.py
+++ b/solution.py
@@ -482,7 +482,7 @@
             jax.ShapeDtypeStruct((blocks, micro_count, tokens, slot), jnp.float32),
             jax.ShapeDtypeStruct((micro_count, 8, blocks * tokens), jnp.float32),
         ],
-        compiler_params=_params(32),
+        compiler_params=_params(36),
         cost_estimate=_cost(11),
         name="attend",
     )(lengths, received)

time: 242 us -> 242 us (level)
  no operation moved by 1% of the time
where the time goes in v8:
time: 242 us; the launch traced here: 241 us
  Pallas kernels  97.1 us (40%)
  waiting for transfers between devices  67.2 us (28%)
  starting transfers between devices  61.5 us (25%)
  local copies, waits for them, and re-layouts  9.62 us (4%)
  other arithmetic  4.84 us (2%)
    ppermute x25, waiting for transfers between devices, _paired(): return lax.ppermute(values, axis, [(i, i ^ bit) for i in range(count)])  44.5 us
    all_to_all x6, starting transfers between devices, swap(): lax.all_to_all(values, 'blk', split_axis=0, concat_axis=0, tiled=True)  34.2 us
    ppermute x25, starting transfers between devices, _paired(): return lax.ppermute(values, axis, [(i, i ^ bit) for i in range(count)])  26.2 us
    all_to_all x6, waiting for transfers between devices, swap(): lax.all_to_all(values, 'blk', split_axis=0, concat_axis=0, tiled=True)  22.8 us
    pallas_call x1, Pallas kernels, grad_middle_call(): pl.pallas_call(kernel, grid_spec=pltpu.PrefetchScalarGridSpec(num_scalar_...  19.5 us
    pallas_call x2, Pallas kernels, attend_back_call(): pl.pallas_call(kernel, grid=(steps,), in_specs=[pl.BlockSpec(memory_space...  17.2 us
    pallas_call x1, Pallas kernels, middle_call(): pl.pallas_call(kernel, grid_spec=pltpu.PrefetchScalarGridSpec(num_scalar_...  15.2 us
    pallas_call x2, Pallas kernels, finish_call(): pl.pallas_call(kernel, grid=(steps,), in_specs=[pl.BlockSpec((per_step, r...  11.9 us
  transfers between devices with their start and end apart: 33, of which 11 were waited for; matrix products, arithmetic and copies ran while one was open for 3% of the time, Pallas kernels for 37%

profile of v8, /device:TPU:0, one launch (start us, length us, event | category | flops | bytes accessed | tf_op | source)
XLA Modules:
  0.0 241.2 jit_solution(173757660222281343)
XLA Ops:
  0.6 5.7 %project.1 = (bf16[8,256,384]{2,1,0:T(8,128)(2,1)}, bf16[96,1024]{1,0:T(8,128)(2,1)}, bf16[160,1024]{1,0:T(8,128)(2,1)}) custom-call(bf16[256,1024]{1,0:T(8,128)(2,1)} %bitcast.43, f32[1,1024]{1,0:T(1,128)} %bitcast.59, f32[1,1024]{1,0:T(1,128)} %bitcast.65, bf16[1024,1024]{1,0:T(8,128)(2,1)} %wq_ref.5, bf16[1024,1024]{1,0:T(8,128)(2,1)} %wk_ref.5, ...), custom_call_target="tpu_custom_call" | custom-call | flops 6000000000 | bytes 1 | tf_op jit(solution)/shard_map/project/pallas_call | solution.py:381
  6.3 7.4 %all-to-all-start = ((bf16[8,256,384]{2,1,0:T(8,128)(2,1)}), bf16[8,256,384]{2,1,0:T(8,128)(2,1)S(1)}, u32[]{:S(2)}, u32[]{:S(2)}) async-start(bf16[8,256,384]{2,1,0:T(8,128)(2,1)} %get-tuple-element.126), calls=%async_computation | async-start | bytes 3145728 | tf_op jit(solution)/shard_map/all_to_all | solution.py:1134
  15.9 21.3 %collective-permute-done = bf16[128,1024]{1,0:T(8,128)(2,1)S(1)} collective-permute-done((bf16[128,1024]{1,0:T(8,128)(2,1)S(1)}, bf16[128,1024]{1,0:T(8,128)(2,1)S(1)}, u32[]{:S(2)}, u32[]{:S(2)}) %collective-permute-start) | collective-permute-done | bytes 262176 | tf_op jit(solution)/shard_map/ppermute | solution.py:903
  37.2 13.5 %all-to-all-done = bf16[8,256,384]{2,1,0:T(8,128)(2,1)S(1)} async-done(((bf16[8,256,384]{2,1,0:T(8,128)(2,1)}), bf16[8,256,384]{2,1,0:T(8,128)(2,1)S(1)}, u32[]{:S(2)}, u32[]{:S(2)}) %all-to-all-start) | async-done | bytes 1572896 | tf_op jit(solution)/shard_map/all_to_all | solution.py:1134
  50.7 9.5 %attend.1 = (bf16[8,2,128,128]{3,2,1,0:T(8,128)(2,1)}, f32[8,2,128,128]{3,2,1,0:T(8,128)S(1)}, f32[2,8,1024]{2,1,0:T(8,128)S(1)}) custom-call(s32[2,8]{1,0:T(2,128)S(1)} %copy-done.10, bf16[8,2,128,384]{3,2,1,0:T(8,128)(2,1)S(1)} %bitcast.36), custom_call_target="tpu_custom_call" | custom-call | flops 11000000512 | bytes 1 | tf_op jit(solution)/shard_map/attend/pallas_call | solution.py:468
  62.0 5.2 %all-to-all-start.1 = ((bf16[8,256,128]{2,1,0:T(8,128)(2,1)}), bf16[8,256,128]{2,1,0:T(8,128)(2,1)S(1)}, u32[]{:S(2)}, u32[]{:S(2)}) async-start(bf16[8,256,128]{2,1,0:T(8,128)(2,1)} %bitcast.8), calls=%async_computation.1 | async-start | bytes 1048576 | tf_op jit(solution)/shard_map/all_to_all | solution.py:1134
  71.6 9.1 %all-to-all-done.1.att_ref = bf16[8,256,128]{2,1,0:T(8,128)(2,1)S(1)} async-done(((bf16[8,256,128]{2,1,0:T(8,128)(2,1)}), bf16[8,256,128]{2,1,0:T(8,128)(2,1)S(1)}, u32[]{:S(2)}, u32[]{:S(2)}) %all-to-all-start.1) | async-done | bytes 524320 | tf_op jit(solution)/shard_map/all_to_all | solution.py:1134
  87.1 15.2 %middle.1 = (bf16[256,1024]{1,0:T(8,128)(2,1)}, f32[256,1024]{1,0:T(8,128)S(1)}, bf16[8,256,128]{2,1,0:T(8,128)(2,1)}, f32[2,1024]{1,0:T(2,128)S(1)}, bf16[256,2...) custom-call(s32[3]{0:T(128)S(1)} %pad_add_fusion.place_ref, ...), custom_call_target="tpu_custom_call" | custom-call | flops 20000000000 | bytes 1 | tf_op jit(solution)/shard_map/middle/pallas_call | solution.py:669
  105.2 4.0 %collective-permute-done.8.refs_2_ = bf16[2,256,1024]{2,1,0:T(8,128)(2,1)} collective-permute-done((bf16[2,256,1024]{2,1,0:T(8,128)(2,1)S(1)}, bf16[2,256,1024]{2,1,0:T(8,128)(2,1)}, u32[]{:S(2)}, u32[]{:S(2)}) %collective-permute-start.8) | collective-permute-done | bytes 1048608 | tf_op jit(solution)/shard_map/ppermute | solution.py:903
  111.1 4.3 %all-to-all-start.2 = ((bf16[8,256,128]{2,1,0:T(8,128)(2,1)}), bf16[8,256,128]{2,1,0:T(8,128)(2,1)}, u32[]{:S(2)}, u32[]{:S(2)}) async-start(bf16[8,256,128]{2,1,0:T(8,128)(2,1)} %get-tuple-element.148), calls=%async_computation.2 | async-start | bytes 1048576 | tf_op jit(solution)/shard_map/all_to_all | solution.py:1134
  118.7 19.5 %grad_middle.1 = (bf16[512,1024]{1,0:T(8,128)(2,1)}, f32[512,1024]{1,0:T(8,128)}, bf16[512,1280]{1,0:T(8,128)(2,1)}, f32[512,1280]{1,0:T(8,128)}) custom-call(s32[3]{0:T(128)S(1)} %pad_add_fusion.place_ref, bf16[2,256,1024]{2,1,0:T(8,128)(2,1)} %copy-done.15, bf16[2,256,1024]{2,1,0:T(8,128)(2,1)} %copy-done.28, ...), custom_call_target="tpu_custom_call" | custom-call | flops 20000000000 | bytes 1 | tf_op jit(solution)/shard_map/grad_middle/pallas_call | solution.py:1015
  138.8 2.6 %collective-permute-done.14 = bf16[320,1024]{1,0:T(8,128)(2,1)S(1)} collective-permute-done((bf16[320,1024]{1,0:T(8,128)(2,1)}, bf16[320,1024]{1,0:T(8,128)(2,1)S(1)}, u32[]{:S(2)}, u32[]{:S(2)}) %collective-permute-start.14) | collective-permute-done | bytes 655392 | tf_op jit(solution)/shard_map/ppermute | solution.py:903
  145.6 6.9 %attend_back.2.refs_4_ = bf16[8,128,384]{2,1,0:T(8,128)(2,1)} custom-call(s32[2,8]{1,0:T(2,128)} %lengths_ref.5, bf16[8,2,128,384]{3,2,1,0:T(8,128)(2,1)} %bitcast.37, bf16[8,2,128,128]{3,2,1,0:T(8,128)(2,1)} %bitcast.14.grads_ref, f32[8,2,128,128]{3,2,1,0:T(8,128)} %copy-done.3, f32[2,8,1024]{2,1,0:T(8,128)} %copy-done.7), custom_call_target="tpu_custom_call" | custom-call | flops 1 | bytes 1 | tf_op jit(solution)/shard_map/attend_back/pallas_call | solution.py:564
  152.4 4.4 %all-to-all-start.3 = ((bf16[8,128,384]{2,1,0:T(8,128)(2,1)}), bf16[8,128,384]{2,1,0:T(8,128)(2,1)}, u32[]{:S(2)}, u32[]{:S(2)}) async-start(bf16[8,128,384]{2,1,0:T(8,128)(2,1)} %attend_back.2.refs_4_), calls=%async_computation.3 | async-start | bytes 1572864 | tf_op jit(solution)/shard_map/all_to_all | solution.py:1134
  156.9 10.3 %attend_back.3.refs_5_ = bf16[8,128,384]{2,1,0:T(8,128)(2,1)} custom-call(s32[2,8]{1,0:T(2,128)} %lengths_ref.5, bf16[8,2,128,384]{3,2,1,0:T(8,128)(2,1)} %bitcast.38, bf16[8,2,128,128]{3,2,1,0:T(8,128)(2,1)} %bitcast.14.grads_ref, f32[8,2,128,128]{3,2,1,0:T(8,128)} %copy-done.3, f32[2,8,1024]{2,1,0:T(8,128)} %copy-done.7), custom_call_target="tpu_custom_call" | custom-call | flops 3000000000 | bytes 1 | tf_op jit(solution)/shard_map/attend_back/pallas_call | solution.py:564
  167.2 9.3 %collective-permute-done.15.got_theirs.got_mine = bf16[4,128,1280]{2,1,0:T(8,128)(2,1)S(1)} collective-permute-done((bf16[4,128,1280]{2,1,0:T(8,128)(2,1)}, bf16[4,128,1280]{2,1,0:T(8,128)(2,1)S(1)}, u32[]{:S(2)}, u32[]{:S(2)}) %collective-permute-start.15) | collective-permute-done | bytes 1310752 | tf_op jit(solution)/shard_map/ppermute | solution.py:903
  185.0 5.0 %all-to-all-start.4 = ((bf16[8,128,384]{2,1,0:T(8,128)(2,1)}), bf16[8,128,384]{2,1,0:T(8,128)(2,1)}, u32[]{:S(2)}, u32[]{:S(2)}) async-start(bf16[8,128,384]{2,1,0:T(8,128)(2,1)} %attend_back.3.refs_5_), calls=%async_computation.4 | async-start | bytes 1572864 | tf_op jit(solution)/shard_map/all_to_all | solution.py:1134
  190.1 8.5 %grad_heads.1 = (bf16[2,8,32,512]{3,2,1,0:T(8,128)(2,1)}, f32[2,8,32,512]{3,2,1,0:T(8,128)}) custom-call(s32[3]{0:T(128)} %copy-done.8, bf16[384,1024]{1,0:T(8,128)(2,1)} %pad_maximum_fusion.1.refs_0_, bf16[384,1024]{1,0:T(8,128)(2,1)} %collective-permute-done.13.refs_1_, bf16[640,1024]{1,0:T(8,128)(2,1)} %pad_maximum_fusion.refs_2_, ...), custom_call_target="tpu_custom_call" | custom-call | flops 20000000000 | bytes 1 | tf_op jit(solution)/shard_map/grad_heads/pallas_call | solution.py:818
  198.6 3.1 %collective-permute-done.18.got_theirs.got_mine = bf16[2,128,1024]{2,1,0:T(8,128)(2,1)S(1)} collective-permute-done((bf16[2,128,1024]{2,1,0:T(8,128)(2,1)S(1)}, bf16[2,128,1024]{2,1,0:T(8,128)(2,1)S(1)}, u32[]{:S(2)}, u32[]{:S(2)}) %collective-permute-start.18) | collective-permute-done | bytes 524320 | tf_op jit(solution)/shard_map/ppermute | solution.py:903
  206.4 4.6 %collective-permute-start.22 = (bf16[1,128,1280]{2,1,0:T(8,128)(2,1)S(1)}, bf16[1,128,1280]{2,1,0:T(8,128)(2,1)S(1)}, u32[]{:S(2)}, u32[]{:S(2)}) collective-permute-start(bf16[1,128,1280]{2,1,0:T(8,128)(2,1)S(1)} %get-tuple-element.211), channel_id=1, source_target_pairs={{0,16},{4,20},{8,24},{12,28},{16,0},{20,4},{24,8},{28,12},{1,17},{... | collective-permute-start | bytes 983048 | tf_op jit(solution)/shard_map/ppermute | solution.py:903
  211.3 6.0 %finish.2.refs_0_ = bf16[2,128,1024]{2,1,0:T(8,128)(2,1)} custom-call(bf16[8,128,384]{2,1,0:T(8,128)(2,1)} %all-to-all-done.3.data_ref, bf16[2,128,1024]{2,1,0:T(8,128)(2,1)} %rows_ref.3, f32[256,1024]{1,0:T(8,128)} %copy-done.4, f32[1,1024]{1,0:T(1,128)} %bitcast.61, bf16[1024,1024]{1,0:T(8,128)(2,1)} %wq_ref.5, bf16[1024,1024]{1,0:T(8,128)(2,1)} %wk_ref.5, ...), custom_call_target="tpu_custom_call" | custom-call | flops 1 | bytes 1 | tf_op jit(solution)/shard_map/finish/pallas_call | solution.py:740
  218.0 7.8 %all-to-all-start.5 = ((bf16[8,32,512]{2,1,0:T(8,128)(2,1)}), bf16[8,32,512]{2,1,0:T(8,128)(2,1)S(1)}, u32[]{:S(2)}, u32[]{:S(2)}) async-start(bf16[8,32,512]{2,1,0:T(8,128)(2,1)} %bitcast.23), calls=%async_computation.5 | async-start | bytes 524288 | tf_op jit(solution)/shard_map/all_to_all | solution.py:1134
  225.8 3.8 %collective-permute-done.22 = bf16[1,128,1280]{2,1,0:T(8,128)(2,1)S(1)} collective-permute-done((bf16[1,128,1280]{2,1,0:T(8,128)(2,1)S(1)}, bf16[1,128,1280]{2,1,0:T(8,128)(2,1)S(1)}, u32[]{:S(2)}, u32[]{:S(2)}) %collective-permute-start.22) | collective-permute-done | bytes 327712 | tf_op jit(solution)/shard_map/ppermute | solution.py:903
  233.4 6.0 %finish.3 = bf16[2,128,1024]{2,1,0:T(8,128)(2,1)} custom-call(bf16[8,128,384]{2,1,0:T(8,128)(2,1)} %all-to-all-done.4.data_ref, bf16[2,128,1024]{2,1,0:T(8,128)(2,1)} %rows_ref.3, f32[256,1024]{1,0:T(8,128)} %copy-done.4, f32[1,1024]{1,0:T(1,128)} %bitcast.62, bf16[1024,1024]{1,0:T(8,128)(2,1)} %wq_ref.5, ...), custom_call_target="tpu_custom_call", output_to_operand_aliasing={{}: (7, {})} | custom-call | flops 20000000000 | bytes 1 | tf_op jit(solution)/shard_map/finish/pallas_call | solution.py:740
  (128 shorter events, 47.3 us)
Async XLA Ops:
  6.3 44.4 %all-to-all-start = ((bf16[8,256,384]{2,1,0:T(8,128)(2,1)}), bf16[8,256,384]{2,1,0:T(8,128)(2,1)S(1)}, u32[]{:S(2)}, u32[]{:S(2)}) async-start(bf16[8,256,384]{2,1,0:T(8,128)(2,1)} %get-tuple-element.126), calls=%async_computation | async-start | bytes 3145728 | tf_op jit(solution)/shard_map/all_to_all | solution.py:1134
  13.8 23.5 %collective-permute-start = (bf16[128,1024]{1,0:T(8,128)(2,1)S(1)}, bf16[128,1024]{1,0:T(8,128)(2,1)S(1)}, u32[]{:S(2)}, u32[]{:S(2)}) collective-permute-start(bf16[128,1024]{1,0:T(8,128)(2,1)S(1)} %get-tuple-element.239), channel_id=1, source_target_pairs={{0,4},{4,0},{8,12},{12,8},{16,20},{20,16},{24,28},{28,24},{1,5},{5... | collective-permute-start | bytes 786440 | tf_op jit(solution)/shard_map/ppermute | solution.py:903
  15.8 46.1 %collective-permute-start.2 = (bf16[128,1024]{1,0:T(8,128)(2,1)S(1)}, bf16[128,1024]{1,0:T(8,128)(2,1)S(1)}, u32[]{:S(2)}, u32[]{:S(2)}) collective-permute-start(bf16[128,1024]{1,0:T(8,128)(2,1)S(1)} %get-tuple-element.238), channel_id=1, source_target_pairs={{0,4},{4,0},{8,12},{12,8},{16,20},{20,16},{24,28},{28,24},{1,5},{5... | collective-permute-start | bytes 786440 | tf_op jit(solution)/shard_map/ppermute | solution.py:903
  50.7 11.2 %collective-permute-start.1 = (bf16[96,1024]{1,0:T(8,128)(2,1)}, bf16[96,1024]{1,0:T(8,128)(2,1)}, u32[]{:S(2)}, u32[]{:S(2)}) collective-permute-start(bf16[96,1024]{1,0:T(8,128)(2,1)} %get-tuple-element.130), channel_id=1, source_target_pairs={{0,16},{4,20},{8,24},{12,28},{16,0},{20,4},{24,8},{28,12},{1,17},{... | collective-permute-start | bytes 589832 | tf_op jit(solution)/shard_map/ppermute | solution.py:903
  62.0 18.7 %all-to-all-start.1 = ((bf16[8,256,128]{2,1,0:T(8,128)(2,1)}), bf16[8,256,128]{2,1,0:T(8,128)(2,1)S(1)}, u32[]{:S(2)}, u32[]{:S(2)}) async-start(bf16[8,256,128]{2,1,0:T(8,128)(2,1)} %bitcast.8), calls=%async_computation.1 | async-start | bytes 1048576 | tf_op jit(solution)/shard_map/all_to_all | solution.py:1134
  83.4 21.8 %collective-permute-start.7 = (bf16[2,256,1024]{2,1,0:T(8,128)(2,1)S(1)}, bf16[2,256,1024]{2,1,0:T(8,128)(2,1)S(1)}, u32[]{:S(2)}, u32[]{:S(2)}) collective-permute-start(bf16[2,256,1024]{2,1,0:T(8,128)(2,1)S(1)} %get-tuple-element.138.norm_ref.refs_0_), channel_id=1, source_target_pairs={{0,1},{1,0},{2,3},{3,2},{4,5},{5,4},{6,7},{7,6},{8,9},{9,8},{10,11... | collective-permute-start | bytes 3145736 | tf_op jit(solution)/shard_map/ppermute | solution.py:903
  83.5 25.7 %collective-permute-start.8 = (bf16[2,256,1024]{2,1,0:T(8,128)(2,1)S(1)}, bf16[2,256,1024]{2,1,0:T(8,128)(2,1)}, u32[]{:S(2)}, u32[]{:S(2)}) collective-permute-start(bf16[2,256,1024]{2,1,0:T(8,128)(2,1)S(1)} %get-tuple-element.138.norm_ref.refs_0_), channel_id=1, source_target_pairs={{0,4},{4,0},{8,12},{12,8},{16,20},{20,16},{24,28},{28,24},{1,5},{5... | collective-permute-start | bytes 3145736 | tf_op jit(solution)/shard_map/ppermute | solution.py:903
  85.0 19.2 %collective-permute-start.5 = (bf16[192,1024]{1,0:T(8,128)(2,1)S(1)}, bf16[192,1024]{1,0:T(8,128)(2,1)S(1)}, u32[]{:S(2)}, u32[]{:S(2)}) collective-permute-start(bf16[192,1024]{1,0:T(8,128)(2,1)S(1)} %copy-done.23), channel_id=1, source_target_pairs={{0,8},{4,12},{8,0},{12,4},{16,24},{20,28},{24,16},{28,20},{1,9},{5... | collective-permute-start | bytes 1179656 | tf_op jit(solution)/shard_map/ppermute | solution.py:903
  85.0 18.3 %collective-permute-start.6 = (bf16[160,1024]{1,0:T(8,128)(2,1)S(1)}, bf16[160,1024]{1,0:T(8,128)(2,1)S(1)}, u32[]{:S(2)}, u32[]{:S(2)}) collective-permute-start(bf16[160,1024]{1,0:T(8,128)(2,1)S(1)} %copy-done.24), channel_id=1, source_target_pairs={{0,16},{4,20},{8,24},{12,28},{16,0},{20,4},{24,8},{28,12},{1,17},{... | collective-permute-start | bytes 983048 | tf_op jit(solution)/shard_map/ppermute | solution.py:903
  109.2 9.5 %collective-permute-start.9 = (bf16[2,256,1024]{2,1,0:T(8,128)(2,1)}, bf16[2,256,1024]{2,1,0:T(8,128)(2,1)}, u32[]{:S(2)}, u32[]{:S(2)}) collective-permute-start(bf16[2,256,1024]{2,1,0:T(8,128)(2,1)} %collective-permute-done.8.refs_2_), channel_id=1, source_target_pairs={{0,1},{1,0},{2,3},{3,2},{4,5},{5,4},{6,7},{7,6},{8,9},{9,8},{10,11... | collective-permute-start | bytes 3145736 | tf_op jit(solution)/shard_map/ppermute | solution.py:903
  109.7 9.0 %collective-permute-start.11 = (bf16[256,256]{1,0:T(8,128)(2,1)S(1)}, bf16[256,256]{1,0:T(8,128)(2,1)S(1)}, u32[]{:S(2)}, u32[]{:S(2)}) collective-permute-start(bf16[256,256]{1,0:T(8,128)(2,1)S(1)} %get-tuple-element.157), channel_id=1, source_target_pairs={{0,4},{4,0},{8,12},{12,8},{16,20},{20,16},{24,28},{28,24},{1,5},{5... | collective-permute-start | bytes 393224 | tf_op jit(solution)/shard_map/ppermute | solution.py:903
  111.1 31.4 %all-to-all-start.2 = ((bf16[8,256,128]{2,1,0:T(8,128)(2,1)}), bf16[8,256,128]{2,1,0:T(8,128)(2,1)}, u32[]{:S(2)}, u32[]{:S(2)}) async-start(bf16[8,256,128]{2,1,0:T(8,128)(2,1)} %get-tuple-element.148), calls=%async_computation.2 | async-start | bytes 1048576 | tf_op jit(solution)/shard_map/all_to_all | solution.py:1134
  115.5 27.0 %collective-permute-start.13 = (bf16[384,1024]{1,0:T(8,128)(2,1)}, bf16[384,1024]{1,0:T(8,128)(2,1)}, u32[]{:S(2)}, u32[]{:S(2)}) collective-permute-start(bf16[384,1024]{1,0:T(8,128)(2,1)} %pad_maximum_fusion.1.refs_0_), channel_id=1, source_target_pairs={{0,4},{4,0},{8,12},{12,8},{16,20},{20,16},{24,28},{28,24},{1,5},{5... | collective-permute-start | bytes 2359304 | tf_op jit(solution)/shard_map/ppermute | solution.py:903
  117.2 24.2 %collective-permute-start.14 = (bf16[320,1024]{1,0:T(8,128)(2,1)}, bf16[320,1024]{1,0:T(8,128)(2,1)S(1)}, u32[]{:S(2)}, u32[]{:S(2)}) collective-permute-start(bf16[320,1024]{1,0:T(8,128)(2,1)} %pad_maximum_fusion.2), channel_id=1, source_target_pairs={{0,8},{4,12},{8,0},{12,4},{16,24},{20,28},{24,16},{28,20},{1,9},{5... | collective-permute-start | bytes 1966088 | tf_op jit(solution)/shard_map/ppermute | solution.py:903
  138.2 38.3 %collective-permute-start.15 = (bf16[4,128,1280]{2,1,0:T(8,128)(2,1)}, bf16[4,128,1280]{2,1,0:T(8,128)(2,1)S(1)}, u32[]{:S(2)}, u32[]{:S(2)}) collective-permute-start(bf16[4,128,1280]{2,1,0:T(8,128)(2,1)} %bitcast.63), channel_id=1, source_target_pairs={{0,8},{4,12},{8,0},{12,4},{16,24},{20,28},{24,16},{28,20},{1,9},{5... | collective-permute-start | bytes 3932168 | tf_op jit(solution)/shard_map/ppermute | solution.py:903
  142.5 36.7 %collective-permute-start.17 = (bf16[640,1024]{1,0:T(8,128)(2,1)}, bf16[640,1024]{1,0:T(8,128)(2,1)}, u32[]{:S(2)}, u32[]{:S(2)}) collective-permute-start(bf16[640,1024]{1,0:T(8,128)(2,1)} %pad_maximum_fusion.refs_2_), channel_id=1, source_target_pairs={{0,4},{4,0},{8,12},{12,8},{16,20},{20,16},{24,28},{28,24},{1,5},{5... | collective-permute-start | bytes 3932168 | tf_op jit(solution)/shard_map/ppermute | solution.py:903
  144.0 35.0 %collective-permute-start.16 = (bf16[4,128,1024]{2,1,0:T(8,128)(2,1)}, bf16[4,128,1024]{2,1,0:T(8,128)(2,1)}, u32[]{:S(2)}, u32[]{:S(2)}) collective-permute-start(bf16[4,128,1024]{2,1,0:T(8,128)(2,1)} %bitcast.64), channel_id=1, source_target_pairs={{0,2},{1,3},{2,0},{3,1},{4,6},{5,7},{6,4},{7,5},{8,10},{9,11},{10,... | collective-permute-start | bytes 3145736 | tf_op jit(solution)/shard_map/ppermute | solution.py:903
  152.4 32.6 %all-to-all-start.3 = ((bf16[8,128,384]{2,1,0:T(8,128)(2,1)}), bf16[8,128,384]{2,1,0:T(8,128)(2,1)}, u32[]{:S(2)}, u32[]{:S(2)}) async-start(bf16[8,128,384]{2,1,0:T(8,128)(2,1)} %attend_back.2.refs_4_), calls=%async_computation.3 | async-start | bytes 1572864 | tf_op jit(solution)/shard_map/all_to_all | solution.py:1134
  181.1 20.5 %collective-permute-start.18 = (bf16[2,128,1024]{2,1,0:T(8,128)(2,1)S(1)}, bf16[2,128,1024]{2,1,0:T(8,128)(2,1)S(1)}, u32[]{:S(2)}, u32[]{:S(2)}) collective-permute-start(bf16[2,128,1024]{2,1,0:T(8,128)(2,1)S(1)} %get-tuple-element.188), channel_id=1, source_target_pairs={{0,8},{4,12},{8,0},{12,4},{16,24},{20,28},{24,16},{28,20},{1,9},{5... | collective-permute-start | bytes 1572872 | tf_op jit(solution)/shard_map/ppermute | solution.py:903
  183.5 18.8 %collective-permute-start.19 = (bf16[2,128,1280]{2,1,0:T(8,128)(2,1)}, bf16[2,128,1280]{2,1,0:T(8,128)(2,1)S(1)}, u32[]{:S(2)}, u32[]{:S(2)}) collective-permute-start(bf16[2,128,1280]{2,1,0:T(8,128)(2,1)} %get-tuple-element.192), channel_id=1, source_target_pairs={{0,2},{1,3},{2,0},{3,1},{4,6},{5,7},{6,4},{7,5},{8,10},{9,11},{10,... | collective-permute-start | bytes 1966088 | tf_op jit(solution)/shard_map/ppermute | solution.py:903
  185.0 32.2 %all-to-all-start.4 = ((bf16[8,128,384]{2,1,0:T(8,128)(2,1)}), bf16[8,128,384]{2,1,0:T(8,128)(2,1)}, u32[]{:S(2)}, u32[]{:S(2)}) async-start(bf16[8,128,384]{2,1,0:T(8,128)(2,1)} %attend_back.3.refs_5_), calls=%async_computation.4 | async-start | bytes 1572864 | tf_op jit(solution)/shard_map/all_to_all | solution.py:1134
  206.4 23.2 %collective-permute-start.22 = (bf16[1,128,1280]{2,1,0:T(8,128)(2,1)S(1)}, bf16[1,128,1280]{2,1,0:T(8,128)(2,1)S(1)}, u32[]{:S(2)}, u32[]{:S(2)}) collective-permute-start(bf16[1,128,1280]{2,1,0:T(8,128)(2,1)S(1)} %get-tuple-element.211), channel_id=1, source_target_pairs={{0,16},{4,20},{8,24},{12,28},{16,0},{20,4},{24,8},{28,12},{1,17},{... | collective-permute-start | bytes 983048 | tf_op jit(solution)/shard_map/ppermute | solution.py:903
  211.1 28.3 %collective-permute-start.26 = (bf16[1,128,1024]{2,1,0:T(8,128)(2,1)S(1)}, bf16[1,128,1024]{2,1,0:T(8,128)(2,1)S(1)}, u32[]{:S(2)}, u32[]{:S(2)}) collective-permute-start(bf16[1,128,1024]{2,1,0:T(8,128)(2,1)S(1)} %get-tuple-element.220), channel_id=1, source_target_pairs={{0,16},{4,20},{8,24},{12,28},{16,0},{20,4},{24,8},{28,12},{1,17},{... | collective-permute-start | bytes 786440 | tf_op jit(solution)/shard_map/ppermute | solution.py:903
  218.0 21.5 %all-to-all-start.5 = ((bf16[8,32,512]{2,1,0:T(8,128)(2,1)}), bf16[8,32,512]{2,1,0:T(8,128)(2,1)S(1)}, u32[]{:S(2)}, u32[]{:S(2)}) async-start(bf16[8,32,512]{2,1,0:T(8,128)(2,1)} %bitcast.23), calls=%async_computation.5 | async-start | bytes 524288 | tf_op jit(solution)/shard_map/all_to_all | solution.py:1134
  (39 other events, 436.2 us)
